TPU v7x, 32 devices: a whole 2x2x4 slice. The times are simulated.
32 devices in a mesh: slab: 2 (over x), line: 8 (over z, y), band: 2 (over core).
Axes of the slice: x: 2, y: 2, z: 4, core: 2. Of those that a mesh axis runs over, the one named last changes fastest.
Arguments:
- cube: bfloat16 [230, 2048, 256], P('band', ('slab', 'line')), parts along dimension 1, may hold values from -6 to 6
- observed: bfloat16 [13, 2048, 256], P(None, ('slab', 'line')), parts along dimension 1, may hold values from -6 to 6
- along_kernels: bfloat16 [3, 128, 128], replicated, may hold values from -0.3125 to 0.3125
- along_offsets: int32 [3], replicated, may hold values from -1 to 1, as said below
- across_kernels: bfloat16 [3, 128, 128], replicated, may hold values from -0.3125 to 0.3125
- across_offsets: int32 [3], replicated, may hold values from -1 to 1, as said below
- resp_start: int32 [13], replicated, may hold values from 0 to 21
- resp_values: bfloat16 [13, 20], replicated, may hold values from 0.049804688 to 0.3984375
Outputs:
- synthetic: float32 [13, 2048, 256], P(None, ('slab', 'line')), parts along dimension 1
- angles: float32 [2048, 256], P(('slab', 'line')), parts along dimension 0
There are 2 independent parts, one for each index of `slab`. A program takes and returns all parts, laid end to end along the dimension named above; an argument that names none is the same for every part. Nothing has to cross between parts.
Inputs may be any that keep to these rules, and one draw needn't show every extreme that they name: `along_offsets`: the three entries are -1, 0 and 1, each once. `across_offsets`: the three entries are -1, 0 and 1, each once.
All inputs are finite; a program needn't handle non-finite values.
Results may differ from a plain program's by a relative error of at most 0.0003.
Values may be sent and summed in bfloat16 or wider, within the bound.
No kernel may reach another device: no remote copies, remote signals or barrier semaphores. Data moves between devices by JAX's collectives and lax.ppermute only.
A program may use at most 192 MiB of HBM per device.

v0:
```python
import functools
import math

import jax
import jax.numpy as jnp
from jax import lax
from jax.experimental import pallas as pl
from jax.experimental.pallas import tpu as pltpu
from jax.sharding import PartitionSpec as P

BLK = 128
SPB = 10
STEPS = 16.0
PEAK = 32000.0


def which(offsets, shift):
    return sum(
        jnp.where(offsets[k] == shift, jnp.int32(k), jnp.int32(0)) for k in range(offsets.shape[0])
    )


def split(value):
    high = value.astype(jnp.bfloat16)
    low = (value - high.astype(jnp.float32)).astype(jnp.bfloat16)
    return high, low


SMEM = pl.BlockSpec(memory_space=pltpu.SMEM)
VMEM = pl.BlockSpec(memory_space=pltpu.VMEM)
HBM = pl.BlockSpec(memory_space=pltpu.HBM)
ROWS = 64


def call(kernel, inputs, specs, outs, scratch=(), out_specs=None, aliases=None, flops=0):
    moved = sum(x.size * x.dtype.itemsize for x in (*inputs, *outs))
    return pl.pallas_call(
        kernel,
        in_specs=specs,
        out_specs=out_specs or [VMEM] * len(outs),
        out_shape=outs,
        scratch_shapes=scratch,
        input_output_aliases=aliases or {},
        compiler_params=pltpu.CompilerParams(vmem_limit_bytes=32 * 2**20),
        cost_estimate=pl.CostEstimate(flops=flops, bytes_accessed=moved, transcendentals=0),
        name=(kernel.func if isinstance(kernel, functools.partial) else kernel).__name__,
    )(*inputs)


def ownership(count):
    pairs = count // 2
    return pairs, count % 2, 2 * pairs + count % 2


def units_of(core, count):
    pairs, odd, _ = ownership(count)
    first = core * (pairs + odd)
    return [(first + i, c) for i in range(pairs) for c in range(2)] + [(pairs, core)] * odd


def fold(
    start_in,
    offsets_in,
    values_in,
    blocks_in,
    cube_in,
    keep,
    send,
    start,
    offsets,
    values,
    wide,
    weights,
    blocks,
    cube,
    folded,
    table,
    order,
    small,
    large,
):
    bands, lines, cols = cube.shape
    count, window = values.shape
    half = cols // 2
    group = math.gcd(SPB, bands)
    me = lax.axis_index("band")
    pairs = ((start_in, start), (values_in, values), (offsets_in, offsets), (blocks_in, blocks))
    copies = [pltpu.make_async_copy(a, b, small.at[i]) for i, (a, b) in enumerate(pairs)]

    def arrive(q):
        at = pl.ds(q * group, group)
        return pltpu.make_async_copy(cube_in.at[at], cube.at[at], large.at[q])

    for copy in copies:
        copy.start()
    for q in range(bands // group):
        arrive(q).start()
    copies[1].wait()
    wide[...] = values[...].astype(jnp.float32)
    spread = pltpu.make_async_copy(wide, weights, small.at[len(pairs)])
    spread.start()
    copies[0].wait()

    places = [SPB * start[m] - bands * me for m in range(count)]
    ranks = [jnp.int32(0)] * count
    for m in range(count):
        for n in range(m + 1, count):
            later = (places[n] < places[m]).astype(jnp.int32)
            ranks[m] = ranks[m] + later
            ranks[n] = ranks[n] + (1 - later)
    before = jnp.int32(0)
    until = jnp.int32(0)
    for m in range(count):
        order[ranks[m]] = jnp.int32(m)
        before = before + (places[m] <= -window).astype(jnp.int32)
        until = until + (places[m] < bands).astype(jnp.int32)

    def clear(n, carry):
        folded[order[n]] = jnp.zeros((lines, cols), jnp.float32)
        return carry

    lax.fori_loop(0, before, clear, 0)
    lax.fori_loop(until, count, clear, 0)
    copies[2].wait()
    copies[3].wait()
    for r in range(2):
        for c in range(2):
            pick = which(offsets, jnp.int32(c - r))
            table[r * half : (r + 1) * half, c * half : (c + 1) * half] = blocks[pick]
    spread.wait()

    def ready(q, carry):
        arrive(q).wait()
        return carry

    def one(n, arrived):
        m = order[n]
        low = SPB * start[m] - bands * me
        stop = jnp.minimum(low + window, bands)
        needed = lax.div(stop + (group - 1), jnp.int32(group))
        lax.fori_loop(arrived, needed, ready, 0)
        whole = jnp.logical_and(low >= 0, low + window <= bands)

        def term(band, weight, r):
            return weight * cube[band, r : r + ROWS, :].astype(jnp.float32)

        @pl.when(whole)
        def _():
            for r in range(0, lines, ROWS):
                total = term(low, weights[m, 0], r)
                for j in range(1, window):
                    total = total + term(low + j, weights[m, j], r)
                folded[m, r : r + ROWS, :] = total

        @pl.when(jnp.logical_not(whole))
        def _():
            first = jnp.maximum(low, 0)
            for r in range(0, lines, ROWS):

                def some(t, total):
                    for i in range(group):
                        band = first + t * group + i
                        total = total + term(band, weights[m, band - low], r)
                    return total

                folded[m, r : r + ROWS, :] = lax.fori_loop(
                    0,
                    lax.div(stop - first, jnp.int32(group)),
                    some,
                    jnp.zeros((ROWS, cols), jnp.float32),
                )

        return jnp.maximum(arrived, needed)

    arrived = lax.fori_loop(before, until, one, jnp.int32(0))
    lax.fori_loop(arrived, bands // group, ready, 0)

    dims = (((1,), (1,)), ((), ()))
    side = table[...]
    planes, odd, units = ownership(count)

    def across(value):
        high, low = split(value)
        out = lax.dot_general(high, side, dims, preferred_element_type=jnp.float32)
        return out + lax.dot_general(low, side, dims, preferred_element_type=jnp.float32)

    for owner, out in ((me, keep), (1 - me, send)):
        base = owner * (planes + odd)
        for i in range(planes):
            made = across(folded[base + i])
            out[2 * i] = made[:, :half]
            out[2 * i + 1] = made[:, half:]
    if odd:
        made = across(folded[planes])
        left, right = made[:, :half], made[:, half:]
        keep[units - 1] = jnp.where(me == 0, left, right)
        send[units - 1] = jnp.where(me == 0, right, left)


def coded_rows(count, lines):
    return count * lines + -(-count // 16) * 16


def encode(count, plane, message):
    levels = []
    for m in range(count):
        value = plane(m)
        lines, half = value.shape
        largest = jnp.max(jnp.abs(value), axis=0, keepdims=True)
        level = jnp.ceil(jnp.log2(jnp.maximum(largest, 1e-30)) * STEPS)
        factor = PEAK * jnp.exp2(level * (-1.0 / STEPS))
        coded = jnp.floor(value * factor + 0.5).astype(jnp.int32)
        message[m * lines : (m + 1) * lines, :] = coded.astype(jnp.int16)
        levels.append(level)
    spare = message.shape[0] - count * lines - count
    levels.append(jnp.zeros((spare, half), jnp.float32))
    levels = jnp.concatenate(levels, axis=0)
    message[count * lines :, :] = levels.astype(jnp.int32).astype(jnp.int16)


def decode(message, count, lines):
    level = message[count * lines :, :].astype(jnp.int32).astype(jnp.float32)
    scale = jnp.exp2(level * (1.0 / STEPS)) * (1.0 / PEAK)

    def plane(m):
        coded = message[m * lines : (m + 1) * lines, :].astype(jnp.int32).astype(jnp.float32)
        return coded * scale[m : m + 1, :]

    return plane


def blurred(block, value):
    high, low = split(value)
    both = jnp.dot(
        block, jnp.concatenate([high, low], axis=1), preferred_element_type=jnp.float32
    )
    return both[:, : value.shape[1]] + both[:, value.shape[1] :]


def side_step():
    return jnp.where(lax.axis_index("line") % 2 == 0, jnp.int32(1), jnp.int32(-1))


def by_core(zero, one):
    me = lax.axis_index("band")
    pl.when(me == 0)(zero)
    pl.when(me != 0)(one)


def share(offsets, blocks, keep, other, total, message):
    units = keep.shape[0]
    total[...] = keep[...] + other[...]
    block = blocks[which(offsets, side_step())]
    by_core(
        lambda: encode(units, lambda m: total[m], message),
        lambda: encode(units, lambda m: blurred(block, total[m]), message),
    )


def centre(offsets, blocks, total, other_total, base, other_base, term):
    units = total.shape[0]
    here = blocks[which(offsets, jnp.int32(0))]
    block = blocks[which(offsets, -side_step())]
    for m in range(units):
        base[m] = blurred(here, total[m])
        other_base[m] = blurred(here, other_total[m])
        term[m] = blurred(block, total[m])


def relay(term, received, message):
    units, lines, _ = term.shape

    def forward():
        message[...] = received[...]

    def add():
        plane = decode(received, units, lines)
        encode(units, lambda m: term[m] + plane(m), message)

    by_core(forward, add)


def beside(offsets, blocks, base, near, other_base, other_near, total):
    units, lines, _ = base.shape
    block = blocks[which(offsets, side_step())]

    def work(source, message):
        plane = decode(message, units, lines)
        for m in range(units):
            total[m] = source[m] + blurred(block, plane(m))

    by_core(lambda: work(base, near), lambda: work(other_base, other_near))

def arccos(x):
    size = jnp.abs(x)
    big = size > 0.5
    z = jnp.where(big, 0.5 * (1.0 - size), size * size)
    root = jnp.where(big, jnp.sqrt(z), size)
    poly = 4.2163199048e-2
    for term in (2.4181311049e-2, 4.5470025998e-2, 7.4953002686e-2, 1.6666752422e-1):
        poly = poly * z + term
    arcsin = poly * z * root + root
    pi = 3.14159265358979
    inner = jnp.where(x < 0, 0.5 * pi + arcsin, 0.5 * pi - arcsin)
    outer = jnp.where(x < 0, pi - 2.0 * arcsin, 2.0 * arcsin)
    return jnp.where(big, outer, inner)


def finish(second, offsets, blocks, observed, spread, summed, message, *rest):
    if second:
        sums, image, angles, made, angle, sems = rest[0], *rest[-5:]
    else:
        image, sums, made, sems = rest
    units, lines, half = spread.shape
    count = observed.shape[0]
    plane = decode(message, units, lines)

    def work(core):
        block = blocks[which(offsets, -side_step())]
        zero = jnp.zeros((lines, half), jnp.float32)
        inner, left = [zero, zero], [zero, zero]
        for n, (m, c) in enumerate(units_of(core, count)):
            at = slice(c * half, (c + 1) * half)
            if core == 0:
                value = spread[n] + blurred(block, plane(n))
            else:
                value = summed[n] + plane(n)
            made[n] = value
            pltpu.make_async_copy(made.at[n], image.at[m, :, at], sems.at[n]).start()
            inner[c] = inner[c] + value * observed[m, :, at].astype(jnp.float32)
            left[c] = left[c] + value * value
        for c in range(2):
            at = slice(c * half, (c + 1) * half)
            if not second:
                sums[0, :, at] = inner[c]
                sums[1, :, at] = left[c]
                continue
            right = zero
            for m in range(count):
                seen = observed[m, :, at].astype(jnp.float32)
                right = right + seen * seen
            bound = jnp.sqrt(left[c] + sums[1, :, at]) * jnp.sqrt(right)
            ratio = (inner[c] + sums[0, :, at]) / jnp.maximum(bound, 1.0)
            angle[:, at] = arccos(jnp.clip(ratio, -1.0, 1.0))
        if second:
            last = pltpu.make_async_copy(angle, angles, sems.at[units])
            last.start()
        for n, (m, c) in enumerate(units_of(core, count)):
            at = slice(c * half, (c + 1) * half)
            pltpu.make_async_copy(made.at[n], image.at[m, :, at], sems.at[n]).wait()
        if second:
            last.wait()

    if second:
        by_core(lambda: work(1), lambda: work(0))
    else:
        by_core(lambda: work(0), lambda: work(1))


def on_device(
    cube,
    observed,
    along_kernels,
    along_offsets,
    across_kernels,
    across_offsets,
    resp_start,
    resp_values,
):
    f32, i16 = jnp.float32, jnp.int16
    size = lax.axis_size("line")
    bands, lines, cols = cube.shape
    count = resp_values.shape[0]
    half = cols // 2
    _, _, units = ownership(count)
    shape = jax.ShapeDtypeStruct
    swap = [(0, 1), (1, 0)]
    partner = [(i, i ^ 1) for i in range(size)]
    even_up = [(i, i + 2) for i in range(0, size - 2, 2)] + [(i, i - 2) for i in range(3, size, 2)]
    odd_up = [(i, i + 2) for i in range(1, size - 2, 2)] + [(i, i - 2) for i in range(2, size, 2)]

    def cores(zero, one):
        return [(2 * a, 2 * b) for a, b in zero] + [(2 * a + 1, 2 * b + 1) for a, b in one]

    along = (along_offsets, along_kernels)
    part = shape((units, lines, half), f32)
    coded = shape((coded_rows(units, lines), half), i16)
    unit = 4 * lines * lines * half

    inputs = (resp_start, across_offsets, resp_values, across_kernels, cube)
    keep, send = call(
        fold,
        [pltpu.with_memory_space_constraint(x, pltpu.HBM) for x in inputs],
        [HBM] * 5,
        [part, part],
        scratch=[
            pltpu.SMEM(resp_start.shape, jnp.int32),
            pltpu.SMEM(across_offsets.shape, jnp.int32),
            pltpu.VMEM(resp_values.shape, resp_values.dtype),
            pltpu.VMEM(resp_values.shape, f32),
            pltpu.SMEM(resp_values.shape, f32),
            pltpu.VMEM(across_kernels.shape, across_kernels.dtype),
            pltpu.VMEM(cube.shape, cube.dtype),
            pltpu.VMEM((count, lines, cols), f32),
            pltpu.VMEM((cols, cols), across_kernels.dtype),
            pltpu.SMEM((count,), jnp.int32),
            pltpu.SemaphoreType.DMA((5,)),
            pltpu.SemaphoreType.DMA((bands // math.gcd(SPB, bands),)),
        ],
        flops=4 * count * lines * cols * cols,
    )
    other = lax.ppermute(send, "band", swap)
    total, message = call(share, (*along, keep, other), [SMEM] + [VMEM] * 3, [part, coded])
    near = lax.ppermute(message, ("line", "band"), cores(partner, odd_up))
    other_total = lax.ppermute(total, "band", swap)
    base, other_base, term = call(
        centre, (*along, total, other_total), [SMEM] + [VMEM] * 3, [part] * 3, flops=unit * units * 3
    )
    near, term = lax.optimization_barrier((near, term))
    (message,) = call(relay, (term, near), [VMEM] * 2, [coded])
    message, near = lax.optimization_barrier((message, near))
    far = lax.ppermute(message, ("line", "band"), cores(even_up, partner))
    other_near = lax.ppermute(near, "band", swap)
    (spread,) = call(
        beside,
        (*along, base, near, other_base, other_near),
        [SMEM] + [VMEM] * 5,
        [part],
        flops=unit * units,
    )
    far, spread = lax.optimization_barrier((far, spread))
    other_far = lax.ppermute(far, "band", swap)
    image = shape((count, lines, cols), f32)
    made = [pltpu.VMEM((units, lines, half), f32)]
    image, sums = call(
        functools.partial(finish, False),
        (*along, observed, spread, base, far),
        [SMEM] + [VMEM] * 5,
        [image, shape((2, lines, cols), f32)],
        scratch=made + [pltpu.SemaphoreType.DMA((units,))],
        out_specs=[HBM, VMEM],
        flops=unit * units,
    )
    image, angles = call(
        functools.partial(finish, True),
        (*along, observed, spread, other_base, other_far, sums, image),
        [SMEM] + [VMEM] * 6 + [HBM],
        [image, shape((lines, cols), f32)],
        scratch=made + [pltpu.VMEM((lines, cols), f32), pltpu.SemaphoreType.DMA((units + 1,))],
        out_specs=[HBM] * 2,
        aliases={7: 0},
        flops=unit * units,
    )
    return image, angles


def solution(mesh):
    placed = (
        P("band", ("slab", "line"), None),
        P(None, ("slab", "line"), None),
        P(),
        P(),
        P(),
        P(),
        P(),
        P(),
    )
    return jax.shard_map(
        on_device,
        mesh=mesh,
        in_specs=placed,
        out_specs=(P(None, ("slab", "line"), None), P(("slab", "line"), None)),
        check_vma=False,
    )
```

profile of v0, /device:TPU:0, one launch (start us, length us, event | category | flops | bytes accessed | tf_op | source)
XLA Modules:
  0.0 36.0 jit_solution(9626323065253743304)
XLA Ops:
  0.6 0.0 copy-start.2
  0.6 0.0 copy-start.1
  0.7 6.9 %fold.1 = (f32[13,128,128]{2,1,0:T(8,128)S(1)}, f32[13,128,128]{2,1,0:T(8,128)S(1)}) custom-call(s32[13]{0:T(128)} %start_in.1, s32[3]{0:T(128)} %offsets_in.1, bf16[13,20]{1,0:T(8,128)(2,1)} %values_in.1, bf16[3,128,128]{2,1,0:T(8,128)(2,1)} %blocks_in.1, bf16[115,128,256]{2,1,0:T(8,128)(2,1)} %cube_in.1), custom_call_target="tpu_custom_call" | custom-call | flops 436207616 | bytes 9339464 | tf_op jit(solution)/shard_map/fold/pallas_call | solution.py:37
  7.6 0.4 %collective-permute-start = (f32[13,128,128]{2,1,0:T(8,128)S(1)}, f32[13,128,128]{2,1,0:T(8,128)S(1)}, u32[]{:S(2)}, u32[]{:S(2)}) collective-permute-start(f32[13,128,128]{2,1,0:T(8,128)S(1)} %get-tuple-element.18), channel_id=1, source_target_pairs={{0,1},{1,0},{2,3},{3,2},{4,5},{5,4},{6,7},{7,6},{8,9},{9,8},{10,11... | collective-permute-start | bytes 2555912 | tf_op jit(solution)/shard_map/ppermute | solution.py:412
  8.0 2.1 %collective-permute-done.other = f32[13,128,128]{2,1,0:T(8,128)S(1)} collective-permute-done((f32[13,128,128]{2,1,0:T(8,128)S(1)}, f32[13,128,128]{2,1,0:T(8,128)S(1)}, u32[]{:S(2)}, u32[]{:S(2)}) %collective-permute-start) | collective-permute-done | bytes 852000 | tf_op jit(solution)/shard_map/ppermute | solution.py:412
  10.0 0.0 copy-done.2
  10.0 0.0 copy-done.1
  10.0 0.9 %share.1 = (f32[13,128,128]{2,1,0:T(8,128)S(1)}, s16[1680,128]{1,0:T(8,128)(2,1)S(1)}) custom-call(s32[3]{0:T(128)S(1)} %copy-done.2, bf16[3,128,128]{2,1,0:T(8,128)(2,1)S(1)} %copy-done.1, f32[13,128,128]{2,1,0:T(8,128)S(1)} %get-tuple-element.17.keep, f32[13,128,128]{2,1,0:T(8,128)S(1)} %collective-permute-done.other), custom_call_target="tpu_custom_call" | custom-call | bytes 3084300 | tf_op jit(solution)/shard_map/share/pallas_call | solution.py:37
  10.9 0.6 %collective-permute-start.2 = (f32[13,128,128]{2,1,0:T(8,128)S(1)}, f32[13,128,128]{2,1,0:T(8,128)S(1)}, u32[]{:S(2)}, u32[]{:S(2)}) collective-permute-start(f32[13,128,128]{2,1,0:T(8,128)S(1)} %get-tuple-element.20.total), channel_id=1, source_target_pairs={{0,1},{1,0},{2,3},{3,2},{4,5},{5,4},{6,7},{7,6},{8,9},{9,8},{10,11... | collective-permute-start | bytes 2555912 | tf_op jit(solution)/shard_map/ppermute | solution.py:415
  11.6 4.7 %collective-permute-start.1 = (s16[1680,128]{1,0:T(8,128)(2,1)S(1)}, s16[1680,128]{1,0:T(8,128)(2,1)S(1)}, u32[]{:S(2)}, u32[]{:S(2)}) collective-permute-start(s16[1680,128]{1,0:T(8,128)(2,1)S(1)} %get-tuple-element.19), channel_id=1, source_target_pairs={{0,2},{2,0},{4,6},{6,4},{8,10},{10,8},{12,14},{14,12},{3,7},{7,11}... | collective-permute-start | bytes 1290248 | tf_op jit(solution)/shard_map/ppermute | solution.py:414
  16.3 0.0 collective-permute-done.2.other_total
  16.3 1.4 %centre.1 = (f32[13,128,128]{2,1,0:T(8,128)S(1)}, f32[13,128,128]{2,1,0:T(8,128)S(1)}, f32[13,128,128]{2,1,0:T(8,128)S(1)}) custom-call(s32[3]{0:T(128)S(1)} %copy-done.2, bf16[3,128,128]{2,1,0:T(8,128)(2,1)S(1)} %copy-done.1, f32[13,128,128]{2,1,0:T(8,128)S(1)} %get-tuple-element.20.total, f32[13,128,128]{2,1,0:T(8,128)S(1)} %collective-permute-done.2.other_total), custom_call_target="tpu_custom_call" | custom-call | flops 327155712 | bytes 4358156 | tf_op jit(solution)/shard_map/centre/pallas_call | solution.py:37
  17.6 4.8 %collective-permute-done.1.received.near = s16[1680,128]{1,0:T(8,128)(2,1)S(1)} collective-permute-done((s16[1680,128]{1,0:T(8,128)(2,1)S(1)}, s16[1680,128]{1,0:T(8,128)(2,1)S(1)}, u32[]{:S(2)}, u32[]{:S(2)}) %collective-permute-start.1) | collective-permute-done | bytes 430112 | tf_op jit(solution)/shard_map/ppermute | solution.py:414
  22.4 0.1 collective-permute-start.4
  22.5 4.0 %collective-permute-start.3 = (s16[1680,128]{1,0:T(8,128)(2,1)S(1)}, s16[1680,128]{1,0:T(8,128)(2,1)S(1)}, u32[]{:S(2)}, u32[]{:S(2)}) collective-permute-start(s16[1680,128]{1,0:T(8,128)(2,1)S(1)} %relay.1), channel_id=1, source_target_pairs={{0,4},{4,8},{8,12},{6,2},{10,6},{14,10},{1,3},{3,1},{5,7},{7,5},{9... | collective-permute-start | bytes 1290248 | tf_op jit(solution)/shard_map/ppermute | solution.py:422
  26.5 0.0 collective-permute-done.4.other_near
  26.5 0.0 copy-start
  26.5 1.0 %beside.1.spread = f32[13,128,128]{2,1,0:T(8,128)S(1)} custom-call(s32[3]{0:T(128)S(1)} %copy-done.2, bf16[3,128,128]{2,1,0:T(8,128)(2,1)S(1)} %copy-done.1, f32[13,128,128]{2,1,0:T(8,128)S(1)} %get-tuple-element.25.base.summed, s16[1680,128]{1,0:T(8,128)(2,1)S(1)} %collective-permute-done.1.received.near, ...), custom_call_target="tpu_custom_call" | custom-call | flops 109051904 | bytes 3514380 | tf_op jit(solution)/shard_map/beside/pallas_call | solution.py:37
  27.5 4.7 %collective-permute-done.3.message = s16[1680,128]{1,0:T(8,128)(2,1)S(1)} collective-permute-done((s16[1680,128]{1,0:T(8,128)(2,1)S(1)}, s16[1680,128]{1,0:T(8,128)(2,1)S(1)}, u32[]{:S(2)}, u32[]{:S(2)}) %collective-permute-start.3) | collective-permute-done | bytes 430112 | tf_op jit(solution)/shard_map/ppermute | solution.py:422
  32.2 0.0 collective-permute-start.5
  32.2 0.0 copy-done
  32.2 1.8 %finish.2 = (f32[13,128,256]{2,1,0:T(8,128)}, f32[2,128,256]{2,1,0:T(8,128)S(1)}) custom-call(s32[3]{0:T(128)S(1)} %copy-done.2, bf16[3,128,128]{2,1,0:T(8,128)(2,1)S(1)} %copy-done.1, bf16[13,128,256]{2,1,0:T(8,128)(2,1)S(1)} %copy-done, f32[13,128,128]{2,1,0:T(8,128)S(1)} %beside.1.spread, f32[13,128,128]{2,1,0:T(8,128)S(1)} %get-tuple-element.25.base.summed, ...), custom_call_target="tpu_custom_call" | custom-call | flops 109051904 | bytes 5050380 | tf_op jit(solution)/shard_map/finish/pallas_call | solution.py:37
  34.0 0.0 collective-permute-done.5.message
  34.0 2.0 %finish.3 = (f32[13,128,256]{2,1,0:T(8,128)}, f32[128,256]{1,0:T(8,128)}) custom-call(s32[3]{0:T(128)S(1)} %copy-done.2, bf16[3,128,128]{2,1,0:T(8,128)(2,1)S(1)} %copy-done.1, bf16[13,128,256]{2,1,0:T(8,128)(2,1)S(1)} %copy-done, f32[13,128,128]{2,1,0:T(8,128)S(1)} %beside.1.spread, ...), custom_call_target="tpu_custom_call", output_to_operand_aliasing={{0}: (7, {})} | custom-call | flops 109051904 | bytes 6885388 | tf_op jit(solution)/shard_map/finish/pallas_call | solution.py:37
  (1 shorter events, 0.0 us)
Async XLA Ops:
  0.6 9.4 %copy-start.2 = (s32[3]{0:T(128)S(1)}, s32[3]{0:T(128)}, u32[]{:S(2)}) copy-start(s32[3]{0:T(128)} %offsets.9) | copy-start | bytes 40
  0.6 9.4 %copy-start.1 = (bf16[3,128,128]{2,1,0:T(8,128)(2,1)S(1)}, bf16[3,128,128]{2,1,0:T(8,128)(2,1)}, u32[]{:S(2)}) copy-start(bf16[3,128,128]{2,1,0:T(8,128)(2,1)} %blocks.9) | copy-start | bytes 294916
  7.6 2.4 %collective-permute-start = (f32[13,128,128]{2,1,0:T(8,128)S(1)}, f32[13,128,128]{2,1,0:T(8,128)S(1)}, u32[]{:S(2)}, u32[]{:S(2)}) collective-permute-start(f32[13,128,128]{2,1,0:T(8,128)S(1)} %get-tuple-element.18), channel_id=1, source_target_pairs={{0,1},{1,0},{2,3},{3,2},{4,5},{5,4},{6,7},{7,6},{8,9},{9,8},{10,11... | collective-permute-start | bytes 2555912 | tf_op jit(solution)/shard_map/ppermute | solution.py:412
  10.9 5.3 %collective-permute-start.2 = (f32[13,128,128]{2,1,0:T(8,128)S(1)}, f32[13,128,128]{2,1,0:T(8,128)S(1)}, u32[]{:S(2)}, u32[]{:S(2)}) collective-permute-start(f32[13,128,128]{2,1,0:T(8,128)S(1)} %get-tuple-element.20.total), channel_id=1, source_target_pairs={{0,1},{1,0},{2,3},{3,2},{4,5},{5,4},{6,7},{7,6},{8,9},{9,8},{10,11... | collective-permute-start | bytes 2555912 | tf_op jit(solution)/shard_map/ppermute | solution.py:415
  11.6 10.8 %collective-permute-start.1 = (s16[1680,128]{1,0:T(8,128)(2,1)S(1)}, s16[1680,128]{1,0:T(8,128)(2,1)S(1)}, u32[]{:S(2)}, u32[]{:S(2)}) collective-permute-start(s16[1680,128]{1,0:T(8,128)(2,1)S(1)} %get-tuple-element.19), channel_id=1, source_target_pairs={{0,2},{2,0},{4,6},{6,4},{8,10},{10,8},{12,14},{14,12},{3,7},{7,11}... | collective-permute-start | bytes 1290248 | tf_op jit(solution)/shard_map/ppermute | solution.py:414
  22.4 4.1 %collective-permute-start.4 = (s16[1680,128]{1,0:T(8,128)(2,1)S(1)}, s16[1680,128]{1,0:T(8,128)(2,1)S(1)}, u32[]{:S(2)}, u32[]{:S(2)}) collective-permute-start(s16[1680,128]{1,0:T(8,128)(2,1)S(1)} %collective-permute-done.1.received.near), channel_id=1, source_target_pairs={{0,1},{1,0},{2,3},{3,2},{4,5},{5,4},{6,7},{7,6},{8,9},{9,8},{10,11... | collective-permute-start | bytes 1290248 | tf_op jit(solution)/shard_map/ppermute | solution.py:423
  22.5 9.6 %collective-permute-start.3 = (s16[1680,128]{1,0:T(8,128)(2,1)S(1)}, s16[1680,128]{1,0:T(8,128)(2,1)S(1)}, u32[]{:S(2)}, u32[]{:S(2)}) collective-permute-start(s16[1680,128]{1,0:T(8,128)(2,1)S(1)} %relay.1), channel_id=1, source_target_pairs={{0,4},{4,8},{8,12},{6,2},{10,6},{14,10},{1,3},{3,1},{5,7},{7,5},{9... | collective-permute-start | bytes 1290248 | tf_op jit(solution)/shard_map/ppermute | solution.py:422
  26.5 5.7 %copy-start = (bf16[13,128,256]{2,1,0:T(8,128)(2,1)S(1)}, bf16[13,128,256]{2,1,0:T(8,128)(2,1)}, u32[]{:S(2)}) copy-start(bf16[13,128,256]{2,1,0:T(8,128)(2,1)} %observed.3) | copy-start | bytes 2555908
  32.2 1.8 %collective-permute-start.5 = (s16[1680,128]{1,0:T(8,128)(2,1)S(1)}, s16[1680,128]{1,0:T(8,128)(2,1)S(1)}, u32[]{:S(2)}, u32[]{:S(2)}) collective-permute-start(s16[1680,128]{1,0:T(8,128)(2,1)S(1)} %collective-permute-done.3.message), channel_id=1, source_target_pairs={{0,1},{1,0},{2,3},{3,2},{4,5},{5,4},{6,7},{7,6},{8,9},{9,8},{10,11... | collective-permute-start | bytes 1290248 | tf_op jit(solution)/shard_map/ppermute | solution.py:432
where the time goes:
time: 36.4 us; the launch traced here: 36 us
  Pallas kernels  14 us (38%)
  waiting for transfers between devices  11.5 us (32%)
  starting transfers between devices  9.77 us (27%)
  between operations  0.75 us (2%)
    pallas_call x7, Pallas kernels, call(): pl.pallas_call(kernel, in_specs=specs, out_specs=out_specs or [VMEM] * le...  14 us
    ppermute x1, waiting for transfers between devices, on_device(): near = lax.ppermute(message, ('line', 'band'), cores(partner, odd_up))  4.76 us
    ppermute x1, starting transfers between devices, on_device(): near = lax.ppermute(message, ('line', 'band'), cores(partner, odd_up))  4.7 us
    ppermute x1, waiting for transfers between devices, on_device(): far = lax.ppermute(message, ('line', 'band'), cores(even_up, partner))  4.65 us
    ppermute x1, starting transfers between devices, on_device(): far = lax.ppermute(message, ('line', 'band'), cores(even_up, partner))  4 us
    ppermute x1, waiting for transfers between devices, on_device(): other = lax.ppermute(send, 'band', swap)  2.08 us
  transfers between devices with their start and end apart: 6, of which 3 were waited for; matrix products, arithmetic and copies ran while one was open for 0% of the time, Pallas kernels for 11%

commit v1 on v0

v1 whole, which is shorter than its diff:
```python
import functools
import math

import jax
import jax.numpy as jnp
from jax import lax
from jax.experimental import pallas as pl
from jax.experimental.pallas import tpu as pltpu
from jax.sharding import PartitionSpec as P

BLK = 128
SPB = 10
STEPS = 16.0
PEAK = 32000.0


def which(offsets, shift):
    return sum(
        jnp.where(offsets[k] == shift, jnp.int32(k), jnp.int32(0)) for k in range(offsets.shape[0])
    )


def split(value):
    high = value.astype(jnp.bfloat16)
    low = (value - high.astype(jnp.float32)).astype(jnp.bfloat16)
    return high, low


SMEM = pl.BlockSpec(memory_space=pltpu.SMEM)
VMEM = pl.BlockSpec(memory_space=pltpu.VMEM)
HBM = pl.BlockSpec(memory_space=pltpu.HBM)
ROWS = 64


def call(kernel, inputs, specs, outs, scratch=(), out_specs=None, aliases=None, flops=0):
    moved = sum(x.size * x.dtype.itemsize for x in (*inputs, *outs))
    return pl.pallas_call(
        kernel,
        in_specs=specs,
        out_specs=out_specs or [VMEM] * len(outs),
        out_shape=outs,
        scratch_shapes=scratch,
        input_output_aliases=aliases or {},
        compiler_params=pltpu.CompilerParams(vmem_limit_bytes=32 * 2**20),
        cost_estimate=pl.CostEstimate(flops=flops, bytes_accessed=moved, transcendentals=0),
        name=(kernel.func if isinstance(kernel, functools.partial) else kernel).__name__,
    )(*inputs)


def ownership(count):
    pairs = count // 2
    return pairs, count % 2, 2 * pairs + count % 2


def units_of(core, count):
    pairs, odd, _ = ownership(count)
    first = core * (pairs + odd)
    return [(first + i, c) for i in range(pairs) for c in range(2)] + [(pairs, core)] * odd


def fold(
    start_in,
    offsets_in,
    values_in,
    blocks_in,
    along_offsets_in,
    along_blocks_in,
    cube_in,
    keep,
    send,
    picked,
    start,
    offsets,
    values,
    wide,
    weights,
    blocks,
    along_offsets,
    along_blocks,
    cube,
    folded,
    table,
    order,
    small,
    large,
):
    bands, lines, cols = cube.shape
    count, window = values.shape
    half = cols // 2
    group = math.gcd(SPB, bands)
    me = lax.axis_index("band")
    pairs = (
        (start_in, start),
        (values_in, values),
        (offsets_in, offsets),
        (blocks_in, blocks),
        (along_offsets_in, along_offsets),
        (along_blocks_in, along_blocks),
    )
    copies = [pltpu.make_async_copy(a, b, small.at[i]) for i, (a, b) in enumerate(pairs)]

    def arrive(q):
        at = pl.ds(q * group, group)
        return pltpu.make_async_copy(cube_in.at[at], cube.at[at], large.at[q])

    for copy in copies:
        copy.start()
    for q in range(bands // group):
        arrive(q).start()
    copies[1].wait()
    wide[...] = values[...].astype(jnp.float32)
    spread = pltpu.make_async_copy(wide, weights, small.at[len(pairs)])
    spread.start()
    copies[0].wait()

    places = [SPB * start[m] - bands * me for m in range(count)]
    ranks = [jnp.int32(0)] * count
    for m in range(count):
        for n in range(m + 1, count):
            later = (places[n] < places[m]).astype(jnp.int32)
            ranks[m] = ranks[m] + later
            ranks[n] = ranks[n] + (1 - later)
    before = jnp.int32(0)
    until = jnp.int32(0)
    for m in range(count):
        order[ranks[m]] = jnp.int32(m)
        before = before + (places[m] <= -window).astype(jnp.int32)
        until = until + (places[m] < bands).astype(jnp.int32)

    def clear(n, carry):
        folded[order[n]] = jnp.zeros((lines, cols), jnp.float32)
        return carry

    lax.fori_loop(0, before, clear, 0)
    lax.fori_loop(until, count, clear, 0)
    for copy in copies[2:]:
        copy.wait()
    for r in range(2):
        for c in range(2):
            block = blocks[which(offsets, jnp.int32(r - c))].astype(jnp.float32).T
            for top in (0, cols):
                at = slice(top + r * half, top + (r + 1) * half)
                table[at, c * half : (c + 1) * half] = block.astype(jnp.bfloat16)
    step = side_step()
    for i, shift in enumerate((jnp.int32(0), step, -step)):
        picked[i] = along_blocks[which(along_offsets, shift)]
    spread.wait()

    def ready(q, carry):
        arrive(q).wait()
        return carry

    def one(n, arrived):
        m = order[n]
        low = SPB * start[m] - bands * me
        stop = jnp.minimum(low + window, bands)
        needed = lax.div(stop + (group - 1), jnp.int32(group))
        lax.fori_loop(arrived, needed, ready, 0)
        whole = jnp.logical_and(low >= 0, low + window <= bands)

        def term(band, weight, r):
            return weight * cube[band, r : r + ROWS, :].astype(jnp.float32)

        @pl.when(whole)
        def _():
            for r in range(0, lines, ROWS):
                total = term(low, weights[m, 0], r)
                for j in range(1, window):
                    total = total + term(low + j, weights[m, j], r)
                folded[m, r : r + ROWS, :] = total

        @pl.when(jnp.logical_not(whole))
        def _():
            first = jnp.maximum(low, 0)
            for r in range(0, lines, ROWS):

                def some(t, total):
                    for i in range(group):
                        band = first + t * group + i
                        total = total + term(band, weights[m, band - low], r)
                    return total

                folded[m, r : r + ROWS, :] = lax.fori_loop(
                    0,
                    lax.div(stop - first, jnp.int32(group)),
                    some,
                    jnp.zeros((ROWS, cols), jnp.float32),
                )

        return jnp.maximum(arrived, needed)

    arrived = lax.fori_loop(before, until, one, jnp.int32(0))
    lax.fori_loop(arrived, bands // group, ready, 0)

    side = table[...]
    planes, odd, units = ownership(count)

    def across(at, planes):
        value = folded[pl.ds(at, planes)].reshape(planes * lines, cols)
        both = jnp.concatenate(split(value), axis=1)
        made = jnp.dot(both, side, preferred_element_type=jnp.float32)
        return made.reshape(planes, lines, cols)

    for owner, out in ((me, keep), (1 - me, send)):
        made = across(owner * (planes + odd), planes)
        for i in range(planes):
            out[2 * i] = made[i, :, :half]
            out[2 * i + 1] = made[i, :, half:]
    if odd:
        made = across(planes, 1)[0]
        left, right = made[:, :half], made[:, half:]
        keep[units - 1] = jnp.where(me == 0, left, right)
        send[units - 1] = jnp.where(me == 0, right, left)


def coded_rows(count, lines):
    return count * lines + -(-count // 16) * 16


def encode(source, message):
    units, lines, half = source.shape
    largest = jnp.max(jnp.abs(source[...]), axis=1)
    level = jnp.ceil(jnp.log2(jnp.maximum(largest, 1e-30)) * STEPS)
    factor = PEAK * jnp.exp2(level * (-1.0 / STEPS))
    for m in range(units):
        coded = jnp.floor(source[m] * factor[m : m + 1, :] + 0.5).astype(jnp.int32)
        message[m * lines : (m + 1) * lines, :] = coded.astype(jnp.int16)
    spare = message.shape[0] - units * lines - units
    level = jnp.concatenate([level, jnp.zeros((spare, half), jnp.float32)], axis=0)
    message[units * lines :, :] = level.astype(jnp.int32).astype(jnp.int16)


def decode(message, count, lines):
    level = message[count * lines :, :].astype(jnp.int32).astype(jnp.float32)
    scale = jnp.exp2(level * (1.0 / STEPS)) * (1.0 / PEAK)

    def plane(m):
        coded = message[m * lines : (m + 1) * lines, :].astype(jnp.int32).astype(jnp.float32)
        return coded * scale[m : m + 1, :]

    return plane


def blurred(filters, count, plane, put):
    wide = jnp.concatenate([filters, filters], axis=1)
    for m in range(0, count, 2):
        parts = [split(plane(n)) for n in range(m, min(m + 2, count))]
        high = jnp.concatenate([p[0] for p in parts], axis=1)
        low = jnp.concatenate([p[1] for p in parts], axis=1)
        made = jnp.dot(
            wide, jnp.concatenate([high, low], axis=0), preferred_element_type=jnp.float32
        )
        half = made.shape[1] // len(parts)
        for i in range(len(parts)):
            put(m + i, made[:, i * half : (i + 1) * half])


def side_step():
    return jnp.where(lax.axis_index("line") % 2 == 0, jnp.int32(1), jnp.int32(-1))


def by_core(zero, one):
    me = lax.axis_index("band")
    pl.when(me == 0)(zero)
    pl.when(me != 0)(one)


def share(picked, keep, other, total, message, product):
    total[...] = keep[...] + other[...]

    def summing():
        def put(m, value):
            product[m] = value

        blurred(picked[1], total.shape[0], lambda m: total[m], put)
        encode(product, message)

    by_core(lambda: encode(total, message), summing)


def centre(picked, total, base, term):
    units, lines, _ = total.shape

    def only(m, value):
        base[m] = value

    def both(m, value):
        base[m] = value[:lines]
        term[m] = value[lines:]

    stack = jnp.concatenate([picked[0], picked[2]], axis=0)
    by_core(
        lambda: blurred(picked[0], units, lambda m: total[m], only),
        lambda: blurred(stack, units, lambda m: total[m], both),
    )


def relay(term, received, message, total):
    units, lines, _ = term.shape

    def forward():
        message[...] = received[...]

    def add():
        plane = decode(received, units, lines)
        for m in range(units):
            total[m] = term[m] + plane(m)
        encode(total, message)

    by_core(forward, add)


def beside(picked, base, near, total):
    units, lines, _ = base.shape

    def put(m, value):
        total[m] = base[m] + value

    def keep():
        total[...] = base[...]

    by_core(lambda: blurred(picked[1], units, decode(near, units, lines), put), keep)


def settle(picked, base, received, total):
    units, lines, _ = base.shape
    plane = decode(received, units, lines)

    def put(m, value):
        total[m] = base[m] + value

    def add():
        for m in range(units):
            put(m, plane(m))

    by_core(lambda: blurred(picked[2], units, plane, put), add)

def arccos(x):
    size = jnp.abs(x)
    big = size > 0.5
    z = jnp.where(big, 0.5 * (1.0 - size), size * size)
    root = jnp.where(big, jnp.sqrt(z), size)
    poly = 4.2163199048e-2
    for term in (2.4181311049e-2, 4.5470025998e-2, 7.4953002686e-2, 1.6666752422e-1):
        poly = poly * z + term
    arcsin = poly * z * root + root
    pi = 3.14159265358979
    inner = jnp.where(x < 0, 0.5 * pi + arcsin, 0.5 * pi - arcsin)
    outer = jnp.where(x < 0, pi - 2.0 * arcsin, 2.0 * arcsin)
    return jnp.where(big, outer, inner)


def finish(second, observed, value, *rest):
    if second:
        sums, _, image, angles, angle, sems = rest
    else:
        image, sums, sems = rest
    units, lines, half = value.shape
    count = observed.shape[0]

    def work(core):
        places = [(m, slice(c * half, (c + 1) * half)) for m, c in units_of(core, count)]
        copies = [
            pltpu.make_async_copy(value.at[n], image.at[m, :, at], sems.at[n])
            for n, (m, at) in enumerate(places)
        ]
        for copy in copies:
            copy.start()
        for c in range(2):
            at = slice(c * half, (c + 1) * half)
            inner = jnp.zeros((lines, half), jnp.float32)
            left = jnp.zeros((lines, half), jnp.float32)
            for n, (m, where) in enumerate(places):
                if where == at:
                    inner = inner + value[n] * observed[m, :, at].astype(jnp.float32)
                    left = left + value[n] * value[n]
            if second:
                bound = jnp.sqrt(left + sums[1, :, at]) * sums[2, :, at]
                ratio = (inner + sums[0, :, at]) / jnp.maximum(bound, 1.0)
                angle[:, at] = arccos(jnp.clip(ratio, -1.0, 1.0))
            else:
                right = jnp.zeros((lines, half), jnp.float32)
                for m in range(count):
                    seen = observed[m, :, at].astype(jnp.float32)
                    right = right + seen * seen
                sums[0, :, at] = inner
                sums[1, :, at] = left
                sums[2, :, at] = jnp.sqrt(right)
        if second:
            copies.append(pltpu.make_async_copy(angle, angles, sems.at[units]))
            copies[-1].start()
        for copy in copies:
            copy.wait()

    if second:
        by_core(lambda: work(1), lambda: work(0))
    else:
        by_core(lambda: work(0), lambda: work(1))


def on_device(
    cube,
    observed,
    along_kernels,
    along_offsets,
    across_kernels,
    across_offsets,
    resp_start,
    resp_values,
):
    f32, i16 = jnp.float32, jnp.int16
    size = lax.axis_size("line")
    bands, lines, cols = cube.shape
    count = resp_values.shape[0]
    half = cols // 2
    _, _, units = ownership(count)
    shape = jax.ShapeDtypeStruct
    swap = [(0, 1), (1, 0)]
    partner = [(i, i ^ 1) for i in range(size)]
    even_up = [(i, i + 2) for i in range(0, size - 2, 2)] + [(i, i - 2) for i in range(3, size, 2)]
    odd_up = [(i, i + 2) for i in range(1, size - 2, 2)] + [(i, i - 2) for i in range(2, size, 2)]

    def cores(zero, one):
        return [(2 * a, 2 * b) for a, b in zero] + [(2 * a + 1, 2 * b + 1) for a, b in one]

    part = shape((units, lines, half), f32)
    coded = shape((coded_rows(units, lines), half), i16)
    unit = 4 * lines * lines * half

    inputs = (
        resp_start,
        across_offsets,
        resp_values,
        across_kernels,
        along_offsets,
        along_kernels,
        cube,
    )
    keep, send, picked = call(
        fold,
        [pltpu.with_memory_space_constraint(x, pltpu.HBM) for x in inputs],
        [HBM] * len(inputs),
        [part, part, shape(along_kernels.shape, along_kernels.dtype)],
        scratch=[
            pltpu.SMEM(resp_start.shape, jnp.int32),
            pltpu.SMEM(across_offsets.shape, jnp.int32),
            pltpu.VMEM(resp_values.shape, resp_values.dtype),
            pltpu.VMEM(resp_values.shape, f32),
            pltpu.SMEM(resp_values.shape, f32),
            pltpu.VMEM(across_kernels.shape, across_kernels.dtype),
            pltpu.SMEM(along_offsets.shape, jnp.int32),
            pltpu.VMEM(along_kernels.shape, along_kernels.dtype),
            pltpu.VMEM(cube.shape, cube.dtype),
            pltpu.VMEM((count, lines, cols), f32),
            pltpu.VMEM((2 * cols, cols), across_kernels.dtype),
            pltpu.SMEM((count,), jnp.int32),
            pltpu.SemaphoreType.DMA((len(inputs),)),
            pltpu.SemaphoreType.DMA((bands // math.gcd(SPB, bands),)),
        ],
        flops=4 * count * lines * cols * cols,
    )
    work = [pltpu.VMEM(part.shape, f32)]
    other = lax.ppermute(send, "band", swap)
    total, message = call(share, (picked, keep, other), [VMEM] * 3, [part, coded], scratch=work)
    near = lax.ppermute(message, ("line", "band"), cores(partner, odd_up))
    base, term = call(centre, (picked, total), [VMEM] * 2, [part] * 2, flops=2 * unit * units)
    near, base, term = lax.optimization_barrier((near, base, term))
    (message,) = call(relay, (term, near), [VMEM] * 2, [coded], scratch=work)
    message, near, base = lax.optimization_barrier((message, near, base))
    far = lax.ppermute(message, ("line", "band"), cores(even_up, partner))
    (base,) = call(beside, (picked, base, near), [VMEM] * 3, [part], flops=unit * units)
    (mine,) = call(settle, (picked, base, far), [VMEM] * 3, [part], flops=unit * units)
    other = lax.ppermute(mine, "band", swap)
    image = shape((count, lines, cols), f32)
    image, sums = call(
        functools.partial(finish, False),
        (observed, mine),
        [VMEM] * 2,
        [image, shape((3, lines, cols), f32)],
        scratch=[pltpu.SemaphoreType.DMA((units,))],
        out_specs=[HBM, VMEM],
    )
    image, angles = call(
        functools.partial(finish, True),
        (observed, other, sums, image),
        [VMEM] * 3 + [HBM],
        [image, shape((lines, cols), f32)],
        scratch=[pltpu.VMEM((lines, cols), f32), pltpu.SemaphoreType.DMA((units + 1,))],
        out_specs=[HBM] * 2,
        aliases={3: 0},
    )
    return image, angles


def solution(mesh):
    placed = (
        P("band", ("slab", "line"), None),
        P(None, ("slab", "line"), None),
        P(),
        P(),
        P(),
        P(),
        P(),
        P(),
    )
    return jax.shard_map(
        on_device,
        mesh=mesh,
        in_specs=placed,
        out_specs=(P(None, ("slab", "line"), None), P(("slab", "line"), None)),
        check_vma=False,
    )
```

time: 36.4 us -> 34.7 us (0.953)
  Pallas kernels: 14 us -> 9.74 us
  waiting for transfers between devices: 11.5 us -> 14.4 us
    pallas_call x7 -> x8, Pallas kernels: 14 us -> 9.74 us  [call(): pl.pallas_call(kernel, in_specs=specs, out_specs=out_specs or [VMEM] * le...]
    ppermute x3 -> x1, waiting for transfers between devices: 0.01 us -> 1.34 us  [on_device(): other = lax.ppermute(mine, 'band', swap)]
    ppermute x1, waiting for transfers between devices: 4.76 us -> 5.81 us  [on_device(): near = lax.ppermute(message, ('line', 'band'), cores(partner, odd_up))]
    ppermute x3 -> x1, starting transfers between devices: 0.72 us -> 0.07 us  [on_device(): other = lax.ppermute(mine, 'band', swap)]
    ppermute x1, waiting for transfers between devices: 4.65 us -> 5.24 us  [on_device(): far = lax.ppermute(message, ('line', 'band'), cores(even_up, partner))]
  transfers between devices with their start and end apart: 6 -> 4, of which waited for: 3 -> 4; matrix products, arithmetic and copies ran while one was open for 0% -> 0% of each run, Pallas kernels for 11% -> 5%
where the time goes in v1:
time: 34.7 us; the launch traced here: 34.4 us
  waiting for transfers between devices  14.4 us (41%)
  Pallas kernels  9.74 us (28%)
  starting transfers between devices  9.52 us (27%)
  between operations  0.73 us (2%)
    pallas_call x8, Pallas kernels, call(): pl.pallas_call(kernel, in_specs=specs, out_specs=out_specs or [VMEM] * le...  9.74 us
    ppermute x1, waiting for transfers between devices, on_device(): near = lax.ppermute(message, ('line', 'band'), cores(partner, odd_up))  5.81 us
    ppermute x1, waiting for transfers between devices, on_device(): far = lax.ppermute(message, ('line', 'band'), cores(even_up, partner))  5.24 us
    ppermute x1, starting transfers between devices, on_device(): near = lax.ppermute(message, ('line', 'band'), cores(partner, odd_up))  4.64 us
    ppermute x1, starting transfers between devices, on_device(): far = lax.ppermute(message, ('line', 'band'), cores(even_up, partner))  4.13 us
    ppermute x1, waiting for transfers between devices, on_device(): other = lax.ppermute(send, 'band', swap)  2.01 us
    ppermute x1, waiting for transfers between devices, on_device(): other = lax.ppermute(mine, 'band', swap)  1.34 us
  transfers between devices with their start and end apart: 4, of which 4 were waited for; matrix products, arithmetic and copies ran while one was open for 0% of the time, Pallas kernels for 5%

profile of v1, /device:TPU:0, one launch (start us, length us, event | category | flops | bytes accessed | tf_op | source)
XLA Modules:
  0.0 34.4 jit_solution(9793931351496170553)
XLA Ops:
  0.6 6.1 %fold.1 = (f32[13,128,128]{2,1,0:T(8,128)S(1)}, f32[13,128,128]{2,1,0:T(8,128)S(1)}, bf16[3,128,128]{2,1,0:T(8,128)(2,1)S(1)}) custom-call(s32[13]{0:T(128)} %start_in.1, s32[3]{0:T(128)} %offsets_in.1, bf16[13,20]{1,0:T(8,128)(2,1)} %values_in.1, bf16[3,128,128]{2,1,0:T(8,128)(2,1)} %blocks_in.1, s32[3]{0:T(128)} %along_offsets_in.1, ...), custom_call_target="tpu_custom_call" | custom-call | flops 436207616 | bytes 9536084 | tf_op jit(solution)/shard_map/fold/pallas_call | solution.py:37
  6.7 0.7 %collective-permute-start = (f32[13,128,128]{2,1,0:T(8,128)S(1)}, f32[13,128,128]{2,1,0:T(8,128)S(1)}, u32[]{:S(2)}, u32[]{:S(2)}) collective-permute-start(f32[13,128,128]{2,1,0:T(8,128)S(1)} %get-tuple-element.19), channel_id=1, source_target_pairs={{0,1},{1,0},{2,3},{3,2},{4,5},{5,4},{6,7},{7,6},{8,9},{9,8},{10,11... | collective-permute-start | bytes 2555912 | tf_op jit(solution)/shard_map/ppermute | solution.py:463
  7.4 2.0 %collective-permute-done.other = f32[13,128,128]{2,1,0:T(8,128)S(1)} collective-permute-done((f32[13,128,128]{2,1,0:T(8,128)S(1)}, f32[13,128,128]{2,1,0:T(8,128)S(1)}, u32[]{:S(2)}, u32[]{:S(2)}) %collective-permute-start) | collective-permute-done | bytes 852000 | tf_op jit(solution)/shard_map/ppermute | solution.py:463
  9.4 0.4 %share.1 = (f32[13,128,128]{2,1,0:T(8,128)S(1)}, s16[1680,128]{1,0:T(8,128)(2,1)S(1)}) custom-call(bf16[3,128,128]{2,1,0:T(8,128)(2,1)S(1)} %get-tuple-element.17.picked, f32[13,128,128]{2,1,0:T(8,128)S(1)} %get-tuple-element.18.keep, f32[13,128,128]{2,1,0:T(8,128)S(1)} %collective-permute-done.other), custom_call_target="tpu_custom_call" | custom-call | bytes 3084288 | tf_op jit(solution)/shard_map/share/pallas_call | solution.py:37
  9.8 4.6 %collective-permute-start.1 = (s16[1680,128]{1,0:T(8,128)(2,1)S(1)}, s16[1680,128]{1,0:T(8,128)(2,1)S(1)}, u32[]{:S(2)}, u32[]{:S(2)}) collective-permute-start(s16[1680,128]{1,0:T(8,128)(2,1)S(1)} %get-tuple-element.20), channel_id=1, source_target_pairs={{0,2},{2,0},{4,6},{6,4},{8,10},{10,8},{12,14},{14,12},{3,7},{7,11}... | collective-permute-start | bytes 1290248 | tf_op jit(solution)/shard_map/ppermute | solution.py:465
  14.4 0.3 centre.1
  14.8 5.8 %collective-permute-done.1.received.near = s16[1680,128]{1,0:T(8,128)(2,1)S(1)} collective-permute-done((s16[1680,128]{1,0:T(8,128)(2,1)S(1)}, s16[1680,128]{1,0:T(8,128)(2,1)S(1)}, u32[]{:S(2)}, u32[]{:S(2)}) %collective-permute-start.1) | collective-permute-done | bytes 430112 | tf_op jit(solution)/shard_map/ppermute | solution.py:465
  20.6 0.0 copy-start
  20.6 4.1 %collective-permute-start.2 = (s16[1680,128]{1,0:T(8,128)(2,1)S(1)}, s16[1680,128]{1,0:T(8,128)(2,1)S(1)}, u32[]{:S(2)}, u32[]{:S(2)}) collective-permute-start(s16[1680,128]{1,0:T(8,128)(2,1)S(1)} %relay.1), channel_id=1, source_target_pairs={{0,4},{4,8},{8,12},{6,2},{10,6},{14,10},{1,3},{3,1},{5,7},{7,5},{9... | collective-permute-start | bytes 1290248 | tf_op jit(solution)/shard_map/ppermute | solution.py:470
  24.8 0.4 %beside.1.base = f32[13,128,128]{2,1,0:T(8,128)S(1)} custom-call(bf16[3,128,128]{2,1,0:T(8,128)(2,1)S(1)} %get-tuple-element.17.picked, f32[13,128,128]{2,1,0:T(8,128)S(1)} %get-tuple-element.27.base, s16[1680,128]{1,0:T(8,128)(2,1)S(1)} %collective-permute-done.1.received.near), custom_call_target="tpu_custom_call" | custom-call | flops 109051904 | bytes 2232320 | tf_op jit(solution)/shard_map/beside/pallas_call | solution.py:37
  25.2 5.2 %collective-permute-done.2.received = s16[1680,128]{1,0:T(8,128)(2,1)S(1)} collective-permute-done((s16[1680,128]{1,0:T(8,128)(2,1)S(1)}, s16[1680,128]{1,0:T(8,128)(2,1)S(1)}, u32[]{:S(2)}, u32[]{:S(2)}) %collective-permute-start.2) | collective-permute-done | bytes 430112 | tf_op jit(solution)/shard_map/ppermute | solution.py:470
  30.4 0.4 %settle.1.value = f32[13,128,128]{2,1,0:T(8,128)S(1)} custom-call(bf16[3,128,128]{2,1,0:T(8,128)(2,1)S(1)} %get-tuple-element.17.picked, f32[13,128,128]{2,1,0:T(8,128)S(1)} %beside.1.base, s16[1680,128]{1,0:T(8,128)(2,1)S(1)} %collective-permute-done.2.received), custom_call_target="tpu_custom_call" | custom-call | flops 109051904 | bytes 2232320 | tf_op jit(solution)/shard_map/settle/pallas_call | solution.py:37
  30.8 0.1 collective-permute-start.3
  30.9 0.0 copy-done
  30.9 1.0 %finish.2 = (f32[13,128,256]{2,1,0:T(8,128)}, f32[3,128,256]{2,1,0:T(8,128)S(1)}) custom-call(bf16[13,128,256]{2,1,0:T(8,128)(2,1)S(1)} %copy-done, f32[13,128,128]{2,1,0:T(8,128)S(1)} %settle.1.value), custom_call_target="tpu_custom_call" | custom-call | bytes 3801088 | tf_op jit(solution)/shard_map/finish/pallas_call | solution.py:37
  31.9 1.3 %collective-permute-done.3.value = f32[13,128,128]{2,1,0:T(8,128)S(1)} collective-permute-done((f32[13,128,128]{2,1,0:T(8,128)S(1)}, f32[13,128,128]{2,1,0:T(8,128)S(1)}, u32[]{:S(2)}, u32[]{:S(2)}) %collective-permute-start.3) | collective-permute-done | bytes 852000 | tf_op jit(solution)/shard_map/ppermute | solution.py:473
  33.3 1.1 %finish.3 = (f32[13,128,256]{2,1,0:T(8,128)}, f32[128,256]{1,0:T(8,128)}) custom-call(bf16[13,128,256]{2,1,0:T(8,128)(2,1)S(1)} %copy-done, f32[13,128,128]{2,1,0:T(8,128)S(1)} %collective-permute-done.3.value, f32[3,128,256]{2,1,0:T(8,128)S(1)} %get-tuple-element.30.rest_0_, f32[13,128,256]{2,1,0:T(8,128)} %get-tuple-element.31.rest_1_), custom_call_target="tpu_custom_call", output_to_operand_aliasing={{0}: (3, {})} | custom-call | bytes 5636096 | tf_op jit(solution)/shard_map/finish/pallas_call | solution.py:37
  (1 shorter events, 0.0 us)
Async XLA Ops:
  6.7 2.7 %collective-permute-start = (f32[13,128,128]{2,1,0:T(8,128)S(1)}, f32[13,128,128]{2,1,0:T(8,128)S(1)}, u32[]{:S(2)}, u32[]{:S(2)}) collective-permute-start(f32[13,128,128]{2,1,0:T(8,128)S(1)} %get-tuple-element.19), channel_id=1, source_target_pairs={{0,1},{1,0},{2,3},{3,2},{4,5},{5,4},{6,7},{7,6},{8,9},{9,8},{10,11... | collective-permute-start | bytes 2555912 | tf_op jit(solution)/shard_map/ppermute | solution.py:463
  9.8 10.8 %collective-permute-start.1 = (s16[1680,128]{1,0:T(8,128)(2,1)S(1)}, s16[1680,128]{1,0:T(8,128)(2,1)S(1)}, u32[]{:S(2)}, u32[]{:S(2)}) collective-permute-start(s16[1680,128]{1,0:T(8,128)(2,1)S(1)} %get-tuple-element.20), channel_id=1, source_target_pairs={{0,2},{2,0},{4,6},{6,4},{8,10},{10,8},{12,14},{14,12},{3,7},{7,11}... | collective-permute-start | bytes 1290248 | tf_op jit(solution)/shard_map/ppermute | solution.py:465
  20.6 10.3 %copy-start = (bf16[13,128,256]{2,1,0:T(8,128)(2,1)S(1)}, bf16[13,128,256]{2,1,0:T(8,128)(2,1)}, u32[]{:S(2)}) copy-start(bf16[13,128,256]{2,1,0:T(8,128)(2,1)} %observed.3) | copy-start | bytes 2555908
  20.6 9.8 %collective-permute-start.2 = (s16[1680,128]{1,0:T(8,128)(2,1)S(1)}, s16[1680,128]{1,0:T(8,128)(2,1)S(1)}, u32[]{:S(2)}, u32[]{:S(2)}) collective-permute-start(s16[1680,128]{1,0:T(8,128)(2,1)S(1)} %relay.1), channel_id=1, source_target_pairs={{0,4},{4,8},{8,12},{6,2},{10,6},{14,10},{1,3},{3,1},{5,7},{7,5},{9... | collective-permute-start | bytes 1290248 | tf_op jit(solution)/shard_map/ppermute | solution.py:470
  30.8 2.4 %collective-permute-start.3 = (f32[13,128,128]{2,1,0:T(8,128)S(1)}, f32[13,128,128]{2,1,0:T(8,128)S(1)}, u32[]{:S(2)}, u32[]{:S(2)}) collective-permute-start(f32[13,128,128]{2,1,0:T(8,128)S(1)} %settle.1.value), channel_id=1, source_target_pairs={{0,1},{1,0},{2,3},{3,2},{4,5},{5,4},{6,7},{7,6},{8,9},{9,8},{10,11... | collective-permute-start | bytes 2555912 | tf_op jit(solution)/shard_map/ppermute | solution.py:473

commit v2 on v1

--- a/solution.py
+++ b/solution.py
@@ -99,14 +99,17 @@
     )
     copies = [pltpu.make_async_copy(a, b, small.at[i]) for i, (a, b) in enumerate(pairs)]
 
-    def arrive(q):
-        at = pl.ds(q * group, group)
+    chunks = -(-bands // window)
+    last = bands - (chunks - 1) * window
+
+    def arrive(q, size):
+        at = pl.ds(q * window, size)
         return pltpu.make_async_copy(cube_in.at[at], cube.at[at], large.at[q])
 
     for copy in copies:
         copy.start()
-    for q in range(bands // group):
-        arrive(q).start()
+    for q in range(chunks):
+        arrive(q, window if q < chunks - 1 else last).start()
     copies[1].wait()
     wide[...] = values[...].astype(jnp.float32)
     spread = pltpu.make_async_copy(wide, weights, small.at[len(pairs)])
@@ -147,14 +150,15 @@
     spread.wait()
 
     def ready(q, carry):
-        arrive(q).wait()
+        pl.when(q < chunks - 1)(lambda: arrive(q, window).wait())
+        pl.when(q == chunks - 1)(lambda: arrive(chunks - 1, last).wait())
         return carry
 
     def one(n, arrived):
         m = order[n]
         low = SPB * start[m] - bands * me
         stop = jnp.minimum(low + window, bands)
-        needed = lax.div(stop + (group - 1), jnp.int32(group))
+        needed = lax.div(stop - 1, jnp.int32(window)) + 1
         lax.fori_loop(arrived, needed, ready, 0)
         whole = jnp.logical_and(low >= 0, low + window <= bands)
 
@@ -190,7 +194,7 @@
         return jnp.maximum(arrived, needed)
 
     arrived = lax.fori_loop(before, until, one, jnp.int32(0))
-    lax.fori_loop(arrived, bands // group, ready, 0)
+    lax.fori_loop(arrived, chunks, ready, 0)
 
     side = table[...]
     planes, odd, units = ownership(count)
@@ -278,20 +282,19 @@
     by_core(lambda: encode(total, message), summing)
 
 
-def centre(picked, total, base, term):
-    units, lines, _ = total.shape
-
-    def only(m, value):
-        base[m] = value
-
-    def both(m, value):
-        base[m] = value[:lines]
-        term[m] = value[lines:]
-
-    stack = jnp.concatenate([picked[0], picked[2]], axis=0)
-    by_core(
-        lambda: blurred(picked[0], units, lambda m: total[m], only),
-        lambda: blurred(stack, units, lambda m: total[m], both),
+def centre(picked, total, other_total, base, other_base, term):
+    units = total.shape[0]
+
+    def into(out):
+        def put(m, value):
+            out[m] = value
+
+        return put
+
+    blurred(picked[0], units, lambda m: total[m], into(base))
+    blurred(picked[0], units, lambda m: other_total[m], into(other_base))
+    pl.when(lax.axis_index("band") != 0)(
+        lambda: blurred(picked[2], units, lambda m: total[m], into(term))
     )
 
 
@@ -310,30 +313,30 @@
     by_core(forward, add)
 
 
-def beside(picked, base, near, total):
-    units, lines, _ = base.shape
+def beside(picked, near, product):
+    units, lines, _ = product.shape
 
     def put(m, value):
-        total[m] = base[m] + value
-
-    def keep():
-        total[...] = base[...]
-
-    by_core(lambda: blurred(picked[1], units, decode(near, units, lines), put), keep)
-
-
-def settle(picked, base, received, total):
-    units, lines, _ = base.shape
-    plane = decode(received, units, lines)
+        product[m] = value
+
+    plane = decode(near, units, lines)
+    pl.when(lax.axis_index("band") == 0)(lambda: blurred(picked[1], units, plane, put))
+
+
+def settle(picked, product, received, message, total):
+    units, lines, _ = product.shape
 
     def put(m, value):
-        total[m] = base[m] + value
+        total[m] = product[m] + value
 
     def add():
-        for m in range(units):
-            put(m, plane(m))
-
-    by_core(lambda: blurred(picked[2], units, plane, put), add)
+        blurred(picked[2], units, decode(received, units, lines), put)
+        encode(total, message)
+
+    def forward():
+        message[...] = received[...]
+
+    by_core(add, forward)
 
 def arccos(x):
     size = jnp.abs(x)
@@ -350,13 +353,14 @@
     return jnp.where(big, outer, inner)
 
 
-def finish(second, observed, value, *rest):
+def finish(second, observed, base, message, *rest):
     if second:
-        sums, _, image, angles, angle, sems = rest
+        sums, _, image, angles, angle, value, sems = rest
     else:
-        image, sums, sems = rest
-    units, lines, half = value.shape
+        image, sums, value, sems = rest
+    units, lines, half = base.shape
     count = observed.shape[0]
+    plane = decode(message, units, lines)
 
     def work(core):
         places = [(m, slice(c * half, (c + 1) * half)) for m, c in units_of(core, count)]
@@ -364,8 +368,9 @@
             pltpu.make_async_copy(value.at[n], image.at[m, :, at], sems.at[n])
             for n, (m, at) in enumerate(places)
         ]
-        for copy in copies:
-            copy.start()
+        for n in range(units):
+            value[n] = base[n] + plane(n)
+            copies[n].start()
         for c in range(2):
             at = slice(c * half, (c + 1) * half)
             inner = jnp.zeros((lines, half), jnp.float32)
@@ -455,7 +460,7 @@
             pltpu.VMEM((2 * cols, cols), across_kernels.dtype),
             pltpu.SMEM((count,), jnp.int32),
             pltpu.SemaphoreType.DMA((len(inputs),)),
-            pltpu.SemaphoreType.DMA((bands // math.gcd(SPB, bands),)),
+            pltpu.SemaphoreType.DMA((-(-bands // resp_values.shape[1]),)),
         ],
         flops=4 * count * lines * cols * cols,
     )
@@ -463,31 +468,36 @@
     other = lax.ppermute(send, "band", swap)
     total, message = call(share, (picked, keep, other), [VMEM] * 3, [part, coded], scratch=work)
     near = lax.ppermute(message, ("line", "band"), cores(partner, odd_up))
-    base, term = call(centre, (picked, total), [VMEM] * 2, [part] * 2, flops=2 * unit * units)
-    near, base, term = lax.optimization_barrier((near, base, term))
+    other_total = lax.ppermute(total, "band", swap)
+    base, other_base, term = call(
+        centre, (picked, total, other_total), [VMEM] * 3, [part] * 3, flops=3 * unit * units
+    )
+    near, base, other_base, term = lax.optimization_barrier((near, base, other_base, term))
     (message,) = call(relay, (term, near), [VMEM] * 2, [coded], scratch=work)
-    message, near, base = lax.optimization_barrier((message, near, base))
+    message, near = lax.optimization_barrier((message, near))
     far = lax.ppermute(message, ("line", "band"), cores(even_up, partner))
-    (base,) = call(beside, (picked, base, near), [VMEM] * 3, [part], flops=unit * units)
-    (mine,) = call(settle, (picked, base, far), [VMEM] * 3, [part], flops=unit * units)
-    other = lax.ppermute(mine, "band", swap)
+    (product,) = call(beside, (picked, near), [VMEM] * 2, [part], flops=unit * units)
+    (message,) = call(
+        settle, (picked, product, far), [VMEM] * 3, [coded], scratch=work, flops=unit * units
+    )
+    other_message = lax.ppermute(message, "band", swap)
     image = shape((count, lines, cols), f32)
     image, sums = call(
         functools.partial(finish, False),
-        (observed, mine),
-        [VMEM] * 2,
+        (observed, base, message),
+        [VMEM] * 3,
         [image, shape((3, lines, cols), f32)],
-        scratch=[pltpu.SemaphoreType.DMA((units,))],
+        scratch=work + [pltpu.SemaphoreType.DMA((units,))],
         out_specs=[HBM, VMEM],
     )
     image, angles = call(
         functools.partial(finish, True),
-        (observed, other, sums, image),
-        [VMEM] * 3 + [HBM],
+        (observed, other_base, other_message, sums, image),
+        [VMEM] * 4 + [HBM],
         [image, shape((lines, cols), f32)],
-        scratch=[pltpu.VMEM((lines, cols), f32), pltpu.SemaphoreType.DMA((units + 1,))],
+        scratch=[pltpu.VMEM((lines, cols), f32), *work, pltpu.SemaphoreType.DMA((units + 1,))],
         out_specs=[HBM] * 2,
-        aliases={3: 0},
+        aliases={4: 0},
     )
     return image, angles
 

time: 34.7 us -> 34.5 us (level)
  waiting for transfers between devices: 14.4 us -> 13.7 us
  starting transfers between devices: 9.52 us -> 9.93 us
    ppermute x1 -> x2, starting transfers between devices: 0.07 us -> 0.74 us  [the longest x1 0.66 us: on_device(): other_total = lax.ppermute(total, 'band', swap)]
    ppermute x1 -> x2, waiting for transfers between devices: 1.34 us -> 0.72 us  [the longest x1 0.72 us: on_device(): other_message = lax.ppermute(message, 'band', swap)]
    ppermute x1, starting transfers between devices: 4.64 us -> 4.24 us  [on_device(): near = lax.ppermute(message, ('line', 'band'), cores(partner, odd_up))]
  transfers between devices with their start and end apart: 4 -> 5, of which waited for: 4 -> 4; matrix products, arithmetic and copies ran while one was open for 0% -> 0% of each run, Pallas kernels for 5% -> 5%
where the time goes in v2:
time: 34.5 us; the launch traced here: 33.9 us
  waiting for transfers between devices  13.7 us (40%)
  starting transfers between devices  9.93 us (29%)
  Pallas kernels  9.56 us (28%)
  between operations  0.73 us (2%)
    pallas_call x8, Pallas kernels, call(): pl.pallas_call(kernel, in_specs=specs, out_specs=out_specs or [VMEM] * le...  9.56 us
    ppermute x1, waiting for transfers between devices, on_device(): near = lax.ppermute(message, ('line', 'band'), cores(partner, odd_up))  5.68 us
    ppermute x1, waiting for transfers between devices, on_device(): far = lax.ppermute(message, ('line', 'band'), cores(even_up, partner))  5.26 us
    ppermute x1, starting transfers between devices, on_device(): near = lax.ppermute(message, ('line', 'band'), cores(partner, odd_up))  4.24 us
    ppermute x1, starting transfers between devices, on_device(): far = lax.ppermute(message, ('line', 'band'), cores(even_up, partner))  4.14 us
    ppermute x1, waiting for transfers between devices, on_device(): other = lax.ppermute(send, 'band', swap)  2.01 us
    ppermute x1, starting transfers between devices, on_device(): other = lax.ppermute(send, 'band', swap)  0.82 us
    ppermute x1, waiting for transfers between devices, on_device(): other_message = lax.ppermute(message, 'band', swap)  0.72 us
  transfers between devices with their start and end apart: 5, of which 4 were waited for; matrix products, arithmetic and copies ran while one was open for 0% of the time, Pallas kernels for 5%

profile of v2, /device:TPU:0, one launch (start us, length us, event | category | flops | bytes accessed | tf_op | source)
XLA Modules:
  0.0 33.9 jit_solution(6077613605299597320)
XLA Ops:
  0.6 5.5 %fold.1 = (f32[13,128,128]{2,1,0:T(8,128)S(1)}, f32[13,128,128]{2,1,0:T(8,128)S(1)}, bf16[3,128,128]{2,1,0:T(8,128)(2,1)S(1)}) custom-call(s32[13]{0:T(128)} %start_in.1, s32[3]{0:T(128)} %offsets_in.1, bf16[13,20]{1,0:T(8,128)(2,1)} %values_in.1, bf16[3,128,128]{2,1,0:T(8,128)(2,1)} %blocks_in.1, s32[3]{0:T(128)} %along_offsets_in.1, ...), custom_call_target="tpu_custom_call" | custom-call | flops 436207616 | bytes 9536084 | tf_op jit(solution)/shard_map/fold/pallas_call | solution.py:37
  6.2 0.8 %collective-permute-start = (f32[13,128,128]{2,1,0:T(8,128)S(1)}, f32[13,128,128]{2,1,0:T(8,128)S(1)}, u32[]{:S(2)}, u32[]{:S(2)}) collective-permute-start(f32[13,128,128]{2,1,0:T(8,128)S(1)} %get-tuple-element.20), channel_id=1, source_target_pairs={{0,1},{1,0},{2,3},{3,2},{4,5},{5,4},{6,7},{7,6},{8,9},{9,8},{10,11... | collective-permute-start | bytes 2555912 | tf_op jit(solution)/shard_map/ppermute | solution.py:468
  7.0 2.0 %collective-permute-done.other = f32[13,128,128]{2,1,0:T(8,128)S(1)} collective-permute-done((f32[13,128,128]{2,1,0:T(8,128)S(1)}, f32[13,128,128]{2,1,0:T(8,128)S(1)}, u32[]{:S(2)}, u32[]{:S(2)}) %collective-permute-start) | collective-permute-done | bytes 852000 | tf_op jit(solution)/shard_map/ppermute | solution.py:468
  9.0 0.3 share.1
  9.3 0.7 %collective-permute-start.2 = (f32[13,128,128]{2,1,0:T(8,128)S(1)}, f32[13,128,128]{2,1,0:T(8,128)S(1)}, u32[]{:S(2)}, u32[]{:S(2)}) collective-permute-start(f32[13,128,128]{2,1,0:T(8,128)S(1)} %get-tuple-element.22.total), channel_id=1, source_target_pairs={{0,1},{1,0},{2,3},{3,2},{4,5},{5,4},{6,7},{7,6},{8,9},{9,8},{10,11... | collective-permute-start | bytes 2555912 | tf_op jit(solution)/shard_map/ppermute | solution.py:471
  10.0 4.2 %collective-permute-start.1 = (s16[1680,128]{1,0:T(8,128)(2,1)S(1)}, s16[1680,128]{1,0:T(8,128)(2,1)S(1)}, u32[]{:S(2)}, u32[]{:S(2)}) collective-permute-start(s16[1680,128]{1,0:T(8,128)(2,1)S(1)} %get-tuple-element.21), channel_id=1, source_target_pairs={{0,2},{2,0},{4,6},{6,4},{8,10},{10,8},{12,14},{14,12},{3,7},{7,11}... | collective-permute-start | bytes 1290248 | tf_op jit(solution)/shard_map/ppermute | solution.py:470
  14.2 0.0 collective-permute-done.2.other_total
  14.3 0.4 %centre.1 = (f32[13,128,128]{2,1,0:T(8,128)S(1)}, f32[13,128,128]{2,1,0:T(8,128)S(1)}, f32[13,128,128]{2,1,0:T(8,128)S(1)}) custom-call(bf16[3,128,128]{2,1,0:T(8,128)(2,1)S(1)} %get-tuple-element.18.picked, f32[13,128,128]{2,1,0:T(8,128)S(1)} %get-tuple-element.22.total, f32[13,128,128]{2,1,0:T(8,128)S(1)} %collective-permute-done.2.other_total), custom_call_target="tpu_custom_call" | custom-call | flops 327155712 | bytes 4358144 | tf_op jit(solution)/shard_map/centre/pallas_call | solution.py:37
  14.7 5.7 %collective-permute-done.1.received.near = s16[1680,128]{1,0:T(8,128)(2,1)S(1)} collective-permute-done((s16[1680,128]{1,0:T(8,128)(2,1)S(1)}, s16[1680,128]{1,0:T(8,128)(2,1)S(1)}, u32[]{:S(2)}, u32[]{:S(2)}) %collective-permute-start.1) | collective-permute-done | bytes 430112 | tf_op jit(solution)/shard_map/ppermute | solution.py:470
  20.4 0.0 copy-start
  20.4 4.1 %collective-permute-start.3 = (s16[1680,128]{1,0:T(8,128)(2,1)S(1)}, s16[1680,128]{1,0:T(8,128)(2,1)S(1)}, u32[]{:S(2)}, u32[]{:S(2)}) collective-permute-start(s16[1680,128]{1,0:T(8,128)(2,1)S(1)} %relay.1), channel_id=1, source_target_pairs={{0,4},{4,8},{8,12},{6,2},{10,6},{14,10},{1,3},{3,1},{5,7},{7,5},{9... | collective-permute-start | bytes 1290248 | tf_op jit(solution)/shard_map/ppermute | solution.py:478
  24.6 0.4 %beside.1.product = f32[13,128,128]{2,1,0:T(8,128)S(1)} custom-call(bf16[3,128,128]{2,1,0:T(8,128)(2,1)S(1)} %get-tuple-element.18.picked, s16[1680,128]{1,0:T(8,128)(2,1)S(1)} %collective-permute-done.1.received.near), custom_call_target="tpu_custom_call" | custom-call | flops 109051904 | bytes 1380352 | tf_op jit(solution)/shard_map/beside/pallas_call | solution.py:37
  25.0 5.3 %collective-permute-done.3.received = s16[1680,128]{1,0:T(8,128)(2,1)S(1)} collective-permute-done((s16[1680,128]{1,0:T(8,128)(2,1)S(1)}, s16[1680,128]{1,0:T(8,128)(2,1)S(1)}, u32[]{:S(2)}, u32[]{:S(2)}) %collective-permute-start.3) | collective-permute-done | bytes 430112 | tf_op jit(solution)/shard_map/ppermute | solution.py:478
  30.2 0.5 %settle.1.message = s16[1680,128]{1,0:T(8,128)(2,1)S(1)} custom-call(bf16[3,128,128]{2,1,0:T(8,128)(2,1)S(1)} %get-tuple-element.18.picked, f32[13,128,128]{2,1,0:T(8,128)S(1)} %beside.1.product, s16[1680,128]{1,0:T(8,128)(2,1)S(1)} %collective-permute-done.3.received), custom_call_target="tpu_custom_call" | custom-call | flops 109051904 | bytes 1810432 | tf_op jit(solution)/shard_map/settle/pallas_call | solution.py:37
  30.8 0.1 collective-permute-start.4
  30.9 0.0 copy-done
  30.9 1.0 %finish.2 = (f32[13,128,256]{2,1,0:T(8,128)}, f32[3,128,256]{2,1,0:T(8,128)S(1)}) custom-call(bf16[13,128,256]{2,1,0:T(8,128)(2,1)S(1)} %copy-done, f32[13,128,128]{2,1,0:T(8,128)S(1)} %get-tuple-element.31.base, s16[1680,128]{1,0:T(8,128)(2,1)S(1)} %settle.1.message), custom_call_target="tpu_custom_call" | custom-call | bytes 4231168 | tf_op jit(solution)/shard_map/finish/pallas_call | solution.py:37
  31.9 0.7 %collective-permute-done.4.message = s16[1680,128]{1,0:T(8,128)(2,1)S(1)} collective-permute-done((s16[1680,128]{1,0:T(8,128)(2,1)S(1)}, s16[1680,128]{1,0:T(8,128)(2,1)S(1)}, u32[]{:S(2)}, u32[]{:S(2)}) %collective-permute-start.4) | collective-permute-done | bytes 430112 | tf_op jit(solution)/shard_map/ppermute | solution.py:483
  32.6 1.3 %finish.3 = (f32[13,128,256]{2,1,0:T(8,128)}, f32[128,256]{1,0:T(8,128)}) custom-call(bf16[13,128,256]{2,1,0:T(8,128)(2,1)S(1)} %copy-done, f32[13,128,128]{2,1,0:T(8,128)S(1)} %get-tuple-element.26.base, s16[1680,128]{1,0:T(8,128)(2,1)S(1)} %collective-permute-done.4.message, ...), custom_call_target="tpu_custom_call", output_to_operand_aliasing={{0}: (4, {})} | custom-call | bytes 6066176 | tf_op jit(solution)/shard_map/finish/pallas_call | solution.py:37
  (1 shorter events, 0.0 us)
Async XLA Ops:
  6.2 2.8 %collective-permute-start = (f32[13,128,128]{2,1,0:T(8,128)S(1)}, f32[13,128,128]{2,1,0:T(8,128)S(1)}, u32[]{:S(2)}, u32[]{:S(2)}) collective-permute-start(f32[13,128,128]{2,1,0:T(8,128)S(1)} %get-tuple-element.20), channel_id=1, source_target_pairs={{0,1},{1,0},{2,3},{3,2},{4,5},{5,4},{6,7},{7,6},{8,9},{9,8},{10,11... | collective-permute-start | bytes 2555912 | tf_op jit(solution)/shard_map/ppermute | solution.py:468
  9.3 4.9 %collective-permute-start.2 = (f32[13,128,128]{2,1,0:T(8,128)S(1)}, f32[13,128,128]{2,1,0:T(8,128)S(1)}, u32[]{:S(2)}, u32[]{:S(2)}) collective-permute-start(f32[13,128,128]{2,1,0:T(8,128)S(1)} %get-tuple-element.22.total), channel_id=1, source_target_pairs={{0,1},{1,0},{2,3},{3,2},{4,5},{5,4},{6,7},{7,6},{8,9},{9,8},{10,11... | collective-permute-start | bytes 2555912 | tf_op jit(solution)/shard_map/ppermute | solution.py:471
  10.0 10.4 %collective-permute-start.1 = (s16[1680,128]{1,0:T(8,128)(2,1)S(1)}, s16[1680,128]{1,0:T(8,128)(2,1)S(1)}, u32[]{:S(2)}, u32[]{:S(2)}) collective-permute-start(s16[1680,128]{1,0:T(8,128)(2,1)S(1)} %get-tuple-element.21), channel_id=1, source_target_pairs={{0,2},{2,0},{4,6},{6,4},{8,10},{10,8},{12,14},{14,12},{3,7},{7,11}... | collective-permute-start | bytes 1290248 | tf_op jit(solution)/shard_map/ppermute | solution.py:470
  20.4 10.4 %copy-start = (bf16[13,128,256]{2,1,0:T(8,128)(2,1)S(1)}, bf16[13,128,256]{2,1,0:T(8,128)(2,1)}, u32[]{:S(2)}) copy-start(bf16[13,128,256]{2,1,0:T(8,128)(2,1)} %observed.3) | copy-start | bytes 2555908
  20.4 9.8 %collective-permute-start.3 = (s16[1680,128]{1,0:T(8,128)(2,1)S(1)}, s16[1680,128]{1,0:T(8,128)(2,1)S(1)}, u32[]{:S(2)}, u32[]{:S(2)}) collective-permute-start(s16[1680,128]{1,0:T(8,128)(2,1)S(1)} %relay.1), channel_id=1, source_target_pairs={{0,4},{4,8},{8,12},{6,2},{10,6},{14,10},{1,3},{3,1},{5,7},{7,5},{9... | collective-permute-start | bytes 1290248 | tf_op jit(solution)/shard_map/ppermute | solution.py:478
  30.8 1.8 %collective-permute-start.4 = (s16[1680,128]{1,0:T(8,128)(2,1)S(1)}, s16[1680,128]{1,0:T(8,128)(2,1)S(1)}, u32[]{:S(2)}, u32[]{:S(2)}) collective-permute-start(s16[1680,128]{1,0:T(8,128)(2,1)S(1)} %settle.1.message), channel_id=1, source_target_pairs={{0,1},{1,0},{2,3},{3,2},{4,5},{5,4},{6,7},{7,6},{8,9},{9,8},{10,11... | collective-permute-start | bytes 1290248 | tf_op jit(solution)/shard_map/ppermute | solution.py:483

commit v3 on v2

--- a/solution.py
+++ b/solution.py
@@ -221,21 +221,23 @@
     return count * lines + -(-count // 16) * 16
 
 
-def encode(source, message):
-    units, lines, half = source.shape
-    largest = jnp.max(jnp.abs(source[...]), axis=1)
+def encode(source, span, message):
+    _, lines, half = source.shape
+    units = span[1] - span[0]
+    largest = jnp.max(jnp.abs(source[span[0] : span[1]]), axis=1)
     level = jnp.ceil(jnp.log2(jnp.maximum(largest, 1e-30)) * STEPS)
     factor = PEAK * jnp.exp2(level * (-1.0 / STEPS))
     for m in range(units):
-        coded = jnp.floor(source[m] * factor[m : m + 1, :] + 0.5).astype(jnp.int32)
+        coded = jnp.floor(source[span[0] + m] * factor[m : m + 1, :] + 0.5).astype(jnp.int32)
         message[m * lines : (m + 1) * lines, :] = coded.astype(jnp.int16)
     spare = message.shape[0] - units * lines - units
     level = jnp.concatenate([level, jnp.zeros((spare, half), jnp.float32)], axis=0)
     message[units * lines :, :] = level.astype(jnp.int32).astype(jnp.int16)
 
 
-def decode(message, count, lines):
-    level = message[count * lines :, :].astype(jnp.int32).astype(jnp.float32)
+def decode(message, span, lines):
+    units = span[1] - span[0]
+    level = message[units * lines :, :].astype(jnp.int32).astype(jnp.float32)
     scale = jnp.exp2(level * (1.0 / STEPS)) * (1.0 / PEAK)
 
     def plane(m):
@@ -269,17 +271,22 @@
     pl.when(me != 0)(one)
 
 
-def share(picked, keep, other, total, message, product):
+def share(spans, picked, keep, other, total, *rest):
+    messages, product = rest[:-1], rest[-1]
     total[...] = keep[...] + other[...]
+
+    def coding(source):
+        for span, message in zip(spans, messages):
+            encode(source, span, message)
 
     def summing():
         def put(m, value):
             product[m] = value
 
         blurred(picked[1], total.shape[0], lambda m: total[m], put)
-        encode(product, message)
-
-    by_core(lambda: encode(total, message), summing)
+        coding(product)
+
+    by_core(lambda: coding(total), summing)
 
 
 def centre(picked, total, other_total, base, other_base, term):
@@ -298,45 +305,44 @@
     )
 
 
-def relay(term, received, message, total):
-    units, lines, _ = term.shape
-
+def relay(span, term, received, message, total):
     def forward():
         message[...] = received[...]
 
     def add():
-        plane = decode(received, units, lines)
-        for m in range(units):
-            total[m] = term[m] + plane(m)
-        encode(total, message)
+        plane = decode(received, span, term.shape[1])
+        for m in range(*span):
+            total[m] = term[m] + plane(m - span[0])
+        encode(total, span, message)
 
     by_core(forward, add)
 
 
-def beside(picked, near, product):
+def beside(span, picked, near, product):
     units, lines, _ = product.shape
 
     def put(m, value):
         product[m] = value
 
-    plane = decode(near, units, lines)
+    plane = decode(near, span, lines)
     pl.when(lax.axis_index("band") == 0)(lambda: blurred(picked[1], units, plane, put))
 
 
-def settle(picked, product, received, message, total):
+def settle(span, picked, product, received, message, total):
     units, lines, _ = product.shape
 
     def put(m, value):
         total[m] = product[m] + value
 
     def add():
-        blurred(picked[2], units, decode(received, units, lines), put)
-        encode(total, message)
+        blurred(picked[2], units, decode(received, span, lines), put)
+        encode(total, (0, units), message)
 
     def forward():
         message[...] = received[...]
 
     by_core(add, forward)
+
 
 def arccos(x):
     size = jnp.abs(x)
@@ -353,23 +359,26 @@
     return jnp.where(big, outer, inner)
 
 
-def finish(second, observed, base, message, *rest):
-    if second:
-        sums, _, image, angles, angle, value, sems = rest
-    else:
-        image, sums, value, sems = rest
-    units, lines, half = base.shape
+def finish(flip, span, given, observed, base, message, *rest):
+    begun, rest = rest[:given], rest[given:]
+    if flip or span[0] > 0:
+        rest = rest[1:]
+    image, out, value, *rest, sems = rest
+    units = span[1] - span[0]
+    _, lines, half = base.shape
     count = observed.shape[0]
-    plane = decode(message, units, lines)
+    plane = decode(message, span, lines)
 
     def work(core):
-        places = [(m, slice(c * half, (c + 1) * half)) for m, c in units_of(core, count)]
+        places = [
+            (m, slice(c * half, (c + 1) * half)) for m, c in units_of(core, count)[slice(*span)]
+        ]
         copies = [
             pltpu.make_async_copy(value.at[n], image.at[m, :, at], sems.at[n])
             for n, (m, at) in enumerate(places)
         ]
         for n in range(units):
-            value[n] = base[n] + plane(n)
+            value[n] = base[span[0] + n] + plane(n)
             copies[n].start()
         for c in range(2):
             at = slice(c * half, (c + 1) * half)
@@ -379,28 +388,31 @@
                 if where == at:
                     inner = inner + value[n] * observed[m, :, at].astype(jnp.float32)
                     left = left + value[n] * value[n]
-            if second:
-                bound = jnp.sqrt(left + sums[1, :, at]) * sums[2, :, at]
-                ratio = (inner + sums[0, :, at]) / jnp.maximum(bound, 1.0)
-                angle[:, at] = arccos(jnp.clip(ratio, -1.0, 1.0))
-            else:
+            if given:
+                inner = inner + begun[0][0, :, at]
+                left = left + begun[0][1, :, at]
+            if given == 2:
+                bound = jnp.sqrt(left + begun[1][1, :, at]) * begun[1][2, :, at]
+                ratio = (inner + begun[1][0, :, at]) / jnp.maximum(bound, 1.0)
+                rest[0][:, at] = arccos(jnp.clip(ratio, -1.0, 1.0))
+                continue
+            out[0, :, at] = inner
+            out[1, :, at] = left
+            if given:
+                out[2, :, at] = begun[0][2, :, at]
+            elif not flip:
                 right = jnp.zeros((lines, half), jnp.float32)
                 for m in range(count):
                     seen = observed[m, :, at].astype(jnp.float32)
                     right = right + seen * seen
-                sums[0, :, at] = inner
-                sums[1, :, at] = left
-                sums[2, :, at] = jnp.sqrt(right)
-        if second:
-            copies.append(pltpu.make_async_copy(angle, angles, sems.at[units]))
+                out[2, :, at] = jnp.sqrt(right)
+        if given == 2:
+            copies.append(pltpu.make_async_copy(rest[0], out, sems.at[units]))
             copies[-1].start()
         for copy in copies:
             copy.wait()
 
-    if second:
-        by_core(lambda: work(1), lambda: work(0))
-    else:
-        by_core(lambda: work(0), lambda: work(1))
+    by_core(lambda: work(1 if flip else 0), lambda: work(0 if flip else 1))
 
 
 def on_device(
@@ -429,7 +441,8 @@
         return [(2 * a, 2 * b) for a, b in zero] + [(2 * a + 1, 2 * b + 1) for a, b in one]
 
     part = shape((units, lines, half), f32)
-    coded = shape((coded_rows(units, lines), half), i16)
+    spans = [(0, (units + 1) // 2), ((units + 1) // 2, units)]
+    coded = [shape((coded_rows(b - a, lines), half), i16) for a, b in spans]
     unit = 4 * lines * lines * half
 
     inputs = (
@@ -466,40 +479,67 @@
     )
     work = [pltpu.VMEM(part.shape, f32)]
     other = lax.ppermute(send, "band", swap)
-    total, message = call(share, (picked, keep, other), [VMEM] * 3, [part, coded], scratch=work)
-    near = lax.ppermute(message, ("line", "band"), cores(partner, odd_up))
+    total, *sent = call(
+        functools.partial(share, spans),
+        (picked, keep, other),
+        [VMEM] * 3,
+        [part, *coded],
+        scratch=work,
+        flops=unit * units,
+    )
+    near = [lax.ppermute(x, ("line", "band"), cores(partner, odd_up)) for x in sent]
     other_total = lax.ppermute(total, "band", swap)
     base, other_base, term = call(
         centre, (picked, total, other_total), [VMEM] * 3, [part] * 3, flops=3 * unit * units
     )
-    near, base, other_base, term = lax.optimization_barrier((near, base, other_base, term))
-    (message,) = call(relay, (term, near), [VMEM] * 2, [coded], scratch=work)
-    message, near = lax.optimization_barrier((message, near))
-    far = lax.ppermute(message, ("line", "band"), cores(even_up, partner))
-    (product,) = call(beside, (picked, near), [VMEM] * 2, [part], flops=unit * units)
-    (message,) = call(
-        settle, (picked, product, far), [VMEM] * 3, [coded], scratch=work, flops=unit * units
-    )
-    other_message = lax.ppermute(message, "band", swap)
+    far, product = [], []
+    for i, span in enumerate(spans):
+        (message,) = call(
+            functools.partial(relay, span), (term, near[i]), [VMEM] * 2, [coded[i]], scratch=work
+        )
+        message, near[i] = lax.optimization_barrier((message, near[i]))
+        far.append(lax.ppermute(message, ("line", "band"), cores(even_up, partner)))
+        planes = shape((span[1] - span[0], lines, half), f32)
+        product += call(
+            functools.partial(beside, span),
+            (picked, near[i]),
+            [VMEM] * 2,
+            [planes],
+            flops=unit * planes.shape[0],
+        )
     image = shape((count, lines, cols), f32)
-    image, sums = call(
-        functools.partial(finish, False),
-        (observed, base, message),
-        [VMEM] * 3,
-        [image, shape((3, lines, cols), f32)],
-        scratch=work + [pltpu.SemaphoreType.DMA((units,))],
-        out_specs=[HBM, VMEM],
-    )
-    image, angles = call(
-        functools.partial(finish, True),
-        (observed, other_base, other_message, sums, image),
-        [VMEM] * 4 + [HBM],
-        [image, shape((lines, cols), f32)],
-        scratch=[pltpu.VMEM((lines, cols), f32), *work, pltpu.SemaphoreType.DMA((units + 1,))],
-        out_specs=[HBM] * 2,
-        aliases={4: 0},
-    )
-    return image, angles
+    three = shape((3, lines, cols), f32)
+    made = None
+    sums = [[], []]
+    for i, span in enumerate(spans):
+        planes = product[i].shape
+        if i:
+            far[i], made, sums = lax.optimization_barrier((far[i], made, sums))
+        (message,) = call(
+            functools.partial(settle, span),
+            (picked, product[i], far[i]),
+            [VMEM] * 3,
+            [coded[i]],
+            scratch=[pltpu.VMEM(planes, f32)],
+            flops=unit * planes[0],
+        )
+        other_message = lax.ppermute(message, "band", swap)
+        for flip, (start, coming) in enumerate(((base, message), (other_base, other_message))):
+            given = sums[flip] + (sums[0] if flip and i else [])
+            last = len(given) == 2
+            inputs = [observed, start, coming, *given]
+            scratch = [pltpu.VMEM(planes, f32)] + [pltpu.VMEM((lines, cols), f32)] * last
+            made, out = call(
+                functools.partial(finish, flip, span, len(given)),
+                inputs + ([] if made is None else [made]),
+                [VMEM] * len(inputs) + ([] if made is None else [HBM]),
+                [image, shape((lines, cols), f32) if last else three],
+                scratch=scratch + [pltpu.SemaphoreType.DMA((planes[0] + 1,))],
+                out_specs=[HBM, HBM if last else VMEM],
+                aliases={} if made is None else {len(inputs): 0},
+            )
+            sums[flip] = [out]
+    return made, out
 
 
 def solution(mesh):

time: 34.5 us -> 40.4 us (1.17)
  starting transfers between devices: 9.93 us -> 15.3 us
  Pallas kernels: 9.56 us -> 11.5 us
  waiting for transfers between devices: 13.7 us -> 12.4 us
    ppermute x2 -> x4, starting transfers between devices: 8.38 us -> 14.2 us  [the longest x2 7.47 us: on_device(): far.append(lax.ppermute(message, ('line', 'band'), cores(even_up, partner)))]
    pallas_call x8 -> x13, Pallas kernels: 9.56 us -> 11.5 us  [call(): pl.pallas_call(kernel, in_specs=specs, out_specs=out_specs or [VMEM] * le...]
    ppermute x2 -> x4, waiting for transfers between devices: 10.9 us -> 9.73 us  [the longest x2 7.32 us: on_device(): lax.ppermute(x, ('line', 'band'), cores(partner, odd_up))]
    ppermute x1, starting transfers between devices: 0.82 us -> 0.36 us  [on_device(): other = lax.ppermute(send, 'band', swap)]
  transfers between devices with their start and end apart: 5 -> 8, of which waited for: 4 -> 6; matrix products, arithmetic and copies ran while one was open for 0% -> 0% of each run, Pallas kernels for 5% -> 10%
where the time goes in v3:
time: 40.4 us; the launch traced here: 40 us
  starting transfers between devices  15.3 us (38%)
  waiting for transfers between devices  12.4 us (31%)
  Pallas kernels  11.5 us (28%)
  between operations  0.81 us (2%)
    pallas_call x13, Pallas kernels, call(): pl.pallas_call(kernel, in_specs=specs, out_specs=out_specs or [VMEM] * le...  11.5 us
    ppermute x2, starting transfers between devices, on_device(): far.append(lax.ppermute(message, ('line', 'band'), cores(even_up, partner)))  7.47 us
    ppermute x2, waiting for transfers between devices, on_device(): lax.ppermute(x, ('line', 'band'), cores(partner, odd_up))  7.32 us
    ppermute x2, starting transfers between devices, on_device(): lax.ppermute(x, ('line', 'band'), cores(partner, odd_up))  6.76 us
    ppermute x2, waiting for transfers between devices, on_device(): far.append(lax.ppermute(message, ('line', 'band'), cores(even_up, partner)))  2.41 us
    ppermute x1, waiting for transfers between devices, on_device(): other = lax.ppermute(send, 'band', swap)  2.09 us
  transfers between devices with their start and end apart: 8, of which 6 were waited for; matrix products, arithmetic and copies ran while one was open for 0% of the time, Pallas kernels for 10%

profile of v3, /device:TPU:0, one launch (start us, length us, event | category | flops | bytes accessed | tf_op | source)
XLA Modules:
  0.0 40.0 jit_solution(14062336191087282581)
XLA Ops:
  0.6 5.8 %fold.1 = (f32[13,128,128]{2,1,0:T(8,128)S(1)}, f32[13,128,128]{2,1,0:T(8,128)S(1)}, bf16[3,128,128]{2,1,0:T(8,128)(2,1)S(1)}) custom-call(s32[13]{0:T(128)} %start_in.1, s32[3]{0:T(128)} %offsets_in.1, bf16[13,20]{1,0:T(8,128)(2,1)} %values_in.1, bf16[3,128,128]{2,1,0:T(8,128)(2,1)} %blocks_in.1, s32[3]{0:T(128)} %along_offsets_in.1, ...), custom_call_target="tpu_custom_call" | custom-call | flops 436207616 | bytes 9536084 | tf_op jit(solution)/shard_map/fold/pallas_call | solution.py:37
  6.5 0.4 collective-permute-start
  6.8 2.1 %collective-permute-done.other = f32[13,128,128]{2,1,0:T(8,128)S(1)} collective-permute-done((f32[13,128,128]{2,1,0:T(8,128)S(1)}, f32[13,128,128]{2,1,0:T(8,128)S(1)}, u32[]{:S(2)}, u32[]{:S(2)}) %collective-permute-start) | collective-permute-done | bytes 852000 | tf_op jit(solution)/shard_map/ppermute | solution.py:481
  8.9 0.4 share.1
  9.3 0.6 %collective-permute-start.1 = (f32[13,128,128]{2,1,0:T(8,128)S(1)}, f32[13,128,128]{2,1,0:T(8,128)S(1)}, u32[]{:S(2)}, u32[]{:S(2)}) collective-permute-start(f32[13,128,128]{2,1,0:T(8,128)S(1)} %get-tuple-element.28.total), channel_id=1, source_target_pairs={{0,1},{1,0},{2,3},{3,2},{4,5},{5,4},{6,7},{7,6},{8,9},{9,8},{10,11... | collective-permute-start | bytes 2555912 | tf_op jit(solution)/shard_map/ppermute | solution.py:491
  9.8 4.7 %collective-permute-start.4 = (s16[912,128]{1,0:T(8,128)(2,1)S(1)}, s16[912,128]{1,0:T(8,128)(2,1)S(1)}, u32[]{:S(2)}, u32[]{:S(2)}) collective-permute-start(s16[912,128]{1,0:T(8,128)(2,1)S(1)} %get-tuple-element.34), channel_id=1, source_target_pairs={{0,2},{2,0},{4,6},{6,4},{8,10},{10,8},{12,14},{14,12},{3,7},{7,11}... | collective-permute-start | bytes 700424 | tf_op jit(solution)/shard_map/ppermute | solution.py:490
  14.6 0.0 collective-permute-done.1.other_total
  14.6 0.4 %centre.1 = (f32[13,128,128]{2,1,0:T(8,128)S(1)}, f32[13,128,128]{2,1,0:T(8,128)S(1)}, f32[13,128,128]{2,1,0:T(8,128)S(1)}) custom-call(bf16[3,128,128]{2,1,0:T(8,128)(2,1)S(1)} %get-tuple-element.25.picked, f32[13,128,128]{2,1,0:T(8,128)S(1)} %get-tuple-element.28.total, f32[13,128,128]{2,1,0:T(8,128)S(1)} %collective-permute-done.1.other_total), custom_call_target="tpu_custom_call" | custom-call | flops 327155712 | bytes 4358144 | tf_op jit(solution)/shard_map/centre/pallas_call | solution.py:37
  15.0 3.6 %collective-permute-done.4.received.near = s16[912,128]{1,0:T(8,128)(2,1)S(1)} collective-permute-done((s16[912,128]{1,0:T(8,128)(2,1)S(1)}, s16[912,128]{1,0:T(8,128)(2,1)S(1)}, u32[]{:S(2)}, u32[]{:S(2)}) %collective-permute-start.4) | collective-permute-done | bytes 233504 | tf_op jit(solution)/shard_map/ppermute | solution.py:490
  18.6 4.0 %collective-permute-start.5 = (s16[912,128]{1,0:T(8,128)(2,1)S(1)}, s16[912,128]{1,0:T(8,128)(2,1)S(1)}, u32[]{:S(2)}, u32[]{:S(2)}) collective-permute-start(s16[912,128]{1,0:T(8,128)(2,1)S(1)} %relay.3), channel_id=1, source_target_pairs={{0,4},{4,8},{8,12},{6,2},{10,6},{14,10},{1,3},{3,1},{5,7},{7,5},{9... | collective-permute-start | bytes 700424 | tf_op jit(solution)/shard_map/ppermute | solution.py:501
  22.6 0.0 copy-start
  22.6 2.1 %collective-permute-start.2 = (s16[784,128]{1,0:T(8,128)(2,1)S(1)}, s16[784,128]{1,0:T(8,128)(2,1)S(1)}, u32[]{:S(2)}, u32[]{:S(2)}) collective-permute-start(s16[784,128]{1,0:T(8,128)(2,1)S(1)} %get-tuple-element.31), channel_id=1, source_target_pairs={{0,2},{2,0},{4,6},{6,4},{8,10},{10,8},{12,14},{14,12},{3,7},{7,11}... | collective-permute-start | bytes 602120 | tf_op jit(solution)/shard_map/ppermute | solution.py:490
  24.7 0.3 beside.3.product
  25.0 1.2 %collective-permute-done.5.received = s16[912,128]{1,0:T(8,128)(2,1)S(1)} collective-permute-done((s16[912,128]{1,0:T(8,128)(2,1)S(1)}, s16[912,128]{1,0:T(8,128)(2,1)S(1)}, u32[]{:S(2)}, u32[]{:S(2)}) %collective-permute-start.5) | collective-permute-done | bytes 233504 | tf_op jit(solution)/shard_map/ppermute | solution.py:501
  26.2 0.4 settle.2.message
  26.6 0.1 collective-permute-start.6
  26.6 3.7 %collective-permute-done.2.received.near = s16[784,128]{1,0:T(8,128)(2,1)S(1)} collective-permute-done((s16[784,128]{1,0:T(8,128)(2,1)S(1)}, s16[784,128]{1,0:T(8,128)(2,1)S(1)}, u32[]{:S(2)}, u32[]{:S(2)}) %collective-permute-start.2) | collective-permute-done | bytes 200736 | tf_op jit(solution)/shard_map/ppermute | solution.py:490
  30.4 3.5 %collective-permute-start.3 = (s16[784,128]{1,0:T(8,128)(2,1)S(1)}, s16[784,128]{1,0:T(8,128)(2,1)S(1)}, u32[]{:S(2)}, u32[]{:S(2)}) collective-permute-start(s16[784,128]{1,0:T(8,128)(2,1)S(1)} %relay.2), channel_id=1, source_target_pairs={{0,4},{4,8},{8,12},{6,2},{10,6},{14,10},{1,3},{3,1},{5,7},{7,5},{9... | collective-permute-start | bytes 602120 | tf_op jit(solution)/shard_map/ppermute | solution.py:501
  33.9 0.2 beside.2.product
  34.1 0.0 copy-done
  34.1 0.9 %finish.4 = (f32[13,128,256]{2,1,0:T(8,128)}, f32[3,128,256]{2,1,0:T(8,128)S(1)}) custom-call(bf16[13,128,256]{2,1,0:T(8,128)(2,1)S(1)} %copy-done, f32[13,128,128]{2,1,0:T(8,128)S(1)} %get-tuple-element.37.base, s16[912,128]{1,0:T(8,128)(2,1)S(1)} %settle.2.message), custom_call_target="tpu_custom_call" | custom-call | bytes 4034560 | tf_op jit(solution)/shard_map/finish/pallas_call | solution.py:37
  35.0 0.0 collective-permute-done.6.message
  35.0 0.9 %finish.5 = (f32[13,128,256]{2,1,0:T(8,128)}, f32[3,128,256]{2,1,0:T(8,128)S(1)}) custom-call(bf16[13,128,256]{2,1,0:T(8,128)(2,1)S(1)} %copy-done, f32[13,128,128]{2,1,0:T(8,128)S(1)} %get-tuple-element.29.base, s16[912,128]{1,0:T(8,128)(2,1)S(1)} %collective-permute-done.6.message, ...), custom_call_target="tpu_custom_call", output_to_operand_aliasing={{0}: (3, {})} | custom-call | bytes 5738496 | tf_op jit(solution)/shard_map/finish/pallas_call | solution.py:37
  35.9 1.2 %collective-permute-done.3.received = s16[784,128]{1,0:T(8,128)(2,1)S(1)} collective-permute-done((s16[784,128]{1,0:T(8,128)(2,1)S(1)}, s16[784,128]{1,0:T(8,128)(2,1)S(1)}, u32[]{:S(2)}, u32[]{:S(2)}) %collective-permute-start.3) | collective-permute-done | bytes 200736 | tf_op jit(solution)/shard_map/ppermute | solution.py:501
  37.1 0.3 settle.3.message
  37.4 0.1 collective-permute-start.7
  37.5 0.8 %finish.6 = (f32[13,128,256]{2,1,0:T(8,128)}, f32[3,128,256]{2,1,0:T(8,128)S(1)}) custom-call(bf16[13,128,256]{2,1,0:T(8,128)(2,1)S(1)} %copy-done, f32[13,128,128]{2,1,0:T(8,128)S(1)} %get-tuple-element.37.base, s16[784,128]{1,0:T(8,128)(2,1)S(1)} %settle.3.message, f32[3,128,256]{2,1,0:T(8,128)S(1)} %get-tuple-element.44.rest_0_, ...), custom_call_target="tpu_custom_call", output_to_operand_aliasing={{0}: (4, {})} | custom-call | bytes 6098944 | tf_op jit(solution)/shard_map/finish/pallas_call | solution.py:37
  38.3 0.6 %collective-permute-done.7.message = s16[784,128]{1,0:T(8,128)(2,1)S(1)} collective-permute-done((s16[784,128]{1,0:T(8,128)(2,1)S(1)}, s16[784,128]{1,0:T(8,128)(2,1)S(1)}, u32[]{:S(2)}, u32[]{:S(2)}) %collective-permute-start.7) | collective-permute-done | bytes 200736 | tf_op jit(solution)/shard_map/ppermute | solution.py:526
  38.9 1.1 %finish.7 = (f32[13,128,256]{2,1,0:T(8,128)}, f32[128,256]{1,0:T(8,128)}) custom-call(bf16[13,128,256]{2,1,0:T(8,128)(2,1)S(1)} %copy-done, f32[13,128,128]{2,1,0:T(8,128)S(1)} %get-tuple-element.29.base, s16[784,128]{1,0:T(8,128)(2,1)S(1)} %collective-permute-done.7.message, ...), custom_call_target="tpu_custom_call", output_to_operand_aliasing={{0}: (5, {})} | custom-call | bytes 6230016 | tf_op jit(solution)/shard_map/finish/pallas_call | solution.py:37
  (2 shorter events, 0.0 us)
Async XLA Ops:
  6.5 2.4 %collective-permute-start = (f32[13,128,128]{2,1,0:T(8,128)S(1)}, f32[13,128,128]{2,1,0:T(8,128)S(1)}, u32[]{:S(2)}, u32[]{:S(2)}) collective-permute-start(f32[13,128,128]{2,1,0:T(8,128)S(1)} %get-tuple-element.27), channel_id=1, source_target_pairs={{0,1},{1,0},{2,3},{3,2},{4,5},{5,4},{6,7},{7,6},{8,9},{9,8},{10,11... | collective-permute-start | bytes 2555912 | tf_op jit(solution)/shard_map/ppermute | solution.py:481
  9.3 5.3 %collective-permute-start.1 = (f32[13,128,128]{2,1,0:T(8,128)S(1)}, f32[13,128,128]{2,1,0:T(8,128)S(1)}, u32[]{:S(2)}, u32[]{:S(2)}) collective-permute-start(f32[13,128,128]{2,1,0:T(8,128)S(1)} %get-tuple-element.28.total), channel_id=1, source_target_pairs={{0,1},{1,0},{2,3},{3,2},{4,5},{5,4},{6,7},{7,6},{8,9},{9,8},{10,11... | collective-permute-start | bytes 2555912 | tf_op jit(solution)/shard_map/ppermute | solution.py:491
  9.8 8.7 %collective-permute-start.4 = (s16[912,128]{1,0:T(8,128)(2,1)S(1)}, s16[912,128]{1,0:T(8,128)(2,1)S(1)}, u32[]{:S(2)}, u32[]{:S(2)}) collective-permute-start(s16[912,128]{1,0:T(8,128)(2,1)S(1)} %get-tuple-element.34), channel_id=1, source_target_pairs={{0,2},{2,0},{4,6},{6,4},{8,10},{10,8},{12,14},{14,12},{3,7},{7,11}... | collective-permute-start | bytes 700424 | tf_op jit(solution)/shard_map/ppermute | solution.py:490
  18.6 7.5 %collective-permute-start.5 = (s16[912,128]{1,0:T(8,128)(2,1)S(1)}, s16[912,128]{1,0:T(8,128)(2,1)S(1)}, u32[]{:S(2)}, u32[]{:S(2)}) collective-permute-start(s16[912,128]{1,0:T(8,128)(2,1)S(1)} %relay.3), channel_id=1, source_target_pairs={{0,4},{4,8},{8,12},{6,2},{10,6},{14,10},{1,3},{3,1},{5,7},{7,5},{9... | collective-permute-start | bytes 700424 | tf_op jit(solution)/shard_map/ppermute | solution.py:501
  22.6 11.5 %copy-start = (bf16[13,128,256]{2,1,0:T(8,128)(2,1)S(1)}, bf16[13,128,256]{2,1,0:T(8,128)(2,1)}, u32[]{:S(2)}) copy-start(bf16[13,128,256]{2,1,0:T(8,128)(2,1)} %observed.7) | copy-start | bytes 2555908
  22.6 7.7 %collective-permute-start.2 = (s16[784,128]{1,0:T(8,128)(2,1)S(1)}, s16[784,128]{1,0:T(8,128)(2,1)S(1)}, u32[]{:S(2)}, u32[]{:S(2)}) collective-permute-start(s16[784,128]{1,0:T(8,128)(2,1)S(1)} %get-tuple-element.31), channel_id=1, source_target_pairs={{0,2},{2,0},{4,6},{6,4},{8,10},{10,8},{12,14},{14,12},{3,7},{7,11}... | collective-permute-start | bytes 602120 | tf_op jit(solution)/shard_map/ppermute | solution.py:490
  26.6 8.4 %collective-permute-start.6 = (s16[912,128]{1,0:T(8,128)(2,1)S(1)}, s16[912,128]{1,0:T(8,128)(2,1)S(1)}, u32[]{:S(2)}, u32[]{:S(2)}) collective-permute-start(s16[912,128]{1,0:T(8,128)(2,1)S(1)} %settle.2.message), channel_id=1, source_target_pairs={{0,1},{1,0},{2,3},{3,2},{4,5},{5,4},{6,7},{7,6},{8,9},{9,8},{10,11... | collective-permute-start | bytes 700424 | tf_op jit(solution)/shard_map/ppermute | solution.py:526
  30.4 6.7 %collective-permute-start.3 = (s16[784,128]{1,0:T(8,128)(2,1)S(1)}, s16[784,128]{1,0:T(8,128)(2,1)S(1)}, u32[]{:S(2)}, u32[]{:S(2)}) collective-permute-start(s16[784,128]{1,0:T(8,128)(2,1)S(1)} %relay.2), channel_id=1, source_target_pairs={{0,4},{4,8},{8,12},{6,2},{10,6},{14,10},{1,3},{3,1},{5,7},{7,5},{9... | collective-permute-start | bytes 602120 | tf_op jit(solution)/shard_map/ppermute | solution.py:501
  37.4 1.5 %collective-permute-start.7 = (s16[784,128]{1,0:T(8,128)(2,1)S(1)}, s16[784,128]{1,0:T(8,128)(2,1)S(1)}, u32[]{:S(2)}, u32[]{:S(2)}) collective-permute-start(s16[784,128]{1,0:T(8,128)(2,1)S(1)} %settle.3.message), channel_id=1, source_target_pairs={{0,1},{1,0},{2,3},{3,2},{4,5},{5,4},{6,7},{7,6},{8,9},{9,8},{10,11... | collective-permute-start | bytes 602120 | tf_op jit(solution)/shard_map/ppermute | solution.py:526

commit v4 on v2

--- a/solution.py
+++ b/solution.py
@@ -301,16 +301,13 @@
 def relay(term, received, message, total):
     units, lines, _ = term.shape
 
-    def forward():
-        message[...] = received[...]
-
     def add():
         plane = decode(received, units, lines)
         for m in range(units):
             total[m] = term[m] + plane(m)
         encode(total, message)
 
-    by_core(forward, add)
+    pl.when(lax.axis_index("band") != 0)(add)
 
 
 def beside(picked, near, product):
@@ -323,7 +320,7 @@
     pl.when(lax.axis_index("band") == 0)(lambda: blurred(picked[1], units, plane, put))
 
 
-def settle(picked, product, received, message, total):
+def settle(picked, product, received, summed, message, total):
     units, lines, _ = product.shape
 
     def put(m, value):
@@ -334,7 +331,7 @@
         encode(total, message)
 
     def forward():
-        message[...] = received[...]
+        message[...] = summed[...]
 
     by_core(add, forward)
 
@@ -467,18 +464,27 @@
     work = [pltpu.VMEM(part.shape, f32)]
     other = lax.ppermute(send, "band", swap)
     total, message = call(share, (picked, keep, other), [VMEM] * 3, [part, coded], scratch=work)
-    near = lax.ppermute(message, ("line", "band"), cores(partner, odd_up))
+    near = lax.ppermute(message, ("line", "band"), cores(partner, []))
+    received = lax.ppermute(message, ("line", "band"), cores([], odd_up))
     other_total = lax.ppermute(total, "band", swap)
     base, other_base, term = call(
         centre, (picked, total, other_total), [VMEM] * 3, [part] * 3, flops=3 * unit * units
     )
-    near, base, other_base, term = lax.optimization_barrier((near, base, other_base, term))
-    (message,) = call(relay, (term, near), [VMEM] * 2, [coded], scratch=work)
+    near, received, base, other_base, term = lax.optimization_barrier(
+        (near, received, base, other_base, term)
+    )
+    (message,) = call(relay, (term, received), [VMEM] * 2, [coded], scratch=work)
     message, near = lax.optimization_barrier((message, near))
-    far = lax.ppermute(message, ("line", "band"), cores(even_up, partner))
+    far = lax.ppermute(near, ("line", "band"), cores(even_up, []))
+    sums = lax.ppermute(message, ("line", "band"), cores([], partner))
     (product,) = call(beside, (picked, near), [VMEM] * 2, [part], flops=unit * units)
     (message,) = call(
-        settle, (picked, product, far), [VMEM] * 3, [coded], scratch=work, flops=unit * units
+        settle,
+        (picked, product, far, sums),
+        [VMEM] * 4,
+        [coded],
+        scratch=work,
+        flops=unit * units,
     )
     other_message = lax.ppermute(message, "band", swap)
     image = shape((count, lines, cols), f32)

time: 34.5 us -> 34.1 us (0.988); the launches traced: 33.9 us -> 33.9 us
  waiting for transfers between devices: 13.7 us -> 12.3 us
  starting transfers between devices: 9.93 us -> 11.3 us
    ppermute x2 -> x4, waiting for transfers between devices: 10.9 us -> 9.57 us  [the longest x1 5 us: on_device(): near = lax.ppermute(message, ('line', 'band'), cores(partner, []))]
    ppermute x2 -> x4, starting transfers between devices: 8.38 us -> 9.75 us  [the longest x1 4.25 us: on_device(): near = lax.ppermute(message, ('line', 'band'), cores(partner, []))]
  transfers between devices with their start and end apart: 5 -> 7, of which waited for: 4 -> 4; matrix products, arithmetic and copies ran while one was open for 0% -> 0% of each run, Pallas kernels for 5% -> 5%
where the time goes in v4:
time: 34.1 us; the launch traced here: 33.9 us
  waiting for transfers between devices  12.3 us (36%)
  starting transfers between devices  11.3 us (33%)
  Pallas kernels  9.53 us (28%)
  between operations  0.73 us (2%)
    pallas_call x8, Pallas kernels, call(): pl.pallas_call(kernel, in_specs=specs, out_specs=out_specs or [VMEM] * le...  9.53 us
    ppermute x1, waiting for transfers between devices, on_device(): near = lax.ppermute(message, ('line', 'band'), cores(partner, []))  5 us
    ppermute x1, waiting for transfers between devices, on_device(): far = lax.ppermute(near, ('line', 'band'), cores(even_up, []))  4.56 us
    ppermute x1, starting transfers between devices, on_device(): near = lax.ppermute(message, ('line', 'band'), cores(partner, []))  4.25 us
    ppermute x1, starting transfers between devices, on_device(): far = lax.ppermute(near, ('line', 'band'), cores(even_up, []))  4.12 us
    ppermute x1, waiting for transfers between devices, on_device(): other = lax.ppermute(send, 'band', swap)  2.01 us
    ppermute x1, starting transfers between devices, on_device(): other = lax.ppermute(send, 'band', swap)  0.81 us
    ppermute x1, waiting for transfers between devices, on_device(): other_message = lax.ppermute(message, 'band', swap)  0.72 us
  transfers between devices with their start and end apart: 7, of which 4 were waited for; matrix products, arithmetic and copies ran while one was open for 0% of the time, Pallas kernels for 5%

profile of v4, /device:TPU:0, one launch (start us, length us, event | category | flops | bytes accessed | tf_op | source)
XLA Modules:
  0.0 33.9 jit_solution(17151865410570951017)
XLA Ops:
  0.6 5.5 %fold.1 = (f32[13,128,128]{2,1,0:T(8,128)S(1)}, f32[13,128,128]{2,1,0:T(8,128)S(1)}, bf16[3,128,128]{2,1,0:T(8,128)(2,1)S(1)}) custom-call(s32[13]{0:T(128)} %start_in.1, s32[3]{0:T(128)} %offsets_in.1, bf16[13,20]{1,0:T(8,128)(2,1)} %values_in.1, bf16[3,128,128]{2,1,0:T(8,128)(2,1)} %blocks_in.1, s32[3]{0:T(128)} %along_offsets_in.1, ...), custom_call_target="tpu_custom_call" | custom-call | flops 436207616 | bytes 9536084 | tf_op jit(solution)/shard_map/fold/pallas_call | solution.py:37
  6.2 0.8 %collective-permute-start = (f32[13,128,128]{2,1,0:T(8,128)S(1)}, f32[13,128,128]{2,1,0:T(8,128)S(1)}, u32[]{:S(2)}, u32[]{:S(2)}) collective-permute-start(f32[13,128,128]{2,1,0:T(8,128)S(1)} %get-tuple-element.21), channel_id=1, source_target_pairs={{0,1},{1,0},{2,3},{3,2},{4,5},{5,4},{6,7},{7,6},{8,9},{9,8},{10,11... | collective-permute-start | bytes 2555912 | tf_op jit(solution)/shard_map/ppermute | solution.py:465
  7.0 2.0 %collective-permute-done.other = f32[13,128,128]{2,1,0:T(8,128)S(1)} collective-permute-done((f32[13,128,128]{2,1,0:T(8,128)S(1)}, f32[13,128,128]{2,1,0:T(8,128)S(1)}, u32[]{:S(2)}, u32[]{:S(2)}) %collective-permute-start) | collective-permute-done | bytes 852000 | tf_op jit(solution)/shard_map/ppermute | solution.py:465
  9.0 0.3 share.1
  9.3 0.7 %collective-permute-start.3 = (f32[13,128,128]{2,1,0:T(8,128)S(1)}, f32[13,128,128]{2,1,0:T(8,128)S(1)}, u32[]{:S(2)}, u32[]{:S(2)}) collective-permute-start(f32[13,128,128]{2,1,0:T(8,128)S(1)} %get-tuple-element.23.total), channel_id=1, source_target_pairs={{0,1},{1,0},{2,3},{3,2},{4,5},{5,4},{6,7},{7,6},{8,9},{9,8},{10,11... | collective-permute-start | bytes 2555912 | tf_op jit(solution)/shard_map/ppermute | solution.py:469
  10.0 4.3 %collective-permute-start.1 = (s16[1680,128]{1,0:T(8,128)(2,1)S(1)}, s16[1680,128]{1,0:T(8,128)(2,1)S(1)}, u32[]{:S(2)}, u32[]{:S(2)}) collective-permute-start(s16[1680,128]{1,0:T(8,128)(2,1)S(1)} %get-tuple-element.22), channel_id=1, source_target_pairs={{0,2},{2,0},{4,6},{6,4},{8,10},{10,8},{12,14},{14,12},{16,18},{18,... | collective-permute-start | bytes 1290248 | tf_op jit(solution)/shard_map/ppermute | solution.py:467
  14.3 0.7 %collective-permute-start.2 = (s16[1680,128]{1,0:T(8,128)(2,1)S(1)}, s16[1680,128]{1,0:T(8,128)(2,1)S(1)}, u32[]{:S(2)}, u32[]{:S(2)}) collective-permute-start(s16[1680,128]{1,0:T(8,128)(2,1)S(1)} %get-tuple-element.22), channel_id=1, source_target_pairs={{3,7},{7,11},{11,15},{5,1},{9,5},{13,9},{19,23},{23,27},{27,31},{2... | collective-permute-start | bytes 1290248 | tf_op jit(solution)/shard_map/ppermute | solution.py:468
  15.0 0.0 collective-permute-done.3.other_total
  15.0 0.4 %centre.1 = (f32[13,128,128]{2,1,0:T(8,128)S(1)}, f32[13,128,128]{2,1,0:T(8,128)S(1)}, f32[13,128,128]{2,1,0:T(8,128)S(1)}) custom-call(bf16[3,128,128]{2,1,0:T(8,128)(2,1)S(1)} %get-tuple-element.19.picked, f32[13,128,128]{2,1,0:T(8,128)S(1)} %get-tuple-element.23.total, f32[13,128,128]{2,1,0:T(8,128)S(1)} %collective-permute-done.3.other_total), custom_call_target="tpu_custom_call" | custom-call | flops 327155712 | bytes 4358144 | tf_op jit(solution)/shard_map/centre/pallas_call | solution.py:37
  15.4 5.0 %collective-permute-done.1.near = s16[1680,128]{1,0:T(8,128)(2,1)S(1)} collective-permute-done((s16[1680,128]{1,0:T(8,128)(2,1)S(1)}, s16[1680,128]{1,0:T(8,128)(2,1)S(1)}, u32[]{:S(2)}, u32[]{:S(2)}) %collective-permute-start.1) | collective-permute-done | bytes 430112 | tf_op jit(solution)/shard_map/ppermute | solution.py:467
  20.4 0.0 collective-permute-done.2.received
  20.4 0.0 copy-start
  20.4 4.1 %collective-permute-start.4 = (s16[1680,128]{1,0:T(8,128)(2,1)S(1)}, s16[1680,128]{1,0:T(8,128)(2,1)S(1)}, u32[]{:S(2)}, u32[]{:S(2)}) collective-permute-start(s16[1680,128]{1,0:T(8,128)(2,1)S(1)} %collective-permute-done.1.near), channel_id=1, source_target_pairs={{0,4},{4,8},{8,12},{6,2},{10,6},{14,10},{16,20},{20,24},{24,28},{2... | collective-permute-start | bytes 1290248 | tf_op jit(solution)/shard_map/ppermute | solution.py:478
  24.5 0.7 %collective-permute-start.5 = (s16[1680,128]{1,0:T(8,128)(2,1)S(1)}, s16[1680,128]{1,0:T(8,128)(2,1)S(1)}, u32[]{:S(2)}, u32[]{:S(2)}) collective-permute-start(s16[1680,128]{1,0:T(8,128)(2,1)S(1)} %relay.1), channel_id=1, source_target_pairs={{1,3},{3,1},{5,7},{7,5},{9,11},{11,9},{13,15},{15,13},{17,19},{19,... | collective-permute-start | bytes 1290248 | tf_op jit(solution)/shard_map/ppermute | solution.py:479
  25.2 0.4 %beside.1.product = f32[13,128,128]{2,1,0:T(8,128)S(1)} custom-call(bf16[3,128,128]{2,1,0:T(8,128)(2,1)S(1)} %get-tuple-element.19.picked, s16[1680,128]{1,0:T(8,128)(2,1)S(1)} %collective-permute-done.1.near), custom_call_target="tpu_custom_call" | custom-call | flops 109051904 | bytes 1380352 | tf_op jit(solution)/shard_map/beside/pallas_call | solution.py:37
  25.6 4.6 %collective-permute-done.4.received = s16[1680,128]{1,0:T(8,128)(2,1)S(1)} collective-permute-done((s16[1680,128]{1,0:T(8,128)(2,1)S(1)}, s16[1680,128]{1,0:T(8,128)(2,1)S(1)}, u32[]{:S(2)}, u32[]{:S(2)}) %collective-permute-start.4) | collective-permute-done | bytes 430112 | tf_op jit(solution)/shard_map/ppermute | solution.py:478
  30.2 0.0 collective-permute-done.5.summed
  30.2 0.6 %settle.1.message = s16[1680,128]{1,0:T(8,128)(2,1)S(1)} custom-call(bf16[3,128,128]{2,1,0:T(8,128)(2,1)S(1)} %get-tuple-element.19.picked, f32[13,128,128]{2,1,0:T(8,128)S(1)} %beside.1.product, s16[1680,128]{1,0:T(8,128)(2,1)S(1)} %collective-permute-done.4.received, s16[1680,128]{1,0:T(8,128)(2,1)S(1)} %collective-permute-done.5.summed), custom_call_target="tpu_custom_call" | custom-call | flops 109051904 | bytes 2240512 | tf_op jit(solution)/shard_map/settle/pallas_call | solution.py:37
  30.7 0.1 collective-permute-start.6
  30.8 0.0 copy-done
  30.8 1.0 %finish.2 = (f32[13,128,256]{2,1,0:T(8,128)}, f32[3,128,256]{2,1,0:T(8,128)S(1)}) custom-call(bf16[13,128,256]{2,1,0:T(8,128)(2,1)S(1)} %copy-done, f32[13,128,128]{2,1,0:T(8,128)S(1)} %get-tuple-element.33.base, s16[1680,128]{1,0:T(8,128)(2,1)S(1)} %settle.1.message), custom_call_target="tpu_custom_call" | custom-call | bytes 4231168 | tf_op jit(solution)/shard_map/finish/pallas_call | solution.py:37
  31.9 0.7 %collective-permute-done.6.message = s16[1680,128]{1,0:T(8,128)(2,1)S(1)} collective-permute-done((s16[1680,128]{1,0:T(8,128)(2,1)S(1)}, s16[1680,128]{1,0:T(8,128)(2,1)S(1)}, u32[]{:S(2)}, u32[]{:S(2)}) %collective-permute-start.6) | collective-permute-done | bytes 430112 | tf_op jit(solution)/shard_map/ppermute | solution.py:489
  32.6 1.3 %finish.3 = (f32[13,128,256]{2,1,0:T(8,128)}, f32[128,256]{1,0:T(8,128)}) custom-call(bf16[13,128,256]{2,1,0:T(8,128)(2,1)S(1)} %copy-done, f32[13,128,128]{2,1,0:T(8,128)S(1)} %get-tuple-element.27.base, s16[1680,128]{1,0:T(8,128)(2,1)S(1)} %collective-permute-done.6.message, ...), custom_call_target="tpu_custom_call", output_to_operand_aliasing={{0}: (4, {})} | custom-call | bytes 6066176 | tf_op jit(solution)/shard_map/finish/pallas_call | solution.py:37
  (1 shorter events, 0.0 us)
Async XLA Ops:
  6.2 2.8 %collective-permute-start = (f32[13,128,128]{2,1,0:T(8,128)S(1)}, f32[13,128,128]{2,1,0:T(8,128)S(1)}, u32[]{:S(2)}, u32[]{:S(2)}) collective-permute-start(f32[13,128,128]{2,1,0:T(8,128)S(1)} %get-tuple-element.21), channel_id=1, source_target_pairs={{0,1},{1,0},{2,3},{3,2},{4,5},{5,4},{6,7},{7,6},{8,9},{9,8},{10,11... | collective-permute-start | bytes 2555912 | tf_op jit(solution)/shard_map/ppermute | solution.py:465
  9.3 5.6 %collective-permute-start.3 = (f32[13,128,128]{2,1,0:T(8,128)S(1)}, f32[13,128,128]{2,1,0:T(8,128)S(1)}, u32[]{:S(2)}, u32[]{:S(2)}) collective-permute-start(f32[13,128,128]{2,1,0:T(8,128)S(1)} %get-tuple-element.23.total), channel_id=1, source_target_pairs={{0,1},{1,0},{2,3},{3,2},{4,5},{5,4},{6,7},{7,6},{8,9},{9,8},{10,11... | collective-permute-start | bytes 2555912 | tf_op jit(solution)/shard_map/ppermute | solution.py:469
  10.0 10.4 %collective-permute-start.1 = (s16[1680,128]{1,0:T(8,128)(2,1)S(1)}, s16[1680,128]{1,0:T(8,128)(2,1)S(1)}, u32[]{:S(2)}, u32[]{:S(2)}) collective-permute-start(s16[1680,128]{1,0:T(8,128)(2,1)S(1)} %get-tuple-element.22), channel_id=1, source_target_pairs={{0,2},{2,0},{4,6},{6,4},{8,10},{10,8},{12,14},{14,12},{16,18},{18,... | collective-permute-start | bytes 1290248 | tf_op jit(solution)/shard_map/ppermute | solution.py:467
  14.3 6.1 %collective-permute-start.2 = (s16[1680,128]{1,0:T(8,128)(2,1)S(1)}, s16[1680,128]{1,0:T(8,128)(2,1)S(1)}, u32[]{:S(2)}, u32[]{:S(2)}) collective-permute-start(s16[1680,128]{1,0:T(8,128)(2,1)S(1)} %get-tuple-element.22), channel_id=1, source_target_pairs={{3,7},{7,11},{11,15},{5,1},{9,5},{13,9},{19,23},{23,27},{27,31},{2... | collective-permute-start | bytes 1290248 | tf_op jit(solution)/shard_map/ppermute | solution.py:468
  20.4 10.4 %copy-start = (bf16[13,128,256]{2,1,0:T(8,128)(2,1)S(1)}, bf16[13,128,256]{2,1,0:T(8,128)(2,1)}, u32[]{:S(2)}) copy-start(bf16[13,128,256]{2,1,0:T(8,128)(2,1)} %observed.3) | copy-start | bytes 2555908
  20.4 9.8 %collective-permute-start.4 = (s16[1680,128]{1,0:T(8,128)(2,1)S(1)}, s16[1680,128]{1,0:T(8,128)(2,1)S(1)}, u32[]{:S(2)}, u32[]{:S(2)}) collective-permute-start(s16[1680,128]{1,0:T(8,128)(2,1)S(1)} %collective-permute-done.1.near), channel_id=1, source_target_pairs={{0,4},{4,8},{8,12},{6,2},{10,6},{14,10},{16,20},{20,24},{24,28},{2... | collective-permute-start | bytes 1290248 | tf_op jit(solution)/shard_map/ppermute | solution.py:478
  24.5 5.6 %collective-permute-start.5 = (s16[1680,128]{1,0:T(8,128)(2,1)S(1)}, s16[1680,128]{1,0:T(8,128)(2,1)S(1)}, u32[]{:S(2)}, u32[]{:S(2)}) collective-permute-start(s16[1680,128]{1,0:T(8,128)(2,1)S(1)} %relay.1), channel_id=1, source_target_pairs={{1,3},{3,1},{5,7},{7,5},{9,11},{11,9},{13,15},{15,13},{17,19},{19,... | collective-permute-start | bytes 1290248 | tf_op jit(solution)/shard_map/ppermute | solution.py:479
  30.7 1.8 %collective-permute-start.6 = (s16[1680,128]{1,0:T(8,128)(2,1)S(1)}, s16[1680,128]{1,0:T(8,128)(2,1)S(1)}, u32[]{:S(2)}, u32[]{:S(2)}) collective-permute-start(s16[1680,128]{1,0:T(8,128)(2,1)S(1)} %settle.1.message), channel_id=1, source_target_pairs={{0,1},{1,0},{2,3},{3,2},{4,5},{5,4},{6,7},{7,6},{8,9},{9,8},{10,11... | collective-permute-start | bytes 1290248 | tf_op jit(solution)/shard_map/ppermute | solution.py:489

commit v5 on v2

--- a/solution.py
+++ b/solution.py
@@ -234,9 +234,9 @@
     message[units * lines :, :] = level.astype(jnp.int32).astype(jnp.int16)
 
 
-def decode(message, count, lines):
+def decode(message, count, lines, valid=True):
     level = message[count * lines :, :].astype(jnp.int32).astype(jnp.float32)
-    scale = jnp.exp2(level * (1.0 / STEPS)) * (1.0 / PEAK)
+    scale = jnp.where(valid, jnp.exp2(level * (1.0 / STEPS)) * (1.0 / PEAK), 0.0)
 
     def plane(m):
         coded = message[m * lines : (m + 1) * lines, :].astype(jnp.int32).astype(jnp.float32)
@@ -263,6 +263,10 @@
     return jnp.where(lax.axis_index("line") % 2 == 0, jnp.int32(1), jnp.int32(-1))
 
 
+def outside(*lines):
+    return functools.reduce(jnp.logical_or, [lax.axis_index("line") == i for i in lines])
+
+
 def by_core(zero, one):
     me = lax.axis_index("band")
     pl.when(me == 0)(zero)
@@ -305,7 +309,8 @@
         message[...] = received[...]
 
     def add():
-        plane = decode(received, units, lines)
+        missing = outside(1, lax.axis_size("line") - 2)
+        plane = decode(received, units, lines, jnp.logical_not(missing))
         for m in range(units):
             total[m] = term[m] + plane(m)
         encode(total, message)
@@ -330,7 +335,9 @@
         total[m] = product[m] + value
 
     def add():
-        blurred(picked[2], units, decode(received, units, lines), put)
+        missing = outside(0, lax.axis_size("line") - 1)
+        plane = decode(received, units, lines, jnp.logical_not(missing))
+        blurred(picked[2], units, plane, put)
         encode(total, message)
 
     def forward():
@@ -422,8 +429,8 @@
     shape = jax.ShapeDtypeStruct
     swap = [(0, 1), (1, 0)]
     partner = [(i, i ^ 1) for i in range(size)]
-    even_up = [(i, i + 2) for i in range(0, size - 2, 2)] + [(i, i - 2) for i in range(3, size, 2)]
-    odd_up = [(i, i + 2) for i in range(1, size - 2, 2)] + [(i, i - 2) for i in range(2, size, 2)]
+    even_up = [(i, (i + 2 - 4 * (i % 2)) % size) for i in range(size)]
+    odd_up = [(j, i) for i, j in even_up]
 
     def cores(zero, one):
         return [(2 * a, 2 * b) for a, b in zero] + [(2 * a + 1, 2 * b + 1) for a, b in one]

time: 34.5 us -> 33.4 us (0.968); the launches traced: 33.9 us -> 33.6 us
  starting transfers between devices: 9.93 us -> 5.67 us
  waiting for transfers between devices: 13.7 us -> 16.6 us
  Pallas kernels: 9.56 us -> 10.6 us
    ppermute x1, waiting for transfers between devices: 5.26 us -> 7.79 us  [on_device(): far = lax.ppermute(message, ('line', 'band'), cores(even_up, partner))]
    ppermute x1, starting transfers between devices: 4.14 us -> 2.13 us  [on_device(): far = lax.ppermute(message, ('line', 'band'), cores(even_up, partner))]
    ppermute x1, starting transfers between devices: 4.24 us -> 2.97 us  [on_device(): near = lax.ppermute(message, ('line', 'band'), cores(partner, odd_up))]
    pallas_call x8, Pallas kernels: 9.56 us -> 10.6 us  [call(): pl.pallas_call(kernel, in_specs=specs, out_specs=out_specs or [VMEM] * le...]
    ppermute x1, starting transfers between devices: 0.82 us -> 0.07 us  [on_device(): other = lax.ppermute(send, 'band', swap)]
    ppermute x1, waiting for transfers between devices: 2.01 us -> 2.37 us  [on_device(): other = lax.ppermute(send, 'band', swap)]
where the time goes in v5:
time: 33.4 us; the launch traced here: 33.6 us
  waiting for transfers between devices  16.6 us (50%)
  Pallas kernels  10.6 us (32%)
  starting transfers between devices  5.67 us (17%)
  between operations  0.72 us (2%)
    pallas_call x8, Pallas kernels, call(): pl.pallas_call(kernel, in_specs=specs, out_specs=out_specs or [VMEM] * le...  10.6 us
    ppermute x1, waiting for transfers between devices, on_device(): far = lax.ppermute(message, ('line', 'band'), cores(even_up, partner))  7.79 us
    ppermute x1, waiting for transfers between devices, on_device(): near = lax.ppermute(message, ('line', 'band'), cores(partner, odd_up))  5.72 us
    ppermute x1, starting transfers between devices, on_device(): near = lax.ppermute(message, ('line', 'band'), cores(partner, odd_up))  2.97 us
    ppermute x1, waiting for transfers between devices, on_device(): other = lax.ppermute(send, 'band', swap)  2.37 us
    ppermute x1, starting transfers between devices, on_device(): far = lax.ppermute(message, ('line', 'band'), cores(even_up, partner))  2.13 us
    ppermute x1, waiting for transfers between devices, on_device(): other_message = lax.ppermute(message, 'band', swap)  0.72 us
  transfers between devices with their start and end apart: 5, of which 4 were waited for; matrix products, arithmetic and copies ran while one was open for 0% of the time, Pallas kernels for 5%

profile of v5, /device:TPU:0, one launch (start us, length us, event | category | flops | bytes accessed | tf_op | source)
XLA Modules:
  0.0 33.6 jit_solution(8785455501425429556)
XLA Ops:
  0.6 6.5 %fold.1 = (f32[13,128,128]{2,1,0:T(8,128)S(1)}, f32[13,128,128]{2,1,0:T(8,128)S(1)}, bf16[3,128,128]{2,1,0:T(8,128)(2,1)S(1)}) custom-call(s32[13]{0:T(128)} %start_in.1, s32[3]{0:T(128)} %offsets_in.1, bf16[13,20]{1,0:T(8,128)(2,1)} %values_in.1, bf16[3,128,128]{2,1,0:T(8,128)(2,1)} %blocks_in.1, s32[3]{0:T(128)} %along_offsets_in.1, ...), custom_call_target="tpu_custom_call" | custom-call | flops 436207616 | bytes 9536084 | tf_op jit(solution)/shard_map/fold/pallas_call | solution.py:37
  7.2 0.1 collective-permute-start
  7.3 2.4 %collective-permute-done.other = f32[13,128,128]{2,1,0:T(8,128)S(1)} collective-permute-done((f32[13,128,128]{2,1,0:T(8,128)S(1)}, f32[13,128,128]{2,1,0:T(8,128)S(1)}, u32[]{:S(2)}, u32[]{:S(2)}) %collective-permute-start) | collective-permute-done | bytes 852000 | tf_op jit(solution)/shard_map/ppermute | solution.py:475
  9.6 0.3 share.1
  10.0 0.4 %collective-permute-start.2 = (f32[13,128,128]{2,1,0:T(8,128)S(1)}, f32[13,128,128]{2,1,0:T(8,128)S(1)}, u32[]{:S(2)}, u32[]{:S(2)}) collective-permute-start(f32[13,128,128]{2,1,0:T(8,128)S(1)} %get-tuple-element.22.total), channel_id=1, source_target_pairs={{0,1},{1,0},{2,3},{3,2},{4,5},{5,4},{6,7},{7,6},{8,9},{9,8},{10,11... | collective-permute-start | bytes 2555912 | tf_op jit(solution)/shard_map/ppermute | solution.py:478
  10.4 3.0 %collective-permute-start.1 = (s16[1680,128]{1,0:T(8,128)(2,1)S(1)}, s16[1680,128]{1,0:T(8,128)(2,1)S(1)}, u32[]{:S(2)}, u32[]{:S(2)}) collective-permute-start(s16[1680,128]{1,0:T(8,128)(2,1)S(1)} %get-tuple-element.21), channel_id=1, source_target_pairs={{0,2},{2,0},{4,6},{6,4},{8,10},{10,8},{12,14},{14,12},{5,1},{15,3}... | collective-permute-start | bytes 1290248 | tf_op jit(solution)/shard_map/ppermute | solution.py:477
  13.4 0.0 collective-permute-done.2.other_total
  13.4 0.4 %centre.1 = (f32[13,128,128]{2,1,0:T(8,128)S(1)}, f32[13,128,128]{2,1,0:T(8,128)S(1)}, f32[13,128,128]{2,1,0:T(8,128)S(1)}) custom-call(bf16[3,128,128]{2,1,0:T(8,128)(2,1)S(1)} %get-tuple-element.18.picked, f32[13,128,128]{2,1,0:T(8,128)S(1)} %get-tuple-element.22.total, f32[13,128,128]{2,1,0:T(8,128)S(1)} %collective-permute-done.2.other_total), custom_call_target="tpu_custom_call" | custom-call | flops 327155712 | bytes 4358144 | tf_op jit(solution)/shard_map/centre/pallas_call | solution.py:37
  13.8 5.7 %collective-permute-done.1.received.near = s16[1680,128]{1,0:T(8,128)(2,1)S(1)} collective-permute-done((s16[1680,128]{1,0:T(8,128)(2,1)S(1)}, s16[1680,128]{1,0:T(8,128)(2,1)S(1)}, u32[]{:S(2)}, u32[]{:S(2)}) %collective-permute-start.1) | collective-permute-done | bytes 430112 | tf_op jit(solution)/shard_map/ppermute | solution.py:477
  19.5 0.0 copy-start
  19.6 2.1 %collective-permute-start.3 = (s16[1680,128]{1,0:T(8,128)(2,1)S(1)}, s16[1680,128]{1,0:T(8,128)(2,1)S(1)}, u32[]{:S(2)}, u32[]{:S(2)}) collective-permute-start(s16[1680,128]{1,0:T(8,128)(2,1)S(1)} %relay.1), channel_id=1, source_target_pairs={{0,4},{2,14},{4,8},{6,2},{8,12},{10,6},{12,0},{14,10},{1,3},{3,1},... | collective-permute-start | bytes 1290248 | tf_op jit(solution)/shard_map/ppermute | solution.py:485
  21.7 0.4 %beside.1.product = f32[13,128,128]{2,1,0:T(8,128)S(1)} custom-call(bf16[3,128,128]{2,1,0:T(8,128)(2,1)S(1)} %get-tuple-element.18.picked, s16[1680,128]{1,0:T(8,128)(2,1)S(1)} %collective-permute-done.1.received.near), custom_call_target="tpu_custom_call" | custom-call | flops 109051904 | bytes 1380352 | tf_op jit(solution)/shard_map/beside/pallas_call | solution.py:37
  22.1 7.8 %collective-permute-done.3.received = s16[1680,128]{1,0:T(8,128)(2,1)S(1)} collective-permute-done((s16[1680,128]{1,0:T(8,128)(2,1)S(1)}, s16[1680,128]{1,0:T(8,128)(2,1)S(1)}, u32[]{:S(2)}, u32[]{:S(2)}) %collective-permute-start.3) | collective-permute-done | bytes 430112 | tf_op jit(solution)/shard_map/ppermute | solution.py:485
  29.9 0.6 %settle.1.message = s16[1680,128]{1,0:T(8,128)(2,1)S(1)} custom-call(bf16[3,128,128]{2,1,0:T(8,128)(2,1)S(1)} %get-tuple-element.18.picked, f32[13,128,128]{2,1,0:T(8,128)S(1)} %beside.1.product, s16[1680,128]{1,0:T(8,128)(2,1)S(1)} %collective-permute-done.3.received), custom_call_target="tpu_custom_call" | custom-call | flops 109051904 | bytes 1810432 | tf_op jit(solution)/shard_map/settle/pallas_call | solution.py:37
  30.4 0.1 collective-permute-start.4
  30.5 0.0 copy-done
  30.5 1.0 %finish.2 = (f32[13,128,256]{2,1,0:T(8,128)}, f32[3,128,256]{2,1,0:T(8,128)S(1)}) custom-call(bf16[13,128,256]{2,1,0:T(8,128)(2,1)S(1)} %copy-done, f32[13,128,128]{2,1,0:T(8,128)S(1)} %get-tuple-element.31.base, s16[1680,128]{1,0:T(8,128)(2,1)S(1)} %settle.1.message), custom_call_target="tpu_custom_call" | custom-call | bytes 4231168 | tf_op jit(solution)/shard_map/finish/pallas_call | solution.py:37
  31.5 0.7 %collective-permute-done.4.message = s16[1680,128]{1,0:T(8,128)(2,1)S(1)} collective-permute-done((s16[1680,128]{1,0:T(8,128)(2,1)S(1)}, s16[1680,128]{1,0:T(8,128)(2,1)S(1)}, u32[]{:S(2)}, u32[]{:S(2)}) %collective-permute-start.4) | collective-permute-done | bytes 430112 | tf_op jit(solution)/shard_map/ppermute | solution.py:490
  32.3 1.3 %finish.3 = (f32[13,128,256]{2,1,0:T(8,128)}, f32[128,256]{1,0:T(8,128)}) custom-call(bf16[13,128,256]{2,1,0:T(8,128)(2,1)S(1)} %copy-done, f32[13,128,128]{2,1,0:T(8,128)S(1)} %get-tuple-element.26.base, s16[1680,128]{1,0:T(8,128)(2,1)S(1)} %collective-permute-done.4.message, ...), custom_call_target="tpu_custom_call", output_to_operand_aliasing={{0}: (4, {})} | custom-call | bytes 6066176 | tf_op jit(solution)/shard_map/finish/pallas_call | solution.py:37
  (1 shorter events, 0.0 us)
Async XLA Ops:
  7.2 2.4 %collective-permute-start = (f32[13,128,128]{2,1,0:T(8,128)S(1)}, f32[13,128,128]{2,1,0:T(8,128)S(1)}, u32[]{:S(2)}, u32[]{:S(2)}) collective-permute-start(f32[13,128,128]{2,1,0:T(8,128)S(1)} %get-tuple-element.20), channel_id=1, source_target_pairs={{0,1},{1,0},{2,3},{3,2},{4,5},{5,4},{6,7},{7,6},{8,9},{9,8},{10,11... | collective-permute-start | bytes 2555912 | tf_op jit(solution)/shard_map/ppermute | solution.py:475
  10.0 3.4 %collective-permute-start.2 = (f32[13,128,128]{2,1,0:T(8,128)S(1)}, f32[13,128,128]{2,1,0:T(8,128)S(1)}, u32[]{:S(2)}, u32[]{:S(2)}) collective-permute-start(f32[13,128,128]{2,1,0:T(8,128)S(1)} %get-tuple-element.22.total), channel_id=1, source_target_pairs={{0,1},{1,0},{2,3},{3,2},{4,5},{5,4},{6,7},{7,6},{8,9},{9,8},{10,11... | collective-permute-start | bytes 2555912 | tf_op jit(solution)/shard_map/ppermute | solution.py:478
  10.4 9.1 %collective-permute-start.1 = (s16[1680,128]{1,0:T(8,128)(2,1)S(1)}, s16[1680,128]{1,0:T(8,128)(2,1)S(1)}, u32[]{:S(2)}, u32[]{:S(2)}) collective-permute-start(s16[1680,128]{1,0:T(8,128)(2,1)S(1)} %get-tuple-element.21), channel_id=1, source_target_pairs={{0,2},{2,0},{4,6},{6,4},{8,10},{10,8},{12,14},{14,12},{5,1},{15,3}... | collective-permute-start | bytes 1290248 | tf_op jit(solution)/shard_map/ppermute | solution.py:477
  19.5 11.0 %copy-start = (bf16[13,128,256]{2,1,0:T(8,128)(2,1)S(1)}, bf16[13,128,256]{2,1,0:T(8,128)(2,1)}, u32[]{:S(2)}) copy-start(bf16[13,128,256]{2,1,0:T(8,128)(2,1)} %observed.3) | copy-start | bytes 2555908
  19.6 10.3 %collective-permute-start.3 = (s16[1680,128]{1,0:T(8,128)(2,1)S(1)}, s16[1680,128]{1,0:T(8,128)(2,1)S(1)}, u32[]{:S(2)}, u32[]{:S(2)}) collective-permute-start(s16[1680,128]{1,0:T(8,128)(2,1)S(1)} %relay.1), channel_id=1, source_target_pairs={{0,4},{2,14},{4,8},{6,2},{8,12},{10,6},{12,0},{14,10},{1,3},{3,1},... | collective-permute-start | bytes 1290248 | tf_op jit(solution)/shard_map/ppermute | solution.py:485
  30.4 1.8 %collective-permute-start.4 = (s16[1680,128]{1,0:T(8,128)(2,1)S(1)}, s16[1680,128]{1,0:T(8,128)(2,1)S(1)}, u32[]{:S(2)}, u32[]{:S(2)}) collective-permute-start(s16[1680,128]{1,0:T(8,128)(2,1)S(1)} %settle.1.message), channel_id=1, source_target_pairs={{0,1},{1,0},{2,3},{3,2},{4,5},{5,4},{6,7},{7,6},{8,9},{9,8},{10,11... | collective-permute-start | bytes 1290248 | tf_op jit(solution)/shard_map/ppermute | solution.py:490

commit v6 on v5

--- a/solution.py
+++ b/solution.py
@@ -32,8 +32,7 @@
 ROWS = 64
 
 
-def call(kernel, inputs, specs, outs, scratch=(), out_specs=None, aliases=None, flops=0):
-    moved = sum(x.size * x.dtype.itemsize for x in (*inputs, *outs))
+def call(kernel, inputs, specs, outs, scratch=(), out_specs=None, aliases=None):
     return pl.pallas_call(
         kernel,
         in_specs=specs,
@@ -42,7 +41,7 @@
         scratch_shapes=scratch,
         input_output_aliases=aliases or {},
         compiler_params=pltpu.CompilerParams(vmem_limit_bytes=32 * 2**20),
-        cost_estimate=pl.CostEstimate(flops=flops, bytes_accessed=moved, transcendentals=0),
+        cost_estimate=pl.CostEstimate(flops=0, bytes_accessed=0, transcendentals=0),
         name=(kernel.func if isinstance(kernel, functools.partial) else kernel).__name__,
     )(*inputs)
 
@@ -221,21 +220,23 @@
     return count * lines + -(-count // 16) * 16
 
 
-def encode(source, message):
-    units, lines, half = source.shape
-    largest = jnp.max(jnp.abs(source[...]), axis=1)
+def encode(source, span, message):
+    _, lines, half = source.shape
+    units = span[1] - span[0]
+    largest = jnp.max(jnp.abs(source[span[0] : span[1]]), axis=1)
     level = jnp.ceil(jnp.log2(jnp.maximum(largest, 1e-30)) * STEPS)
     factor = PEAK * jnp.exp2(level * (-1.0 / STEPS))
     for m in range(units):
-        coded = jnp.floor(source[m] * factor[m : m + 1, :] + 0.5).astype(jnp.int32)
+        coded = jnp.floor(source[span[0] + m] * factor[m : m + 1, :] + 0.5).astype(jnp.int32)
         message[m * lines : (m + 1) * lines, :] = coded.astype(jnp.int16)
     spare = message.shape[0] - units * lines - units
     level = jnp.concatenate([level, jnp.zeros((spare, half), jnp.float32)], axis=0)
     message[units * lines :, :] = level.astype(jnp.int32).astype(jnp.int16)
 
 
-def decode(message, count, lines, valid=True):
-    level = message[count * lines :, :].astype(jnp.int32).astype(jnp.float32)
+def decode(message, span, lines, valid=True):
+    units = span[1] - span[0]
+    level = message[units * lines :, :].astype(jnp.int32).astype(jnp.float32)
     scale = jnp.where(valid, jnp.exp2(level * (1.0 / STEPS)) * (1.0 / PEAK), 0.0)
 
     def plane(m):
@@ -273,17 +274,22 @@
     pl.when(me != 0)(one)
 
 
-def share(picked, keep, other, total, message, product):
+def share(spans, picked, keep, other, total, *rest):
+    messages, product = rest[:-1], rest[-1]
     total[...] = keep[...] + other[...]
+
+    def coding(source):
+        for span, message in zip(spans, messages):
+            encode(source, span, message)
 
     def summing():
         def put(m, value):
             product[m] = value
 
         blurred(picked[1], total.shape[0], lambda m: total[m], put)
-        encode(product, message)
-
-    by_core(lambda: encode(total, message), summing)
+        coding(product)
+
+    by_core(lambda: coding(total), summing)
 
 
 def centre(picked, total, other_total, base, other_base, term):
@@ -302,33 +308,31 @@
     )
 
 
-def relay(term, received, message, total):
-    units, lines, _ = term.shape
-
+def relay(span, term, received, message, total):
     def forward():
         message[...] = received[...]
 
     def add():
         missing = outside(1, lax.axis_size("line") - 2)
-        plane = decode(received, units, lines, jnp.logical_not(missing))
-        for m in range(units):
-            total[m] = term[m] + plane(m)
-        encode(total, message)
+        plane = decode(received, span, term.shape[1], jnp.logical_not(missing))
+        for m in range(*span):
+            total[m] = term[m] + plane(m - span[0])
+        encode(total, span, message)
 
     by_core(forward, add)
 
 
-def beside(picked, near, product):
+def beside(span, picked, near, product):
     units, lines, _ = product.shape
 
     def put(m, value):
         product[m] = value
 
-    plane = decode(near, units, lines)
+    plane = decode(near, span, lines)
     pl.when(lax.axis_index("band") == 0)(lambda: blurred(picked[1], units, plane, put))
 
 
-def settle(picked, product, received, message, total):
+def settle(span, picked, product, received, message, total):
     units, lines, _ = product.shape
 
     def put(m, value):
@@ -336,14 +340,15 @@
 
     def add():
         missing = outside(0, lax.axis_size("line") - 1)
-        plane = decode(received, units, lines, jnp.logical_not(missing))
+        plane = decode(received, span, lines, jnp.logical_not(missing))
         blurred(picked[2], units, plane, put)
-        encode(total, message)
+        encode(total, (0, units), message)
 
     def forward():
         message[...] = received[...]
 
     by_core(add, forward)
+
 
 def arccos(x):
     size = jnp.abs(x)
@@ -360,14 +365,14 @@
     return jnp.where(big, outer, inner)
 
 
-def finish(second, observed, base, message, *rest):
+def finish(second, spans, observed, base, *rest):
+    messages, rest = rest[: len(spans)], rest[len(spans) :]
     if second:
         sums, _, image, angles, angle, value, sems = rest
     else:
         image, sums, value, sems = rest
     units, lines, half = base.shape
     count = observed.shape[0]
-    plane = decode(message, units, lines)
 
     def work(core):
         places = [(m, slice(c * half, (c + 1) * half)) for m, c in units_of(core, count)]
@@ -375,9 +380,11 @@
             pltpu.make_async_copy(value.at[n], image.at[m, :, at], sems.at[n])
             for n, (m, at) in enumerate(places)
         ]
-        for n in range(units):
-            value[n] = base[n] + plane(n)
-            copies[n].start()
+        for span, message in zip(spans, messages):
+            plane = decode(message, span, lines)
+            for n in range(*span):
+                value[n] = base[n] + plane(n - span[0])
+                copies[n].start()
         for c in range(2):
             at = slice(c * half, (c + 1) * half)
             inner = jnp.zeros((lines, half), jnp.float32)
@@ -436,8 +443,8 @@
         return [(2 * a, 2 * b) for a, b in zero] + [(2 * a + 1, 2 * b + 1) for a, b in one]
 
     part = shape((units, lines, half), f32)
-    coded = shape((coded_rows(units, lines), half), i16)
-    unit = 4 * lines * lines * half
+    spans = [(0, (units + 1) // 2), ((units + 1) // 2, units)]
+    coded = [shape((coded_rows(b - a, lines), half), i16) for a, b in spans]
 
     inputs = (
         resp_start,
@@ -469,42 +476,64 @@
             pltpu.SemaphoreType.DMA((len(inputs),)),
             pltpu.SemaphoreType.DMA((-(-bands // resp_values.shape[1]),)),
         ],
-        flops=4 * count * lines * cols * cols,
     )
     work = [pltpu.VMEM(part.shape, f32)]
     other = lax.ppermute(send, "band", swap)
-    total, message = call(share, (picked, keep, other), [VMEM] * 3, [part, coded], scratch=work)
-    near = lax.ppermute(message, ("line", "band"), cores(partner, odd_up))
+    total, *sent = call(
+        functools.partial(share, spans),
+        (picked, keep, other),
+        [VMEM] * 3,
+        [part, *coded],
+        scratch=work,
+    )
+    near = [lax.ppermute(x, ("line", "band"), cores(partner, odd_up)) for x in sent]
     other_total = lax.ppermute(total, "band", swap)
     base, other_base, term = call(
-        centre, (picked, total, other_total), [VMEM] * 3, [part] * 3, flops=3 * unit * units
-    )
-    near, base, other_base, term = lax.optimization_barrier((near, base, other_base, term))
-    (message,) = call(relay, (term, near), [VMEM] * 2, [coded], scratch=work)
-    message, near = lax.optimization_barrier((message, near))
-    far = lax.ppermute(message, ("line", "band"), cores(even_up, partner))
-    (product,) = call(beside, (picked, near), [VMEM] * 2, [part], flops=unit * units)
-    (message,) = call(
-        settle, (picked, product, far), [VMEM] * 3, [coded], scratch=work, flops=unit * units
-    )
-    other_message = lax.ppermute(message, "band", swap)
+        centre, (picked, total, other_total), [VMEM] * 3, [part] * 3
+    )
+    far, product = [], []
+    for i, span in enumerate(spans):
+        (message,) = call(
+            functools.partial(relay, span), (term, near[i]), [VMEM] * 2, [coded[i]], scratch=work
+        )
+        message, near[i] = lax.optimization_barrier((message, near[i]))
+        far.append(lax.ppermute(message, ("line", "band"), cores(even_up, partner)))
+        planes = shape((span[1] - span[0], lines, half), f32)
+        product += call(
+            functools.partial(beside, span),
+            (picked, near[i]),
+            [VMEM] * 2,
+            [planes],
+        )
+    messages, others = [], []
+    for i, span in enumerate(spans):
+        planes = product[i].shape
+        messages += call(
+            functools.partial(settle, span),
+            (picked, product[i], far[i]),
+            [VMEM] * 3,
+            [coded[i]],
+            scratch=[pltpu.VMEM(planes, f32)],
+        )
+        others.append(lax.ppermute(messages[i], "band", swap))
     image = shape((count, lines, cols), f32)
+    some = 2 + len(spans)
     image, sums = call(
-        functools.partial(finish, False),
-        (observed, base, message),
-        [VMEM] * 3,
+        functools.partial(finish, False, spans),
+        (observed, base, *messages),
+        [VMEM] * some,
         [image, shape((3, lines, cols), f32)],
         scratch=work + [pltpu.SemaphoreType.DMA((units,))],
         out_specs=[HBM, VMEM],
     )
     image, angles = call(
-        functools.partial(finish, True),
-        (observed, other_base, other_message, sums, image),
-        [VMEM] * 4 + [HBM],
+        functools.partial(finish, True, spans),
+        (observed, other_base, *others, sums, image),
+        [VMEM] * (some + 1) + [HBM],
         [image, shape((lines, cols), f32)],
         scratch=[pltpu.VMEM((lines, cols), f32), *work, pltpu.SemaphoreType.DMA((units + 1,))],
         out_specs=[HBM] * 2,
-        aliases={4: 0},
+        aliases={some + 1: 0},
     )
     return image, angles
 

time: 33.4 us -> 30.8 us (0.922)
  waiting for transfers between devices: 16.6 us -> 11 us
  starting transfers between devices: 5.67 us -> 10 us
  Pallas kernels: 10.6 us -> 9.03 us
    ppermute x3 -> x6, waiting for transfers between devices: 14.2 us -> 9 us  [the longest x2 5.03 us: on_device(): far.append(lax.ppermute(message, ('line', 'band'), cores(even_up, partner)))]
    ppermute x1, starting transfers between devices: 0.07 us -> 2.56 us  [on_device(): other = lax.ppermute(send, 'band', swap)]
    ppermute x3 -> x6, starting transfers between devices: 5.17 us -> 6.8 us  [the longest x2 4.28 us: on_device(): far.append(lax.ppermute(message, ('line', 'band'), cores(even_up, partner)))]
    pallas_call x8 -> x11, Pallas kernels: 10.6 us -> 9.03 us  [call(): pl.pallas_call(kernel, in_specs=specs, out_specs=out_specs or [VMEM] * le...]
    ppermute x1, waiting for transfers between devices: 2.37 us -> 2.01 us  [on_device(): other = lax.ppermute(send, 'band', swap)]
  transfers between devices with their start and end apart: 5 -> 8, of which waited for: 4 -> 5; matrix products, arithmetic and copies ran while one was open for 0% -> 0% of each run, Pallas kernels for 5% -> 9%
where the time goes in v6:
time: 30.8 us
  waiting for transfers between devices  11 us (36%)
  starting transfers between devices  10 us (32%)
  Pallas kernels  9.03 us (29%)
  between operations  0.75 us (2%)
    pallas_call x11, Pallas kernels, call(): pl.pallas_call(kernel, in_specs=specs, out_specs=out_specs or [VMEM] * le...  9.03 us
    ppermute x2, waiting for transfers between devices, on_device(): far.append(lax.ppermute(message, ('line', 'band'), cores(even_up, partner)))  5.03 us
    ppermute x2, starting transfers between devices, on_device(): far.append(lax.ppermute(message, ('line', 'band'), cores(even_up, partner)))  4.28 us
    ppermute x2, waiting for transfers between devices, on_device(): lax.ppermute(x, ('line', 'band'), cores(partner, odd_up))  3.58 us
    ppermute x1, starting transfers between devices, on_device(): other = lax.ppermute(send, 'band', swap)  2.56 us
    ppermute x2, starting transfers between devices, on_device(): lax.ppermute(x, ('line', 'band'), cores(partner, odd_up))  2.38 us
    ppermute x1, waiting for transfers between devices, on_device(): other = lax.ppermute(send, 'band', swap)  2.01 us
    ppermute x1, starting transfers between devices, on_device(): other_total = lax.ppermute(total, 'band', swap)  0.66 us
  transfers between devices with their start and end apart: 8, of which 5 were waited for; matrix products, arithmetic and copies ran while one was open for 0% of the time, Pallas kernels for 9%

profile of v6, /device:TPU:0, one launch (start us, length us, event | category | flops | bytes accessed | tf_op | source)
XLA Modules:
  0.0 30.8 jit_solution(7977433792372789811)
XLA Ops:
  0.6 4.7 %fold.1 = (f32[13,128,128]{2,1,0:T(8,128)S(1)}, f32[13,128,128]{2,1,0:T(8,128)S(1)}, bf16[3,128,128]{2,1,0:T(8,128)(2,1)S(1)}) custom-call(s32[13]{0:T(128)} %start_in.1, s32[3]{0:T(128)} %offsets_in.1, bf16[13,20]{1,0:T(8,128)(2,1)} %values_in.1, bf16[3,128,128]{2,1,0:T(8,128)(2,1)} %blocks_in.1, s32[3]{0:T(128)} %along_offsets_in.1, ...), custom_call_target="tpu_custom_call" | custom-call | tf_op jit(solution)/shard_map/fold/pallas_call | solution.py:36
  5.3 2.6 %collective-permute-start = (f32[13,128,128]{2,1,0:T(8,128)S(1)}, f32[13,128,128]{2,1,0:T(8,128)S(1)}, u32[]{:S(2)}, u32[]{:S(2)}) collective-permute-start(f32[13,128,128]{2,1,0:T(8,128)S(1)} %get-tuple-element.19), channel_id=1, source_target_pairs={{0,1},{1,0},{2,3},{3,2},{4,5},{5,4},{6,7},{7,6},{8,9},{9,8},{10,11... | collective-permute-start | bytes 2555912 | tf_op jit(solution)/shard_map/ppermute | solution.py:481
  7.9 2.0 %collective-permute-done.other = f32[13,128,128]{2,1,0:T(8,128)S(1)} collective-permute-done((f32[13,128,128]{2,1,0:T(8,128)S(1)}, f32[13,128,128]{2,1,0:T(8,128)S(1)}, u32[]{:S(2)}, u32[]{:S(2)}) %collective-permute-start) | collective-permute-done | bytes 852000 | tf_op jit(solution)/shard_map/ppermute | solution.py:481
  9.9 0.3 %share.1 = (f32[13,128,128]{2,1,0:T(8,128)S(1)}, s16[912,128]{1,0:T(8,128)(2,1)S(1)}, s16[784,128]{1,0:T(8,128)(2,1)S(1)}) custom-call(bf16[3,128,128]{2,1,0:T(8,128)(2,1)S(1)} %get-tuple-element.17.picked, f32[13,128,128]{2,1,0:T(8,128)S(1)} %get-tuple-element.18.keep, f32[13,128,128]{2,1,0:T(8,128)S(1)} %collective-permute-done.other), custom_call_target="tpu_custom_call" | custom-call | tf_op jit(solution)/shard_map/share/pallas_call | solution.py:36
  10.2 0.7 %collective-permute-start.1 = (f32[13,128,128]{2,1,0:T(8,128)S(1)}, f32[13,128,128]{2,1,0:T(8,128)S(1)}, u32[]{:S(2)}, u32[]{:S(2)}) collective-permute-start(f32[13,128,128]{2,1,0:T(8,128)S(1)} %get-tuple-element.20.total), channel_id=1, source_target_pairs={{0,1},{1,0},{2,3},{3,2},{4,5},{5,4},{6,7},{7,6},{8,9},{9,8},{10,11... | collective-permute-start | bytes 2555912 | tf_op jit(solution)/shard_map/ppermute | solution.py:490
  10.9 2.3 %collective-permute-start.2 = (s16[912,128]{1,0:T(8,128)(2,1)S(1)}, s16[912,128]{1,0:T(8,128)(2,1)S(1)}, u32[]{:S(2)}, u32[]{:S(2)}) collective-permute-start(s16[912,128]{1,0:T(8,128)(2,1)S(1)} %get-tuple-element.23), channel_id=1, source_target_pairs={{0,2},{2,0},{4,6},{6,4},{8,10},{10,8},{12,14},{14,12},{5,1},{15,3}... | collective-permute-start | bytes 700424 | tf_op jit(solution)/shard_map/ppermute | solution.py:489
  13.2 0.0 collective-permute-start.5
  13.3 0.0 collective-permute-done.1.other_total
  13.3 0.4 %centre.1 = (f32[13,128,128]{2,1,0:T(8,128)S(1)}, f32[13,128,128]{2,1,0:T(8,128)S(1)}, f32[13,128,128]{2,1,0:T(8,128)S(1)}) custom-call(bf16[3,128,128]{2,1,0:T(8,128)(2,1)S(1)} %get-tuple-element.17.picked, f32[13,128,128]{2,1,0:T(8,128)S(1)} %get-tuple-element.20.total, f32[13,128,128]{2,1,0:T(8,128)S(1)} %collective-permute-done.1.other_total), custom_call_target="tpu_custom_call" | custom-call | tf_op jit(solution)/shard_map/centre/pallas_call | solution.py:36
  13.7 3.6 %collective-permute-done.2.received.near = s16[912,128]{1,0:T(8,128)(2,1)S(1)} collective-permute-done((s16[912,128]{1,0:T(8,128)(2,1)S(1)}, s16[912,128]{1,0:T(8,128)(2,1)S(1)}, u32[]{:S(2)}, u32[]{:S(2)}) %collective-permute-start.2) | collective-permute-done | bytes 233504 | tf_op jit(solution)/shard_map/ppermute | solution.py:489
  17.3 2.1 %collective-permute-start.3 = (s16[912,128]{1,0:T(8,128)(2,1)S(1)}, s16[912,128]{1,0:T(8,128)(2,1)S(1)}, u32[]{:S(2)}, u32[]{:S(2)}) collective-permute-start(s16[912,128]{1,0:T(8,128)(2,1)S(1)} %relay.2), channel_id=1, source_target_pairs={{0,4},{2,14},{4,8},{6,2},{8,12},{10,6},{12,0},{14,10},{1,3},{3,1},... | collective-permute-start | bytes 700424 | tf_op jit(solution)/shard_map/ppermute | solution.py:500
  19.4 0.0 collective-permute-done.5.received.near
  19.4 0.0 copy-start
  19.5 2.1 %collective-permute-start.6 = (s16[784,128]{1,0:T(8,128)(2,1)S(1)}, s16[784,128]{1,0:T(8,128)(2,1)S(1)}, u32[]{:S(2)}, u32[]{:S(2)}) collective-permute-start(s16[784,128]{1,0:T(8,128)(2,1)S(1)} %relay.3), channel_id=1, source_target_pairs={{0,4},{2,14},{4,8},{6,2},{8,12},{10,6},{12,0},{14,10},{1,3},{3,1},... | collective-permute-start | bytes 602120 | tf_op jit(solution)/shard_map/ppermute | solution.py:500
  21.6 0.3 beside.2.product
  21.9 3.6 %collective-permute-done.3.received = s16[912,128]{1,0:T(8,128)(2,1)S(1)} collective-permute-done((s16[912,128]{1,0:T(8,128)(2,1)S(1)}, s16[912,128]{1,0:T(8,128)(2,1)S(1)}, u32[]{:S(2)}, u32[]{:S(2)}) %collective-permute-start.3) | collective-permute-done | bytes 233504 | tf_op jit(solution)/shard_map/ppermute | solution.py:500
  25.5 0.4 %settle.2.rest_0_ = s16[912,128]{1,0:T(8,128)(2,1)S(1)} custom-call(bf16[3,128,128]{2,1,0:T(8,128)(2,1)S(1)} %get-tuple-element.17.picked, f32[7,128,128]{2,1,0:T(8,128)S(1)} %beside.2.product, s16[912,128]{1,0:T(8,128)(2,1)S(1)} %collective-permute-done.3.received), custom_call_target="tpu_custom_call" | custom-call | tf_op jit(solution)/shard_map/settle/pallas_call | solution.py:36
  25.9 0.1 collective-permute-start.4
  26.0 0.2 beside.3.product
  26.2 1.4 %collective-permute-done.6.received = s16[784,128]{1,0:T(8,128)(2,1)S(1)} collective-permute-done((s16[784,128]{1,0:T(8,128)(2,1)S(1)}, s16[784,128]{1,0:T(8,128)(2,1)S(1)}, u32[]{:S(2)}, u32[]{:S(2)}) %collective-permute-start.6) | collective-permute-done | bytes 200736 | tf_op jit(solution)/shard_map/ppermute | solution.py:500
  27.6 0.4 %settle.3.rest_1_ = s16[784,128]{1,0:T(8,128)(2,1)S(1)} custom-call(bf16[3,128,128]{2,1,0:T(8,128)(2,1)S(1)} %get-tuple-element.17.picked, f32[6,128,128]{2,1,0:T(8,128)S(1)} %beside.3.product, s16[784,128]{1,0:T(8,128)(2,1)S(1)} %collective-permute-done.6.received), custom_call_target="tpu_custom_call" | custom-call | tf_op jit(solution)/shard_map/settle/pallas_call | solution.py:36
  28.0 0.1 collective-permute-start.7
  28.1 0.0 copy-done
  28.1 1.0 %finish.2 = (f32[13,128,256]{2,1,0:T(8,128)}, f32[3,128,256]{2,1,0:T(8,128)S(1)}) custom-call(bf16[13,128,256]{2,1,0:T(8,128)(2,1)S(1)} %copy-done, f32[13,128,128]{2,1,0:T(8,128)S(1)} %get-tuple-element.29.base, s16[912,128]{1,0:T(8,128)(2,1)S(1)} %settle.2.rest_0_, s16[784,128]{1,0:T(8,128)(2,1)S(1)} %settle.3.rest_1_), custom_call_target="tpu_custom_call" | custom-call | tf_op jit(solution)/shard_map/finish/pallas_call | solution.py:36
  29.1 0.4 %collective-permute-done.7.rest_1_ = s16[784,128]{1,0:T(8,128)(2,1)S(1)} collective-permute-done((s16[784,128]{1,0:T(8,128)(2,1)S(1)}, s16[784,128]{1,0:T(8,128)(2,1)S(1)}, u32[]{:S(2)}, u32[]{:S(2)}) %collective-permute-start.7) | collective-permute-done | bytes 200736 | tf_op jit(solution)/shard_map/ppermute | solution.py:518
  29.5 0.0 collective-permute-done.4.rest_0_
  29.5 1.3 %finish.3 = (f32[13,128,256]{2,1,0:T(8,128)}, f32[128,256]{1,0:T(8,128)}) custom-call(bf16[13,128,256]{2,1,0:T(8,128)(2,1)S(1)} %copy-done, f32[13,128,128]{2,1,0:T(8,128)S(1)} %get-tuple-element.21.base, s16[912,128]{1,0:T(8,128)(2,1)S(1)} %collective-permute-done.4.rest_0_, ...), custom_call_target="tpu_custom_call", output_to_operand_aliasing={{0}: (5, {})} | custom-call | tf_op jit(solution)/shard_map/finish/pallas_call | solution.py:36
  (2 shorter events, 0.0 us)
Async XLA Ops:
  5.3 4.6 %collective-permute-start = (f32[13,128,128]{2,1,0:T(8,128)S(1)}, f32[13,128,128]{2,1,0:T(8,128)S(1)}, u32[]{:S(2)}, u32[]{:S(2)}) collective-permute-start(f32[13,128,128]{2,1,0:T(8,128)S(1)} %get-tuple-element.19), channel_id=1, source_target_pairs={{0,1},{1,0},{2,3},{3,2},{4,5},{5,4},{6,7},{7,6},{8,9},{9,8},{10,11... | collective-permute-start | bytes 2555912 | tf_op jit(solution)/shard_map/ppermute | solution.py:481
  10.2 3.0 %collective-permute-start.1 = (f32[13,128,128]{2,1,0:T(8,128)S(1)}, f32[13,128,128]{2,1,0:T(8,128)S(1)}, u32[]{:S(2)}, u32[]{:S(2)}) collective-permute-start(f32[13,128,128]{2,1,0:T(8,128)S(1)} %get-tuple-element.20.total), channel_id=1, source_target_pairs={{0,1},{1,0},{2,3},{3,2},{4,5},{5,4},{6,7},{7,6},{8,9},{9,8},{10,11... | collective-permute-start | bytes 2555912 | tf_op jit(solution)/shard_map/ppermute | solution.py:490
  10.9 6.4 %collective-permute-start.2 = (s16[912,128]{1,0:T(8,128)(2,1)S(1)}, s16[912,128]{1,0:T(8,128)(2,1)S(1)}, u32[]{:S(2)}, u32[]{:S(2)}) collective-permute-start(s16[912,128]{1,0:T(8,128)(2,1)S(1)} %get-tuple-element.23), channel_id=1, source_target_pairs={{0,2},{2,0},{4,6},{6,4},{8,10},{10,8},{12,14},{14,12},{5,1},{15,3}... | collective-permute-start | bytes 700424 | tf_op jit(solution)/shard_map/ppermute | solution.py:489
  13.2 6.2 %collective-permute-start.5 = (s16[784,128]{1,0:T(8,128)(2,1)S(1)}, s16[784,128]{1,0:T(8,128)(2,1)S(1)}, u32[]{:S(2)}, u32[]{:S(2)}) collective-permute-start(s16[784,128]{1,0:T(8,128)(2,1)S(1)} %get-tuple-element.26), channel_id=1, source_target_pairs={{0,2},{2,0},{4,6},{6,4},{8,10},{10,8},{12,14},{14,12},{5,1},{15,3}... | collective-permute-start | bytes 602120 | tf_op jit(solution)/shard_map/ppermute | solution.py:489
  17.3 8.2 %collective-permute-start.3 = (s16[912,128]{1,0:T(8,128)(2,1)S(1)}, s16[912,128]{1,0:T(8,128)(2,1)S(1)}, u32[]{:S(2)}, u32[]{:S(2)}) collective-permute-start(s16[912,128]{1,0:T(8,128)(2,1)S(1)} %relay.2), channel_id=1, source_target_pairs={{0,4},{2,14},{4,8},{6,2},{8,12},{10,6},{12,0},{14,10},{1,3},{3,1},... | collective-permute-start | bytes 700424 | tf_op jit(solution)/shard_map/ppermute | solution.py:500
  19.4 8.6 %copy-start = (bf16[13,128,256]{2,1,0:T(8,128)(2,1)S(1)}, bf16[13,128,256]{2,1,0:T(8,128)(2,1)}, u32[]{:S(2)}) copy-start(bf16[13,128,256]{2,1,0:T(8,128)(2,1)} %observed.3) | copy-start | bytes 2555908
  19.5 8.2 %collective-permute-start.6 = (s16[784,128]{1,0:T(8,128)(2,1)S(1)}, s16[784,128]{1,0:T(8,128)(2,1)S(1)}, u32[]{:S(2)}, u32[]{:S(2)}) collective-permute-start(s16[784,128]{1,0:T(8,128)(2,1)S(1)} %relay.3), channel_id=1, source_target_pairs={{0,4},{2,14},{4,8},{6,2},{8,12},{10,6},{12,0},{14,10},{1,3},{3,1},... | collective-permute-start | bytes 602120 | tf_op jit(solution)/shard_map/ppermute | solution.py:500
  25.9 3.6 %collective-permute-start.4 = (s16[912,128]{1,0:T(8,128)(2,1)S(1)}, s16[912,128]{1,0:T(8,128)(2,1)S(1)}, u32[]{:S(2)}, u32[]{:S(2)}) collective-permute-start(s16[912,128]{1,0:T(8,128)(2,1)S(1)} %settle.2.rest_0_), channel_id=1, source_target_pairs={{0,1},{1,0},{2,3},{3,2},{4,5},{5,4},{6,7},{7,6},{8,9},{9,8},{10,11... | collective-permute-start | bytes 700424 | tf_op jit(solution)/shard_map/ppermute | solution.py:518
  28.0 1.5 %collective-permute-start.7 = (s16[784,128]{1,0:T(8,128)(2,1)S(1)}, s16[784,128]{1,0:T(8,128)(2,1)S(1)}, u32[]{:S(2)}, u32[]{:S(2)}) collective-permute-start(s16[784,128]{1,0:T(8,128)(2,1)S(1)} %settle.3.rest_1_), channel_id=1, source_target_pairs={{0,1},{1,0},{2,3},{3,2},{4,5},{5,4},{6,7},{7,6},{8,9},{9,8},{10,11... | collective-permute-start | bytes 602120 | tf_op jit(solution)/shard_map/ppermute | solution.py:518

commit v7 on v6

--- a/solution.py
+++ b/solution.py
@@ -77,6 +77,7 @@
     along_offsets,
     along_blocks,
     cube,
+    bands_out,
     folded,
     table,
     order,
@@ -140,29 +141,43 @@
     for r in range(2):
         for c in range(2):
             block = blocks[which(offsets, jnp.int32(r - c))].astype(jnp.float32).T
-            for top in (0, cols):
-                at = slice(top + r * half, top + (r + 1) * half)
-                table[at, c * half : (c + 1) * half] = block.astype(jnp.bfloat16)
+            at = slice(r * half, (r + 1) * half)
+            table[at, c * half : (c + 1) * half] = block.astype(jnp.bfloat16)
     step = side_step()
     for i, shift in enumerate((jnp.int32(0), step, -step)):
         picked[i] = along_blocks[which(along_offsets, shift)]
     spread.wait()
 
-    def ready(q, carry):
-        pl.when(q < chunks - 1)(lambda: arrive(q, window).wait())
-        pl.when(q == chunks - 1)(lambda: arrive(chunks - 1, last).wait())
+    side = table[...]
+
+    def across(band, carry):
+        value = cube[pl.ds(band, group)].reshape(group * lines, cols)
+        made = jnp.dot(value, side, preferred_element_type=jnp.float32)
+        bands_out[pl.ds(band, group)] = made.reshape(group, lines, cols)
         return carry
+
+    def ready(q, used):
+        def take(size):
+            arrive(q, size).wait()
+
+            @pl.when(used)
+            def _():
+                lax.fori_loop(0, size // group, lambda t, c: across(q * window + t * group, c), 0)
+
+        pl.when(q < chunks - 1)(lambda: take(window))
+        pl.when(q == chunks - 1)(lambda: take(last))
+        return used
 
     def one(n, arrived):
         m = order[n]
         low = SPB * start[m] - bands * me
         stop = jnp.minimum(low + window, bands)
         needed = lax.div(stop - 1, jnp.int32(window)) + 1
-        lax.fori_loop(arrived, needed, ready, 0)
+        lax.fori_loop(arrived, needed, ready, True)
         whole = jnp.logical_and(low >= 0, low + window <= bands)
 
         def term(band, weight, r):
-            return weight * cube[band, r : r + ROWS, :].astype(jnp.float32)
+            return weight * bands_out[band, r : r + ROWS, :]
 
         @pl.when(whole)
         def _():
@@ -193,25 +208,16 @@
         return jnp.maximum(arrived, needed)
 
     arrived = lax.fori_loop(before, until, one, jnp.int32(0))
-    lax.fori_loop(arrived, chunks, ready, 0)
-
-    side = table[...]
+    lax.fori_loop(arrived, chunks, ready, False)
+
     planes, odd, units = ownership(count)
-
-    def across(at, planes):
-        value = folded[pl.ds(at, planes)].reshape(planes * lines, cols)
-        both = jnp.concatenate(split(value), axis=1)
-        made = jnp.dot(both, side, preferred_element_type=jnp.float32)
-        return made.reshape(planes, lines, cols)
-
     for owner, out in ((me, keep), (1 - me, send)):
-        made = across(owner * (planes + odd), planes)
         for i in range(planes):
-            out[2 * i] = made[i, :, :half]
-            out[2 * i + 1] = made[i, :, half:]
+            made = folded[owner * (planes + odd) + i]
+            out[2 * i] = made[:, :half]
+            out[2 * i + 1] = made[:, half:]
     if odd:
-        made = across(planes, 1)[0]
-        left, right = made[:, :half], made[:, half:]
+        left, right = folded[planes, :, :half], folded[planes, :, half:]
         keep[units - 1] = jnp.where(me == 0, left, right)
         send[units - 1] = jnp.where(me == 0, right, left)
 
@@ -470,8 +476,9 @@
             pltpu.SMEM(along_offsets.shape, jnp.int32),
             pltpu.VMEM(along_kernels.shape, along_kernels.dtype),
             pltpu.VMEM(cube.shape, cube.dtype),
+            pltpu.VMEM(cube.shape, f32),
             pltpu.VMEM((count, lines, cols), f32),
-            pltpu.VMEM((2 * cols, cols), across_kernels.dtype),
+            pltpu.VMEM((cols, cols), across_kernels.dtype),
             pltpu.SMEM((count,), jnp.int32),
             pltpu.SemaphoreType.DMA((len(inputs),)),
             pltpu.SemaphoreType.DMA((-(-bands // resp_values.shape[1]),)),

time: 30.8 us -> 35.4 us (1.15)
  Pallas kernels: 9.03 us -> 15 us
  starting transfers between devices: 10 us -> 7.88 us
  waiting for transfers between devices: 11 us -> 11.4 us
    pallas_call x11, Pallas kernels: 9.03 us -> 15 us  [call(): pl.pallas_call(kernel, in_specs=specs, out_specs=out_specs or [VMEM] * le...]
    ppermute x1, starting transfers between devices: 2.56 us -> 0.07 us  [on_device(): other = lax.ppermute(send, 'band', swap)]
    ppermute x2, starting transfers between devices: 2.38 us -> 3 us  [on_device(): lax.ppermute(x, ('line', 'band'), cores(partner, odd_up))]
    ppermute x1, waiting for transfers between devices: 2.01 us -> 2.37 us  [on_device(): other = lax.ppermute(send, 'band', swap)]
  transfers between devices with their start and end apart: 8 -> 8, of which waited for: 5 -> 5; matrix products, arithmetic and copies ran while one was open for 0% -> 0% of each run, Pallas kernels for 9% -> 8%
where the time goes in v7:
time: 35.4 us; the launch traced here: 35.1 us
  Pallas kernels  15 us (42%)
  waiting for transfers between devices  11.4 us (32%)
  starting transfers between devices  7.88 us (22%)
  between operations  0.76 us (2%)
    pallas_call x11, Pallas kernels, call(): pl.pallas_call(kernel, in_specs=specs, out_specs=out_specs or [VMEM] * le...  15 us
    ppermute x2, waiting for transfers between devices, on_device(): far.append(lax.ppermute(message, ('line', 'band'), cores(even_up, partner)))  5.08 us
    ppermute x2, starting transfers between devices, on_device(): far.append(lax.ppermute(message, ('line', 'band'), cores(even_up, partner)))  4.25 us
    ppermute x2, waiting for transfers between devices, on_device(): lax.ppermute(x, ('line', 'band'), cores(partner, odd_up))  3.57 us
    ppermute x2, starting transfers between devices, on_device(): lax.ppermute(x, ('line', 'band'), cores(partner, odd_up))  3 us
    ppermute x1, waiting for transfers between devices, on_device(): other = lax.ppermute(send, 'band', swap)  2.37 us
  transfers between devices with their start and end apart: 8, of which 5 were waited for; matrix products, arithmetic and copies ran while one was open for 0% of the time, Pallas kernels for 8%

profile of v7, /device:TPU:0, one launch (start us, length us, event | category | flops | bytes accessed | tf_op | source)
XLA Modules:
  0.0 35.1 jit_solution(7147037691624086599)
XLA Ops:
  0.6 10.7 %fold.1 = (f32[13,128,128]{2,1,0:T(8,128)S(1)}, f32[13,128,128]{2,1,0:T(8,128)S(1)}, bf16[3,128,128]{2,1,0:T(8,128)(2,1)S(1)}) custom-call(s32[13]{0:T(128)} %start_in.1, s32[3]{0:T(128)} %offsets_in.1, bf16[13,20]{1,0:T(8,128)(2,1)} %values_in.1, bf16[3,128,128]{2,1,0:T(8,128)(2,1)} %blocks_in.1, s32[3]{0:T(128)} %along_offsets_in.1, ...), custom_call_target="tpu_custom_call" | custom-call | tf_op jit(solution)/shard_map/fold/pallas_call | solution.py:36
  11.3 0.1 collective-permute-start
  11.4 2.4 %collective-permute-done.other = f32[13,128,128]{2,1,0:T(8,128)S(1)} collective-permute-done((f32[13,128,128]{2,1,0:T(8,128)S(1)}, f32[13,128,128]{2,1,0:T(8,128)S(1)}, u32[]{:S(2)}, u32[]{:S(2)}) %collective-permute-start) | collective-permute-done | bytes 852000 | tf_op jit(solution)/shard_map/ppermute | solution.py:488
  13.8 0.3 share.1
  14.1 0.4 %collective-permute-start.1 = (f32[13,128,128]{2,1,0:T(8,128)S(1)}, f32[13,128,128]{2,1,0:T(8,128)S(1)}, u32[]{:S(2)}, u32[]{:S(2)}) collective-permute-start(f32[13,128,128]{2,1,0:T(8,128)S(1)} %get-tuple-element.20.total), channel_id=1, source_target_pairs={{0,1},{1,0},{2,3},{3,2},{4,5},{5,4},{6,7},{7,6},{8,9},{9,8},{10,11... | collective-permute-start | bytes 2555912 | tf_op jit(solution)/shard_map/ppermute | solution.py:497
  14.5 3.0 %collective-permute-start.2 = (s16[912,128]{1,0:T(8,128)(2,1)S(1)}, s16[912,128]{1,0:T(8,128)(2,1)S(1)}, u32[]{:S(2)}, u32[]{:S(2)}) collective-permute-start(s16[912,128]{1,0:T(8,128)(2,1)S(1)} %get-tuple-element.23), channel_id=1, source_target_pairs={{0,2},{2,0},{4,6},{6,4},{8,10},{10,8},{12,14},{14,12},{5,1},{15,3}... | collective-permute-start | bytes 700424 | tf_op jit(solution)/shard_map/ppermute | solution.py:496
  17.5 0.0 collective-permute-start.5
  17.5 0.0 collective-permute-done.1.other_total
  17.5 0.4 %centre.1 = (f32[13,128,128]{2,1,0:T(8,128)S(1)}, f32[13,128,128]{2,1,0:T(8,128)S(1)}, f32[13,128,128]{2,1,0:T(8,128)S(1)}) custom-call(bf16[3,128,128]{2,1,0:T(8,128)(2,1)S(1)} %get-tuple-element.17.picked, f32[13,128,128]{2,1,0:T(8,128)S(1)} %get-tuple-element.20.total, f32[13,128,128]{2,1,0:T(8,128)S(1)} %collective-permute-done.1.other_total), custom_call_target="tpu_custom_call" | custom-call | tf_op jit(solution)/shard_map/centre/pallas_call | solution.py:36
  18.0 3.6 %collective-permute-done.2.received.near = s16[912,128]{1,0:T(8,128)(2,1)S(1)} collective-permute-done((s16[912,128]{1,0:T(8,128)(2,1)S(1)}, s16[912,128]{1,0:T(8,128)(2,1)S(1)}, u32[]{:S(2)}, u32[]{:S(2)}) %collective-permute-start.2) | collective-permute-done | bytes 233504 | tf_op jit(solution)/shard_map/ppermute | solution.py:496
  21.6 2.1 %collective-permute-start.3 = (s16[912,128]{1,0:T(8,128)(2,1)S(1)}, s16[912,128]{1,0:T(8,128)(2,1)S(1)}, u32[]{:S(2)}, u32[]{:S(2)}) collective-permute-start(s16[912,128]{1,0:T(8,128)(2,1)S(1)} %relay.2), channel_id=1, source_target_pairs={{0,4},{2,14},{4,8},{6,2},{8,12},{10,6},{12,0},{14,10},{1,3},{3,1},... | collective-permute-start | bytes 700424 | tf_op jit(solution)/shard_map/ppermute | solution.py:507
  23.7 0.0 collective-permute-done.5.received.near
  23.7 0.0 copy-start
  23.7 2.1 %collective-permute-start.6 = (s16[784,128]{1,0:T(8,128)(2,1)S(1)}, s16[784,128]{1,0:T(8,128)(2,1)S(1)}, u32[]{:S(2)}, u32[]{:S(2)}) collective-permute-start(s16[784,128]{1,0:T(8,128)(2,1)S(1)} %relay.3), channel_id=1, source_target_pairs={{0,4},{2,14},{4,8},{6,2},{8,12},{10,6},{12,0},{14,10},{1,3},{3,1},... | collective-permute-start | bytes 602120 | tf_op jit(solution)/shard_map/ppermute | solution.py:507
  25.8 0.3 beside.2.product
  26.1 3.7 %collective-permute-done.3.received = s16[912,128]{1,0:T(8,128)(2,1)S(1)} collective-permute-done((s16[912,128]{1,0:T(8,128)(2,1)S(1)}, s16[912,128]{1,0:T(8,128)(2,1)S(1)}, u32[]{:S(2)}, u32[]{:S(2)}) %collective-permute-start.3) | collective-permute-done | bytes 233504 | tf_op jit(solution)/shard_map/ppermute | solution.py:507
  29.8 0.4 %settle.2.rest_0_ = s16[912,128]{1,0:T(8,128)(2,1)S(1)} custom-call(bf16[3,128,128]{2,1,0:T(8,128)(2,1)S(1)} %get-tuple-element.17.picked, f32[7,128,128]{2,1,0:T(8,128)S(1)} %beside.2.product, s16[912,128]{1,0:T(8,128)(2,1)S(1)} %collective-permute-done.3.received), custom_call_target="tpu_custom_call" | custom-call | tf_op jit(solution)/shard_map/settle/pallas_call | solution.py:36
  30.2 0.1 collective-permute-start.4
  30.3 0.2 beside.3.product
  30.5 1.4 %collective-permute-done.6.received = s16[784,128]{1,0:T(8,128)(2,1)S(1)} collective-permute-done((s16[784,128]{1,0:T(8,128)(2,1)S(1)}, s16[784,128]{1,0:T(8,128)(2,1)S(1)}, u32[]{:S(2)}, u32[]{:S(2)}) %collective-permute-start.6) | collective-permute-done | bytes 200736 | tf_op jit(solution)/shard_map/ppermute | solution.py:507
  31.9 0.4 settle.3.rest_1_
  32.3 0.1 collective-permute-start.7
  32.4 0.0 copy-done
  32.4 1.0 %finish.2 = (f32[13,128,256]{2,1,0:T(8,128)}, f32[3,128,256]{2,1,0:T(8,128)S(1)}) custom-call(bf16[13,128,256]{2,1,0:T(8,128)(2,1)S(1)} %copy-done, f32[13,128,128]{2,1,0:T(8,128)S(1)} %get-tuple-element.29.base, s16[912,128]{1,0:T(8,128)(2,1)S(1)} %settle.2.rest_0_, s16[784,128]{1,0:T(8,128)(2,1)S(1)} %settle.3.rest_1_), custom_call_target="tpu_custom_call" | custom-call | tf_op jit(solution)/shard_map/finish/pallas_call | solution.py:36
  33.4 0.4 %collective-permute-done.7.rest_1_ = s16[784,128]{1,0:T(8,128)(2,1)S(1)} collective-permute-done((s16[784,128]{1,0:T(8,128)(2,1)S(1)}, s16[784,128]{1,0:T(8,128)(2,1)S(1)}, u32[]{:S(2)}, u32[]{:S(2)}) %collective-permute-start.7) | collective-permute-done | bytes 200736 | tf_op jit(solution)/shard_map/ppermute | solution.py:525
  33.8 0.0 collective-permute-done.4.rest_0_
  33.8 1.3 %finish.3 = (f32[13,128,256]{2,1,0:T(8,128)}, f32[128,256]{1,0:T(8,128)}) custom-call(bf16[13,128,256]{2,1,0:T(8,128)(2,1)S(1)} %copy-done, f32[13,128,128]{2,1,0:T(8,128)S(1)} %get-tuple-element.21.base, s16[912,128]{1,0:T(8,128)(2,1)S(1)} %collective-permute-done.4.rest_0_, ...), custom_call_target="tpu_custom_call", output_to_operand_aliasing={{0}: (5, {})} | custom-call | tf_op jit(solution)/shard_map/finish/pallas_call | solution.py:36
  (2 shorter events, 0.0 us)
Async XLA Ops:
  11.3 2.4 %collective-permute-start = (f32[13,128,128]{2,1,0:T(8,128)S(1)}, f32[13,128,128]{2,1,0:T(8,128)S(1)}, u32[]{:S(2)}, u32[]{:S(2)}) collective-permute-start(f32[13,128,128]{2,1,0:T(8,128)S(1)} %get-tuple-element.19), channel_id=1, source_target_pairs={{0,1},{1,0},{2,3},{3,2},{4,5},{5,4},{6,7},{7,6},{8,9},{9,8},{10,11... | collective-permute-start | bytes 2555912 | tf_op jit(solution)/shard_map/ppermute | solution.py:488
  14.1 3.4 %collective-permute-start.1 = (f32[13,128,128]{2,1,0:T(8,128)S(1)}, f32[13,128,128]{2,1,0:T(8,128)S(1)}, u32[]{:S(2)}, u32[]{:S(2)}) collective-permute-start(f32[13,128,128]{2,1,0:T(8,128)S(1)} %get-tuple-element.20.total), channel_id=1, source_target_pairs={{0,1},{1,0},{2,3},{3,2},{4,5},{5,4},{6,7},{7,6},{8,9},{9,8},{10,11... | collective-permute-start | bytes 2555912 | tf_op jit(solution)/shard_map/ppermute | solution.py:497
  14.5 7.0 %collective-permute-start.2 = (s16[912,128]{1,0:T(8,128)(2,1)S(1)}, s16[912,128]{1,0:T(8,128)(2,1)S(1)}, u32[]{:S(2)}, u32[]{:S(2)}) collective-permute-start(s16[912,128]{1,0:T(8,128)(2,1)S(1)} %get-tuple-element.23), channel_id=1, source_target_pairs={{0,2},{2,0},{4,6},{6,4},{8,10},{10,8},{12,14},{14,12},{5,1},{15,3}... | collective-permute-start | bytes 700424 | tf_op jit(solution)/shard_map/ppermute | solution.py:496
  17.5 6.2 %collective-permute-start.5 = (s16[784,128]{1,0:T(8,128)(2,1)S(1)}, s16[784,128]{1,0:T(8,128)(2,1)S(1)}, u32[]{:S(2)}, u32[]{:S(2)}) collective-permute-start(s16[784,128]{1,0:T(8,128)(2,1)S(1)} %get-tuple-element.26), channel_id=1, source_target_pairs={{0,2},{2,0},{4,6},{6,4},{8,10},{10,8},{12,14},{14,12},{5,1},{15,3}... | collective-permute-start | bytes 602120 | tf_op jit(solution)/shard_map/ppermute | solution.py:496
  21.6 8.2 %collective-permute-start.3 = (s16[912,128]{1,0:T(8,128)(2,1)S(1)}, s16[912,128]{1,0:T(8,128)(2,1)S(1)}, u32[]{:S(2)}, u32[]{:S(2)}) collective-permute-start(s16[912,128]{1,0:T(8,128)(2,1)S(1)} %relay.2), channel_id=1, source_target_pairs={{0,4},{2,14},{4,8},{6,2},{8,12},{10,6},{12,0},{14,10},{1,3},{3,1},... | collective-permute-start | bytes 700424 | tf_op jit(solution)/shard_map/ppermute | solution.py:507
  23.7 8.7 %copy-start = (bf16[13,128,256]{2,1,0:T(8,128)(2,1)S(1)}, bf16[13,128,256]{2,1,0:T(8,128)(2,1)}, u32[]{:S(2)}) copy-start(bf16[13,128,256]{2,1,0:T(8,128)(2,1)} %observed.3) | copy-start | bytes 2555908
  23.7 8.2 %collective-permute-start.6 = (s16[784,128]{1,0:T(8,128)(2,1)S(1)}, s16[784,128]{1,0:T(8,128)(2,1)S(1)}, u32[]{:S(2)}, u32[]{:S(2)}) collective-permute-start(s16[784,128]{1,0:T(8,128)(2,1)S(1)} %relay.3), channel_id=1, source_target_pairs={{0,4},{2,14},{4,8},{6,2},{8,12},{10,6},{12,0},{14,10},{1,3},{3,1},... | collective-permute-start | bytes 602120 | tf_op jit(solution)/shard_map/ppermute | solution.py:507
  30.2 3.6 %collective-permute-start.4 = (s16[912,128]{1,0:T(8,128)(2,1)S(1)}, s16[912,128]{1,0:T(8,128)(2,1)S(1)}, u32[]{:S(2)}, u32[]{:S(2)}) collective-permute-start(s16[912,128]{1,0:T(8,128)(2,1)S(1)} %settle.2.rest_0_), channel_id=1, source_target_pairs={{0,1},{1,0},{2,3},{3,2},{4,5},{5,4},{6,7},{7,6},{8,9},{9,8},{10,11... | collective-permute-start | bytes 700424 | tf_op jit(solution)/shard_map/ppermute | solution.py:525
  32.3 1.5 %collective-permute-start.7 = (s16[784,128]{1,0:T(8,128)(2,1)S(1)}, s16[784,128]{1,0:T(8,128)(2,1)S(1)}, u32[]{:S(2)}, u32[]{:S(2)}) collective-permute-start(s16[784,128]{1,0:T(8,128)(2,1)S(1)} %settle.3.rest_1_), channel_id=1, source_target_pairs={{0,1},{1,0},{2,3},{3,2},{4,5},{5,4},{6,7},{7,6},{8,9},{9,8},{10,11... | collective-permute-start | bytes 602120 | tf_op jit(solution)/shard_map/ppermute | solution.py:525

commit v8 on v6

--- a/solution.py
+++ b/solution.py
@@ -37,7 +37,7 @@
         kernel,
         in_specs=specs,
         out_specs=out_specs or [VMEM] * len(outs),
-        out_shape=outs,
+        out_shape=[jax.ShapeDtypeStruct(x.shape, x.dtype) for x in outs],
         scratch_shapes=scratch,
         input_output_aliases=aliases or {},
         compiler_params=pltpu.CompilerParams(vmem_limit_bytes=32 * 2**20),
@@ -57,7 +57,91 @@
     return [(first + i, c) for i in range(pairs) for c in range(2)] + [(pairs, core)] * odd
 
 
-def fold(
+def sum_windows(number, plane_of, start, weights, cube, folded, order, ready=None):
+    bands, lines, cols = cube.shape
+    window = weights.shape[1]
+    group = math.gcd(SPB, bands)
+    first = bands * lax.axis_index("band")
+    places = [SPB * start[plane_of(i)] - first for i in range(number)]
+    ranks = [jnp.int32(0)] * number
+    for m in range(number):
+        for n in range(m + 1, number):
+            later = (places[n] < places[m]).astype(jnp.int32)
+            ranks[m] = ranks[m] + later
+            ranks[n] = ranks[n] + (1 - later)
+    before = jnp.int32(0)
+    until = jnp.int32(0)
+    for m in range(number):
+        order[ranks[m]] = jnp.int32(m)
+        before = before + (places[m] <= -window).astype(jnp.int32)
+        until = until + (places[m] < bands).astype(jnp.int32)
+
+    def clear(n, carry):
+        folded[order[n]] = jnp.zeros((lines, cols), jnp.float32)
+        return carry
+
+    lax.fori_loop(0, before, clear, 0)
+    lax.fori_loop(until, number, clear, 0)
+
+    def one(n, arrived):
+        i = order[n]
+        m = plane_of(i)
+        low = SPB * start[m] - first
+        stop = jnp.minimum(low + window, bands)
+        needed = lax.div(stop - 1, jnp.int32(window)) + 1
+        if ready is not None:
+            ready(arrived, needed)
+        whole = jnp.logical_and(low >= 0, low + window <= bands)
+
+        def term(band, weight, r):
+            return weight * cube[band, r : r + ROWS, :].astype(jnp.float32)
+
+        @pl.when(whole)
+        def _():
+            for r in range(0, lines, ROWS):
+                total = term(low, weights[m, 0], r)
+                for j in range(1, window):
+                    total = total + term(low + j, weights[m, j], r)
+                folded[i, r : r + ROWS, :] = total
+
+        @pl.when(jnp.logical_not(whole))
+        def _():
+            begin = jnp.maximum(low, 0)
+            for r in range(0, lines, ROWS):
+
+                def some(t, total):
+                    for k in range(group):
+                        band = begin + t * group + k
+                        total = total + term(band, weights[m, band - low], r)
+                    return total
+
+                folded[i, r : r + ROWS, :] = lax.fori_loop(
+                    0,
+                    lax.div(stop - begin, jnp.int32(group)),
+                    some,
+                    jnp.zeros((ROWS, cols), jnp.float32),
+                )
+
+        return jnp.maximum(arrived, needed)
+
+    return lax.fori_loop(before, until, one, jnp.int32(0))
+
+
+def across(value, table):
+    planes, lines, cols = value.shape
+    both = jnp.concatenate(split(value.reshape(planes * lines, cols)), axis=1)
+    made = jnp.dot(both, table, preferred_element_type=jnp.float32)
+    return made.reshape(planes, lines, cols)
+
+
+def spread_out(made, out):
+    half = made.shape[2] // 2
+    for i in range(made.shape[0]):
+        out[2 * i] = made[i, :, :half]
+        out[2 * i + 1] = made[i, :, half:]
+
+
+def fold_other(
     start_in,
     offsets_in,
     values_in,
@@ -65,20 +149,20 @@
     along_offsets_in,
     along_blocks_in,
     cube_in,
-    keep,
     send,
+    middle,
+    cube,
+    wide,
+    table,
     picked,
     start,
     offsets,
     values,
-    wide,
     weights,
     blocks,
     along_offsets,
     along_blocks,
-    cube,
     folded,
-    table,
     order,
     small,
     large,
@@ -86,7 +170,7 @@
     bands, lines, cols = cube.shape
     count, window = values.shape
     half = cols // 2
-    group = math.gcd(SPB, bands)
+    planes, odd, units = ownership(count)
     me = lax.axis_index("band")
     pairs = (
         (start_in, start),
@@ -97,7 +181,6 @@
         (along_blocks_in, along_blocks),
     )
     copies = [pltpu.make_async_copy(a, b, small.at[i]) for i, (a, b) in enumerate(pairs)]
-
     chunks = -(-bands // window)
     last = bands - (chunks - 1) * window
 
@@ -113,29 +196,7 @@
     wide[...] = values[...].astype(jnp.float32)
     spread = pltpu.make_async_copy(wide, weights, small.at[len(pairs)])
     spread.start()
-    copies[0].wait()
-
-    places = [SPB * start[m] - bands * me for m in range(count)]
-    ranks = [jnp.int32(0)] * count
-    for m in range(count):
-        for n in range(m + 1, count):
-            later = (places[n] < places[m]).astype(jnp.int32)
-            ranks[m] = ranks[m] + later
-            ranks[n] = ranks[n] + (1 - later)
-    before = jnp.int32(0)
-    until = jnp.int32(0)
-    for m in range(count):
-        order[ranks[m]] = jnp.int32(m)
-        before = before + (places[m] <= -window).astype(jnp.int32)
-        until = until + (places[m] < bands).astype(jnp.int32)
-
-    def clear(n, carry):
-        folded[order[n]] = jnp.zeros((lines, cols), jnp.float32)
-        return carry
-
-    lax.fori_loop(0, before, clear, 0)
-    lax.fori_loop(until, count, clear, 0)
-    for copy in copies[2:]:
+    for copy in copies[:1] + copies[2:]:
         copy.wait()
     for r in range(2):
         for c in range(2):
@@ -148,72 +209,44 @@
         picked[i] = along_blocks[which(along_offsets, shift)]
     spread.wait()
 
-    def ready(q, carry):
+    def one(q, carry):
         pl.when(q < chunks - 1)(lambda: arrive(q, window).wait())
         pl.when(q == chunks - 1)(lambda: arrive(chunks - 1, last).wait())
         return carry
 
-    def one(n, arrived):
-        m = order[n]
-        low = SPB * start[m] - bands * me
-        stop = jnp.minimum(low + window, bands)
-        needed = lax.div(stop - 1, jnp.int32(window)) + 1
-        lax.fori_loop(arrived, needed, ready, 0)
-        whole = jnp.logical_and(low >= 0, low + window <= bands)
-
-        def term(band, weight, r):
-            return weight * cube[band, r : r + ROWS, :].astype(jnp.float32)
-
-        @pl.when(whole)
-        def _():
-            for r in range(0, lines, ROWS):
-                total = term(low, weights[m, 0], r)
-                for j in range(1, window):
-                    total = total + term(low + j, weights[m, j], r)
-                folded[m, r : r + ROWS, :] = total
-
-        @pl.when(jnp.logical_not(whole))
-        def _():
-            first = jnp.maximum(low, 0)
-            for r in range(0, lines, ROWS):
-
-                def some(t, total):
-                    for i in range(group):
-                        band = first + t * group + i
-                        total = total + term(band, weights[m, band - low], r)
-                    return total
-
-                folded[m, r : r + ROWS, :] = lax.fori_loop(
-                    0,
-                    lax.div(stop - first, jnp.int32(group)),
-                    some,
-                    jnp.zeros((ROWS, cols), jnp.float32),
-                )
-
-        return jnp.maximum(arrived, needed)
-
-    arrived = lax.fori_loop(before, until, one, jnp.int32(0))
-    lax.fori_loop(arrived, chunks, ready, 0)
-
-    side = table[...]
-    planes, odd, units = ownership(count)
-
-    def across(at, planes):
-        value = folded[pl.ds(at, planes)].reshape(planes * lines, cols)
-        both = jnp.concatenate(split(value), axis=1)
-        made = jnp.dot(both, side, preferred_element_type=jnp.float32)
-        return made.reshape(planes, lines, cols)
-
-    for owner, out in ((me, keep), (1 - me, send)):
-        made = across(owner * (planes + odd), planes)
-        for i in range(planes):
-            out[2 * i] = made[i, :, :half]
-            out[2 * i + 1] = made[i, :, half:]
+    def ready(a, b):
+        lax.fori_loop(a, b, one, 0)
+
+    base = (1 - me) * (planes + odd)
+
+    def plane_of(i):
+        return jnp.where(i == planes, planes, base + i) if odd else base + i
+
+    arrived = sum_windows(planes + odd, plane_of, start, weights, cube, folded, order, ready)
+    ready(arrived, chunks)
+    made = across(folded[...], table[...])
+    spread_out(made[:planes], send)
     if odd:
-        made = across(planes, 1)[0]
-        left, right = made[:, :half], made[:, half:]
-        keep[units - 1] = jnp.where(me == 0, left, right)
+        left, right = made[planes, :, :half], made[planes, :, half:]
+        middle[0] = jnp.where(me == 0, left, right)
         send[units - 1] = jnp.where(me == 0, right, left)
+
+
+def fold_own(start_in, wide, cube, table, middle, keep, start, weights, folded, order, sems):
+    planes, odd, units = ownership(wide.shape[0])
+    copies = [
+        pltpu.make_async_copy(start_in, start, sems.at[0]),
+        pltpu.make_async_copy(wide, weights, sems.at[1]),
+    ]
+    for copy in copies:
+        copy.start()
+    for copy in copies:
+        copy.wait()
+    base = lax.axis_index("band") * (planes + odd)
+    sum_windows(planes, lambda i: base + i, start, weights, cube, folded, order)
+    spread_out(across(folded[...], table[...]), keep)
+    if odd:
+        keep[units - 1] = middle[0]
 
 
 def coded_rows(count, lines):
@@ -455,26 +488,40 @@
         along_kernels,
         cube,
     )
-    keep, send, picked = call(
-        fold,
-        [pltpu.with_memory_space_constraint(x, pltpu.HBM) for x in inputs],
+    inputs = [pltpu.with_memory_space_constraint(x, pltpu.HBM) for x in inputs]
+    planes, odd, _ = ownership(count)
+    wide = shape(resp_values.shape, f32)
+    table = shape((2 * cols, cols), across_kernels.dtype)
+    send, middle, local, wide, table, picked = call(
+        fold_other,
+        inputs,
         [HBM] * len(inputs),
-        [part, part, shape(along_kernels.shape, along_kernels.dtype)],
+        [part, shape((1, lines, half), f32), cube, wide, table, along_kernels],
         scratch=[
             pltpu.SMEM(resp_start.shape, jnp.int32),
             pltpu.SMEM(across_offsets.shape, jnp.int32),
             pltpu.VMEM(resp_values.shape, resp_values.dtype),
-            pltpu.VMEM(resp_values.shape, f32),
             pltpu.SMEM(resp_values.shape, f32),
             pltpu.VMEM(across_kernels.shape, across_kernels.dtype),
             pltpu.SMEM(along_offsets.shape, jnp.int32),
             pltpu.VMEM(along_kernels.shape, along_kernels.dtype),
-            pltpu.VMEM(cube.shape, cube.dtype),
-            pltpu.VMEM((count, lines, cols), f32),
-            pltpu.VMEM((2 * cols, cols), across_kernels.dtype),
+            pltpu.VMEM((planes + odd, lines, cols), f32),
             pltpu.SMEM((count,), jnp.int32),
             pltpu.SemaphoreType.DMA((len(inputs),)),
             pltpu.SemaphoreType.DMA((-(-bands // resp_values.shape[1]),)),
+        ],
+    )
+    (keep,) = call(
+        fold_own,
+        (inputs[0], wide, local, table, middle),
+        [HBM] + [VMEM] * 4,
+        [part],
+        scratch=[
+            pltpu.SMEM(resp_start.shape, jnp.int32),
+            pltpu.SMEM(resp_values.shape, f32),
+            pltpu.VMEM((planes, lines, cols), f32),
+            pltpu.SMEM((count,), jnp.int32),
+            pltpu.SemaphoreType.DMA((2,)),
         ],
     )
     work = [pltpu.VMEM(part.shape, f32)]

time: 30.8 us -> 29.7 us (0.964)
  Pallas kernels: 9.03 us -> 11.8 us
  starting transfers between devices: 10 us -> 7.96 us
  waiting for transfers between devices: 11 us -> 9.04 us
    pallas_call x11 -> x12, Pallas kernels: 9.03 us -> 11.8 us  [call(): pl.pallas_call(kernel, in_specs=specs, out_specs=out_specs or [VMEM] * le...]
    ppermute x1, starting transfers between devices: 2.56 us -> 0.07 us  [on_device(): other = lax.ppermute(send, 'band', swap)]
    ppermute x1, waiting for transfers between devices: 2.01 us -> 0.01 us  [on_device(): other = lax.ppermute(send, 'band', swap)]
    ppermute x2, starting transfers between devices: 2.38 us -> 3 us  [on_device(): lax.ppermute(x, ('line', 'band'), cores(partner, odd_up))]
  transfers between devices with their start and end apart: 8 -> 8, of which waited for: 5 -> 4; matrix products, arithmetic and copies ran while one was open for 0% -> 0% of each run, Pallas kernels for 9% -> 17%
where the time goes in v8:
time: 29.7 us; the launch traced here: 29.6 us
  Pallas kernels  11.8 us (40%)
  waiting for transfers between devices  9.04 us (30%)
  starting transfers between devices  7.96 us (27%)
  between operations  0.77 us (3%)
    pallas_call x12, Pallas kernels, call(): pl.pallas_call(kernel, in_specs=specs, out_specs=out_specs or [VMEM] * le...  11.8 us
    ppermute x2, waiting for transfers between devices, on_device(): far.append(lax.ppermute(message, ('line', 'band'), cores(even_up, partner)))  5.06 us
    ppermute x2, starting transfers between devices, on_device(): far.append(lax.ppermute(message, ('line', 'band'), cores(even_up, partner)))  4.26 us
    ppermute x2, waiting for transfers between devices, on_device(): lax.ppermute(x, ('line', 'band'), cores(partner, odd_up))  3.58 us
    ppermute x2, starting transfers between devices, on_device(): lax.ppermute(x, ('line', 'band'), cores(partner, odd_up))  3 us
  transfers between devices with their start and end apart: 8, of which 4 were waited for; matrix products, arithmetic and copies ran while one was open for 0% of the time, Pallas kernels for 17%

profile of v8, /device:TPU:0, one launch (start us, length us, event | category | flops | bytes accessed | tf_op | source)
XLA Modules:
  0.0 29.6 jit_solution(1797406622039167663)
XLA Ops:
  0.6 5.0 %fold_other.1 = (f32[13,128,128]{2,1,0:T(8,128)S(1)}, f32[1,128,128]{2,1,0:T(8,128)S(1)}, bf16[115,128,256]{2,1,0:T(8,128)(2,1)S(1)}, f32[13,20]{1,0:T(8,128)S(1...) custom-call(s32[13]{0:T(128)} %start_in.3, s32[3]{0:T(128)} %offsets_in.1, bf16[13,20]{1,0:T(8,128)(2,1)} %values_in.1, ...), custom_call_target="tpu_custom_call" | custom-call | tf_op jit(solution)/shard_map/fold_other/pallas_call | solution.py:36
  5.6 0.1 collective-permute-start
  5.7 0.0 copy-start
  5.7 2.4 %fold_own.1.keep = f32[13,128,128]{2,1,0:T(8,128)S(1)} custom-call(s32[13]{0:T(128)} %start_in.3, f32[13,20]{1,0:T(8,128)S(1)} %get-tuple-element.21.wide, bf16[115,128,256]{2,1,0:T(8,128)(2,1)S(1)} %get-tuple-element.22.cube, bf16[512,256]{1,0:T(8,128)(2,1)S(1)} %get-tuple-element.23.table, f32[1,128,128]{2,1,0:T(8,128)S(1)} %get-tuple-element.24.middle), custom_call_target="tpu_custom_call" | custom-call | tf_op jit(solution)/shard_map/fold_own/pallas_call | solution.py:36
  8.1 0.0 collective-permute-done.other
  8.2 0.4 %share.1 = (f32[13,128,128]{2,1,0:T(8,128)S(1)}, s16[912,128]{1,0:T(8,128)(2,1)S(1)}, s16[784,128]{1,0:T(8,128)(2,1)S(1)}) custom-call(bf16[3,128,128]{2,1,0:T(8,128)(2,1)S(1)} %get-tuple-element.20.picked, f32[13,128,128]{2,1,0:T(8,128)S(1)} %fold_own.1.keep, f32[13,128,128]{2,1,0:T(8,128)S(1)} %collective-permute-done.other), custom_call_target="tpu_custom_call" | custom-call | tf_op jit(solution)/shard_map/share/pallas_call | solution.py:36
  8.5 0.5 %collective-permute-start.1 = (f32[13,128,128]{2,1,0:T(8,128)S(1)}, f32[13,128,128]{2,1,0:T(8,128)S(1)}, u32[]{:S(2)}, u32[]{:S(2)}) collective-permute-start(f32[13,128,128]{2,1,0:T(8,128)S(1)} %get-tuple-element.26.total), channel_id=1, source_target_pairs={{0,1},{1,0},{2,3},{3,2},{4,5},{5,4},{6,7},{7,6},{8,9},{9,8},{10,11... | collective-permute-start | bytes 2555912 | tf_op jit(solution)/shard_map/ppermute | solution.py:537
  9.0 3.0 %collective-permute-start.2 = (s16[912,128]{1,0:T(8,128)(2,1)S(1)}, s16[912,128]{1,0:T(8,128)(2,1)S(1)}, u32[]{:S(2)}, u32[]{:S(2)}) collective-permute-start(s16[912,128]{1,0:T(8,128)(2,1)S(1)} %get-tuple-element.29), channel_id=1, source_target_pairs={{0,2},{2,0},{4,6},{6,4},{8,10},{10,8},{12,14},{14,12},{5,1},{15,3}... | collective-permute-start | bytes 700424 | tf_op jit(solution)/shard_map/ppermute | solution.py:536
  12.0 0.0 collective-permute-start.5
  12.0 0.0 collective-permute-done.1.other_total
  12.0 0.4 %centre.1 = (f32[13,128,128]{2,1,0:T(8,128)S(1)}, f32[13,128,128]{2,1,0:T(8,128)S(1)}, f32[13,128,128]{2,1,0:T(8,128)S(1)}) custom-call(bf16[3,128,128]{2,1,0:T(8,128)(2,1)S(1)} %get-tuple-element.20.picked, f32[13,128,128]{2,1,0:T(8,128)S(1)} %get-tuple-element.26.total, f32[13,128,128]{2,1,0:T(8,128)S(1)} %collective-permute-done.1.other_total), custom_call_target="tpu_custom_call" | custom-call | tf_op jit(solution)/shard_map/centre/pallas_call | solution.py:36
  12.4 3.6 %collective-permute-done.2.received.near = s16[912,128]{1,0:T(8,128)(2,1)S(1)} collective-permute-done((s16[912,128]{1,0:T(8,128)(2,1)S(1)}, s16[912,128]{1,0:T(8,128)(2,1)S(1)}, u32[]{:S(2)}, u32[]{:S(2)}) %collective-permute-start.2) | collective-permute-done | bytes 233504 | tf_op jit(solution)/shard_map/ppermute | solution.py:536
  16.0 2.1 %collective-permute-start.3 = (s16[912,128]{1,0:T(8,128)(2,1)S(1)}, s16[912,128]{1,0:T(8,128)(2,1)S(1)}, u32[]{:S(2)}, u32[]{:S(2)}) collective-permute-start(s16[912,128]{1,0:T(8,128)(2,1)S(1)} %relay.2), channel_id=1, source_target_pairs={{0,4},{2,14},{4,8},{6,2},{8,12},{10,6},{12,0},{14,10},{1,3},{3,1},... | collective-permute-start | bytes 700424 | tf_op jit(solution)/shard_map/ppermute | solution.py:547
  18.2 0.0 collective-permute-done.5.received.near
  18.2 2.1 %collective-permute-start.6 = (s16[784,128]{1,0:T(8,128)(2,1)S(1)}, s16[784,128]{1,0:T(8,128)(2,1)S(1)}, u32[]{:S(2)}, u32[]{:S(2)}) collective-permute-start(s16[784,128]{1,0:T(8,128)(2,1)S(1)} %relay.3), channel_id=1, source_target_pairs={{0,4},{2,14},{4,8},{6,2},{8,12},{10,6},{12,0},{14,10},{1,3},{3,1},... | collective-permute-start | bytes 602120 | tf_op jit(solution)/shard_map/ppermute | solution.py:547
  20.3 0.3 beside.2.product
  20.6 3.6 %collective-permute-done.3.received = s16[912,128]{1,0:T(8,128)(2,1)S(1)} collective-permute-done((s16[912,128]{1,0:T(8,128)(2,1)S(1)}, s16[912,128]{1,0:T(8,128)(2,1)S(1)}, u32[]{:S(2)}, u32[]{:S(2)}) %collective-permute-start.3) | collective-permute-done | bytes 233504 | tf_op jit(solution)/shard_map/ppermute | solution.py:547
  24.3 0.4 %settle.2.rest_0_ = s16[912,128]{1,0:T(8,128)(2,1)S(1)} custom-call(bf16[3,128,128]{2,1,0:T(8,128)(2,1)S(1)} %get-tuple-element.20.picked, f32[7,128,128]{2,1,0:T(8,128)S(1)} %beside.2.product, s16[912,128]{1,0:T(8,128)(2,1)S(1)} %collective-permute-done.3.received), custom_call_target="tpu_custom_call" | custom-call | tf_op jit(solution)/shard_map/settle/pallas_call | solution.py:36
  24.6 0.1 collective-permute-start.4
  24.7 0.2 beside.3.product
  25.0 1.4 %collective-permute-done.6.received = s16[784,128]{1,0:T(8,128)(2,1)S(1)} collective-permute-done((s16[784,128]{1,0:T(8,128)(2,1)S(1)}, s16[784,128]{1,0:T(8,128)(2,1)S(1)}, u32[]{:S(2)}, u32[]{:S(2)}) %collective-permute-start.6) | collective-permute-done | bytes 200736 | tf_op jit(solution)/shard_map/ppermute | solution.py:547
  26.4 0.4 %settle.3.rest_1_ = s16[784,128]{1,0:T(8,128)(2,1)S(1)} custom-call(bf16[3,128,128]{2,1,0:T(8,128)(2,1)S(1)} %get-tuple-element.20.picked, f32[6,128,128]{2,1,0:T(8,128)S(1)} %beside.3.product, s16[784,128]{1,0:T(8,128)(2,1)S(1)} %collective-permute-done.6.received), custom_call_target="tpu_custom_call" | custom-call | tf_op jit(solution)/shard_map/settle/pallas_call | solution.py:36
  26.8 0.1 collective-permute-start.7
  26.8 0.0 copy-done
  26.9 1.0 %finish.2 = (f32[13,128,256]{2,1,0:T(8,128)}, f32[3,128,256]{2,1,0:T(8,128)S(1)}) custom-call(bf16[13,128,256]{2,1,0:T(8,128)(2,1)S(1)} %copy-done, f32[13,128,128]{2,1,0:T(8,128)S(1)} %get-tuple-element.35.base, s16[912,128]{1,0:T(8,128)(2,1)S(1)} %settle.2.rest_0_, s16[784,128]{1,0:T(8,128)(2,1)S(1)} %settle.3.rest_1_), custom_call_target="tpu_custom_call" | custom-call | tf_op jit(solution)/shard_map/finish/pallas_call | solution.py:36
  27.9 0.4 %collective-permute-done.7.rest_1_ = s16[784,128]{1,0:T(8,128)(2,1)S(1)} collective-permute-done((s16[784,128]{1,0:T(8,128)(2,1)S(1)}, s16[784,128]{1,0:T(8,128)(2,1)S(1)}, u32[]{:S(2)}, u32[]{:S(2)}) %collective-permute-start.7) | collective-permute-done | bytes 200736 | tf_op jit(solution)/shard_map/ppermute | solution.py:565
  28.3 0.0 collective-permute-done.4.rest_0_
  28.3 1.3 %finish.3 = (f32[13,128,256]{2,1,0:T(8,128)}, f32[128,256]{1,0:T(8,128)}) custom-call(bf16[13,128,256]{2,1,0:T(8,128)(2,1)S(1)} %copy-done, f32[13,128,128]{2,1,0:T(8,128)S(1)} %get-tuple-element.27.base, s16[912,128]{1,0:T(8,128)(2,1)S(1)} %collective-permute-done.4.rest_0_, ...), custom_call_target="tpu_custom_call", output_to_operand_aliasing={{0}: (5, {})} | custom-call | tf_op jit(solution)/shard_map/finish/pallas_call | solution.py:36
  (2 shorter events, 0.0 us)
Async XLA Ops:
  5.6 2.5 %collective-permute-start = (f32[13,128,128]{2,1,0:T(8,128)S(1)}, f32[13,128,128]{2,1,0:T(8,128)S(1)}, u32[]{:S(2)}, u32[]{:S(2)}) collective-permute-start(f32[13,128,128]{2,1,0:T(8,128)S(1)} %get-tuple-element.25), channel_id=1, source_target_pairs={{0,1},{1,0},{2,3},{3,2},{4,5},{5,4},{6,7},{7,6},{8,9},{9,8},{10,11... | collective-permute-start | bytes 2555912 | tf_op jit(solution)/shard_map/ppermute | solution.py:528
  5.7 21.1 %copy-start = (bf16[13,128,256]{2,1,0:T(8,128)(2,1)S(1)}, bf16[13,128,256]{2,1,0:T(8,128)(2,1)}, u32[]{:S(2)}) copy-start(bf16[13,128,256]{2,1,0:T(8,128)(2,1)} %observed.3) | copy-start | bytes 2555908
  8.5 3.5 %collective-permute-start.1 = (f32[13,128,128]{2,1,0:T(8,128)S(1)}, f32[13,128,128]{2,1,0:T(8,128)S(1)}, u32[]{:S(2)}, u32[]{:S(2)}) collective-permute-start(f32[13,128,128]{2,1,0:T(8,128)S(1)} %get-tuple-element.26.total), channel_id=1, source_target_pairs={{0,1},{1,0},{2,3},{3,2},{4,5},{5,4},{6,7},{7,6},{8,9},{9,8},{10,11... | collective-permute-start | bytes 2555912 | tf_op jit(solution)/shard_map/ppermute | solution.py:537
  9.0 7.0 %collective-permute-start.2 = (s16[912,128]{1,0:T(8,128)(2,1)S(1)}, s16[912,128]{1,0:T(8,128)(2,1)S(1)}, u32[]{:S(2)}, u32[]{:S(2)}) collective-permute-start(s16[912,128]{1,0:T(8,128)(2,1)S(1)} %get-tuple-element.29), channel_id=1, source_target_pairs={{0,2},{2,0},{4,6},{6,4},{8,10},{10,8},{12,14},{14,12},{5,1},{15,3}... | collective-permute-start | bytes 700424 | tf_op jit(solution)/shard_map/ppermute | solution.py:536
  12.0 6.2 %collective-permute-start.5 = (s16[784,128]{1,0:T(8,128)(2,1)S(1)}, s16[784,128]{1,0:T(8,128)(2,1)S(1)}, u32[]{:S(2)}, u32[]{:S(2)}) collective-permute-start(s16[784,128]{1,0:T(8,128)(2,1)S(1)} %get-tuple-element.32), channel_id=1, source_target_pairs={{0,2},{2,0},{4,6},{6,4},{8,10},{10,8},{12,14},{14,12},{5,1},{15,3}... | collective-permute-start | bytes 602120 | tf_op jit(solution)/shard_map/ppermute | solution.py:536
  16.0 8.2 %collective-permute-start.3 = (s16[912,128]{1,0:T(8,128)(2,1)S(1)}, s16[912,128]{1,0:T(8,128)(2,1)S(1)}, u32[]{:S(2)}, u32[]{:S(2)}) collective-permute-start(s16[912,128]{1,0:T(8,128)(2,1)S(1)} %relay.2), channel_id=1, source_target_pairs={{0,4},{2,14},{4,8},{6,2},{8,12},{10,6},{12,0},{14,10},{1,3},{3,1},... | collective-permute-start | bytes 700424 | tf_op jit(solution)/shard_map/ppermute | solution.py:547
  18.2 8.2 %collective-permute-start.6 = (s16[784,128]{1,0:T(8,128)(2,1)S(1)}, s16[784,128]{1,0:T(8,128)(2,1)S(1)}, u32[]{:S(2)}, u32[]{:S(2)}) collective-permute-start(s16[784,128]{1,0:T(8,128)(2,1)S(1)} %relay.3), channel_id=1, source_target_pairs={{0,4},{2,14},{4,8},{6,2},{8,12},{10,6},{12,0},{14,10},{1,3},{3,1},... | collective-permute-start | bytes 602120 | tf_op jit(solution)/shard_map/ppermute | solution.py:547
  24.6 3.6 %collective-permute-start.4 = (s16[912,128]{1,0:T(8,128)(2,1)S(1)}, s16[912,128]{1,0:T(8,128)(2,1)S(1)}, u32[]{:S(2)}, u32[]{:S(2)}) collective-permute-start(s16[912,128]{1,0:T(8,128)(2,1)S(1)} %settle.2.rest_0_), channel_id=1, source_target_pairs={{0,1},{1,0},{2,3},{3,2},{4,5},{5,4},{6,7},{7,6},{8,9},{9,8},{10,11... | collective-permute-start | bytes 700424 | tf_op jit(solution)/shard_map/ppermute | solution.py:565
  26.8 1.5 %collective-permute-start.7 = (s16[784,128]{1,0:T(8,128)(2,1)S(1)}, s16[784,128]{1,0:T(8,128)(2,1)S(1)}, u32[]{:S(2)}, u32[]{:S(2)}) collective-permute-start(s16[784,128]{1,0:T(8,128)(2,1)S(1)} %settle.3.rest_1_), channel_id=1, source_target_pairs={{0,1},{1,0},{2,3},{3,2},{4,5},{5,4},{6,7},{7,6},{8,9},{9,8},{10,11... | collective-permute-start | bytes 602120 | tf_op jit(solution)/shard_map/ppermute | solution.py:565

commit v9 on v8

--- a/solution.py
+++ b/solution.py
@@ -30,6 +30,7 @@
 VMEM = pl.BlockSpec(memory_space=pltpu.VMEM)
 HBM = pl.BlockSpec(memory_space=pltpu.HBM)
 ROWS = 64
+CHUNKS = 3
 
 
 def call(kernel, inputs, specs, outs, scratch=(), out_specs=None, aliases=None):
@@ -398,56 +399,89 @@
     return jnp.where(big, outer, inner)
 
 
-def finish(second, spans, observed, base, *rest):
-    messages, rest = rest[: len(spans)], rest[len(spans) :]
-    if second:
-        sums, _, image, angles, angle, value, sems = rest
-    else:
-        image, sums, value, sems = rest
+def finish_units(core, parts, observed, base, value, image, sem, sums):
+    _, lines, half = base.shape
+    copies = []
+    for span, message in parts:
+        plane = decode(message, span, lines)
+        for n in range(*span):
+            m, c = units_of(core, observed.shape[0])[n]
+            at = slice(c * half, (c + 1) * half)
+            made = base[n] + plane(n - span[0])
+            value[n] = made
+            copies.append(pltpu.make_async_copy(value.at[n], image.at[m, :, at], sem(n)))
+            copies[-1].start()
+            seen = observed[m, :, at].astype(jnp.float32)
+            sums[c] = (sums[c][0] + made * seen, sums[c][1] + made * made)
+    return copies
+
+
+def finish_most(spans, observed, base, other_base, *rest):
+    chunks = len(spans)
+    messages, others, rest = rest[:chunks], rest[chunks : 2 * chunks - 1], rest[2 * chunks - 1 :]
+    image, own, theirs, value, other_value, sems = rest
     units, lines, half = base.shape
-    count = observed.shape[0]
+    zero = jnp.zeros((lines, half), jnp.float32)
 
     def work(core):
-        places = [(m, slice(c * half, (c + 1) * half)) for m, c in units_of(core, count)]
-        copies = [
-            pltpu.make_async_copy(value.at[n], image.at[m, :, at], sems.at[n])
-            for n, (m, at) in enumerate(places)
-        ]
-        for span, message in zip(spans, messages):
-            plane = decode(message, span, lines)
-            for n in range(*span):
-                value[n] = base[n] + plane(n - span[0])
-                copies[n].start()
+        sums, other_sums = [(zero, zero)] * 2, [(zero, zero)] * 2
+        parts = list(zip(spans, messages))
+        copies = finish_units(
+            core, parts, observed, base, value, image, lambda n: sems.at[n], sums
+        )
+        parts = list(zip(spans[:-1], others))
+        copies += finish_units(
+            1 - core,
+            parts,
+            observed,
+            other_base,
+            other_value,
+            image,
+            lambda n: sems.at[units + n],
+            other_sums,
+        )
         for c in range(2):
             at = slice(c * half, (c + 1) * half)
-            inner = jnp.zeros((lines, half), jnp.float32)
-            left = jnp.zeros((lines, half), jnp.float32)
-            for n, (m, where) in enumerate(places):
-                if where == at:
-                    inner = inner + value[n] * observed[m, :, at].astype(jnp.float32)
-                    left = left + value[n] * value[n]
-            if second:
-                bound = jnp.sqrt(left + sums[1, :, at]) * sums[2, :, at]
-                ratio = (inner + sums[0, :, at]) / jnp.maximum(bound, 1.0)
-                angle[:, at] = arccos(jnp.clip(ratio, -1.0, 1.0))
-            else:
-                right = jnp.zeros((lines, half), jnp.float32)
-                for m in range(count):
-                    seen = observed[m, :, at].astype(jnp.float32)
-                    right = right + seen * seen
-                sums[0, :, at] = inner
-                sums[1, :, at] = left
-                sums[2, :, at] = jnp.sqrt(right)
-        if second:
-            copies.append(pltpu.make_async_copy(angle, angles, sems.at[units]))
-            copies[-1].start()
+            right = zero
+            for m in range(observed.shape[0]):
+                seen = observed[m, :, at].astype(jnp.float32)
+                right = right + seen * seen
+            own[0, :, at], own[1, :, at] = sums[c]
+            own[2, :, at] = jnp.sqrt(right)
+            theirs[0, :, at], theirs[1, :, at] = other_sums[c]
         for copy in copies:
             copy.wait()
 
-    if second:
-        by_core(lambda: work(1), lambda: work(0))
-    else:
-        by_core(lambda: work(0), lambda: work(1))
+    by_core(lambda: work(0), lambda: work(1))
+
+
+def finish_last(span, observed, other_base, message, own, theirs, _, *rest):
+    image, angles, angle, value, sems = rest
+    units, lines, half = other_base.shape
+
+    def work(core):
+        columns = [slice(c * half, (c + 1) * half) for c in range(2)]
+        sums = [(theirs[0, :, at], theirs[1, :, at]) for at in columns]
+        copies = finish_units(
+            core,
+            [(span, message)],
+            observed,
+            other_base,
+            value,
+            image,
+            lambda n: sems.at[n],
+            sums,
+        )
+        for (inner, left), at in zip(sums, columns):
+            bound = jnp.sqrt(left + own[1, :, at]) * own[2, :, at]
+            ratio = (inner + own[0, :, at]) / jnp.maximum(bound, 1.0)
+            angle[:, at] = arccos(jnp.clip(ratio, -1.0, 1.0))
+        copies.append(pltpu.make_async_copy(angle, angles, sems.at[units]))
+        copies[-1].start()
+        for copy in copies:
+            copy.wait()
+
+    by_core(lambda: work(1), lambda: work(0))
 
 
 def on_device(
@@ -476,7 +510,8 @@
         return [(2 * a, 2 * b) for a, b in zero] + [(2 * a + 1, 2 * b + 1) for a, b in one]
 
     part = shape((units, lines, half), f32)
-    spans = [(0, (units + 1) // 2), ((units + 1) // 2, units)]
+    edges = [-(-units * i // CHUNKS) for i in range(CHUNKS + 1)]
+    spans = list(zip(edges[:-1], edges[1:]))
     coded = [shape((coded_rows(b - a, lines), half), i16) for a, b in spans]
 
     inputs = (
@@ -564,23 +599,24 @@
         )
         others.append(lax.ppermute(messages[i], "band", swap))
     image = shape((count, lines, cols), f32)
-    some = 2 + len(spans)
-    image, sums = call(
-        functools.partial(finish, False, spans),
-        (observed, base, *messages),
-        [VMEM] * some,
-        [image, shape((3, lines, cols), f32)],
-        scratch=work + [pltpu.SemaphoreType.DMA((units,))],
-        out_specs=[HBM, VMEM],
+    three = shape((3, lines, cols), f32)
+    inputs = [observed, base, other_base, *messages, *others[:-1]]
+    image, own, theirs = call(
+        functools.partial(finish_most, spans),
+        inputs,
+        [VMEM] * len(inputs),
+        [image, three, three],
+        scratch=work * 2 + [pltpu.SemaphoreType.DMA((2 * units,))],
+        out_specs=[HBM, VMEM, VMEM],
     )
     image, angles = call(
-        functools.partial(finish, True, spans),
-        (observed, other_base, *others, sums, image),
-        [VMEM] * (some + 1) + [HBM],
+        functools.partial(finish_last, spans[-1]),
+        (observed, other_base, others[-1], own, theirs, image),
+        [VMEM] * 5 + [HBM],
         [image, shape((lines, cols), f32)],
         scratch=[pltpu.VMEM((lines, cols), f32), *work, pltpu.SemaphoreType.DMA((units + 1,))],
         out_specs=[HBM] * 2,
-        aliases={some + 1: 0},
+        aliases={5: 0},
     )
     return image, angles
 

time: 29.7 us -> 28.9 us (0.973)
  waiting for transfers between devices: 9.04 us -> 4.24 us
  starting transfers between devices: 7.96 us -> 11.6 us
  Pallas kernels: 11.8 us -> 12.1 us
    ppermute x2 -> x3, waiting for transfers between devices: 3.58 us -> 0.89 us  [on_device(): lax.ppermute(x, ('line', 'band'), cores(partner, odd_up))]
    ppermute x2 -> x3, starting transfers between devices: 3 us -> 4.99 us  [on_device(): lax.ppermute(x, ('line', 'band'), cores(partner, odd_up))]
    ppermute x2 -> x3, waiting for transfers between devices: 5.06 us -> 3.34 us  [on_device(): far.append(lax.ppermute(message, ('line', 'band'), cores(even_up, partner)))]
    ppermute x2 -> x3, starting transfers between devices: 4.26 us -> 5.78 us  [on_device(): far.append(lax.ppermute(message, ('line', 'band'), cores(even_up, partner)))]
    ppermute x2 -> x3, waiting for transfers between devices: 0.39 us -> 0.01 us  [on_device(): others.append(lax.ppermute(messages[i], 'band', swap))]
    pallas_call x12 -> x15, Pallas kernels: 11.8 us -> 12.1 us  [call(): pl.pallas_call(kernel, in_specs=specs, out_specs=out_specs or [VMEM] * le...]
  transfers between devices with their start and end apart: 8 -> 11, of which waited for: 4 -> 4; matrix products, arithmetic and copies ran while one was open for 0% -> 0% of each run, Pallas kernels for 17% -> 21%
where the time goes in v9:
time: 28.9 us; the launch traced here: 28.8 us
  Pallas kernels  12.1 us (42%)
  starting transfers between devices  11.6 us (40%)
  waiting for transfers between devices  4.24 us (15%)
  between operations  0.83 us (3%)
    pallas_call x15, Pallas kernels, call(): pl.pallas_call(kernel, in_specs=specs, out_specs=out_specs or [VMEM] * le...  12.1 us
    ppermute x3, starting transfers between devices, on_device(): far.append(lax.ppermute(message, ('line', 'band'), cores(even_up, partner)))  5.78 us
    ppermute x3, starting transfers between devices, on_device(): lax.ppermute(x, ('line', 'band'), cores(partner, odd_up))  4.99 us
    ppermute x3, waiting for transfers between devices, on_device(): far.append(lax.ppermute(message, ('line', 'band'), cores(even_up, partner)))  3.34 us
    ppermute x3, waiting for transfers between devices, on_device(): lax.ppermute(x, ('line', 'band'), cores(partner, odd_up))  0.89 us
  transfers between devices with their start and end apart: 11, of which 4 were waited for; matrix products, arithmetic and copies ran while one was open for 0% of the time, Pallas kernels for 21%

profile of v9, /device:TPU:0, one launch (start us, length us, event | category | flops | bytes accessed | tf_op | source)
XLA Modules:
  0.0 28.8 jit_solution(1020451710514725012)
XLA Ops:
  0.6 4.6 %fold_other.1 = (f32[13,128,128]{2,1,0:T(8,128)S(1)}, f32[1,128,128]{2,1,0:T(8,128)S(1)}, bf16[115,128,256]{2,1,0:T(8,128)(2,1)S(1)}, f32[13,20]{1,0:T(8,128)S(1...) custom-call(s32[13]{0:T(128)} %start_in.3, s32[3]{0:T(128)} %offsets_in.1, bf16[13,20]{1,0:T(8,128)(2,1)} %values_in.1, ...), custom_call_target="tpu_custom_call" | custom-call | tf_op jit(solution)/shard_map/fold_other/pallas_call | solution.py:37
  5.2 0.1 collective-permute-start
  5.3 0.0 copy-start
  5.3 2.7 %fold_own.1.keep = f32[13,128,128]{2,1,0:T(8,128)S(1)} custom-call(s32[13]{0:T(128)} %start_in.3, f32[13,20]{1,0:T(8,128)S(1)} %get-tuple-element.25.wide, bf16[115,128,256]{2,1,0:T(8,128)(2,1)S(1)} %get-tuple-element.26.cube, bf16[512,256]{1,0:T(8,128)(2,1)S(1)} %get-tuple-element.27.table, f32[1,128,128]{2,1,0:T(8,128)S(1)} %get-tuple-element.28.middle), custom_call_target="tpu_custom_call" | custom-call | tf_op jit(solution)/shard_map/fold_own/pallas_call | solution.py:37
  8.0 0.0 collective-permute-done.other
  8.0 0.4 %share.1 = (f32[13,128,128]{2,1,0:T(8,128)S(1)}, s16[656,128]{1,0:T(8,128)(2,1)S(1)}, s16[528,128]{1,0:T(8,128)(2,1)S(1)}, s16[528,128]{1,0:T(8,128)(2,1)S(1)}) custom-call(bf16[3,128,128]{2,1,0:T(8,128)(2,1)S(1)} %get-tuple-element.24.picked, f32[13,128,128]{2,1,0:T(8,128)S(1)} %fold_own.1.keep, f32[13,128,128]{2,1,0:T(8,128)S(1)} %collective-permute-done.other), custom_call_target="tpu_custom_call" | custom-call | tf_op jit(solution)/shard_map/share/pallas_call | solution.py:37
  8.4 0.5 %collective-permute-start.1 = (f32[13,128,128]{2,1,0:T(8,128)S(1)}, f32[13,128,128]{2,1,0:T(8,128)S(1)}, u32[]{:S(2)}, u32[]{:S(2)}) collective-permute-start(f32[13,128,128]{2,1,0:T(8,128)S(1)} %get-tuple-element.30.total), channel_id=1, source_target_pairs={{0,1},{1,0},{2,3},{3,2},{4,5},{5,4},{6,7},{7,6},{8,9},{9,8},{10,11... | collective-permute-start | bytes 2555912 | tf_op jit(solution)/shard_map/ppermute | solution.py:572
  8.9 3.0 %collective-permute-start.5 = (s16[656,128]{1,0:T(8,128)(2,1)S(1)}, s16[656,128]{1,0:T(8,128)(2,1)S(1)}, u32[]{:S(2)}, u32[]{:S(2)}) collective-permute-start(s16[656,128]{1,0:T(8,128)(2,1)S(1)} %get-tuple-element.37), channel_id=1, source_target_pairs={{0,2},{2,0},{4,6},{6,4},{8,10},{10,8},{12,14},{14,12},{5,1},{15,3}... | collective-permute-start | bytes 503816 | tf_op jit(solution)/shard_map/ppermute | solution.py:571
  11.9 0.0 collective-permute-start.7
  11.9 2.0 %collective-permute-start.2 = (s16[528,128]{1,0:T(8,128)(2,1)S(1)}, s16[528,128]{1,0:T(8,128)(2,1)S(1)}, u32[]{:S(2)}, u32[]{:S(2)}) collective-permute-start(s16[528,128]{1,0:T(8,128)(2,1)S(1)} %get-tuple-element.33), channel_id=1, source_target_pairs={{0,2},{2,0},{4,6},{6,4},{8,10},{10,8},{12,14},{14,12},{5,1},{15,3}... | collective-permute-start | bytes 405512 | tf_op jit(solution)/shard_map/ppermute | solution.py:571
  13.9 0.0 collective-permute-done.1.other_total
  13.9 0.4 %centre.1 = (f32[13,128,128]{2,1,0:T(8,128)S(1)}, f32[13,128,128]{2,1,0:T(8,128)S(1)}, f32[13,128,128]{2,1,0:T(8,128)S(1)}) custom-call(bf16[3,128,128]{2,1,0:T(8,128)(2,1)S(1)} %get-tuple-element.24.picked, f32[13,128,128]{2,1,0:T(8,128)S(1)} %get-tuple-element.30.total, f32[13,128,128]{2,1,0:T(8,128)S(1)} %collective-permute-done.1.other_total), custom_call_target="tpu_custom_call" | custom-call | tf_op jit(solution)/shard_map/centre/pallas_call | solution.py:37
  14.3 0.9 %collective-permute-done.5.received.near = s16[656,128]{1,0:T(8,128)(2,1)S(1)} collective-permute-done((s16[656,128]{1,0:T(8,128)(2,1)S(1)}, s16[656,128]{1,0:T(8,128)(2,1)S(1)}, u32[]{:S(2)}, u32[]{:S(2)}) %collective-permute-start.5) | collective-permute-done | bytes 167968 | tf_op jit(solution)/shard_map/ppermute | solution.py:571
  15.2 2.1 %collective-permute-start.6 = (s16[656,128]{1,0:T(8,128)(2,1)S(1)}, s16[656,128]{1,0:T(8,128)(2,1)S(1)}, u32[]{:S(2)}, u32[]{:S(2)}) collective-permute-start(s16[656,128]{1,0:T(8,128)(2,1)S(1)} %relay.4), channel_id=1, source_target_pairs={{0,4},{2,14},{4,8},{6,2},{8,12},{10,6},{12,0},{14,10},{1,3},{3,1},... | collective-permute-start | bytes 503816 | tf_op jit(solution)/shard_map/ppermute | solution.py:582
  17.3 0.0 collective-permute-done.7.received.near
  17.4 1.6 %collective-permute-start.8 = (s16[528,128]{1,0:T(8,128)(2,1)S(1)}, s16[528,128]{1,0:T(8,128)(2,1)S(1)}, u32[]{:S(2)}, u32[]{:S(2)}) collective-permute-start(s16[528,128]{1,0:T(8,128)(2,1)S(1)} %relay.5), channel_id=1, source_target_pairs={{0,4},{2,14},{4,8},{6,2},{8,12},{10,6},{12,0},{14,10},{1,3},{3,1},... | collective-permute-start | bytes 405512 | tf_op jit(solution)/shard_map/ppermute | solution.py:582
  19.0 2.0 %collective-permute-start.3 = (s16[528,128]{1,0:T(8,128)(2,1)S(1)}, s16[528,128]{1,0:T(8,128)(2,1)S(1)}, u32[]{:S(2)}, u32[]{:S(2)}) collective-permute-start(s16[528,128]{1,0:T(8,128)(2,1)S(1)} %relay.3), channel_id=1, source_target_pairs={{0,4},{2,14},{4,8},{6,2},{8,12},{10,6},{12,0},{14,10},{1,3},{3,1},... | collective-permute-start | bytes 405512 | tf_op jit(solution)/shard_map/ppermute | solution.py:582
  21.0 0.2 beside.4.product
  21.3 1.4 %collective-permute-done.6.received = s16[656,128]{1,0:T(8,128)(2,1)S(1)} collective-permute-done((s16[656,128]{1,0:T(8,128)(2,1)S(1)}, s16[656,128]{1,0:T(8,128)(2,1)S(1)}, u32[]{:S(2)}, u32[]{:S(2)}) %collective-permute-start.6) | collective-permute-done | bytes 167968 | tf_op jit(solution)/shard_map/ppermute | solution.py:582
  22.7 0.3 %settle.4.rest_0_ = s16[656,128]{1,0:T(8,128)(2,1)S(1)} custom-call(bf16[3,128,128]{2,1,0:T(8,128)(2,1)S(1)} %get-tuple-element.24.picked, f32[5,128,128]{2,1,0:T(8,128)S(1)} %beside.4.product, s16[656,128]{1,0:T(8,128)(2,1)S(1)} %collective-permute-done.6.received), custom_call_target="tpu_custom_call" | custom-call | tf_op jit(solution)/shard_map/settle/pallas_call | solution.py:37
  23.1 0.1 collective-permute-start.9
  23.1 0.2 beside.5.product
  23.4 0.9 %collective-permute-done.8.received = s16[528,128]{1,0:T(8,128)(2,1)S(1)} collective-permute-done((s16[528,128]{1,0:T(8,128)(2,1)S(1)}, s16[528,128]{1,0:T(8,128)(2,1)S(1)}, u32[]{:S(2)}, u32[]{:S(2)}) %collective-permute-start.8) | collective-permute-done | bytes 135200 | tf_op jit(solution)/shard_map/ppermute | solution.py:582
  24.2 0.3 %settle.5.rest_1_ = s16[528,128]{1,0:T(8,128)(2,1)S(1)} custom-call(bf16[3,128,128]{2,1,0:T(8,128)(2,1)S(1)} %get-tuple-element.24.picked, f32[4,128,128]{2,1,0:T(8,128)S(1)} %beside.5.product, s16[528,128]{1,0:T(8,128)(2,1)S(1)} %collective-permute-done.8.received), custom_call_target="tpu_custom_call" | custom-call | tf_op jit(solution)/shard_map/settle/pallas_call | solution.py:37
  24.5 0.1 collective-permute-start.10
  24.6 0.2 beside.3.product
  24.8 1.0 %collective-permute-done.3.received = s16[528,128]{1,0:T(8,128)(2,1)S(1)} collective-permute-done((s16[528,128]{1,0:T(8,128)(2,1)S(1)}, s16[528,128]{1,0:T(8,128)(2,1)S(1)}, u32[]{:S(2)}, u32[]{:S(2)}) %collective-permute-start.3) | collective-permute-done | bytes 135200 | tf_op jit(solution)/shard_map/ppermute | solution.py:582
  25.9 0.3 %settle.3.rest_2_ = s16[528,128]{1,0:T(8,128)(2,1)S(1)} custom-call(bf16[3,128,128]{2,1,0:T(8,128)(2,1)S(1)} %get-tuple-element.24.picked, f32[4,128,128]{2,1,0:T(8,128)S(1)} %beside.3.product, s16[528,128]{1,0:T(8,128)(2,1)S(1)} %collective-permute-done.3.received), custom_call_target="tpu_custom_call" | custom-call | tf_op jit(solution)/shard_map/settle/pallas_call | solution.py:37
  26.2 0.1 collective-permute-start.4
  26.3 0.0 collective-permute-done.9.rest_3_
  26.3 1.3 %finish_most.1 = (f32[13,128,256]{2,1,0:T(8,128)}, f32[3,128,256]{2,1,0:T(8,128)S(1)}, f32[3,128,256]{2,1,0:T(8,128)S(1)}) custom-call(bf16[13,128,256]{2,1,0:T(8,128)(2,1)S(1)} %copy-done, f32[13,128,128]{2,1,0:T(8,128)S(1)} %get-tuple-element.36.base, f32[13,128,128]{2,1,0:T(8,128)S(1)} %get-tuple-element.31.other_base, ...), custom_call_target="tpu_custom_call" | custom-call | tf_op jit(solution)/shard_map/finish_most/pallas_call | solution.py:37
  27.7 1.1 %finish_last.1 = (f32[13,128,256]{2,1,0:T(8,128)}, f32[128,256]{1,0:T(8,128)}) custom-call(bf16[13,128,256]{2,1,0:T(8,128)(2,1)S(1)} %copy-done, f32[13,128,128]{2,1,0:T(8,128)S(1)} %get-tuple-element.31.other_base, s16[528,128]{1,0:T(8,128)(2,1)S(1)} %collective-permute-done.4.message, ...), custom_call_target="tpu_custom_call", output_to_operand_aliasing={{0}: (5, {})} | custom-call | tf_op jit(solution)/shard_map/finish_last/pallas_call | solution.py:37
  (7 shorter events, 0.0 us)
Async XLA Ops:
  5.2 2.8 %collective-permute-start = (f32[13,128,128]{2,1,0:T(8,128)S(1)}, f32[13,128,128]{2,1,0:T(8,128)S(1)}, u32[]{:S(2)}, u32[]{:S(2)}) collective-permute-start(f32[13,128,128]{2,1,0:T(8,128)S(1)} %get-tuple-element.29), channel_id=1, source_target_pairs={{0,1},{1,0},{2,3},{3,2},{4,5},{5,4},{6,7},{7,6},{8,9},{9,8},{10,11... | collective-permute-start | bytes 2555912 | tf_op jit(solution)/shard_map/ppermute | solution.py:563
  5.3 21.0 %copy-start = (bf16[13,128,256]{2,1,0:T(8,128)(2,1)S(1)}, bf16[13,128,256]{2,1,0:T(8,128)(2,1)}, u32[]{:S(2)}) copy-start(bf16[13,128,256]{2,1,0:T(8,128)(2,1)} %observed.3) | copy-start | bytes 2555908
  8.4 5.5 %collective-permute-start.1 = (f32[13,128,128]{2,1,0:T(8,128)S(1)}, f32[13,128,128]{2,1,0:T(8,128)S(1)}, u32[]{:S(2)}, u32[]{:S(2)}) collective-permute-start(f32[13,128,128]{2,1,0:T(8,128)S(1)} %get-tuple-element.30.total), channel_id=1, source_target_pairs={{0,1},{1,0},{2,3},{3,2},{4,5},{5,4},{6,7},{7,6},{8,9},{9,8},{10,11... | collective-permute-start | bytes 2555912 | tf_op jit(solution)/shard_map/ppermute | solution.py:572
  8.9 6.3 %collective-permute-start.5 = (s16[656,128]{1,0:T(8,128)(2,1)S(1)}, s16[656,128]{1,0:T(8,128)(2,1)S(1)}, u32[]{:S(2)}, u32[]{:S(2)}) collective-permute-start(s16[656,128]{1,0:T(8,128)(2,1)S(1)} %get-tuple-element.37), channel_id=1, source_target_pairs={{0,2},{2,0},{4,6},{6,4},{8,10},{10,8},{12,14},{14,12},{5,1},{15,3}... | collective-permute-start | bytes 503816 | tf_op jit(solution)/shard_map/ppermute | solution.py:571
  11.9 5.5 %collective-permute-start.7 = (s16[528,128]{1,0:T(8,128)(2,1)S(1)}, s16[528,128]{1,0:T(8,128)(2,1)S(1)}, u32[]{:S(2)}, u32[]{:S(2)}) collective-permute-start(s16[528,128]{1,0:T(8,128)(2,1)S(1)} %get-tuple-element.40), channel_id=1, source_target_pairs={{0,2},{2,0},{4,6},{6,4},{8,10},{10,8},{12,14},{14,12},{5,1},{15,3}... | collective-permute-start | bytes 405512 | tf_op jit(solution)/shard_map/ppermute | solution.py:571
  11.9 7.1 %collective-permute-start.2 = (s16[528,128]{1,0:T(8,128)(2,1)S(1)}, s16[528,128]{1,0:T(8,128)(2,1)S(1)}, u32[]{:S(2)}, u32[]{:S(2)}) collective-permute-start(s16[528,128]{1,0:T(8,128)(2,1)S(1)} %get-tuple-element.33), channel_id=1, source_target_pairs={{0,2},{2,0},{4,6},{6,4},{8,10},{10,8},{12,14},{14,12},{5,1},{15,3}... | collective-permute-start | bytes 405512 | tf_op jit(solution)/shard_map/ppermute | solution.py:571
  15.2 7.5 %collective-permute-start.6 = (s16[656,128]{1,0:T(8,128)(2,1)S(1)}, s16[656,128]{1,0:T(8,128)(2,1)S(1)}, u32[]{:S(2)}, u32[]{:S(2)}) collective-permute-start(s16[656,128]{1,0:T(8,128)(2,1)S(1)} %relay.4), channel_id=1, source_target_pairs={{0,4},{2,14},{4,8},{6,2},{8,12},{10,6},{12,0},{14,10},{1,3},{3,1},... | collective-permute-start | bytes 503816 | tf_op jit(solution)/shard_map/ppermute | solution.py:582
  17.4 6.9 %collective-permute-start.8 = (s16[528,128]{1,0:T(8,128)(2,1)S(1)}, s16[528,128]{1,0:T(8,128)(2,1)S(1)}, u32[]{:S(2)}, u32[]{:S(2)}) collective-permute-start(s16[528,128]{1,0:T(8,128)(2,1)S(1)} %relay.5), channel_id=1, source_target_pairs={{0,4},{2,14},{4,8},{6,2},{8,12},{10,6},{12,0},{14,10},{1,3},{3,1},... | collective-permute-start | bytes 405512 | tf_op jit(solution)/shard_map/ppermute | solution.py:582
  19.0 6.9 %collective-permute-start.3 = (s16[528,128]{1,0:T(8,128)(2,1)S(1)}, s16[528,128]{1,0:T(8,128)(2,1)S(1)}, u32[]{:S(2)}, u32[]{:S(2)}) collective-permute-start(s16[528,128]{1,0:T(8,128)(2,1)S(1)} %relay.3), channel_id=1, source_target_pairs={{0,4},{2,14},{4,8},{6,2},{8,12},{10,6},{12,0},{14,10},{1,3},{3,1},... | collective-permute-start | bytes 405512 | tf_op jit(solution)/shard_map/ppermute | solution.py:582
  23.1 3.2 %collective-permute-start.9 = (s16[656,128]{1,0:T(8,128)(2,1)S(1)}, s16[656,128]{1,0:T(8,128)(2,1)S(1)}, u32[]{:S(2)}, u32[]{:S(2)}) collective-permute-start(s16[656,128]{1,0:T(8,128)(2,1)S(1)} %settle.4.rest_0_), channel_id=1, source_target_pairs={{0,1},{1,0},{2,3},{3,2},{4,5},{5,4},{6,7},{7,6},{8,9},{9,8},{10,11... | collective-permute-start | bytes 503816 | tf_op jit(solution)/shard_map/ppermute | solution.py:600
  24.5 1.7 %collective-permute-start.10 = (s16[528,128]{1,0:T(8,128)(2,1)S(1)}, s16[528,128]{1,0:T(8,128)(2,1)S(1)}, u32[]{:S(2)}, u32[]{:S(2)}) collective-permute-start(s16[528,128]{1,0:T(8,128)(2,1)S(1)} %settle.5.rest_1_), channel_id=1, source_target_pairs={{0,1},{1,0},{2,3},{3,2},{4,5},{5,4},{6,7},{7,6},{8,9},{9,8},{10,11... | collective-permute-start | bytes 405512 | tf_op jit(solution)/shard_map/ppermute | solution.py:600
  26.2 1.5 %collective-permute-start.4 = (s16[528,128]{1,0:T(8,128)(2,1)S(1)}, s16[528,128]{1,0:T(8,128)(2,1)S(1)}, u32[]{:S(2)}, u32[]{:S(2)}) collective-permute-start(s16[528,128]{1,0:T(8,128)(2,1)S(1)} %settle.3.rest_2_), channel_id=1, source_target_pairs={{0,1},{1,0},{2,3},{3,2},{4,5},{5,4},{6,7},{7,6},{8,9},{9,8},{10,11... | collective-permute-start | bytes 405512 | tf_op jit(solution)/shard_map/ppermute | solution.py:600

commit v10 on v9

--- a/solution.py
+++ b/solution.py
@@ -495,19 +495,30 @@
     resp_values,
 ):
     f32, i16 = jnp.float32, jnp.int16
-    size = lax.axis_size("line")
+    slabs, size = lax.axis_size("slab"), lax.axis_size("line")
     bands, lines, cols = cube.shape
     count = resp_values.shape[0]
     half = cols // 2
     _, _, units = ownership(count)
     shape = jax.ShapeDtypeStruct
     swap = [(0, 1), (1, 0)]
-    partner = [(i, i ^ 1) for i in range(size)]
-    even_up = [(i, (i + 2 - 4 * (i % 2)) % size) for i in range(size)]
+    blocks = [(s, i) for s in range(slabs) for i in range(size)]
+    partner = [((s, i), (s, i ^ 1)) for s, i in blocks]
+
+    def two_on(s, i):
+        i = i + 2 - 4 * (i % 2)
+        return (s, i) if 0 <= i < size else ((s + 1) % slabs, i % size)
+
+    even_up = [(block, two_on(*block)) for block in blocks]
     odd_up = [(j, i) for i, j in even_up]
-
-    def cores(zero, one):
-        return [(2 * a, 2 * b) for a, b in zero] + [(2 * a + 1, 2 * b + 1) for a, b in one]
+    everywhere = ("slab", "line", "band")
+
+    def cores(*pairs):
+        return [
+            ((a * size + b) * 2 + core, (c * size + d) * 2 + core)
+            for core in range(2)
+            for (a, b), (c, d) in pairs[core]
+        ]
 
     part = shape((units, lines, half), f32)
     edges = [-(-units * i // CHUNKS) for i in range(CHUNKS + 1)]
@@ -568,7 +579,7 @@
         [part, *coded],
         scratch=work,
     )
-    near = [lax.ppermute(x, ("line", "band"), cores(partner, odd_up)) for x in sent]
+    near = [lax.ppermute(x, everywhere, cores(partner, odd_up)) for x in sent]
     other_total = lax.ppermute(total, "band", swap)
     base, other_base, term = call(
         centre, (picked, total, other_total), [VMEM] * 3, [part] * 3
@@ -579,7 +590,7 @@
             functools.partial(relay, span), (term, near[i]), [VMEM] * 2, [coded[i]], scratch=work
         )
         message, near[i] = lax.optimization_barrier((message, near[i]))
-        far.append(lax.ppermute(message, ("line", "band"), cores(even_up, partner)))
+        far.append(lax.ppermute(message, everywhere, cores(even_up, partner)))
         planes = shape((span[1] - span[0], lines, half), f32)
         product += call(
             functools.partial(beside, span),

time: 28.9 us -> 29.8 us (1.031)
  waiting for transfers between devices: 4.24 us -> 5.54 us
  starting transfers between devices: 11.6 us -> 11.2 us
  Pallas kernels: 12.1 us -> 11.8 us
    ppermute x6, waiting for transfers between devices: 4.23 us -> 5.53 us  [the longest x3 4.64 us: on_device(): far.append(lax.ppermute(message, everywhere, cores(even_up, partner)))]
    ppermute x6, starting transfers between devices: 10.8 us -> 10.2 us  [the longest x3 5.39 us: on_device(): far.append(lax.ppermute(message, everywhere, cores(even_up, partner)))]
    ppermute x1, starting transfers between devices: 0.07 us -> 0.52 us  [on_device(): other = lax.ppermute(send, 'band', swap)]
  transfers between devices with their start and end apart: 11 -> 11, of which waited for: 4 -> 4; matrix products, arithmetic and copies ran while one was open for 0% -> 0% of each run, Pallas kernels for 21% -> 20%
where the time goes in v10:
time: 29.8 us; the launch traced here: 29.4 us
  Pallas kernels  11.8 us (40%)
  starting transfers between devices  11.2 us (38%)
  waiting for transfers between devices  5.54 us (19%)
  between operations  0.81 us (3%)
    pallas_call x15, Pallas kernels, call(): pl.pallas_call(kernel, in_specs=specs, out_specs=out_specs or [VMEM] * le...  11.8 us
    ppermute x3, starting transfers between devices, on_device(): far.append(lax.ppermute(message, everywhere, cores(even_up, partner)))  5.39 us
    ppermute x3, starting transfers between devices, on_device(): near = [lax.ppermute(x, everywhere, cores(partner, odd_up)) for x in sent]  4.84 us
    ppermute x3, waiting for transfers between devices, on_device(): far.append(lax.ppermute(message, everywhere, cores(even_up, partner)))  4.64 us
    ppermute x3, waiting for transfers between devices, on_device(): near = [lax.ppermute(x, everywhere, cores(partner, odd_up)) for x in sent]  0.89 us
  transfers between devices with their start and end apart: 11, of which 4 were waited for; matrix products, arithmetic and copies ran while one was open for 0% of the time, Pallas kernels for 20%

profile of v10, /device:TPU:0, one launch (start us, length us, event | category | flops | bytes accessed | tf_op | source)
XLA Modules:
  0.0 29.4 jit_solution(16124196161948753474)
XLA Ops:
  0.6 4.6 %fold_other.1 = (f32[13,128,128]{2,1,0:T(8,128)S(1)}, f32[1,128,128]{2,1,0:T(8,128)S(1)}, bf16[115,128,256]{2,1,0:T(8,128)(2,1)S(1)}, f32[13,20]{1,0:T(8,128)S(1...) custom-call(s32[13]{0:T(128)} %start_in.3, s32[3]{0:T(128)} %offsets_in.1, bf16[13,20]{1,0:T(8,128)(2,1)} %values_in.1, ...), custom_call_target="tpu_custom_call" | custom-call | tf_op jit(solution)/shard_map/fold_other/pallas_call | solution.py:37
  5.2 0.5 %collective-permute-start = (f32[13,128,128]{2,1,0:T(8,128)S(1)}, f32[13,128,128]{2,1,0:T(8,128)S(1)}, u32[]{:S(2)}, u32[]{:S(2)}) collective-permute-start(f32[13,128,128]{2,1,0:T(8,128)S(1)} %get-tuple-element.29), channel_id=1, source_target_pairs={{0,1},{1,0},{2,3},{3,2},{4,5},{5,4},{6,7},{7,6},{8,9},{9,8},{10,11... | collective-permute-start | bytes 2555912 | tf_op jit(solution)/shard_map/ppermute | solution.py:574
  5.8 2.4 %fold_own.1.keep = f32[13,128,128]{2,1,0:T(8,128)S(1)} custom-call(s32[13]{0:T(128)} %start_in.3, f32[13,20]{1,0:T(8,128)S(1)} %get-tuple-element.25.wide, bf16[115,128,256]{2,1,0:T(8,128)(2,1)S(1)} %get-tuple-element.26.cube, bf16[512,256]{1,0:T(8,128)(2,1)S(1)} %get-tuple-element.27.table, f32[1,128,128]{2,1,0:T(8,128)S(1)} %get-tuple-element.28.middle), custom_call_target="tpu_custom_call" | custom-call | tf_op jit(solution)/shard_map/fold_own/pallas_call | solution.py:37
  8.2 0.0 collective-permute-done.other
  8.2 0.4 %share.1 = (f32[13,128,128]{2,1,0:T(8,128)S(1)}, s16[656,128]{1,0:T(8,128)(2,1)S(1)}, s16[528,128]{1,0:T(8,128)(2,1)S(1)}, s16[528,128]{1,0:T(8,128)(2,1)S(1)}) custom-call(bf16[3,128,128]{2,1,0:T(8,128)(2,1)S(1)} %get-tuple-element.24.picked, f32[13,128,128]{2,1,0:T(8,128)S(1)} %fold_own.1.keep, f32[13,128,128]{2,1,0:T(8,128)S(1)} %collective-permute-done.other), custom_call_target="tpu_custom_call" | custom-call | tf_op jit(solution)/shard_map/share/pallas_call | solution.py:37
  8.6 0.2 collective-permute-start.1
  8.8 2.8 %collective-permute-start.5 = (s16[656,128]{1,0:T(8,128)(2,1)S(1)}, s16[656,128]{1,0:T(8,128)(2,1)S(1)}, u32[]{:S(2)}, u32[]{:S(2)}) collective-permute-start(s16[656,128]{1,0:T(8,128)(2,1)S(1)} %get-tuple-element.37), channel_id=1, source_target_pairs={{0,2},{2,0},{4,6},{6,4},{8,10},{10,8},{12,14},{14,12},{16,18},{18,... | collective-permute-start | bytes 503816 | tf_op jit(solution)/shard_map/ppermute | solution.py:582
  11.6 0.0 collective-permute-start.7
  11.6 2.0 %collective-permute-start.2 = (s16[528,128]{1,0:T(8,128)(2,1)S(1)}, s16[528,128]{1,0:T(8,128)(2,1)S(1)}, u32[]{:S(2)}, u32[]{:S(2)}) collective-permute-start(s16[528,128]{1,0:T(8,128)(2,1)S(1)} %get-tuple-element.33), channel_id=1, source_target_pairs={{0,2},{2,0},{4,6},{6,4},{8,10},{10,8},{12,14},{14,12},{16,18},{18,... | collective-permute-start | bytes 405512 | tf_op jit(solution)/shard_map/ppermute | solution.py:582
  13.6 0.4 %centre.1 = (f32[13,128,128]{2,1,0:T(8,128)S(1)}, f32[13,128,128]{2,1,0:T(8,128)S(1)}, f32[13,128,128]{2,1,0:T(8,128)S(1)}) custom-call(bf16[3,128,128]{2,1,0:T(8,128)(2,1)S(1)} %get-tuple-element.24.picked, f32[13,128,128]{2,1,0:T(8,128)S(1)} %get-tuple-element.30.total, f32[13,128,128]{2,1,0:T(8,128)S(1)} %collective-permute-done.1.other_total), custom_call_target="tpu_custom_call" | custom-call | tf_op jit(solution)/shard_map/centre/pallas_call | solution.py:37
  14.0 0.9 %collective-permute-done.5.received.near = s16[656,128]{1,0:T(8,128)(2,1)S(1)} collective-permute-done((s16[656,128]{1,0:T(8,128)(2,1)S(1)}, s16[656,128]{1,0:T(8,128)(2,1)S(1)}, u32[]{:S(2)}, u32[]{:S(2)}) %collective-permute-start.5) | collective-permute-done | bytes 167968 | tf_op jit(solution)/shard_map/ppermute | solution.py:582
  14.9 2.1 %collective-permute-start.6 = (s16[656,128]{1,0:T(8,128)(2,1)S(1)}, s16[656,128]{1,0:T(8,128)(2,1)S(1)}, u32[]{:S(2)}, u32[]{:S(2)}) collective-permute-start(s16[656,128]{1,0:T(8,128)(2,1)S(1)} %relay.4), channel_id=1, source_target_pairs={{0,4},{2,30},{4,8},{6,2},{8,12},{10,6},{12,16},{14,10},{16,20},{18... | collective-permute-start | bytes 503816 | tf_op jit(solution)/shard_map/ppermute | solution.py:593
  17.1 1.6 %collective-permute-start.8 = (s16[528,128]{1,0:T(8,128)(2,1)S(1)}, s16[528,128]{1,0:T(8,128)(2,1)S(1)}, u32[]{:S(2)}, u32[]{:S(2)}) collective-permute-start(s16[528,128]{1,0:T(8,128)(2,1)S(1)} %relay.5), channel_id=1, source_target_pairs={{0,4},{2,30},{4,8},{6,2},{8,12},{10,6},{12,16},{14,10},{16,20},{18... | collective-permute-start | bytes 405512 | tf_op jit(solution)/shard_map/ppermute | solution.py:593
  18.7 0.0 collective-permute-done.2.received.near
  18.8 1.6 %collective-permute-start.3 = (s16[528,128]{1,0:T(8,128)(2,1)S(1)}, s16[528,128]{1,0:T(8,128)(2,1)S(1)}, u32[]{:S(2)}, u32[]{:S(2)}) collective-permute-start(s16[528,128]{1,0:T(8,128)(2,1)S(1)} %relay.3), channel_id=1, source_target_pairs={{0,4},{2,30},{4,8},{6,2},{8,12},{10,6},{12,16},{14,10},{16,20},{18... | collective-permute-start | bytes 405512 | tf_op jit(solution)/shard_map/ppermute | solution.py:593
  20.4 0.2 beside.4.product
  20.6 2.7 %collective-permute-done.6.received = s16[656,128]{1,0:T(8,128)(2,1)S(1)} collective-permute-done((s16[656,128]{1,0:T(8,128)(2,1)S(1)}, s16[656,128]{1,0:T(8,128)(2,1)S(1)}, u32[]{:S(2)}, u32[]{:S(2)}) %collective-permute-start.6) | collective-permute-done | bytes 167968 | tf_op jit(solution)/shard_map/ppermute | solution.py:593
  23.4 0.3 %settle.4.rest_0_ = s16[656,128]{1,0:T(8,128)(2,1)S(1)} custom-call(bf16[3,128,128]{2,1,0:T(8,128)(2,1)S(1)} %get-tuple-element.24.picked, f32[5,128,128]{2,1,0:T(8,128)S(1)} %beside.4.product, s16[656,128]{1,0:T(8,128)(2,1)S(1)} %collective-permute-done.6.received), custom_call_target="tpu_custom_call" | custom-call | tf_op jit(solution)/shard_map/settle/pallas_call | solution.py:37
  23.7 0.1 collective-permute-start.9
  23.8 0.2 beside.5.product
  24.0 0.8 %collective-permute-done.8.received = s16[528,128]{1,0:T(8,128)(2,1)S(1)} collective-permute-done((s16[528,128]{1,0:T(8,128)(2,1)S(1)}, s16[528,128]{1,0:T(8,128)(2,1)S(1)}, u32[]{:S(2)}, u32[]{:S(2)}) %collective-permute-start.8) | collective-permute-done | bytes 135200 | tf_op jit(solution)/shard_map/ppermute | solution.py:593
  24.9 0.3 %settle.5.rest_1_ = s16[528,128]{1,0:T(8,128)(2,1)S(1)} custom-call(bf16[3,128,128]{2,1,0:T(8,128)(2,1)S(1)} %get-tuple-element.24.picked, f32[4,128,128]{2,1,0:T(8,128)S(1)} %beside.5.product, s16[528,128]{1,0:T(8,128)(2,1)S(1)} %collective-permute-done.8.received), custom_call_target="tpu_custom_call" | custom-call | tf_op jit(solution)/shard_map/settle/pallas_call | solution.py:37
  25.2 0.1 collective-permute-start.10
  25.2 0.2 beside.3.product
  25.5 1.1 %collective-permute-done.3.received = s16[528,128]{1,0:T(8,128)(2,1)S(1)} collective-permute-done((s16[528,128]{1,0:T(8,128)(2,1)S(1)}, s16[528,128]{1,0:T(8,128)(2,1)S(1)}, u32[]{:S(2)}, u32[]{:S(2)}) %collective-permute-start.3) | collective-permute-done | bytes 135200 | tf_op jit(solution)/shard_map/ppermute | solution.py:593
  26.5 0.3 %settle.3.rest_2_ = s16[528,128]{1,0:T(8,128)(2,1)S(1)} custom-call(bf16[3,128,128]{2,1,0:T(8,128)(2,1)S(1)} %get-tuple-element.24.picked, f32[4,128,128]{2,1,0:T(8,128)S(1)} %beside.3.product, s16[528,128]{1,0:T(8,128)(2,1)S(1)} %collective-permute-done.3.received), custom_call_target="tpu_custom_call" | custom-call | tf_op jit(solution)/shard_map/settle/pallas_call | solution.py:37
  26.8 0.1 collective-permute-start.4
  26.9 0.0 collective-permute-done.10.rest_4_
  26.9 0.0 collective-permute-done.9.rest_3_
  26.9 1.3 %finish_most.1 = (f32[13,128,256]{2,1,0:T(8,128)}, f32[3,128,256]{2,1,0:T(8,128)S(1)}, f32[3,128,256]{2,1,0:T(8,128)S(1)}) custom-call(bf16[13,128,256]{2,1,0:T(8,128)(2,1)S(1)} %copy-done, f32[13,128,128]{2,1,0:T(8,128)S(1)} %get-tuple-element.36.base, f32[13,128,128]{2,1,0:T(8,128)S(1)} %get-tuple-element.31.other_base, ...), custom_call_target="tpu_custom_call" | custom-call | tf_op jit(solution)/shard_map/finish_most/pallas_call | solution.py:37
  28.3 0.0 collective-permute-done.4.message
  28.3 1.1 %finish_last.1 = (f32[13,128,256]{2,1,0:T(8,128)}, f32[128,256]{1,0:T(8,128)}) custom-call(bf16[13,128,256]{2,1,0:T(8,128)(2,1)S(1)} %copy-done, f32[13,128,128]{2,1,0:T(8,128)S(1)} %get-tuple-element.31.other_base, s16[528,128]{1,0:T(8,128)(2,1)S(1)} %collective-permute-done.4.message, ...), custom_call_target="tpu_custom_call", output_to_operand_aliasing={{0}: (5, {})} | custom-call | tf_op jit(solution)/shard_map/finish_last/pallas_call | solution.py:37
  (7 shorter events, 0.0 us)
Async XLA Ops:
  5.2 3.0 %collective-permute-start = (f32[13,128,128]{2,1,0:T(8,128)S(1)}, f32[13,128,128]{2,1,0:T(8,128)S(1)}, u32[]{:S(2)}, u32[]{:S(2)}) collective-permute-start(f32[13,128,128]{2,1,0:T(8,128)S(1)} %get-tuple-element.29), channel_id=1, source_target_pairs={{0,1},{1,0},{2,3},{3,2},{4,5},{5,4},{6,7},{7,6},{8,9},{9,8},{10,11... | collective-permute-start | bytes 2555912 | tf_op jit(solution)/shard_map/ppermute | solution.py:574
  5.7 21.2 %copy-start = (bf16[13,128,256]{2,1,0:T(8,128)(2,1)S(1)}, bf16[13,128,256]{2,1,0:T(8,128)(2,1)}, u32[]{:S(2)}) copy-start(bf16[13,128,256]{2,1,0:T(8,128)(2,1)} %observed.3) | copy-start | bytes 2555908
  8.6 5.1 %collective-permute-start.1 = (f32[13,128,128]{2,1,0:T(8,128)S(1)}, f32[13,128,128]{2,1,0:T(8,128)S(1)}, u32[]{:S(2)}, u32[]{:S(2)}) collective-permute-start(f32[13,128,128]{2,1,0:T(8,128)S(1)} %get-tuple-element.30.total), channel_id=1, source_target_pairs={{0,1},{1,0},{2,3},{3,2},{4,5},{5,4},{6,7},{7,6},{8,9},{9,8},{10,11... | collective-permute-start | bytes 2555912 | tf_op jit(solution)/shard_map/ppermute | solution.py:583
  8.8 6.1 %collective-permute-start.5 = (s16[656,128]{1,0:T(8,128)(2,1)S(1)}, s16[656,128]{1,0:T(8,128)(2,1)S(1)}, u32[]{:S(2)}, u32[]{:S(2)}) collective-permute-start(s16[656,128]{1,0:T(8,128)(2,1)S(1)} %get-tuple-element.37), channel_id=1, source_target_pairs={{0,2},{2,0},{4,6},{6,4},{8,10},{10,8},{12,14},{14,12},{16,18},{18,... | collective-permute-start | bytes 503816 | tf_op jit(solution)/shard_map/ppermute | solution.py:582
  11.6 5.5 %collective-permute-start.7 = (s16[528,128]{1,0:T(8,128)(2,1)S(1)}, s16[528,128]{1,0:T(8,128)(2,1)S(1)}, u32[]{:S(2)}, u32[]{:S(2)}) collective-permute-start(s16[528,128]{1,0:T(8,128)(2,1)S(1)} %get-tuple-element.40), channel_id=1, source_target_pairs={{0,2},{2,0},{4,6},{6,4},{8,10},{10,8},{12,14},{14,12},{16,18},{18,... | collective-permute-start | bytes 405512 | tf_op jit(solution)/shard_map/ppermute | solution.py:582
  11.6 7.1 %collective-permute-start.2 = (s16[528,128]{1,0:T(8,128)(2,1)S(1)}, s16[528,128]{1,0:T(8,128)(2,1)S(1)}, u32[]{:S(2)}, u32[]{:S(2)}) collective-permute-start(s16[528,128]{1,0:T(8,128)(2,1)S(1)} %get-tuple-element.33), channel_id=1, source_target_pairs={{0,2},{2,0},{4,6},{6,4},{8,10},{10,8},{12,14},{14,12},{16,18},{18,... | collective-permute-start | bytes 405512 | tf_op jit(solution)/shard_map/ppermute | solution.py:582
  14.9 8.4 %collective-permute-start.6 = (s16[656,128]{1,0:T(8,128)(2,1)S(1)}, s16[656,128]{1,0:T(8,128)(2,1)S(1)}, u32[]{:S(2)}, u32[]{:S(2)}) collective-permute-start(s16[656,128]{1,0:T(8,128)(2,1)S(1)} %relay.4), channel_id=1, source_target_pairs={{0,4},{2,30},{4,8},{6,2},{8,12},{10,6},{12,16},{14,10},{16,20},{18... | collective-permute-start | bytes 503816 | tf_op jit(solution)/shard_map/ppermute | solution.py:593
  17.1 7.8 %collective-permute-start.8 = (s16[528,128]{1,0:T(8,128)(2,1)S(1)}, s16[528,128]{1,0:T(8,128)(2,1)S(1)}, u32[]{:S(2)}, u32[]{:S(2)}) collective-permute-start(s16[528,128]{1,0:T(8,128)(2,1)S(1)} %relay.5), channel_id=1, source_target_pairs={{0,4},{2,30},{4,8},{6,2},{8,12},{10,6},{12,16},{14,10},{16,20},{18... | collective-permute-start | bytes 405512 | tf_op jit(solution)/shard_map/ppermute | solution.py:593
  18.8 7.8 %collective-permute-start.3 = (s16[528,128]{1,0:T(8,128)(2,1)S(1)}, s16[528,128]{1,0:T(8,128)(2,1)S(1)}, u32[]{:S(2)}, u32[]{:S(2)}) collective-permute-start(s16[528,128]{1,0:T(8,128)(2,1)S(1)} %relay.3), channel_id=1, source_target_pairs={{0,4},{2,30},{4,8},{6,2},{8,12},{10,6},{12,16},{14,10},{16,20},{18... | collective-permute-start | bytes 405512 | tf_op jit(solution)/shard_map/ppermute | solution.py:593
  23.7 3.2 %collective-permute-start.9 = (s16[656,128]{1,0:T(8,128)(2,1)S(1)}, s16[656,128]{1,0:T(8,128)(2,1)S(1)}, u32[]{:S(2)}, u32[]{:S(2)}) collective-permute-start(s16[656,128]{1,0:T(8,128)(2,1)S(1)} %settle.4.rest_0_), channel_id=1, source_target_pairs={{0,1},{1,0},{2,3},{3,2},{4,5},{5,4},{6,7},{7,6},{8,9},{9,8},{10,11... | collective-permute-start | bytes 503816 | tf_op jit(solution)/shard_map/ppermute | solution.py:611
  25.2 1.7 %collective-permute-start.10 = (s16[528,128]{1,0:T(8,128)(2,1)S(1)}, s16[528,128]{1,0:T(8,128)(2,1)S(1)}, u32[]{:S(2)}, u32[]{:S(2)}) collective-permute-start(s16[528,128]{1,0:T(8,128)(2,1)S(1)} %settle.5.rest_1_), channel_id=1, source_target_pairs={{0,1},{1,0},{2,3},{3,2},{4,5},{5,4},{6,7},{7,6},{8,9},{9,8},{10,11... | collective-permute-start | bytes 405512 | tf_op jit(solution)/shard_map/ppermute | solution.py:611
  26.8 1.5 %collective-permute-start.4 = (s16[528,128]{1,0:T(8,128)(2,1)S(1)}, s16[528,128]{1,0:T(8,128)(2,1)S(1)}, u32[]{:S(2)}, u32[]{:S(2)}) collective-permute-start(s16[528,128]{1,0:T(8,128)(2,1)S(1)} %settle.3.rest_2_), channel_id=1, source_target_pairs={{0,1},{1,0},{2,3},{3,2},{4,5},{5,4},{6,7},{7,6},{8,9},{9,8},{10,11... | collective-permute-start | bytes 405512 | tf_op jit(solution)/shard_map/ppermute | solution.py:611

commit v11 on v9

--- a/solution.py
+++ b/solution.py
@@ -326,19 +326,16 @@
     by_core(lambda: coding(total), summing)
 
 
-def centre(picked, total, other_total, base, other_base, term):
-    units = total.shape[0]
-
+def centre(picked, total, base, term):
     def into(out):
         def put(m, value):
             out[m] = value
 
         return put
 
-    blurred(picked[0], units, lambda m: total[m], into(base))
-    blurred(picked[0], units, lambda m: other_total[m], into(other_base))
+    blurred(picked[0], total.shape[0], lambda m: total[m], into(base))
     pl.when(lax.axis_index("band") != 0)(
-        lambda: blurred(picked[2], units, lambda m: total[m], into(term))
+        lambda: blurred(picked[2], total.shape[0], lambda m: total[m], into(term))
     )
 
 
@@ -356,32 +353,34 @@
     by_core(forward, add)
 
 
-def beside(span, picked, near, product):
+def beside(span, picked, base, near, product):
     units, lines, _ = product.shape
 
     def put(m, value):
-        product[m] = value
+        product[m] = base[span[0] + m] + value
 
     plane = decode(near, span, lines)
     pl.when(lax.axis_index("band") == 0)(lambda: blurred(picked[1], units, plane, put))
 
 
-def settle(span, picked, product, received, message, total):
+def settle(span, picked, base, product, received, message, total):
     units, lines, _ = product.shape
 
     def put(m, value):
         total[m] = product[m] + value
 
-    def add():
+    def spreading():
         missing = outside(0, lax.axis_size("line") - 1)
         plane = decode(received, span, lines, jnp.logical_not(missing))
         blurred(picked[2], units, plane, put)
-        encode(total, (0, units), message)
-
-    def forward():
-        message[...] = received[...]
-
-    by_core(add, forward)
+
+    def summing():
+        plane = decode(received, span, lines)
+        for m in range(units):
+            total[m] = base[span[0] + m] + plane(m)
+
+    by_core(spreading, summing)
+    encode(total, (0, units), message)
 
 
 def arccos(x):
@@ -399,15 +398,15 @@
     return jnp.where(big, outer, inner)
 
 
-def finish_units(core, parts, observed, base, value, image, sem, sums):
-    _, lines, half = base.shape
+def finish_units(core, parts, observed, value, image, sem, sums):
+    _, lines, half = value.shape
     copies = []
     for span, message in parts:
         plane = decode(message, span, lines)
         for n in range(*span):
             m, c = units_of(core, observed.shape[0])[n]
             at = slice(c * half, (c + 1) * half)
-            made = base[n] + plane(n - span[0])
+            made = plane(n - span[0])
             value[n] = made
             copies.append(pltpu.make_async_copy(value.at[n], image.at[m, :, at], sem(n)))
             copies[-1].start()
@@ -416,25 +415,24 @@
     return copies
 
 
-def finish_most(spans, observed, base, other_base, *rest):
+def finish_most(spans, observed, *rest):
     chunks = len(spans)
     messages, others, rest = rest[:chunks], rest[chunks : 2 * chunks - 1], rest[2 * chunks - 1 :]
     image, own, theirs, value, other_value, sems = rest
-    units, lines, half = base.shape
+    units, lines, half = value.shape
     zero = jnp.zeros((lines, half), jnp.float32)
 
     def work(core):
         sums, other_sums = [(zero, zero)] * 2, [(zero, zero)] * 2
         parts = list(zip(spans, messages))
         copies = finish_units(
-            core, parts, observed, base, value, image, lambda n: sems.at[n], sums
+            core, parts, observed, value, image, lambda n: sems.at[n], sums
         )
         parts = list(zip(spans[:-1], others))
         copies += finish_units(
             1 - core,
             parts,
             observed,
-            other_base,
             other_value,
             image,
             lambda n: sems.at[units + n],
@@ -455,9 +453,9 @@
     by_core(lambda: work(0), lambda: work(1))
 
 
-def finish_last(span, observed, other_base, message, own, theirs, _, *rest):
+def finish_last(span, observed, message, own, theirs, _, *rest):
     image, angles, angle, value, sems = rest
-    units, lines, half = other_base.shape
+    units, lines, half = value.shape
 
     def work(core):
         columns = [slice(c * half, (c + 1) * half) for c in range(2)]
@@ -466,7 +464,6 @@
             core,
             [(span, message)],
             observed,
-            other_base,
             value,
             image,
             lambda n: sems.at[n],
@@ -569,10 +566,7 @@
         scratch=work,
     )
     near = [lax.ppermute(x, ("line", "band"), cores(partner, odd_up)) for x in sent]
-    other_total = lax.ppermute(total, "band", swap)
-    base, other_base, term = call(
-        centre, (picked, total, other_total), [VMEM] * 3, [part] * 3
-    )
+    base, term = call(centre, (picked, total), [VMEM] * 2, [part] * 2)
     far, product = [], []
     for i, span in enumerate(spans):
         (message,) = call(
@@ -583,8 +577,8 @@
         planes = shape((span[1] - span[0], lines, half), f32)
         product += call(
             functools.partial(beside, span),
-            (picked, near[i]),
-            [VMEM] * 2,
+            (picked, base, near[i]),
+            [VMEM] * 3,
             [planes],
         )
     messages, others = [], []
@@ -592,15 +586,15 @@
         planes = product[i].shape
         messages += call(
             functools.partial(settle, span),
-            (picked, product[i], far[i]),
-            [VMEM] * 3,
+            (picked, base, product[i], far[i]),
+            [VMEM] * 4,
             [coded[i]],
             scratch=[pltpu.VMEM(planes, f32)],
         )
         others.append(lax.ppermute(messages[i], "band", swap))
     image = shape((count, lines, cols), f32)
     three = shape((3, lines, cols), f32)
-    inputs = [observed, base, other_base, *messages, *others[:-1]]
+    inputs = [observed, *messages, *others[:-1]]
     image, own, theirs = call(
         functools.partial(finish_most, spans),
         inputs,
@@ -611,12 +605,12 @@
     )
     image, angles = call(
         functools.partial(finish_last, spans[-1]),
-        (observed, other_base, others[-1], own, theirs, image),
-        [VMEM] * 5 + [HBM],
+        (observed, others[-1], own, theirs, image),
+        [VMEM] * 4 + [HBM],
         [image, shape((lines, cols), f32)],
         scratch=[pltpu.VMEM((lines, cols), f32), *work, pltpu.SemaphoreType.DMA((units + 1,))],
         out_specs=[HBM] * 2,
-        aliases={5: 0},
+        aliases={4: 0},
     )
     return image, angles
 

time: 28.9 us -> 28.4 us (0.983); the launches traced: 28.8 us -> 28 us
  Pallas kernels: 12.1 us -> 11.2 us
  waiting for transfers between devices: 4.24 us -> 4.87 us
  starting transfers between devices: 11.6 us -> 11.1 us
    ppermute x1, starting transfers between devices: 0.07 us -> 1.08 us  [on_device(): other = lax.ppermute(send, 'band', swap)]
    pallas_call x15, Pallas kernels: 12.1 us -> 11.2 us  [call(): pl.pallas_call(kernel, in_specs=specs, out_specs=out_specs or [VMEM] * le...]
    ppermute x3, starting transfers between devices: 4.99 us -> 4.43 us  [on_device(): lax.ppermute(x, ('line', 'band'), cores(partner, odd_up))]
    ppermute x1 -> x0, starting transfers between devices: 0.5 us -> none  [on_device(): other_total = lax.ppermute(total, 'band', swap)]
    ppermute x3, starting transfers between devices: 5.78 us -> 5.39 us  [on_device(): far.append(lax.ppermute(message, ('line', 'band'), cores(even_up, partner)))]
    ppermute x3, waiting for transfers between devices: 3.34 us -> 3.71 us  [on_device(): far.append(lax.ppermute(message, ('line', 'band'), cores(even_up, partner)))]
  transfers between devices with their start and end apart: 11 -> 10, of which waited for: 4 -> 5; matrix products, arithmetic and copies ran while one was open for 0% -> 0% of each run, Pallas kernels for 21% -> 18%
where the time goes in v11:
time: 28.4 us; the launch traced here: 28 us
  Pallas kernels  11.2 us (39%)
  starting transfers between devices  11.1 us (39%)
  waiting for transfers between devices  4.87 us (17%)
  between operations  0.81 us (3%)
    pallas_call x15, Pallas kernels, call(): pl.pallas_call(kernel, in_specs=specs, out_specs=out_specs or [VMEM] * le...  11.2 us
    ppermute x3, starting transfers between devices, on_device(): far.append(lax.ppermute(message, ('line', 'band'), cores(even_up, partner)))  5.39 us
    ppermute x3, starting transfers between devices, on_device(): lax.ppermute(x, ('line', 'band'), cores(partner, odd_up))  4.43 us
    ppermute x3, waiting for transfers between devices, on_device(): far.append(lax.ppermute(message, ('line', 'band'), cores(even_up, partner)))  3.71 us
    ppermute x1, starting transfers between devices, on_device(): other = lax.ppermute(send, 'band', swap)  1.08 us
    ppermute x3, waiting for transfers between devices, on_device(): lax.ppermute(x, ('line', 'band'), cores(partner, odd_up))  1.02 us
  transfers between devices with their start and end apart: 10, of which 5 were waited for; matrix products, arithmetic and copies ran while one was open for 0% of the time, Pallas kernels for 18%

profile of v11, /device:TPU:0, one launch (start us, length us, event | category | flops | bytes accessed | tf_op | source)
XLA Modules:
  0.0 28.0 jit_solution(49739010358573367)
XLA Ops:
  0.6 4.6 %fold_other.1 = (f32[13,128,128]{2,1,0:T(8,128)S(1)}, f32[1,128,128]{2,1,0:T(8,128)S(1)}, bf16[115,128,256]{2,1,0:T(8,128)(2,1)S(1)}, f32[13,20]{1,0:T(8,128)S(1...) custom-call(s32[13]{0:T(128)} %start_in.3, s32[3]{0:T(128)} %offsets_in.1, bf16[13,20]{1,0:T(8,128)(2,1)} %values_in.1, ...), custom_call_target="tpu_custom_call" | custom-call | tf_op jit(solution)/shard_map/fold_other/pallas_call | solution.py:37
  5.2 1.1 %collective-permute-start = (f32[13,128,128]{2,1,0:T(8,128)S(1)}, f32[13,128,128]{2,1,0:T(8,128)S(1)}, u32[]{:S(2)}, u32[]{:S(2)}) collective-permute-start(f32[13,128,128]{2,1,0:T(8,128)S(1)} %get-tuple-element.28), channel_id=1, source_target_pairs={{0,1},{1,0},{2,3},{3,2},{4,5},{5,4},{6,7},{7,6},{8,9},{9,8},{10,11... | collective-permute-start | bytes 2555912 | tf_op jit(solution)/shard_map/ppermute | solution.py:560
  6.3 1.9 %fold_own.1.keep = f32[13,128,128]{2,1,0:T(8,128)S(1)} custom-call(s32[13]{0:T(128)} %start_in.3, f32[13,20]{1,0:T(8,128)S(1)} %get-tuple-element.24.wide, bf16[115,128,256]{2,1,0:T(8,128)(2,1)S(1)} %get-tuple-element.25.cube, bf16[512,256]{1,0:T(8,128)(2,1)S(1)} %get-tuple-element.26.table, f32[1,128,128]{2,1,0:T(8,128)S(1)} %get-tuple-element.27.middle), custom_call_target="tpu_custom_call" | custom-call | tf_op jit(solution)/shard_map/fold_own/pallas_call | solution.py:37
  8.2 0.0 copy-start
  8.2 0.1 collective-permute-done.other
  8.3 0.4 %share.1 = (f32[13,128,128]{2,1,0:T(8,128)S(1)}, s16[656,128]{1,0:T(8,128)(2,1)S(1)}, s16[528,128]{1,0:T(8,128)(2,1)S(1)}, s16[528,128]{1,0:T(8,128)(2,1)S(1)}) custom-call(bf16[3,128,128]{2,1,0:T(8,128)(2,1)S(1)} %get-tuple-element.23.picked, f32[13,128,128]{2,1,0:T(8,128)S(1)} %fold_own.1.keep, f32[13,128,128]{2,1,0:T(8,128)S(1)} %collective-permute-done.other), custom_call_target="tpu_custom_call" | custom-call | tf_op jit(solution)/shard_map/share/pallas_call | solution.py:37
  8.7 2.4 %collective-permute-start.4 = (s16[656,128]{1,0:T(8,128)(2,1)S(1)}, s16[656,128]{1,0:T(8,128)(2,1)S(1)}, u32[]{:S(2)}, u32[]{:S(2)}) collective-permute-start(s16[656,128]{1,0:T(8,128)(2,1)S(1)} %get-tuple-element.35), channel_id=1, source_target_pairs={{0,2},{2,0},{4,6},{6,4},{8,10},{10,8},{12,14},{14,12},{5,1},{15,3}... | collective-permute-start | bytes 503816 | tf_op jit(solution)/shard_map/ppermute | solution.py:568
  11.1 0.1 collective-permute-start.6
  11.1 2.0 %collective-permute-start.1 = (s16[528,128]{1,0:T(8,128)(2,1)S(1)}, s16[528,128]{1,0:T(8,128)(2,1)S(1)}, u32[]{:S(2)}, u32[]{:S(2)}) collective-permute-start(s16[528,128]{1,0:T(8,128)(2,1)S(1)} %get-tuple-element.32), channel_id=1, source_target_pairs={{0,2},{2,0},{4,6},{6,4},{8,10},{10,8},{12,14},{14,12},{5,1},{15,3}... | collective-permute-start | bytes 405512 | tf_op jit(solution)/shard_map/ppermute | solution.py:568
  13.1 0.3 %centre.1 = (f32[13,128,128]{2,1,0:T(8,128)S(1)}, f32[13,128,128]{2,1,0:T(8,128)S(1)}) custom-call(bf16[3,128,128]{2,1,0:T(8,128)(2,1)S(1)} %get-tuple-element.23.picked, f32[13,128,128]{2,1,0:T(8,128)S(1)} %get-tuple-element.29.total), custom_call_target="tpu_custom_call" | custom-call | tf_op jit(solution)/shard_map/centre/pallas_call | solution.py:37
  13.4 1.0 %collective-permute-done.4.received.near = s16[656,128]{1,0:T(8,128)(2,1)S(1)} collective-permute-done((s16[656,128]{1,0:T(8,128)(2,1)S(1)}, s16[656,128]{1,0:T(8,128)(2,1)S(1)}, u32[]{:S(2)}, u32[]{:S(2)}) %collective-permute-start.4) | collective-permute-done | bytes 167968 | tf_op jit(solution)/shard_map/ppermute | solution.py:568
  14.4 2.1 %collective-permute-start.5 = (s16[656,128]{1,0:T(8,128)(2,1)S(1)}, s16[656,128]{1,0:T(8,128)(2,1)S(1)}, u32[]{:S(2)}, u32[]{:S(2)}) collective-permute-start(s16[656,128]{1,0:T(8,128)(2,1)S(1)} %relay.4), channel_id=1, source_target_pairs={{0,4},{2,14},{4,8},{6,2},{8,12},{10,6},{12,0},{14,10},{1,3},{3,1},... | collective-permute-start | bytes 503816 | tf_op jit(solution)/shard_map/ppermute | solution.py:576
  16.6 0.0 collective-permute-done.6.received.near
  16.6 1.6 %collective-permute-start.7 = (s16[528,128]{1,0:T(8,128)(2,1)S(1)}, s16[528,128]{1,0:T(8,128)(2,1)S(1)}, u32[]{:S(2)}, u32[]{:S(2)}) collective-permute-start(s16[528,128]{1,0:T(8,128)(2,1)S(1)} %relay.5), channel_id=1, source_target_pairs={{0,4},{2,14},{4,8},{6,2},{8,12},{10,6},{12,0},{14,10},{1,3},{3,1},... | collective-permute-start | bytes 405512 | tf_op jit(solution)/shard_map/ppermute | solution.py:576
  18.2 0.0 collective-permute-done.1.received.near
  18.2 1.6 %collective-permute-start.2 = (s16[528,128]{1,0:T(8,128)(2,1)S(1)}, s16[528,128]{1,0:T(8,128)(2,1)S(1)}, u32[]{:S(2)}, u32[]{:S(2)}) collective-permute-start(s16[528,128]{1,0:T(8,128)(2,1)S(1)} %relay.3), channel_id=1, source_target_pairs={{0,4},{2,14},{4,8},{6,2},{8,12},{10,6},{12,0},{14,10},{1,3},{3,1},... | collective-permute-start | bytes 405512 | tf_op jit(solution)/shard_map/ppermute | solution.py:576
  19.9 0.2 beside.4.product
  20.1 1.8 %collective-permute-done.5.received = s16[656,128]{1,0:T(8,128)(2,1)S(1)} collective-permute-done((s16[656,128]{1,0:T(8,128)(2,1)S(1)}, s16[656,128]{1,0:T(8,128)(2,1)S(1)}, u32[]{:S(2)}, u32[]{:S(2)}) %collective-permute-start.5) | collective-permute-done | bytes 167968 | tf_op jit(solution)/shard_map/ppermute | solution.py:576
  21.9 0.3 %settle.4.rest_0_ = s16[656,128]{1,0:T(8,128)(2,1)S(1)} custom-call(bf16[3,128,128]{2,1,0:T(8,128)(2,1)S(1)} %get-tuple-element.23.picked, f32[13,128,128]{2,1,0:T(8,128)S(1)} %get-tuple-element.30.base, f32[5,128,128]{2,1,0:T(8,128)S(1)} %beside.4.product, s16[656,128]{1,0:T(8,128)(2,1)S(1)} %collective-permute-done.5.received), custom_call_target="tpu_custom_call" | custom-call | tf_op jit(solution)/shard_map/settle/pallas_call | solution.py:37
  22.3 0.1 collective-permute-start.8
  22.4 0.2 beside.5.product
  22.6 0.9 %collective-permute-done.7.received = s16[528,128]{1,0:T(8,128)(2,1)S(1)} collective-permute-done((s16[528,128]{1,0:T(8,128)(2,1)S(1)}, s16[528,128]{1,0:T(8,128)(2,1)S(1)}, u32[]{:S(2)}, u32[]{:S(2)}) %collective-permute-start.7) | collective-permute-done | bytes 135200 | tf_op jit(solution)/shard_map/ppermute | solution.py:576
  23.4 0.3 %settle.5.rest_1_ = s16[528,128]{1,0:T(8,128)(2,1)S(1)} custom-call(bf16[3,128,128]{2,1,0:T(8,128)(2,1)S(1)} %get-tuple-element.23.picked, f32[13,128,128]{2,1,0:T(8,128)S(1)} %get-tuple-element.30.base, f32[4,128,128]{2,1,0:T(8,128)S(1)} %beside.5.product, s16[528,128]{1,0:T(8,128)(2,1)S(1)} %collective-permute-done.7.received), custom_call_target="tpu_custom_call" | custom-call | tf_op jit(solution)/shard_map/settle/pallas_call | solution.py:37
  23.8 0.1 collective-permute-start.9
  23.8 0.2 beside.3.product
  24.1 1.0 %collective-permute-done.2.received = s16[528,128]{1,0:T(8,128)(2,1)S(1)} collective-permute-done((s16[528,128]{1,0:T(8,128)(2,1)S(1)}, s16[528,128]{1,0:T(8,128)(2,1)S(1)}, u32[]{:S(2)}, u32[]{:S(2)}) %collective-permute-start.2) | collective-permute-done | bytes 135200 | tf_op jit(solution)/shard_map/ppermute | solution.py:576
  25.1 0.3 %settle.3.rest_2_ = s16[528,128]{1,0:T(8,128)(2,1)S(1)} custom-call(bf16[3,128,128]{2,1,0:T(8,128)(2,1)S(1)} %get-tuple-element.23.picked, f32[13,128,128]{2,1,0:T(8,128)S(1)} %get-tuple-element.30.base, f32[4,128,128]{2,1,0:T(8,128)S(1)} %beside.3.product, s16[528,128]{1,0:T(8,128)(2,1)S(1)} %collective-permute-done.2.received), custom_call_target="tpu_custom_call" | custom-call | tf_op jit(solution)/shard_map/settle/pallas_call | solution.py:37
  25.4 0.1 collective-permute-start.3
  25.5 0.0 collective-permute-done.9.rest_4_
  25.5 0.0 collective-permute-done.8.rest_3_
  25.5 1.3 %finish_most.1 = (f32[13,128,256]{2,1,0:T(8,128)}, f32[3,128,256]{2,1,0:T(8,128)S(1)}, f32[3,128,256]{2,1,0:T(8,128)S(1)}) custom-call(bf16[13,128,256]{2,1,0:T(8,128)(2,1)S(1)} %copy-done, s16[656,128]{1,0:T(8,128)(2,1)S(1)} %settle.4.rest_0_, s16[528,128]{1,0:T(8,128)(2,1)S(1)} %settle.5.rest_1_, s16[528,128]{1,0:T(8,128)(2,1)S(1)} %settle.3.rest_2_, ...), custom_call_target="tpu_custom_call" | custom-call | tf_op jit(solution)/shard_map/finish_most/pallas_call | solution.py:37
  26.9 1.1 %finish_last.1 = (f32[13,128,256]{2,1,0:T(8,128)}, f32[128,256]{1,0:T(8,128)}) custom-call(bf16[13,128,256]{2,1,0:T(8,128)(2,1)S(1)} %copy-done, s16[528,128]{1,0:T(8,128)(2,1)S(1)} %collective-permute-done.3.message, f32[3,128,256]{2,1,0:T(8,128)S(1)} %get-tuple-element.41.own, ...), custom_call_target="tpu_custom_call", output_to_operand_aliasing={{0}: (4, {})} | custom-call | tf_op jit(solution)/shard_map/finish_last/pallas_call | solution.py:37
  (5 shorter events, 0.0 us)
Async XLA Ops:
  5.2 3.1 %collective-permute-start = (f32[13,128,128]{2,1,0:T(8,128)S(1)}, f32[13,128,128]{2,1,0:T(8,128)S(1)}, u32[]{:S(2)}, u32[]{:S(2)}) collective-permute-start(f32[13,128,128]{2,1,0:T(8,128)S(1)} %get-tuple-element.28), channel_id=1, source_target_pairs={{0,1},{1,0},{2,3},{3,2},{4,5},{5,4},{6,7},{7,6},{8,9},{9,8},{10,11... | collective-permute-start | bytes 2555912 | tf_op jit(solution)/shard_map/ppermute | solution.py:560
  8.2 17.3 %copy-start = (bf16[13,128,256]{2,1,0:T(8,128)(2,1)S(1)}, bf16[13,128,256]{2,1,0:T(8,128)(2,1)}, u32[]{:S(2)}) copy-start(bf16[13,128,256]{2,1,0:T(8,128)(2,1)} %observed.3) | copy-start | bytes 2555908
  8.7 5.7 %collective-permute-start.4 = (s16[656,128]{1,0:T(8,128)(2,1)S(1)}, s16[656,128]{1,0:T(8,128)(2,1)S(1)}, u32[]{:S(2)}, u32[]{:S(2)}) collective-permute-start(s16[656,128]{1,0:T(8,128)(2,1)S(1)} %get-tuple-element.35), channel_id=1, source_target_pairs={{0,2},{2,0},{4,6},{6,4},{8,10},{10,8},{12,14},{14,12},{5,1},{15,3}... | collective-permute-start | bytes 503816 | tf_op jit(solution)/shard_map/ppermute | solution.py:568
  11.1 5.5 %collective-permute-start.6 = (s16[528,128]{1,0:T(8,128)(2,1)S(1)}, s16[528,128]{1,0:T(8,128)(2,1)S(1)}, u32[]{:S(2)}, u32[]{:S(2)}) collective-permute-start(s16[528,128]{1,0:T(8,128)(2,1)S(1)} %get-tuple-element.38), channel_id=1, source_target_pairs={{0,2},{2,0},{4,6},{6,4},{8,10},{10,8},{12,14},{14,12},{5,1},{15,3}... | collective-permute-start | bytes 405512 | tf_op jit(solution)/shard_map/ppermute | solution.py:568
  11.1 7.1 %collective-permute-start.1 = (s16[528,128]{1,0:T(8,128)(2,1)S(1)}, s16[528,128]{1,0:T(8,128)(2,1)S(1)}, u32[]{:S(2)}, u32[]{:S(2)}) collective-permute-start(s16[528,128]{1,0:T(8,128)(2,1)S(1)} %get-tuple-element.32), channel_id=1, source_target_pairs={{0,2},{2,0},{4,6},{6,4},{8,10},{10,8},{12,14},{14,12},{5,1},{15,3}... | collective-permute-start | bytes 405512 | tf_op jit(solution)/shard_map/ppermute | solution.py:568
  14.4 7.5 %collective-permute-start.5 = (s16[656,128]{1,0:T(8,128)(2,1)S(1)}, s16[656,128]{1,0:T(8,128)(2,1)S(1)}, u32[]{:S(2)}, u32[]{:S(2)}) collective-permute-start(s16[656,128]{1,0:T(8,128)(2,1)S(1)} %relay.4), channel_id=1, source_target_pairs={{0,4},{2,14},{4,8},{6,2},{8,12},{10,6},{12,0},{14,10},{1,3},{3,1},... | collective-permute-start | bytes 503816 | tf_op jit(solution)/shard_map/ppermute | solution.py:576
  16.6 6.9 %collective-permute-start.7 = (s16[528,128]{1,0:T(8,128)(2,1)S(1)}, s16[528,128]{1,0:T(8,128)(2,1)S(1)}, u32[]{:S(2)}, u32[]{:S(2)}) collective-permute-start(s16[528,128]{1,0:T(8,128)(2,1)S(1)} %relay.5), channel_id=1, source_target_pairs={{0,4},{2,14},{4,8},{6,2},{8,12},{10,6},{12,0},{14,10},{1,3},{3,1},... | collective-permute-start | bytes 405512 | tf_op jit(solution)/shard_map/ppermute | solution.py:576
  18.2 6.9 %collective-permute-start.2 = (s16[528,128]{1,0:T(8,128)(2,1)S(1)}, s16[528,128]{1,0:T(8,128)(2,1)S(1)}, u32[]{:S(2)}, u32[]{:S(2)}) collective-permute-start(s16[528,128]{1,0:T(8,128)(2,1)S(1)} %relay.3), channel_id=1, source_target_pairs={{0,4},{2,14},{4,8},{6,2},{8,12},{10,6},{12,0},{14,10},{1,3},{3,1},... | collective-permute-start | bytes 405512 | tf_op jit(solution)/shard_map/ppermute | solution.py:576
  22.3 3.2 %collective-permute-start.8 = (s16[656,128]{1,0:T(8,128)(2,1)S(1)}, s16[656,128]{1,0:T(8,128)(2,1)S(1)}, u32[]{:S(2)}, u32[]{:S(2)}) collective-permute-start(s16[656,128]{1,0:T(8,128)(2,1)S(1)} %settle.4.rest_0_), channel_id=1, source_target_pairs={{0,1},{1,0},{2,3},{3,2},{4,5},{5,4},{6,7},{7,6},{8,9},{9,8},{10,11... | collective-permute-start | bytes 503816 | tf_op jit(solution)/shard_map/ppermute | solution.py:594
  23.8 1.7 %collective-permute-start.9 = (s16[528,128]{1,0:T(8,128)(2,1)S(1)}, s16[528,128]{1,0:T(8,128)(2,1)S(1)}, u32[]{:S(2)}, u32[]{:S(2)}) collective-permute-start(s16[528,128]{1,0:T(8,128)(2,1)S(1)} %settle.5.rest_1_), channel_id=1, source_target_pairs={{0,1},{1,0},{2,3},{3,2},{4,5},{5,4},{6,7},{7,6},{8,9},{9,8},{10,11... | collective-permute-start | bytes 405512 | tf_op jit(solution)/shard_map/ppermute | solution.py:594
  25.4 1.5 %collective-permute-start.3 = (s16[528,128]{1,0:T(8,128)(2,1)S(1)}, s16[528,128]{1,0:T(8,128)(2,1)S(1)}, u32[]{:S(2)}, u32[]{:S(2)}) collective-permute-start(s16[528,128]{1,0:T(8,128)(2,1)S(1)} %settle.3.rest_2_), channel_id=1, source_target_pairs={{0,1},{1,0},{2,3},{3,2},{4,5},{5,4},{6,7},{7,6},{8,9},{9,8},{10,11... | collective-permute-start | bytes 405512 | tf_op jit(solution)/shard_map/ppermute | solution.py:594

commit v12 on v11

--- a/solution.py
+++ b/solution.py
@@ -29,7 +29,7 @@
 SMEM = pl.BlockSpec(memory_space=pltpu.SMEM)
 VMEM = pl.BlockSpec(memory_space=pltpu.VMEM)
 HBM = pl.BlockSpec(memory_space=pltpu.HBM)
-ROWS = 64
+ROWS = 128
 CHUNKS = 3
 
 
@@ -326,7 +326,7 @@
     by_core(lambda: coding(total), summing)
 
 
-def centre(picked, total, base, term):
+def centre(picked, total, observed, base, term, norm):
     def into(out):
         def put(m, value):
             out[m] = value
@@ -337,6 +337,11 @@
     pl.when(lax.axis_index("band") != 0)(
         lambda: blurred(picked[2], total.shape[0], lambda m: total[m], into(term))
     )
+    right = jnp.zeros(norm.shape, jnp.float32)
+    for m in range(observed.shape[0]):
+        seen = observed[m].astype(jnp.float32)
+        right = right + seen * seen
+    norm[...] = jnp.sqrt(right)
 
 
 def relay(span, term, received, message, total):
@@ -440,12 +445,7 @@
         )
         for c in range(2):
             at = slice(c * half, (c + 1) * half)
-            right = zero
-            for m in range(observed.shape[0]):
-                seen = observed[m, :, at].astype(jnp.float32)
-                right = right + seen * seen
             own[0, :, at], own[1, :, at] = sums[c]
-            own[2, :, at] = jnp.sqrt(right)
             theirs[0, :, at], theirs[1, :, at] = other_sums[c]
         for copy in copies:
             copy.wait()
@@ -453,7 +453,7 @@
     by_core(lambda: work(0), lambda: work(1))
 
 
-def finish_last(span, observed, message, own, theirs, _, *rest):
+def finish_last(span, observed, message, norm, own, theirs, _, *rest):
     image, angles, angle, value, sems = rest
     units, lines, half = value.shape
 
@@ -470,7 +470,7 @@
             sums,
         )
         for (inner, left), at in zip(sums, columns):
-            bound = jnp.sqrt(left + own[1, :, at]) * own[2, :, at]
+            bound = jnp.sqrt(left + own[1, :, at]) * norm[:, at]
             ratio = (inner + own[0, :, at]) / jnp.maximum(bound, 1.0)
             angle[:, at] = arccos(jnp.clip(ratio, -1.0, 1.0))
         copies.append(pltpu.make_async_copy(angle, angles, sems.at[units]))
@@ -566,7 +566,9 @@
         scratch=work,
     )
     near = [lax.ppermute(x, ("line", "band"), cores(partner, odd_up)) for x in sent]
-    base, term = call(centre, (picked, total), [VMEM] * 2, [part] * 2)
+    base, term, norm = call(
+        centre, (picked, total, observed), [VMEM] * 3, [part, part, shape((lines, cols), f32)]
+    )
     far, product = [], []
     for i, span in enumerate(spans):
         (message,) = call(
@@ -593,24 +595,24 @@
         )
         others.append(lax.ppermute(messages[i], "band", swap))
     image = shape((count, lines, cols), f32)
-    three = shape((3, lines, cols), f32)
+    pair = shape((2, lines, cols), f32)
     inputs = [observed, *messages, *others[:-1]]
     image, own, theirs = call(
         functools.partial(finish_most, spans),
         inputs,
         [VMEM] * len(inputs),
-        [image, three, three],
+        [image, pair, pair],
         scratch=work * 2 + [pltpu.SemaphoreType.DMA((2 * units,))],
         out_specs=[HBM, VMEM, VMEM],
     )
     image, angles = call(
         functools.partial(finish_last, spans[-1]),
-        (observed, others[-1], own, theirs, image),
-        [VMEM] * 4 + [HBM],
+        (observed, others[-1], norm, own, theirs, image),
+        [VMEM] * 5 + [HBM],
         [image, shape((lines, cols), f32)],
         scratch=[pltpu.VMEM((lines, cols), f32), *work, pltpu.SemaphoreType.DMA((units + 1,))],
         out_specs=[HBM] * 2,
-        aliases={4: 0},
+        aliases={5: 0},
     )
     return image, angles
 

time: 28.4 us -> 28.4 us (level)
  Pallas kernels: 11.2 us -> 12 us
  starting transfers between devices: 11.1 us -> 10.8 us
  waiting for transfers between devices: 4.87 us -> 4.58 us
    ppermute x1, starting transfers between devices: 1.08 us -> 0.13 us  [on_device(): other = lax.ppermute(send, 'band', swap)]
    pallas_call x15, Pallas kernels: 11.2 us -> 12 us  [call(): pl.pallas_call(kernel, in_specs=specs, out_specs=out_specs or [VMEM] * le...]
    ppermute x3, starting transfers between devices: 4.43 us -> 5.04 us  [on_device(): lax.ppermute(x, ('line', 'band'), cores(partner, odd_up))]
  transfers between devices with their start and end apart: 10 -> 10, of which waited for: 5 -> 4; matrix products, arithmetic and copies ran while one was open for 0% -> 0% of each run, Pallas kernels for 18% -> 20%
where the time goes in v12:
time: 28.4 us; the launch traced here: 28.1 us
  Pallas kernels  12 us (42%)
  starting transfers between devices  10.8 us (38%)
  waiting for transfers between devices  4.58 us (16%)
  between operations  0.8 us (3%)
    pallas_call x15, Pallas kernels, call(): pl.pallas_call(kernel, in_specs=specs, out_specs=out_specs or [VMEM] * le...  12 us
    ppermute x3, starting transfers between devices, on_device(): far.append(lax.ppermute(message, ('line', 'band'), cores(even_up, partner)))  5.39 us
    ppermute x3, starting transfers between devices, on_device(): lax.ppermute(x, ('line', 'band'), cores(partner, odd_up))  5.04 us
    ppermute x3, waiting for transfers between devices, on_device(): far.append(lax.ppermute(message, ('line', 'band'), cores(even_up, partner)))  3.71 us
    ppermute x3, waiting for transfers between devices, on_device(): lax.ppermute(x, ('line', 'band'), cores(partner, odd_up))  0.83 us
  transfers between devices with their start and end apart: 10, of which 4 were waited for; matrix products, arithmetic and copies ran while one was open for 0% of the time, Pallas kernels for 20%

profile of v12, /device:TPU:0, one launch (start us, length us, event | category | flops | bytes accessed | tf_op | source)
XLA Modules:
  0.0 28.1 jit_solution(15504699599243816955)
XLA Ops:
  0.6 4.8 %fold_other.1 = (f32[13,128,128]{2,1,0:T(8,128)S(1)}, f32[1,128,128]{2,1,0:T(8,128)S(1)}, bf16[115,128,256]{2,1,0:T(8,128)(2,1)S(1)}, f32[13,20]{1,0:T(8,128)S(1...) custom-call(s32[13]{0:T(128)} %start_in.3, s32[3]{0:T(128)} %offsets_in.1, bf16[13,20]{1,0:T(8,128)(2,1)} %values_in.1, ...), custom_call_target="tpu_custom_call" | custom-call | tf_op jit(solution)/shard_map/fold_other/pallas_call | solution.py:37
  5.4 0.1 collective-permute-start
  5.6 2.3 %fold_own.1.keep = f32[13,128,128]{2,1,0:T(8,128)S(1)} custom-call(s32[13]{0:T(128)} %start_in.3, f32[13,20]{1,0:T(8,128)S(1)} %get-tuple-element.25.wide, bf16[115,128,256]{2,1,0:T(8,128)(2,1)S(1)} %get-tuple-element.26.cube, bf16[512,256]{1,0:T(8,128)(2,1)S(1)} %get-tuple-element.27.table, f32[1,128,128]{2,1,0:T(8,128)S(1)} %get-tuple-element.28.middle), custom_call_target="tpu_custom_call" | custom-call | tf_op jit(solution)/shard_map/fold_own/pallas_call | solution.py:37
  7.8 0.0 collective-permute-done.other
  7.9 0.4 %share.1 = (f32[13,128,128]{2,1,0:T(8,128)S(1)}, s16[656,128]{1,0:T(8,128)(2,1)S(1)}, s16[528,128]{1,0:T(8,128)(2,1)S(1)}, s16[528,128]{1,0:T(8,128)(2,1)S(1)}) custom-call(bf16[3,128,128]{2,1,0:T(8,128)(2,1)S(1)} %get-tuple-element.24.picked, f32[13,128,128]{2,1,0:T(8,128)S(1)} %fold_own.1.keep, f32[13,128,128]{2,1,0:T(8,128)S(1)} %collective-permute-done.other), custom_call_target="tpu_custom_call" | custom-call | tf_op jit(solution)/shard_map/share/pallas_call | solution.py:37
  8.2 3.0 %collective-permute-start.4 = (s16[656,128]{1,0:T(8,128)(2,1)S(1)}, s16[656,128]{1,0:T(8,128)(2,1)S(1)}, u32[]{:S(2)}, u32[]{:S(2)}) collective-permute-start(s16[656,128]{1,0:T(8,128)(2,1)S(1)} %get-tuple-element.37), channel_id=1, source_target_pairs={{0,2},{2,0},{4,6},{6,4},{8,10},{10,8},{12,14},{14,12},{5,1},{15,3}... | collective-permute-start | bytes 503816 | tf_op jit(solution)/shard_map/ppermute | solution.py:568
  11.2 0.1 collective-permute-start.6
  11.3 2.0 %collective-permute-start.1 = (s16[528,128]{1,0:T(8,128)(2,1)S(1)}, s16[528,128]{1,0:T(8,128)(2,1)S(1)}, u32[]{:S(2)}, u32[]{:S(2)}) collective-permute-start(s16[528,128]{1,0:T(8,128)(2,1)S(1)} %get-tuple-element.33), channel_id=1, source_target_pairs={{0,2},{2,0},{4,6},{6,4},{8,10},{10,8},{12,14},{14,12},{5,1},{15,3}... | collective-permute-start | bytes 405512 | tf_op jit(solution)/shard_map/ppermute | solution.py:568
  13.3 0.5 %centre.1 = (f32[13,128,128]{2,1,0:T(8,128)S(1)}, f32[13,128,128]{2,1,0:T(8,128)S(1)}, f32[128,256]{1,0:T(8,128)S(1)}) custom-call(bf16[3,128,128]{2,1,0:T(8,128)(2,1)S(1)} %get-tuple-element.24.picked, f32[13,128,128]{2,1,0:T(8,128)S(1)} %get-tuple-element.30.total, bf16[13,128,256]{2,1,0:T(8,128)(2,1)S(1)} %copy-done), custom_call_target="tpu_custom_call" | custom-call | tf_op jit(solution)/shard_map/centre/pallas_call | solution.py:37
  13.8 0.8 %collective-permute-done.4.received.near = s16[656,128]{1,0:T(8,128)(2,1)S(1)} collective-permute-done((s16[656,128]{1,0:T(8,128)(2,1)S(1)}, s16[656,128]{1,0:T(8,128)(2,1)S(1)}, u32[]{:S(2)}, u32[]{:S(2)}) %collective-permute-start.4) | collective-permute-done | bytes 167968 | tf_op jit(solution)/shard_map/ppermute | solution.py:568
  14.6 2.1 %collective-permute-start.5 = (s16[656,128]{1,0:T(8,128)(2,1)S(1)}, s16[656,128]{1,0:T(8,128)(2,1)S(1)}, u32[]{:S(2)}, u32[]{:S(2)}) collective-permute-start(s16[656,128]{1,0:T(8,128)(2,1)S(1)} %relay.4), channel_id=1, source_target_pairs={{0,4},{2,14},{4,8},{6,2},{8,12},{10,6},{12,0},{14,10},{1,3},{3,1},... | collective-permute-start | bytes 503816 | tf_op jit(solution)/shard_map/ppermute | solution.py:578
  16.7 0.0 collective-permute-done.6.received.near
  16.8 1.6 %collective-permute-start.7 = (s16[528,128]{1,0:T(8,128)(2,1)S(1)}, s16[528,128]{1,0:T(8,128)(2,1)S(1)}, u32[]{:S(2)}, u32[]{:S(2)}) collective-permute-start(s16[528,128]{1,0:T(8,128)(2,1)S(1)} %relay.5), channel_id=1, source_target_pairs={{0,4},{2,14},{4,8},{6,2},{8,12},{10,6},{12,0},{14,10},{1,3},{3,1},... | collective-permute-start | bytes 405512 | tf_op jit(solution)/shard_map/ppermute | solution.py:578
  18.4 0.0 collective-permute-done.1.received.near
  18.4 1.6 %collective-permute-start.2 = (s16[528,128]{1,0:T(8,128)(2,1)S(1)}, s16[528,128]{1,0:T(8,128)(2,1)S(1)}, u32[]{:S(2)}, u32[]{:S(2)}) collective-permute-start(s16[528,128]{1,0:T(8,128)(2,1)S(1)} %relay.3), channel_id=1, source_target_pairs={{0,4},{2,14},{4,8},{6,2},{8,12},{10,6},{12,0},{14,10},{1,3},{3,1},... | collective-permute-start | bytes 405512 | tf_op jit(solution)/shard_map/ppermute | solution.py:578
  20.0 0.2 beside.4.product
  20.3 1.8 %collective-permute-done.5.received = s16[656,128]{1,0:T(8,128)(2,1)S(1)} collective-permute-done((s16[656,128]{1,0:T(8,128)(2,1)S(1)}, s16[656,128]{1,0:T(8,128)(2,1)S(1)}, u32[]{:S(2)}, u32[]{:S(2)}) %collective-permute-start.5) | collective-permute-done | bytes 167968 | tf_op jit(solution)/shard_map/ppermute | solution.py:578
  22.1 0.3 %settle.4.rest_0_ = s16[656,128]{1,0:T(8,128)(2,1)S(1)} custom-call(bf16[3,128,128]{2,1,0:T(8,128)(2,1)S(1)} %get-tuple-element.24.picked, f32[13,128,128]{2,1,0:T(8,128)S(1)} %get-tuple-element.31.base, f32[5,128,128]{2,1,0:T(8,128)S(1)} %beside.4.product, s16[656,128]{1,0:T(8,128)(2,1)S(1)} %collective-permute-done.5.received), custom_call_target="tpu_custom_call" | custom-call | tf_op jit(solution)/shard_map/settle/pallas_call | solution.py:37
  22.5 0.1 collective-permute-start.8
  22.5 0.2 beside.5.product
  22.8 0.2 beside.3.product
  23.0 0.6 %collective-permute-done.7.received = s16[528,128]{1,0:T(8,128)(2,1)S(1)} collective-permute-done((s16[528,128]{1,0:T(8,128)(2,1)S(1)}, s16[528,128]{1,0:T(8,128)(2,1)S(1)}, u32[]{:S(2)}, u32[]{:S(2)}) %collective-permute-start.7) | collective-permute-done | bytes 135200 | tf_op jit(solution)/shard_map/ppermute | solution.py:578
  23.6 0.3 %settle.5.rest_1_ = s16[528,128]{1,0:T(8,128)(2,1)S(1)} custom-call(bf16[3,128,128]{2,1,0:T(8,128)(2,1)S(1)} %get-tuple-element.24.picked, f32[13,128,128]{2,1,0:T(8,128)S(1)} %get-tuple-element.31.base, f32[4,128,128]{2,1,0:T(8,128)S(1)} %beside.5.product, s16[528,128]{1,0:T(8,128)(2,1)S(1)} %collective-permute-done.7.received), custom_call_target="tpu_custom_call" | custom-call | tf_op jit(solution)/shard_map/settle/pallas_call | solution.py:37
  23.9 0.1 collective-permute-start.9
  24.0 1.3 %collective-permute-done.2.received = s16[528,128]{1,0:T(8,128)(2,1)S(1)} collective-permute-done((s16[528,128]{1,0:T(8,128)(2,1)S(1)}, s16[528,128]{1,0:T(8,128)(2,1)S(1)}, u32[]{:S(2)}, u32[]{:S(2)}) %collective-permute-start.2) | collective-permute-done | bytes 135200 | tf_op jit(solution)/shard_map/ppermute | solution.py:578
  25.3 0.3 %settle.3.rest_2_ = s16[528,128]{1,0:T(8,128)(2,1)S(1)} custom-call(bf16[3,128,128]{2,1,0:T(8,128)(2,1)S(1)} %get-tuple-element.24.picked, f32[13,128,128]{2,1,0:T(8,128)S(1)} %get-tuple-element.31.base, f32[4,128,128]{2,1,0:T(8,128)S(1)} %beside.3.product, s16[528,128]{1,0:T(8,128)(2,1)S(1)} %collective-permute-done.2.received), custom_call_target="tpu_custom_call" | custom-call | tf_op jit(solution)/shard_map/settle/pallas_call | solution.py:37
  25.6 0.1 collective-permute-start.3
  25.7 0.0 collective-permute-done.9.rest_4_
  25.7 0.0 collective-permute-done.8.rest_3_
  25.7 1.3 %finish_most.1 = (f32[13,128,256]{2,1,0:T(8,128)}, f32[2,128,256]{2,1,0:T(8,128)S(1)}, f32[2,128,256]{2,1,0:T(8,128)S(1)}) custom-call(bf16[13,128,256]{2,1,0:T(8,128)(2,1)S(1)} %copy-done, s16[656,128]{1,0:T(8,128)(2,1)S(1)} %settle.4.rest_0_, s16[528,128]{1,0:T(8,128)(2,1)S(1)} %settle.5.rest_1_, s16[528,128]{1,0:T(8,128)(2,1)S(1)} %settle.3.rest_2_, ...), custom_call_target="tpu_custom_call" | custom-call | tf_op jit(solution)/shard_map/finish_most/pallas_call | solution.py:37
  27.0 0.0 collective-permute-done.3.message
  27.0 1.1 %finish_last.1 = (f32[13,128,256]{2,1,0:T(8,128)}, f32[128,256]{1,0:T(8,128)}) custom-call(bf16[13,128,256]{2,1,0:T(8,128)(2,1)S(1)} %copy-done, s16[528,128]{1,0:T(8,128)(2,1)S(1)} %collective-permute-done.3.message, f32[128,256]{1,0:T(8,128)S(1)} %get-tuple-element.36.norm, ...), custom_call_target="tpu_custom_call", output_to_operand_aliasing={{0}: (5, {})} | custom-call | tf_op jit(solution)/shard_map/finish_last/pallas_call | solution.py:37
  (5 shorter events, 0.0 us)
Async XLA Ops:
  0.6 12.6 %copy-start = (bf16[13,128,256]{2,1,0:T(8,128)(2,1)S(1)}, bf16[13,128,256]{2,1,0:T(8,128)(2,1)}, u32[]{:S(2)}) copy-start(bf16[13,128,256]{2,1,0:T(8,128)(2,1)} %observed.5) | copy-start | bytes 2555908
  5.4 2.4 %collective-permute-start = (f32[13,128,128]{2,1,0:T(8,128)S(1)}, f32[13,128,128]{2,1,0:T(8,128)S(1)}, u32[]{:S(2)}, u32[]{:S(2)}) collective-permute-start(f32[13,128,128]{2,1,0:T(8,128)S(1)} %get-tuple-element.29), channel_id=1, source_target_pairs={{0,1},{1,0},{2,3},{3,2},{4,5},{5,4},{6,7},{7,6},{8,9},{9,8},{10,11... | collective-permute-start | bytes 2555912 | tf_op jit(solution)/shard_map/ppermute | solution.py:560
  8.2 6.4 %collective-permute-start.4 = (s16[656,128]{1,0:T(8,128)(2,1)S(1)}, s16[656,128]{1,0:T(8,128)(2,1)S(1)}, u32[]{:S(2)}, u32[]{:S(2)}) collective-permute-start(s16[656,128]{1,0:T(8,128)(2,1)S(1)} %get-tuple-element.37), channel_id=1, source_target_pairs={{0,2},{2,0},{4,6},{6,4},{8,10},{10,8},{12,14},{14,12},{5,1},{15,3}... | collective-permute-start | bytes 503816 | tf_op jit(solution)/shard_map/ppermute | solution.py:568
  11.2 5.5 %collective-permute-start.6 = (s16[528,128]{1,0:T(8,128)(2,1)S(1)}, s16[528,128]{1,0:T(8,128)(2,1)S(1)}, u32[]{:S(2)}, u32[]{:S(2)}) collective-permute-start(s16[528,128]{1,0:T(8,128)(2,1)S(1)} %get-tuple-element.40), channel_id=1, source_target_pairs={{0,2},{2,0},{4,6},{6,4},{8,10},{10,8},{12,14},{14,12},{5,1},{15,3}... | collective-permute-start | bytes 405512 | tf_op jit(solution)/shard_map/ppermute | solution.py:568
  11.3 7.1 %collective-permute-start.1 = (s16[528,128]{1,0:T(8,128)(2,1)S(1)}, s16[528,128]{1,0:T(8,128)(2,1)S(1)}, u32[]{:S(2)}, u32[]{:S(2)}) collective-permute-start(s16[528,128]{1,0:T(8,128)(2,1)S(1)} %get-tuple-element.33), channel_id=1, source_target_pairs={{0,2},{2,0},{4,6},{6,4},{8,10},{10,8},{12,14},{14,12},{5,1},{15,3}... | collective-permute-start | bytes 405512 | tf_op jit(solution)/shard_map/ppermute | solution.py:568
  14.6 7.5 %collective-permute-start.5 = (s16[656,128]{1,0:T(8,128)(2,1)S(1)}, s16[656,128]{1,0:T(8,128)(2,1)S(1)}, u32[]{:S(2)}, u32[]{:S(2)}) collective-permute-start(s16[656,128]{1,0:T(8,128)(2,1)S(1)} %relay.4), channel_id=1, source_target_pairs={{0,4},{2,14},{4,8},{6,2},{8,12},{10,6},{12,0},{14,10},{1,3},{3,1},... | collective-permute-start | bytes 503816 | tf_op jit(solution)/shard_map/ppermute | solution.py:578
  16.8 6.9 %collective-permute-start.7 = (s16[528,128]{1,0:T(8,128)(2,1)S(1)}, s16[528,128]{1,0:T(8,128)(2,1)S(1)}, u32[]{:S(2)}, u32[]{:S(2)}) collective-permute-start(s16[528,128]{1,0:T(8,128)(2,1)S(1)} %relay.5), channel_id=1, source_target_pairs={{0,4},{2,14},{4,8},{6,2},{8,12},{10,6},{12,0},{14,10},{1,3},{3,1},... | collective-permute-start | bytes 405512 | tf_op jit(solution)/shard_map/ppermute | solution.py:578
  18.4 6.9 %collective-permute-start.2 = (s16[528,128]{1,0:T(8,128)(2,1)S(1)}, s16[528,128]{1,0:T(8,128)(2,1)S(1)}, u32[]{:S(2)}, u32[]{:S(2)}) collective-permute-start(s16[528,128]{1,0:T(8,128)(2,1)S(1)} %relay.3), channel_id=1, source_target_pairs={{0,4},{2,14},{4,8},{6,2},{8,12},{10,6},{12,0},{14,10},{1,3},{3,1},... | collective-permute-start | bytes 405512 | tf_op jit(solution)/shard_map/ppermute | solution.py:578
  22.5 3.2 %collective-permute-start.8 = (s16[656,128]{1,0:T(8,128)(2,1)S(1)}, s16[656,128]{1,0:T(8,128)(2,1)S(1)}, u32[]{:S(2)}, u32[]{:S(2)}) collective-permute-start(s16[656,128]{1,0:T(8,128)(2,1)S(1)} %settle.4.rest_0_), channel_id=1, source_target_pairs={{0,1},{1,0},{2,3},{3,2},{4,5},{5,4},{6,7},{7,6},{8,9},{9,8},{10,11... | collective-permute-start | bytes 503816 | tf_op jit(solution)/shard_map/ppermute | solution.py:596
  23.9 1.7 %collective-permute-start.9 = (s16[528,128]{1,0:T(8,128)(2,1)S(1)}, s16[528,128]{1,0:T(8,128)(2,1)S(1)}, u32[]{:S(2)}, u32[]{:S(2)}) collective-permute-start(s16[528,128]{1,0:T(8,128)(2,1)S(1)} %settle.5.rest_1_), channel_id=1, source_target_pairs={{0,1},{1,0},{2,3},{3,2},{4,5},{5,4},{6,7},{7,6},{8,9},{9,8},{10,11... | collective-permute-start | bytes 405512 | tf_op jit(solution)/shard_map/ppermute | solution.py:596
  25.6 1.4 %collective-permute-start.3 = (s16[528,128]{1,0:T(8,128)(2,1)S(1)}, s16[528,128]{1,0:T(8,128)(2,1)S(1)}, u32[]{:S(2)}, u32[]{:S(2)}) collective-permute-start(s16[528,128]{1,0:T(8,128)(2,1)S(1)} %settle.3.rest_2_), channel_id=1, source_target_pairs={{0,1},{1,0},{2,3},{3,2},{4,5},{5,4},{6,7},{7,6},{8,9},{9,8},{10,11... | collective-permute-start | bytes 405512 | tf_op jit(solution)/shard_map/ppermute | solution.py:596

commit v13 on v11

--- a/solution.py
+++ b/solution.py
@@ -308,35 +308,33 @@
     pl.when(me != 0)(one)
 
 
-def share(spans, picked, keep, other, total, *rest):
-    messages, product = rest[:-1], rest[-1]
-    total[...] = keep[...] + other[...]
-
-    def coding(source):
-        for span, message in zip(spans, messages):
-            encode(source, span, message)
+def share(span, picked, keep, other, total, message, product):
+    units = span[1] - span[0]
+    total[...] = keep[slice(*span)] + other[slice(*span)]
 
     def summing():
         def put(m, value):
             product[m] = value
 
-        blurred(picked[1], total.shape[0], lambda m: total[m], put)
-        coding(product)
-
-    by_core(lambda: coding(total), summing)
-
-
-def centre(picked, total, base, term):
-    def into(out):
-        def put(m, value):
-            out[m] = value
-
-        return put
-
-    blurred(picked[0], total.shape[0], lambda m: total[m], into(base))
-    pl.when(lax.axis_index("band") != 0)(
-        lambda: blurred(picked[2], total.shape[0], lambda m: total[m], into(term))
-    )
+        blurred(picked[1], units, lambda m: total[m], put)
+        encode(product, (0, units), message)
+
+    by_core(lambda: encode(total, (0, units), message), summing)
+
+
+def centre(spans, picked, *rest):
+    totals, (base, term) = rest[:-2], rest[-2:]
+
+    def work(block, out):
+        for span, total in zip(spans, totals):
+
+            def put(m, value):
+                out[span[0] + m] = value
+
+            blurred(block, span[1] - span[0], lambda m: total[m], put)
+
+    work(picked[0], base)
+    pl.when(lax.axis_index("band") != 0)(lambda: work(picked[2], term))
 
 
 def relay(span, term, received, message, total):
@@ -558,15 +556,24 @@
     )
     work = [pltpu.VMEM(part.shape, f32)]
     other = lax.ppermute(send, "band", swap)
-    total, *sent = call(
-        functools.partial(share, spans),
-        (picked, keep, other),
-        [VMEM] * 3,
-        [part, *coded],
-        scratch=work,
-    )
-    near = [lax.ppermute(x, ("line", "band"), cores(partner, odd_up)) for x in sent]
-    base, term = call(centre, (picked, total), [VMEM] * 2, [part] * 2)
+    totals, near = [], []
+    for i, span in enumerate(spans):
+        planes = shape((span[1] - span[0], lines, half), f32)
+        total, message = call(
+            functools.partial(share, span),
+            (picked, keep, other),
+            [VMEM] * 3,
+            [planes, coded[i]],
+            scratch=[pltpu.VMEM(planes.shape, f32)],
+        )
+        totals.append(total)
+        near.append(lax.ppermute(message, ("line", "band"), cores(partner, odd_up)))
+    base, term = call(
+        functools.partial(centre, spans),
+        (picked, *totals),
+        [VMEM] * (1 + len(spans)),
+        [part] * 2,
+    )
     far, product = [], []
     for i, span in enumerate(spans):
         (message,) = call(

time: 28.4 us -> 27.9 us (0.982)
  waiting for transfers between devices: 4.87 us -> 4.51 us
    ppermute x3, waiting for transfers between devices: 1.02 us -> 0.66 us  [on_device(): near.append(lax.ppermute(message, ('line', 'band'), cores(partner, odd_up)))]
    ppermute x3, starting transfers between devices: 4.43 us -> 4.78 us  [on_device(): near.append(lax.ppermute(message, ('line', 'band'), cores(partner, odd_up)))]
    pallas_call x15 -> x17, Pallas kernels: 11.2 us -> 11.2 us  [call(): pl.pallas_call(kernel, in_specs=specs, out_specs=out_specs or [VMEM] * le...]
  transfers between devices with their start and end apart: 10 -> 10, of which waited for: 5 -> 5; matrix products, arithmetic and copies ran while one was open for 0% -> 0% of each run, Pallas kernels for 18% -> 19%
where the time goes in v13:
time: 27.9 us; the launch traced here: 27.7 us
  Pallas kernels  11.2 us (40%)
  starting transfers between devices  11.2 us (40%)
  waiting for transfers between devices  4.51 us (16%)
  between operations  0.83 us (3%)
    pallas_call x17, Pallas kernels, call(): pl.pallas_call(kernel, in_specs=specs, out_specs=out_specs or [VMEM] * le...  11.2 us
    ppermute x3, starting transfers between devices, on_device(): far.append(lax.ppermute(message, ('line', 'band'), cores(even_up, partner)))  5.39 us
    ppermute x3, starting transfers between devices, on_device(): near.append(lax.ppermute(message, ('line', 'band'), cores(partner, odd_up)))  4.78 us
    ppermute x3, waiting for transfers between devices, on_device(): far.append(lax.ppermute(message, ('line', 'band'), cores(even_up, partner)))  3.71 us
    ppermute x1, starting transfers between devices, on_device(): other = lax.ppermute(send, 'band', swap)  0.8 us
    ppermute x3, waiting for transfers between devices, on_device(): near.append(lax.ppermute(message, ('line', 'band'), cores(partner, odd_up)))  0.66 us
  transfers between devices with their start and end apart: 10, of which 5 were waited for; matrix products, arithmetic and copies ran while one was open for 0% of the time, Pallas kernels for 19%

profile of v13, /device:TPU:0, one launch (start us, length us, event | category | flops | bytes accessed | tf_op | source)
XLA Modules:
  0.0 27.7 jit_solution(8105038384295217707)
XLA Ops:
  0.6 4.6 %fold_other.1 = (f32[13,128,128]{2,1,0:T(8,128)S(1)}, f32[1,128,128]{2,1,0:T(8,128)S(1)}, bf16[115,128,256]{2,1,0:T(8,128)(2,1)S(1)}, f32[13,20]{1,0:T(8,128)S(1...) custom-call(s32[13]{0:T(128)} %start_in.3, s32[3]{0:T(128)} %offsets_in.1, bf16[13,20]{1,0:T(8,128)(2,1)} %values_in.1, ...), custom_call_target="tpu_custom_call" | custom-call | tf_op jit(solution)/shard_map/fold_other/pallas_call | solution.py:37
  5.2 0.8 %collective-permute-start = (f32[13,128,128]{2,1,0:T(8,128)S(1)}, f32[13,128,128]{2,1,0:T(8,128)S(1)}, u32[]{:S(2)}, u32[]{:S(2)}) collective-permute-start(f32[13,128,128]{2,1,0:T(8,128)S(1)} %get-tuple-element.30), channel_id=1, source_target_pairs={{0,1},{1,0},{2,3},{3,2},{4,5},{5,4},{6,7},{7,6},{8,9},{9,8},{10,11... | collective-permute-start | bytes 2555912 | tf_op jit(solution)/shard_map/ppermute | solution.py:558
  6.0 1.9 %fold_own.1.keep = f32[13,128,128]{2,1,0:T(8,128)S(1)} custom-call(s32[13]{0:T(128)} %start_in.3, f32[13,20]{1,0:T(8,128)S(1)} %get-tuple-element.26.wide, bf16[115,128,256]{2,1,0:T(8,128)(2,1)S(1)} %get-tuple-element.27.cube, bf16[512,256]{1,0:T(8,128)(2,1)S(1)} %get-tuple-element.28.table, f32[1,128,128]{2,1,0:T(8,128)S(1)} %get-tuple-element.29.middle), custom_call_target="tpu_custom_call" | custom-call | tf_op jit(solution)/shard_map/fold_own/pallas_call | solution.py:37
  7.9 0.1 collective-permute-done.other
  8.0 0.1 share.3
  8.2 2.7 %collective-permute-start.4 = (s16[656,128]{1,0:T(8,128)(2,1)S(1)}, s16[656,128]{1,0:T(8,128)(2,1)S(1)}, u32[]{:S(2)}, u32[]{:S(2)}) collective-permute-start(s16[656,128]{1,0:T(8,128)(2,1)S(1)} %get-tuple-element.39), channel_id=1, source_target_pairs={{0,2},{2,0},{4,6},{6,4},{8,10},{10,8},{12,14},{14,12},{5,1},{15,3}... | collective-permute-start | bytes 503816 | tf_op jit(solution)/shard_map/ppermute | solution.py:570
  10.8 0.1 share.4
  11.0 0.0 copy-start
  11.0 0.1 collective-permute-start.6
  11.0 0.1 share.5
  11.2 2.1 %collective-permute-start.1 = (s16[528,128]{1,0:T(8,128)(2,1)S(1)}, s16[528,128]{1,0:T(8,128)(2,1)S(1)}, u32[]{:S(2)}, u32[]{:S(2)}) collective-permute-start(s16[528,128]{1,0:T(8,128)(2,1)S(1)} %get-tuple-element.36), channel_id=1, source_target_pairs={{0,2},{2,0},{4,6},{6,4},{8,10},{10,8},{12,14},{14,12},{5,1},{15,3}... | collective-permute-start | bytes 405512 | tf_op jit(solution)/shard_map/ppermute | solution.py:570
  13.2 0.3 %centre.1 = (f32[13,128,128]{2,1,0:T(8,128)S(1)}, f32[13,128,128]{2,1,0:T(8,128)S(1)}) custom-call(bf16[3,128,128]{2,1,0:T(8,128)(2,1)S(1)} %get-tuple-element.25.picked, f32[5,128,128]{2,1,0:T(8,128)S(1)} %get-tuple-element.31.rest_0_, f32[4,128,128]{2,1,0:T(8,128)S(1)} %get-tuple-element.32.rest_1_, f32[4,128,128]{2,1,0:T(8,128)S(1)} %get-tuple-element.33.rest_2_), custom_call_target="tpu_custom_call" | custom-call | tf_op jit(solution)/shard_map/centre/pallas_call | solution.py:37
  13.5 0.7 %collective-permute-done.4.received.near = s16[656,128]{1,0:T(8,128)(2,1)S(1)} collective-permute-done((s16[656,128]{1,0:T(8,128)(2,1)S(1)}, s16[656,128]{1,0:T(8,128)(2,1)S(1)}, u32[]{:S(2)}, u32[]{:S(2)}) %collective-permute-start.4) | collective-permute-done | bytes 167968 | tf_op jit(solution)/shard_map/ppermute | solution.py:570
  14.2 2.1 %collective-permute-start.5 = (s16[656,128]{1,0:T(8,128)(2,1)S(1)}, s16[656,128]{1,0:T(8,128)(2,1)S(1)}, u32[]{:S(2)}, u32[]{:S(2)}) collective-permute-start(s16[656,128]{1,0:T(8,128)(2,1)S(1)} %relay.4), channel_id=1, source_target_pairs={{0,4},{2,14},{4,8},{6,2},{8,12},{10,6},{12,0},{14,10},{1,3},{3,1},... | collective-permute-start | bytes 503816 | tf_op jit(solution)/shard_map/ppermute | solution.py:583
  16.3 0.0 collective-permute-done.6.received.near
  16.3 1.6 %collective-permute-start.7 = (s16[528,128]{1,0:T(8,128)(2,1)S(1)}, s16[528,128]{1,0:T(8,128)(2,1)S(1)}, u32[]{:S(2)}, u32[]{:S(2)}) collective-permute-start(s16[528,128]{1,0:T(8,128)(2,1)S(1)} %relay.5), channel_id=1, source_target_pairs={{0,4},{2,14},{4,8},{6,2},{8,12},{10,6},{12,0},{14,10},{1,3},{3,1},... | collective-permute-start | bytes 405512 | tf_op jit(solution)/shard_map/ppermute | solution.py:583
  18.0 1.6 %collective-permute-start.2 = (s16[528,128]{1,0:T(8,128)(2,1)S(1)}, s16[528,128]{1,0:T(8,128)(2,1)S(1)}, u32[]{:S(2)}, u32[]{:S(2)}) collective-permute-start(s16[528,128]{1,0:T(8,128)(2,1)S(1)} %relay.3), channel_id=1, source_target_pairs={{0,4},{2,14},{4,8},{6,2},{8,12},{10,6},{12,0},{14,10},{1,3},{3,1},... | collective-permute-start | bytes 405512 | tf_op jit(solution)/shard_map/ppermute | solution.py:583
  19.6 0.2 beside.4.product
  19.9 1.8 %collective-permute-done.5.received = s16[656,128]{1,0:T(8,128)(2,1)S(1)} collective-permute-done((s16[656,128]{1,0:T(8,128)(2,1)S(1)}, s16[656,128]{1,0:T(8,128)(2,1)S(1)}, u32[]{:S(2)}, u32[]{:S(2)}) %collective-permute-start.5) | collective-permute-done | bytes 167968 | tf_op jit(solution)/shard_map/ppermute | solution.py:583
  21.7 0.3 %settle.4.rest_0_ = s16[656,128]{1,0:T(8,128)(2,1)S(1)} custom-call(bf16[3,128,128]{2,1,0:T(8,128)(2,1)S(1)} %get-tuple-element.25.picked, f32[13,128,128]{2,1,0:T(8,128)S(1)} %get-tuple-element.34.base, f32[5,128,128]{2,1,0:T(8,128)S(1)} %beside.4.product, s16[656,128]{1,0:T(8,128)(2,1)S(1)} %collective-permute-done.5.received), custom_call_target="tpu_custom_call" | custom-call | tf_op jit(solution)/shard_map/settle/pallas_call | solution.py:37
  22.0 0.1 collective-permute-start.8
  22.1 0.2 beside.5.product
  22.4 0.9 %collective-permute-done.7.received = s16[528,128]{1,0:T(8,128)(2,1)S(1)} collective-permute-done((s16[528,128]{1,0:T(8,128)(2,1)S(1)}, s16[528,128]{1,0:T(8,128)(2,1)S(1)}, u32[]{:S(2)}, u32[]{:S(2)}) %collective-permute-start.7) | collective-permute-done | bytes 135200 | tf_op jit(solution)/shard_map/ppermute | solution.py:583
  23.2 0.3 %settle.5.rest_1_ = s16[528,128]{1,0:T(8,128)(2,1)S(1)} custom-call(bf16[3,128,128]{2,1,0:T(8,128)(2,1)S(1)} %get-tuple-element.25.picked, f32[13,128,128]{2,1,0:T(8,128)S(1)} %get-tuple-element.34.base, f32[4,128,128]{2,1,0:T(8,128)S(1)} %beside.5.product, s16[528,128]{1,0:T(8,128)(2,1)S(1)} %collective-permute-done.7.received), custom_call_target="tpu_custom_call" | custom-call | tf_op jit(solution)/shard_map/settle/pallas_call | solution.py:37
  23.5 0.1 collective-permute-start.9
  23.6 0.2 beside.3.product
  23.8 1.0 %collective-permute-done.2.received = s16[528,128]{1,0:T(8,128)(2,1)S(1)} collective-permute-done((s16[528,128]{1,0:T(8,128)(2,1)S(1)}, s16[528,128]{1,0:T(8,128)(2,1)S(1)}, u32[]{:S(2)}, u32[]{:S(2)}) %collective-permute-start.2) | collective-permute-done | bytes 135200 | tf_op jit(solution)/shard_map/ppermute | solution.py:583
  24.9 0.3 %settle.3.rest_2_ = s16[528,128]{1,0:T(8,128)(2,1)S(1)} custom-call(bf16[3,128,128]{2,1,0:T(8,128)(2,1)S(1)} %get-tuple-element.25.picked, f32[13,128,128]{2,1,0:T(8,128)S(1)} %get-tuple-element.34.base, f32[4,128,128]{2,1,0:T(8,128)S(1)} %beside.3.product, s16[528,128]{1,0:T(8,128)(2,1)S(1)} %collective-permute-done.2.received), custom_call_target="tpu_custom_call" | custom-call | tf_op jit(solution)/shard_map/settle/pallas_call | solution.py:37
  25.2 0.1 collective-permute-start.3
  25.3 0.0 collective-permute-done.9.rest_4_
  25.3 1.3 %finish_most.1 = (f32[13,128,256]{2,1,0:T(8,128)}, f32[3,128,256]{2,1,0:T(8,128)S(1)}, f32[3,128,256]{2,1,0:T(8,128)S(1)}) custom-call(bf16[13,128,256]{2,1,0:T(8,128)(2,1)S(1)} %copy-done, s16[656,128]{1,0:T(8,128)(2,1)S(1)} %settle.4.rest_0_, s16[528,128]{1,0:T(8,128)(2,1)S(1)} %settle.5.rest_1_, s16[528,128]{1,0:T(8,128)(2,1)S(1)} %settle.3.rest_2_, ...), custom_call_target="tpu_custom_call" | custom-call | tf_op jit(solution)/shard_map/finish_most/pallas_call | solution.py:37
  26.6 1.1 %finish_last.1 = (f32[13,128,256]{2,1,0:T(8,128)}, f32[128,256]{1,0:T(8,128)}) custom-call(bf16[13,128,256]{2,1,0:T(8,128)(2,1)S(1)} %copy-done, s16[528,128]{1,0:T(8,128)(2,1)S(1)} %collective-permute-done.3.message, f32[3,128,256]{2,1,0:T(8,128)S(1)} %get-tuple-element.45.own, ...), custom_call_target="tpu_custom_call", output_to_operand_aliasing={{0}: (4, {})} | custom-call | tf_op jit(solution)/shard_map/finish_last/pallas_call | solution.py:37
  (7 shorter events, 0.0 us)
Async XLA Ops:
  5.2 2.8 %collective-permute-start = (f32[13,128,128]{2,1,0:T(8,128)S(1)}, f32[13,128,128]{2,1,0:T(8,128)S(1)}, u32[]{:S(2)}, u32[]{:S(2)}) collective-permute-start(f32[13,128,128]{2,1,0:T(8,128)S(1)} %get-tuple-element.30), channel_id=1, source_target_pairs={{0,1},{1,0},{2,3},{3,2},{4,5},{5,4},{6,7},{7,6},{8,9},{9,8},{10,11... | collective-permute-start | bytes 2555912 | tf_op jit(solution)/shard_map/ppermute | solution.py:558
  8.2 6.0 %collective-permute-start.4 = (s16[656,128]{1,0:T(8,128)(2,1)S(1)}, s16[656,128]{1,0:T(8,128)(2,1)S(1)}, u32[]{:S(2)}, u32[]{:S(2)}) collective-permute-start(s16[656,128]{1,0:T(8,128)(2,1)S(1)} %get-tuple-element.39), channel_id=1, source_target_pairs={{0,2},{2,0},{4,6},{6,4},{8,10},{10,8},{12,14},{14,12},{5,1},{15,3}... | collective-permute-start | bytes 503816 | tf_op jit(solution)/shard_map/ppermute | solution.py:570
  11.0 14.3 %copy-start = (bf16[13,128,256]{2,1,0:T(8,128)(2,1)S(1)}, bf16[13,128,256]{2,1,0:T(8,128)(2,1)}, u32[]{:S(2)}) copy-start(bf16[13,128,256]{2,1,0:T(8,128)(2,1)} %observed.3) | copy-start | bytes 2555908
  11.0 5.4 %collective-permute-start.6 = (s16[528,128]{1,0:T(8,128)(2,1)S(1)}, s16[528,128]{1,0:T(8,128)(2,1)S(1)}, u32[]{:S(2)}, u32[]{:S(2)}) collective-permute-start(s16[528,128]{1,0:T(8,128)(2,1)S(1)} %get-tuple-element.42), channel_id=1, source_target_pairs={{0,2},{2,0},{4,6},{6,4},{8,10},{10,8},{12,14},{14,12},{5,1},{15,3}... | collective-permute-start | bytes 405512 | tf_op jit(solution)/shard_map/ppermute | solution.py:570
  11.2 6.8 %collective-permute-start.1 = (s16[528,128]{1,0:T(8,128)(2,1)S(1)}, s16[528,128]{1,0:T(8,128)(2,1)S(1)}, u32[]{:S(2)}, u32[]{:S(2)}) collective-permute-start(s16[528,128]{1,0:T(8,128)(2,1)S(1)} %get-tuple-element.36), channel_id=1, source_target_pairs={{0,2},{2,0},{4,6},{6,4},{8,10},{10,8},{12,14},{14,12},{5,1},{15,3}... | collective-permute-start | bytes 405512 | tf_op jit(solution)/shard_map/ppermute | solution.py:570
  14.2 7.5 %collective-permute-start.5 = (s16[656,128]{1,0:T(8,128)(2,1)S(1)}, s16[656,128]{1,0:T(8,128)(2,1)S(1)}, u32[]{:S(2)}, u32[]{:S(2)}) collective-permute-start(s16[656,128]{1,0:T(8,128)(2,1)S(1)} %relay.4), channel_id=1, source_target_pairs={{0,4},{2,14},{4,8},{6,2},{8,12},{10,6},{12,0},{14,10},{1,3},{3,1},... | collective-permute-start | bytes 503816 | tf_op jit(solution)/shard_map/ppermute | solution.py:583
  16.3 6.9 %collective-permute-start.7 = (s16[528,128]{1,0:T(8,128)(2,1)S(1)}, s16[528,128]{1,0:T(8,128)(2,1)S(1)}, u32[]{:S(2)}, u32[]{:S(2)}) collective-permute-start(s16[528,128]{1,0:T(8,128)(2,1)S(1)} %relay.5), channel_id=1, source_target_pairs={{0,4},{2,14},{4,8},{6,2},{8,12},{10,6},{12,0},{14,10},{1,3},{3,1},... | collective-permute-start | bytes 405512 | tf_op jit(solution)/shard_map/ppermute | solution.py:583
  18.0 6.9 %collective-permute-start.2 = (s16[528,128]{1,0:T(8,128)(2,1)S(1)}, s16[528,128]{1,0:T(8,128)(2,1)S(1)}, u32[]{:S(2)}, u32[]{:S(2)}) collective-permute-start(s16[528,128]{1,0:T(8,128)(2,1)S(1)} %relay.3), channel_id=1, source_target_pairs={{0,4},{2,14},{4,8},{6,2},{8,12},{10,6},{12,0},{14,10},{1,3},{3,1},... | collective-permute-start | bytes 405512 | tf_op jit(solution)/shard_map/ppermute | solution.py:583
  22.0 3.2 %collective-permute-start.8 = (s16[656,128]{1,0:T(8,128)(2,1)S(1)}, s16[656,128]{1,0:T(8,128)(2,1)S(1)}, u32[]{:S(2)}, u32[]{:S(2)}) collective-permute-start(s16[656,128]{1,0:T(8,128)(2,1)S(1)} %settle.4.rest_0_), channel_id=1, source_target_pairs={{0,1},{1,0},{2,3},{3,2},{4,5},{5,4},{6,7},{7,6},{8,9},{9,8},{10,11... | collective-permute-start | bytes 503816 | tf_op jit(solution)/shard_map/ppermute | solution.py:601
  23.5 1.7 %collective-permute-start.9 = (s16[528,128]{1,0:T(8,128)(2,1)S(1)}, s16[528,128]{1,0:T(8,128)(2,1)S(1)}, u32[]{:S(2)}, u32[]{:S(2)}) collective-permute-start(s16[528,128]{1,0:T(8,128)(2,1)S(1)} %settle.5.rest_1_), channel_id=1, source_target_pairs={{0,1},{1,0},{2,3},{3,2},{4,5},{5,4},{6,7},{7,6},{8,9},{9,8},{10,11... | collective-permute-start | bytes 405512 | tf_op jit(solution)/shard_map/ppermute | solution.py:601
  25.2 1.5 %collective-permute-start.3 = (s16[528,128]{1,0:T(8,128)(2,1)S(1)}, s16[528,128]{1,0:T(8,128)(2,1)S(1)}, u32[]{:S(2)}, u32[]{:S(2)}) collective-permute-start(s16[528,128]{1,0:T(8,128)(2,1)S(1)} %settle.3.rest_2_), channel_id=1, source_target_pairs={{0,1},{1,0},{2,3},{3,2},{4,5},{5,4},{6,7},{7,6},{8,9},{9,8},{10,11... | collective-permute-start | bytes 405512 | tf_op jit(solution)/shard_map/ppermute | solution.py:601

commit v14 on v13

--- a/solution.py
+++ b/solution.py
@@ -135,11 +135,11 @@
     return made.reshape(planes, lines, cols)
 
 
-def spread_out(made, out):
+def spread_out(made, put):
     half = made.shape[2] // 2
     for i in range(made.shape[0]):
-        out[2 * i] = made[i, :, :half]
-        out[2 * i + 1] = made[i, :, half:]
+        put(2 * i, made[i, :, :half])
+        put(2 * i + 1, made[i, :, half:])
 
 
 def fold_other(
@@ -151,6 +151,7 @@
     along_blocks_in,
     cube_in,
     send,
+    send_rest,
     middle,
     cube,
     wide,
@@ -226,11 +227,18 @@
     arrived = sum_windows(planes + odd, plane_of, start, weights, cube, folded, order, ready)
     ready(arrived, chunks)
     made = across(folded[...], table[...])
-    spread_out(made[:planes], send)
+
+    def put(n, value):
+        if n < send.shape[0]:
+            send[n] = value
+        else:
+            send_rest[n - send.shape[0]] = value
+
+    spread_out(made[:planes], put)
     if odd:
         left, right = made[planes, :, :half], made[planes, :, half:]
         middle[0] = jnp.where(me == 0, left, right)
-        send[units - 1] = jnp.where(me == 0, right, left)
+        put(units - 1, jnp.where(me == 0, right, left))
 
 
 def fold_own(start_in, wide, cube, table, middle, keep, start, weights, folded, order, sems):
@@ -245,7 +253,11 @@
         copy.wait()
     base = lax.axis_index("band") * (planes + odd)
     sum_windows(planes, lambda i: base + i, start, weights, cube, folded, order)
-    spread_out(across(folded[...], table[...]), keep)
+
+    def put(n, value):
+        keep[n] = value
+
+    spread_out(across(folded[...], table[...]), put)
     if odd:
         keep[units - 1] = middle[0]
 
@@ -308,9 +320,9 @@
     pl.when(me != 0)(one)
 
 
-def share(span, picked, keep, other, total, message, product):
+def share(span, begin, picked, keep, other, total, message, product):
     units = span[1] - span[0]
-    total[...] = keep[slice(*span)] + other[slice(*span)]
+    total[...] = keep[slice(*span)] + other[span[0] - begin : span[1] - begin]
 
     def summing():
         def put(m, value):
@@ -522,11 +534,13 @@
     planes, odd, _ = ownership(count)
     wide = shape(resp_values.shape, f32)
     table = shape((2 * cols, cols), across_kernels.dtype)
-    send, middle, local, wide, table, picked = call(
+    first = spans[-1][0]
+    parts = [shape((n, lines, half), f32) for n in (first, units - first)]
+    *sent, middle, local, wide, table, picked = call(
         fold_other,
         inputs,
         [HBM] * len(inputs),
-        [part, shape((1, lines, half), f32), cube, wide, table, along_kernels],
+        [*parts, shape((1, lines, half), f32), cube, wide, table, along_kernels],
         scratch=[
             pltpu.SMEM(resp_start.shape, jnp.int32),
             pltpu.SMEM(across_offsets.shape, jnp.int32),
@@ -555,13 +569,13 @@
         ],
     )
     work = [pltpu.VMEM(part.shape, f32)]
-    other = lax.ppermute(send, "band", swap)
+    other = [lax.ppermute(x, "band", swap) for x in sent]
     totals, near = [], []
     for i, span in enumerate(spans):
         planes = shape((span[1] - span[0], lines, half), f32)
         total, message = call(
-            functools.partial(share, span),
-            (picked, keep, other),
+            functools.partial(share, span, first * (span[0] >= first)),
+            (picked, keep, other[span[0] >= first]),
             [VMEM] * 3,
             [planes, coded[i]],
             scratch=[pltpu.VMEM(planes.shape, f32)],

time: 27.9 us -> 28.1 us (level)
    ppermute x1 -> x2, starting transfers between devices: 0.8 us -> 0.71 us  [on_device(): other = [lax.ppermute(x, 'band', swap) for x in sent]]
  transfers between devices with their start and end apart: 10 -> 11, of which waited for: 5 -> 4; matrix products, arithmetic and copies ran while one was open for 0% -> 0% of each run, Pallas kernels for 19% -> 20%
where the time goes in v14:
time: 28.1 us; the launch traced here: 27.9 us
  Pallas kernels  11.4 us (41%)
  starting transfers between devices  11.3 us (40%)
  waiting for transfers between devices  4.36 us (16%)
  between operations  0.84 us (3%)
    pallas_call x17, Pallas kernels, call(): pl.pallas_call(kernel, in_specs=specs, out_specs=out_specs or [VMEM] * le...  11.4 us
    ppermute x3, starting transfers between devices, on_device(): far.append(lax.ppermute(message, ('line', 'band'), cores(even_up, partner)))  5.39 us
    ppermute x3, starting transfers between devices, on_device(): near.append(lax.ppermute(message, ('line', 'band'), cores(partner, odd_up)))  5 us
    ppermute x3, waiting for transfers between devices, on_device(): far.append(lax.ppermute(message, ('line', 'band'), cores(even_up, partner)))  3.71 us
    ppermute x2, starting transfers between devices, on_device(): other = [lax.ppermute(x, 'band', swap) for x in sent]  0.71 us
    ppermute x3, waiting for transfers between devices, on_device(): near.append(lax.ppermute(message, ('line', 'band'), cores(partner, odd_up)))  0.63 us
  transfers between devices with their start and end apart: 11, of which 4 were waited for; matrix products, arithmetic and copies ran while one was open for 0% of the time, Pallas kernels for 20%

profile of v14, /device:TPU:0, one launch (start us, length us, event | category | flops | bytes accessed | tf_op | source)
XLA Modules:
  0.0 27.9 jit_solution(3526448982037138382)
XLA Ops:
  0.6 4.9 %fold_other.1 = (f32[9,128,128]{2,1,0:T(8,128)S(1)}, f32[4,128,128]{2,1,0:T(8,128)S(1)}, f32[1,128,128]{2,1,0:T(8,128)S(1)}, bf16[115,128,256]{2,1,0:T(8,128)(2,...) custom-call(s32[13]{0:T(128)} %start_in.3, s32[3]{0:T(128)} %offsets_in.1, ...), custom_call_target="tpu_custom_call" | custom-call | tf_op jit(solution)/shard_map/fold_other/pallas_call | solution.py:37
  5.5 0.6 %collective-permute-start = (f32[9,128,128]{2,1,0:T(8,128)S(1)}, f32[9,128,128]{2,1,0:T(8,128)S(1)}, u32[]{:S(2)}, u32[]{:S(2)}) collective-permute-start(f32[9,128,128]{2,1,0:T(8,128)S(1)} %get-tuple-element.31), channel_id=1, source_target_pairs={{0,1},{1,0},{2,3},{3,2},{4,5},{5,4},{6,7},{7,6},{8,9},{9,8},{10,11... | collective-permute-start | bytes 1769480 | tf_op jit(solution)/shard_map/ppermute | solution.py:572
  6.1 0.1 collective-permute-start.1
  6.2 1.7 %fold_own.1.keep = f32[13,128,128]{2,1,0:T(8,128)S(1)} custom-call(s32[13]{0:T(128)} %start_in.3, f32[13,20]{1,0:T(8,128)S(1)} %get-tuple-element.27.wide, bf16[115,128,256]{2,1,0:T(8,128)(2,1)S(1)} %get-tuple-element.28.cube, bf16[512,256]{1,0:T(8,128)(2,1)S(1)} %get-tuple-element.29.table, f32[1,128,128]{2,1,0:T(8,128)S(1)} %get-tuple-element.30.middle), custom_call_target="tpu_custom_call" | custom-call | tf_op jit(solution)/shard_map/fold_own/pallas_call | solution.py:37
  8.0 0.0 collective-permute-done.other
  8.0 0.2 share.3
  8.1 2.9 %collective-permute-start.5 = (s16[656,128]{1,0:T(8,128)(2,1)S(1)}, s16[656,128]{1,0:T(8,128)(2,1)S(1)}, u32[]{:S(2)}, u32[]{:S(2)}) collective-permute-start(s16[656,128]{1,0:T(8,128)(2,1)S(1)} %get-tuple-element.41), channel_id=1, source_target_pairs={{0,2},{2,0},{4,6},{6,4},{8,10},{10,8},{12,14},{14,12},{5,1},{15,3}... | collective-permute-start | bytes 503816 | tf_op jit(solution)/shard_map/ppermute | solution.py:584
  11.0 0.1 share.4
  11.2 0.0 copy-start
  11.2 0.1 collective-permute-start.7
  11.2 0.0 collective-permute-done.1.other
  11.2 0.1 share.5
  11.4 2.1 %collective-permute-start.2 = (s16[528,128]{1,0:T(8,128)(2,1)S(1)}, s16[528,128]{1,0:T(8,128)(2,1)S(1)}, u32[]{:S(2)}, u32[]{:S(2)}) collective-permute-start(s16[528,128]{1,0:T(8,128)(2,1)S(1)} %get-tuple-element.38), channel_id=1, source_target_pairs={{0,2},{2,0},{4,6},{6,4},{8,10},{10,8},{12,14},{14,12},{5,1},{15,3}... | collective-permute-start | bytes 405512 | tf_op jit(solution)/shard_map/ppermute | solution.py:584
  13.4 0.3 %centre.1 = (f32[13,128,128]{2,1,0:T(8,128)S(1)}, f32[13,128,128]{2,1,0:T(8,128)S(1)}) custom-call(bf16[3,128,128]{2,1,0:T(8,128)(2,1)S(1)} %get-tuple-element.26.picked, f32[5,128,128]{2,1,0:T(8,128)S(1)} %get-tuple-element.32.rest_0_, f32[4,128,128]{2,1,0:T(8,128)S(1)} %get-tuple-element.33.rest_1_, f32[4,128,128]{2,1,0:T(8,128)S(1)} %get-tuple-element.35.rest_2_), custom_call_target="tpu_custom_call" | custom-call | tf_op jit(solution)/shard_map/centre/pallas_call | solution.py:37
  13.7 0.6 %collective-permute-done.5.received.near = s16[656,128]{1,0:T(8,128)(2,1)S(1)} collective-permute-done((s16[656,128]{1,0:T(8,128)(2,1)S(1)}, s16[656,128]{1,0:T(8,128)(2,1)S(1)}, u32[]{:S(2)}, u32[]{:S(2)}) %collective-permute-start.5) | collective-permute-done | bytes 167968 | tf_op jit(solution)/shard_map/ppermute | solution.py:584
  14.4 2.1 %collective-permute-start.6 = (s16[656,128]{1,0:T(8,128)(2,1)S(1)}, s16[656,128]{1,0:T(8,128)(2,1)S(1)}, u32[]{:S(2)}, u32[]{:S(2)}) collective-permute-start(s16[656,128]{1,0:T(8,128)(2,1)S(1)} %relay.4), channel_id=1, source_target_pairs={{0,4},{2,14},{4,8},{6,2},{8,12},{10,6},{12,0},{14,10},{1,3},{3,1},... | collective-permute-start | bytes 503816 | tf_op jit(solution)/shard_map/ppermute | solution.py:597
  16.5 1.6 %collective-permute-start.8 = (s16[528,128]{1,0:T(8,128)(2,1)S(1)}, s16[528,128]{1,0:T(8,128)(2,1)S(1)}, u32[]{:S(2)}, u32[]{:S(2)}) collective-permute-start(s16[528,128]{1,0:T(8,128)(2,1)S(1)} %relay.5), channel_id=1, source_target_pairs={{0,4},{2,14},{4,8},{6,2},{8,12},{10,6},{12,0},{14,10},{1,3},{3,1},... | collective-permute-start | bytes 405512 | tf_op jit(solution)/shard_map/ppermute | solution.py:597
  18.2 1.6 %collective-permute-start.3 = (s16[528,128]{1,0:T(8,128)(2,1)S(1)}, s16[528,128]{1,0:T(8,128)(2,1)S(1)}, u32[]{:S(2)}, u32[]{:S(2)}) collective-permute-start(s16[528,128]{1,0:T(8,128)(2,1)S(1)} %relay.3), channel_id=1, source_target_pairs={{0,4},{2,14},{4,8},{6,2},{8,12},{10,6},{12,0},{14,10},{1,3},{3,1},... | collective-permute-start | bytes 405512 | tf_op jit(solution)/shard_map/ppermute | solution.py:597
  19.8 0.2 beside.4.product
  20.1 1.8 %collective-permute-done.6.received = s16[656,128]{1,0:T(8,128)(2,1)S(1)} collective-permute-done((s16[656,128]{1,0:T(8,128)(2,1)S(1)}, s16[656,128]{1,0:T(8,128)(2,1)S(1)}, u32[]{:S(2)}, u32[]{:S(2)}) %collective-permute-start.6) | collective-permute-done | bytes 167968 | tf_op jit(solution)/shard_map/ppermute | solution.py:597
  21.9 0.3 %settle.4.rest_0_ = s16[656,128]{1,0:T(8,128)(2,1)S(1)} custom-call(bf16[3,128,128]{2,1,0:T(8,128)(2,1)S(1)} %get-tuple-element.26.picked, f32[13,128,128]{2,1,0:T(8,128)S(1)} %get-tuple-element.36.base, f32[5,128,128]{2,1,0:T(8,128)S(1)} %beside.4.product, s16[656,128]{1,0:T(8,128)(2,1)S(1)} %collective-permute-done.6.received), custom_call_target="tpu_custom_call" | custom-call | tf_op jit(solution)/shard_map/settle/pallas_call | solution.py:37
  22.2 0.1 collective-permute-start.9
  22.3 0.2 beside.5.product
  22.5 0.9 %collective-permute-done.8.received = s16[528,128]{1,0:T(8,128)(2,1)S(1)} collective-permute-done((s16[528,128]{1,0:T(8,128)(2,1)S(1)}, s16[528,128]{1,0:T(8,128)(2,1)S(1)}, u32[]{:S(2)}, u32[]{:S(2)}) %collective-permute-start.8) | collective-permute-done | bytes 135200 | tf_op jit(solution)/shard_map/ppermute | solution.py:597
  23.4 0.3 %settle.5.rest_1_ = s16[528,128]{1,0:T(8,128)(2,1)S(1)} custom-call(bf16[3,128,128]{2,1,0:T(8,128)(2,1)S(1)} %get-tuple-element.26.picked, f32[13,128,128]{2,1,0:T(8,128)S(1)} %get-tuple-element.36.base, f32[4,128,128]{2,1,0:T(8,128)S(1)} %beside.5.product, s16[528,128]{1,0:T(8,128)(2,1)S(1)} %collective-permute-done.8.received), custom_call_target="tpu_custom_call" | custom-call | tf_op jit(solution)/shard_map/settle/pallas_call | solution.py:37
  23.7 0.1 collective-permute-start.10
  23.8 0.2 beside.3.product
  24.0 1.0 %collective-permute-done.3.received = s16[528,128]{1,0:T(8,128)(2,1)S(1)} collective-permute-done((s16[528,128]{1,0:T(8,128)(2,1)S(1)}, s16[528,128]{1,0:T(8,128)(2,1)S(1)}, u32[]{:S(2)}, u32[]{:S(2)}) %collective-permute-start.3) | collective-permute-done | bytes 135200 | tf_op jit(solution)/shard_map/ppermute | solution.py:597
  25.1 0.3 %settle.3.rest_2_ = s16[528,128]{1,0:T(8,128)(2,1)S(1)} custom-call(bf16[3,128,128]{2,1,0:T(8,128)(2,1)S(1)} %get-tuple-element.26.picked, f32[13,128,128]{2,1,0:T(8,128)S(1)} %get-tuple-element.36.base, f32[4,128,128]{2,1,0:T(8,128)S(1)} %beside.3.product, s16[528,128]{1,0:T(8,128)(2,1)S(1)} %collective-permute-done.3.received), custom_call_target="tpu_custom_call" | custom-call | tf_op jit(solution)/shard_map/settle/pallas_call | solution.py:37
  25.4 0.1 collective-permute-start.4
  25.5 1.3 %finish_most.1 = (f32[13,128,256]{2,1,0:T(8,128)}, f32[3,128,256]{2,1,0:T(8,128)S(1)}, f32[3,128,256]{2,1,0:T(8,128)S(1)}) custom-call(bf16[13,128,256]{2,1,0:T(8,128)(2,1)S(1)} %copy-done, s16[656,128]{1,0:T(8,128)(2,1)S(1)} %settle.4.rest_0_, s16[528,128]{1,0:T(8,128)(2,1)S(1)} %settle.5.rest_1_, s16[528,128]{1,0:T(8,128)(2,1)S(1)} %settle.3.rest_2_, ...), custom_call_target="tpu_custom_call" | custom-call | tf_op jit(solution)/shard_map/finish_most/pallas_call | solution.py:37
  26.8 1.1 %finish_last.1 = (f32[13,128,256]{2,1,0:T(8,128)}, f32[128,256]{1,0:T(8,128)}) custom-call(bf16[13,128,256]{2,1,0:T(8,128)(2,1)S(1)} %copy-done, s16[528,128]{1,0:T(8,128)(2,1)S(1)} %collective-permute-done.4.message, f32[3,128,256]{2,1,0:T(8,128)S(1)} %get-tuple-element.47.own, ...), custom_call_target="tpu_custom_call", output_to_operand_aliasing={{0}: (4, {})} | custom-call | tf_op jit(solution)/shard_map/finish_last/pallas_call | solution.py:37
  (9 shorter events, 0.1 us)
Async XLA Ops:
  5.5 2.5 %collective-permute-start = (f32[9,128,128]{2,1,0:T(8,128)S(1)}, f32[9,128,128]{2,1,0:T(8,128)S(1)}, u32[]{:S(2)}, u32[]{:S(2)}) collective-permute-start(f32[9,128,128]{2,1,0:T(8,128)S(1)} %get-tuple-element.31), channel_id=1, source_target_pairs={{0,1},{1,0},{2,3},{3,2},{4,5},{5,4},{6,7},{7,6},{8,9},{9,8},{10,11... | collective-permute-start | bytes 1769480 | tf_op jit(solution)/shard_map/ppermute | solution.py:572
  6.1 5.1 %collective-permute-start.1 = (f32[4,128,128]{2,1,0:T(8,128)S(1)}, f32[4,128,128]{2,1,0:T(8,128)S(1)}, u32[]{:S(2)}, u32[]{:S(2)}) collective-permute-start(f32[4,128,128]{2,1,0:T(8,128)S(1)} %get-tuple-element.34), channel_id=1, source_target_pairs={{0,1},{1,0},{2,3},{3,2},{4,5},{5,4},{6,7},{7,6},{8,9},{9,8},{10,11... | collective-permute-start | bytes 786440 | tf_op jit(solution)/shard_map/ppermute | solution.py:572
  8.1 6.2 %collective-permute-start.5 = (s16[656,128]{1,0:T(8,128)(2,1)S(1)}, s16[656,128]{1,0:T(8,128)(2,1)S(1)}, u32[]{:S(2)}, u32[]{:S(2)}) collective-permute-start(s16[656,128]{1,0:T(8,128)(2,1)S(1)} %get-tuple-element.41), channel_id=1, source_target_pairs={{0,2},{2,0},{4,6},{6,4},{8,10},{10,8},{12,14},{14,12},{5,1},{15,3}... | collective-permute-start | bytes 503816 | tf_op jit(solution)/shard_map/ppermute | solution.py:584
  11.2 14.3 %copy-start = (bf16[13,128,256]{2,1,0:T(8,128)(2,1)S(1)}, bf16[13,128,256]{2,1,0:T(8,128)(2,1)}, u32[]{:S(2)}) copy-start(bf16[13,128,256]{2,1,0:T(8,128)(2,1)} %observed.3) | copy-start | bytes 2555908
  11.2 5.4 %collective-permute-start.7 = (s16[528,128]{1,0:T(8,128)(2,1)S(1)}, s16[528,128]{1,0:T(8,128)(2,1)S(1)}, u32[]{:S(2)}, u32[]{:S(2)}) collective-permute-start(s16[528,128]{1,0:T(8,128)(2,1)S(1)} %get-tuple-element.44), channel_id=1, source_target_pairs={{0,2},{2,0},{4,6},{6,4},{8,10},{10,8},{12,14},{14,12},{5,1},{15,3}... | collective-permute-start | bytes 405512 | tf_op jit(solution)/shard_map/ppermute | solution.py:584
  11.4 6.8 %collective-permute-start.2 = (s16[528,128]{1,0:T(8,128)(2,1)S(1)}, s16[528,128]{1,0:T(8,128)(2,1)S(1)}, u32[]{:S(2)}, u32[]{:S(2)}) collective-permute-start(s16[528,128]{1,0:T(8,128)(2,1)S(1)} %get-tuple-element.38), channel_id=1, source_target_pairs={{0,2},{2,0},{4,6},{6,4},{8,10},{10,8},{12,14},{14,12},{5,1},{15,3}... | collective-permute-start | bytes 405512 | tf_op jit(solution)/shard_map/ppermute | solution.py:584
  14.4 7.5 %collective-permute-start.6 = (s16[656,128]{1,0:T(8,128)(2,1)S(1)}, s16[656,128]{1,0:T(8,128)(2,1)S(1)}, u32[]{:S(2)}, u32[]{:S(2)}) collective-permute-start(s16[656,128]{1,0:T(8,128)(2,1)S(1)} %relay.4), channel_id=1, source_target_pairs={{0,4},{2,14},{4,8},{6,2},{8,12},{10,6},{12,0},{14,10},{1,3},{3,1},... | collective-permute-start | bytes 503816 | tf_op jit(solution)/shard_map/ppermute | solution.py:597
  16.5 6.9 %collective-permute-start.8 = (s16[528,128]{1,0:T(8,128)(2,1)S(1)}, s16[528,128]{1,0:T(8,128)(2,1)S(1)}, u32[]{:S(2)}, u32[]{:S(2)}) collective-permute-start(s16[528,128]{1,0:T(8,128)(2,1)S(1)} %relay.5), channel_id=1, source_target_pairs={{0,4},{2,14},{4,8},{6,2},{8,12},{10,6},{12,0},{14,10},{1,3},{3,1},... | collective-permute-start | bytes 405512 | tf_op jit(solution)/shard_map/ppermute | solution.py:597
  18.2 6.9 %collective-permute-start.3 = (s16[528,128]{1,0:T(8,128)(2,1)S(1)}, s16[528,128]{1,0:T(8,128)(2,1)S(1)}, u32[]{:S(2)}, u32[]{:S(2)}) collective-permute-start(s16[528,128]{1,0:T(8,128)(2,1)S(1)} %relay.3), channel_id=1, source_target_pairs={{0,4},{2,14},{4,8},{6,2},{8,12},{10,6},{12,0},{14,10},{1,3},{3,1},... | collective-permute-start | bytes 405512 | tf_op jit(solution)/shard_map/ppermute | solution.py:597
  22.2 3.2 %collective-permute-start.9 = (s16[656,128]{1,0:T(8,128)(2,1)S(1)}, s16[656,128]{1,0:T(8,128)(2,1)S(1)}, u32[]{:S(2)}, u32[]{:S(2)}) collective-permute-start(s16[656,128]{1,0:T(8,128)(2,1)S(1)} %settle.4.rest_0_), channel_id=1, source_target_pairs={{0,1},{1,0},{2,3},{3,2},{4,5},{5,4},{6,7},{7,6},{8,9},{9,8},{10,11... | collective-permute-start | bytes 503816 | tf_op jit(solution)/shard_map/ppermute | solution.py:615
  23.7 1.7 %collective-permute-start.10 = (s16[528,128]{1,0:T(8,128)(2,1)S(1)}, s16[528,128]{1,0:T(8,128)(2,1)S(1)}, u32[]{:S(2)}, u32[]{:S(2)}) collective-permute-start(s16[528,128]{1,0:T(8,128)(2,1)S(1)} %settle.5.rest_1_), channel_id=1, source_target_pairs={{0,1},{1,0},{2,3},{3,2},{4,5},{5,4},{6,7},{7,6},{8,9},{9,8},{10,11... | collective-permute-start | bytes 405512 | tf_op jit(solution)/shard_map/ppermute | solution.py:615
  25.4 1.5 %collective-permute-start.4 = (s16[528,128]{1,0:T(8,128)(2,1)S(1)}, s16[528,128]{1,0:T(8,128)(2,1)S(1)}, u32[]{:S(2)}, u32[]{:S(2)}) collective-permute-start(s16[528,128]{1,0:T(8,128)(2,1)S(1)} %settle.3.rest_2_), channel_id=1, source_target_pairs={{0,1},{1,0},{2,3},{3,2},{4,5},{5,4},{6,7},{7,6},{8,9},{9,8},{10,11... | collective-permute-start | bytes 405512 | tf_op jit(solution)/shard_map/ppermute | solution.py:615

commit v15 on v13

--- a/solution.py
+++ b/solution.py
@@ -471,8 +471,9 @@
             bound = jnp.sqrt(left + own[1, :, at]) * own[2, :, at]
             ratio = (inner + own[0, :, at]) / jnp.maximum(bound, 1.0)
             angle[:, at] = arccos(jnp.clip(ratio, -1.0, 1.0))
-        copies.append(pltpu.make_async_copy(angle, angles, sems.at[units]))
-        copies[-1].start()
+            here = sems.at[units + len(copies) - (span[1] - span[0])]
+            copies.append(pltpu.make_async_copy(angle.at[:, at], angles.at[:, at], here))
+            copies[-1].start()
         for copy in copies:
             copy.wait()
 
@@ -615,7 +616,7 @@
         (observed, others[-1], own, theirs, image),
         [VMEM] * 4 + [HBM],
         [image, shape((lines, cols), f32)],
-        scratch=[pltpu.VMEM((lines, cols), f32), *work, pltpu.SemaphoreType.DMA((units + 1,))],
+        scratch=[pltpu.VMEM((lines, cols), f32), *work, pltpu.SemaphoreType.DMA((units + 2,))],
         out_specs=[HBM] * 2,
         aliases={4: 0},
     )

time: 27.9 us -> 28.6 us (1.025)
  the two profiles are of different devices: /device:TPU:0 before, /device:TPU:1 now
where the time goes in v15:
time: 28.6 us; the launch traced here: 28 us
  starting transfers between devices  14.6 us (51%)
  Pallas kernels  11.4 us (40%)
  waiting for transfers between devices  1.34 us (5%)
  between operations  0.75 us (3%)
    pallas_call x17, Pallas kernels, call(): pl.pallas_call(kernel, in_specs=specs, out_specs=out_specs or [VMEM] * le...  11.4 us
    ppermute x3, starting transfers between devices, on_device(): near.append(lax.ppermute(message, ('line', 'band'), cores(partner, odd_up)))  5.25 us
    ppermute x3, starting transfers between devices, on_device(): others.append(lax.ppermute(messages[i], 'band', swap))  5.03 us
    ppermute x3, starting transfers between devices, on_device(): far.append(lax.ppermute(message, ('line', 'band'), cores(even_up, partner)))  3.88 us
    ppermute x3, waiting for transfers between devices, on_device(): near.append(lax.ppermute(message, ('line', 'band'), cores(partner, odd_up)))  1.18 us
  transfers between devices with their start and end apart: 10, of which 4 were waited for; matrix products, arithmetic and copies ran while one was open for 0% of the time, Pallas kernels for 19%

profile of v15, /device:TPU:1, one launch (start us, length us, event | category | flops | bytes accessed | tf_op | source)
XLA Modules:
  0.0 28.0 jit_solution(14188867549928961000)
XLA Ops:
  0.6 4.6 %fold_other.1 = (f32[13,128,128]{2,1,0:T(8,128)S(1)}, f32[1,128,128]{2,1,0:T(8,128)S(1)}, bf16[115,128,256]{2,1,0:T(8,128)(2,1)S(1)}, f32[13,20]{1,0:T(8,128)S(1...) custom-call(s32[13]{0:T(128)} %start_in.3, s32[3]{0:T(128)} %offsets_in.1, bf16[13,20]{1,0:T(8,128)(2,1)} %values_in.1, ...), custom_call_target="tpu_custom_call" | custom-call | tf_op jit(solution)/shard_map/fold_other/pallas_call | solution.py:37
  5.2 0.4 %collective-permute-start = (f32[13,128,128]{2,1,0:T(8,128)S(1)}, f32[13,128,128]{2,1,0:T(8,128)S(1)}, u32[]{:S(2)}, u32[]{:S(2)}) collective-permute-start(f32[13,128,128]{2,1,0:T(8,128)S(1)} %get-tuple-element.30), channel_id=1, source_target_pairs={{0,1},{1,0},{2,3},{3,2},{4,5},{5,4},{6,7},{7,6},{8,9},{9,8},{10,11... | collective-permute-start | bytes 2555912 | tf_op jit(solution)/shard_map/ppermute | solution.py:559
  5.6 2.0 %fold_own.1.keep = f32[13,128,128]{2,1,0:T(8,128)S(1)} custom-call(s32[13]{0:T(128)} %start_in.3, f32[13,20]{1,0:T(8,128)S(1)} %get-tuple-element.26.wide, bf16[115,128,256]{2,1,0:T(8,128)(2,1)S(1)} %get-tuple-element.27.cube, bf16[512,256]{1,0:T(8,128)(2,1)S(1)} %get-tuple-element.28.table, f32[1,128,128]{2,1,0:T(8,128)S(1)} %get-tuple-element.29.middle), custom_call_target="tpu_custom_call" | custom-call | tf_op jit(solution)/shard_map/fold_own/pallas_call | solution.py:37
  7.7 0.0 collective-permute-done.other
  7.7 0.3 %share.3 = (f32[5,128,128]{2,1,0:T(8,128)S(1)}, s16[656,128]{1,0:T(8,128)(2,1)S(1)}) custom-call(bf16[3,128,128]{2,1,0:T(8,128)(2,1)S(1)} %get-tuple-element.25.picked, f32[13,128,128]{2,1,0:T(8,128)S(1)} %fold_own.1.keep, f32[13,128,128]{2,1,0:T(8,128)S(1)} %collective-permute-done.other), custom_call_target="tpu_custom_call" | custom-call | tf_op jit(solution)/shard_map/share/pallas_call | solution.py:37
  8.0 4.8 %collective-permute-start.4 = (s16[656,128]{1,0:T(8,128)(2,1)S(1)}, s16[656,128]{1,0:T(8,128)(2,1)S(1)}, u32[]{:S(2)}, u32[]{:S(2)}) collective-permute-start(s16[656,128]{1,0:T(8,128)(2,1)S(1)} %get-tuple-element.39), channel_id=1, source_target_pairs={{0,2},{2,0},{4,6},{6,4},{8,10},{10,8},{12,14},{14,12},{5,1},{15,3}... | collective-permute-start | bytes 503816 | tf_op jit(solution)/shard_map/ppermute | solution.py:571
  12.8 0.3 %share.4 = (f32[4,128,128]{2,1,0:T(8,128)S(1)}, s16[528,128]{1,0:T(8,128)(2,1)S(1)}) custom-call(bf16[3,128,128]{2,1,0:T(8,128)(2,1)S(1)} %get-tuple-element.25.picked, f32[13,128,128]{2,1,0:T(8,128)S(1)} %fold_own.1.keep, f32[13,128,128]{2,1,0:T(8,128)S(1)} %collective-permute-done.other), custom_call_target="tpu_custom_call" | custom-call | tf_op jit(solution)/shard_map/share/pallas_call | solution.py:37
  13.1 0.0 copy-start
  13.2 0.2 collective-permute-start.6
  13.4 0.3 %share.5 = (f32[4,128,128]{2,1,0:T(8,128)S(1)}, s16[528,128]{1,0:T(8,128)(2,1)S(1)}) custom-call(bf16[3,128,128]{2,1,0:T(8,128)(2,1)S(1)} %get-tuple-element.25.picked, f32[13,128,128]{2,1,0:T(8,128)S(1)} %fold_own.1.keep, f32[13,128,128]{2,1,0:T(8,128)S(1)} %collective-permute-done.other), custom_call_target="tpu_custom_call" | custom-call | tf_op jit(solution)/shard_map/share/pallas_call | solution.py:37
  13.7 0.2 collective-permute-start.1
  13.9 0.6 %centre.1 = (f32[13,128,128]{2,1,0:T(8,128)S(1)}, f32[13,128,128]{2,1,0:T(8,128)S(1)}) custom-call(bf16[3,128,128]{2,1,0:T(8,128)(2,1)S(1)} %get-tuple-element.25.picked, f32[5,128,128]{2,1,0:T(8,128)S(1)} %get-tuple-element.31.rest_0_, f32[4,128,128]{2,1,0:T(8,128)S(1)} %get-tuple-element.32.rest_1_, f32[4,128,128]{2,1,0:T(8,128)S(1)} %get-tuple-element.33.rest_2_), custom_call_target="tpu_custom_call" | custom-call | tf_op jit(solution)/shard_map/centre/pallas_call | solution.py:37
  14.5 0.7 %collective-permute-done.4.received.near = s16[656,128]{1,0:T(8,128)(2,1)S(1)} collective-permute-done((s16[656,128]{1,0:T(8,128)(2,1)S(1)}, s16[656,128]{1,0:T(8,128)(2,1)S(1)}, u32[]{:S(2)}, u32[]{:S(2)}) %collective-permute-start.4) | collective-permute-done | bytes 167968 | tf_op jit(solution)/shard_map/ppermute | solution.py:571
  15.1 0.1 relay.4
  15.3 1.7 %collective-permute-start.5 = (s16[656,128]{1,0:T(8,128)(2,1)S(1)}, s16[656,128]{1,0:T(8,128)(2,1)S(1)}, u32[]{:S(2)}, u32[]{:S(2)}) collective-permute-start(s16[656,128]{1,0:T(8,128)(2,1)S(1)} %relay.4), channel_id=1, source_target_pairs={{0,4},{2,14},{4,8},{6,2},{8,12},{10,6},{12,0},{14,10},{1,3},{3,1},... | collective-permute-start | bytes 503816 | tf_op jit(solution)/shard_map/ppermute | solution.py:584
  17.0 0.3 %collective-permute-done.6.received.near = s16[528,128]{1,0:T(8,128)(2,1)S(1)} collective-permute-done((s16[528,128]{1,0:T(8,128)(2,1)S(1)}, s16[528,128]{1,0:T(8,128)(2,1)S(1)}, u32[]{:S(2)}, u32[]{:S(2)}) %collective-permute-start.6) | collective-permute-done | bytes 135200 | tf_op jit(solution)/shard_map/ppermute | solution.py:571
  17.4 0.1 relay.5
  17.5 1.0 %collective-permute-start.7 = (s16[528,128]{1,0:T(8,128)(2,1)S(1)}, s16[528,128]{1,0:T(8,128)(2,1)S(1)}, u32[]{:S(2)}, u32[]{:S(2)}) collective-permute-start(s16[528,128]{1,0:T(8,128)(2,1)S(1)} %relay.5), channel_id=1, source_target_pairs={{0,4},{2,14},{4,8},{6,2},{8,12},{10,6},{12,0},{14,10},{1,3},{3,1},... | collective-permute-start | bytes 405512 | tf_op jit(solution)/shard_map/ppermute | solution.py:584
  18.5 0.2 collective-permute-done.1.received.near
  18.7 0.1 relay.3
  18.8 1.2 %collective-permute-start.2 = (s16[528,128]{1,0:T(8,128)(2,1)S(1)}, s16[528,128]{1,0:T(8,128)(2,1)S(1)}, u32[]{:S(2)}, u32[]{:S(2)}) collective-permute-start(s16[528,128]{1,0:T(8,128)(2,1)S(1)} %relay.3), channel_id=1, source_target_pairs={{0,4},{2,14},{4,8},{6,2},{8,12},{10,6},{12,0},{14,10},{1,3},{3,1},... | collective-permute-start | bytes 405512 | tf_op jit(solution)/shard_map/ppermute | solution.py:584
  20.0 0.1 collective-permute-done.5.received
  20.1 0.2 settle.4.rest_0_
  20.2 2.2 %collective-permute-start.8 = (s16[656,128]{1,0:T(8,128)(2,1)S(1)}, s16[656,128]{1,0:T(8,128)(2,1)S(1)}, u32[]{:S(2)}, u32[]{:S(2)}) collective-permute-start(s16[656,128]{1,0:T(8,128)(2,1)S(1)} %settle.4.rest_0_), channel_id=1, source_target_pairs={{0,1},{1,0},{2,3},{3,2},{4,5},{5,4},{6,7},{7,6},{8,9},{9,8},{10,11... | collective-permute-start | bytes 503816 | tf_op jit(solution)/shard_map/ppermute | solution.py:602
  22.5 0.0 collective-permute-done.7.received
  22.5 0.1 settle.5.rest_1_
  22.6 1.3 %collective-permute-start.9 = (s16[528,128]{1,0:T(8,128)(2,1)S(1)}, s16[528,128]{1,0:T(8,128)(2,1)S(1)}, u32[]{:S(2)}, u32[]{:S(2)}) collective-permute-start(s16[528,128]{1,0:T(8,128)(2,1)S(1)} %settle.5.rest_1_), channel_id=1, source_target_pairs={{0,1},{1,0},{2,3},{3,2},{4,5},{5,4},{6,7},{7,6},{8,9},{9,8},{10,11... | collective-permute-start | bytes 405512 | tf_op jit(solution)/shard_map/ppermute | solution.py:602
  23.9 0.0 collective-permute-done.2.received
  23.9 0.1 settle.3.rest_2_
  24.1 1.5 %collective-permute-start.3 = (s16[528,128]{1,0:T(8,128)(2,1)S(1)}, s16[528,128]{1,0:T(8,128)(2,1)S(1)}, u32[]{:S(2)}, u32[]{:S(2)}) collective-permute-start(s16[528,128]{1,0:T(8,128)(2,1)S(1)} %settle.3.rest_2_), channel_id=1, source_target_pairs={{0,1},{1,0},{2,3},{3,2},{4,5},{5,4},{6,7},{7,6},{8,9},{9,8},{10,11... | collective-permute-start | bytes 405512 | tf_op jit(solution)/shard_map/ppermute | solution.py:602
  25.6 1.3 %finish_most.1 = (f32[13,128,256]{2,1,0:T(8,128)}, f32[3,128,256]{2,1,0:T(8,128)S(1)}, f32[3,128,256]{2,1,0:T(8,128)S(1)}) custom-call(bf16[13,128,256]{2,1,0:T(8,128)(2,1)S(1)} %copy-done, s16[656,128]{1,0:T(8,128)(2,1)S(1)} %settle.4.rest_0_, s16[528,128]{1,0:T(8,128)(2,1)S(1)} %settle.5.rest_1_, s16[528,128]{1,0:T(8,128)(2,1)S(1)} %settle.3.rest_2_, ...), custom_call_target="tpu_custom_call" | custom-call | tf_op jit(solution)/shard_map/finish_most/pallas_call | solution.py:37
  27.0 1.1 %finish_last.1 = (f32[13,128,256]{2,1,0:T(8,128)}, f32[128,256]{1,0:T(8,128)}) custom-call(bf16[13,128,256]{2,1,0:T(8,128)(2,1)S(1)} %copy-done, s16[528,128]{1,0:T(8,128)(2,1)S(1)} %collective-permute-done.3.message, f32[3,128,256]{2,1,0:T(8,128)S(1)} %get-tuple-element.45.own, ...), custom_call_target="tpu_custom_call", output_to_operand_aliasing={{0}: (4, {})} | custom-call | tf_op jit(solution)/shard_map/finish_last/pallas_call | solution.py:37
  (7 shorter events, 0.0 us)
Async XLA Ops:
  5.2 2.4 %collective-permute-start = (f32[13,128,128]{2,1,0:T(8,128)S(1)}, f32[13,128,128]{2,1,0:T(8,128)S(1)}, u32[]{:S(2)}, u32[]{:S(2)}) collective-permute-start(f32[13,128,128]{2,1,0:T(8,128)S(1)} %get-tuple-element.30), channel_id=1, source_target_pairs={{0,1},{1,0},{2,3},{3,2},{4,5},{5,4},{6,7},{7,6},{8,9},{9,8},{10,11... | collective-permute-start | bytes 2555912 | tf_op jit(solution)/shard_map/ppermute | solution.py:559
  8.0 7.1 %collective-permute-start.4 = (s16[656,128]{1,0:T(8,128)(2,1)S(1)}, s16[656,128]{1,0:T(8,128)(2,1)S(1)}, u32[]{:S(2)}, u32[]{:S(2)}) collective-permute-start(s16[656,128]{1,0:T(8,128)(2,1)S(1)} %get-tuple-element.39), channel_id=1, source_target_pairs={{0,2},{2,0},{4,6},{6,4},{8,10},{10,8},{12,14},{14,12},{5,1},{15,3}... | collective-permute-start | bytes 503816 | tf_op jit(solution)/shard_map/ppermute | solution.py:571
  13.1 12.4 %copy-start = (bf16[13,128,256]{2,1,0:T(8,128)(2,1)S(1)}, bf16[13,128,256]{2,1,0:T(8,128)(2,1)}, u32[]{:S(2)}) copy-start(bf16[13,128,256]{2,1,0:T(8,128)(2,1)} %observed.3) | copy-start | bytes 2555908
  13.2 4.2 %collective-permute-start.6 = (s16[528,128]{1,0:T(8,128)(2,1)S(1)}, s16[528,128]{1,0:T(8,128)(2,1)S(1)}, u32[]{:S(2)}, u32[]{:S(2)}) collective-permute-start(s16[528,128]{1,0:T(8,128)(2,1)S(1)} %get-tuple-element.42), channel_id=1, source_target_pairs={{0,2},{2,0},{4,6},{6,4},{8,10},{10,8},{12,14},{14,12},{5,1},{15,3}... | collective-permute-start | bytes 405512 | tf_op jit(solution)/shard_map/ppermute | solution.py:571
  13.7 5.0 %collective-permute-start.1 = (s16[528,128]{1,0:T(8,128)(2,1)S(1)}, s16[528,128]{1,0:T(8,128)(2,1)S(1)}, u32[]{:S(2)}, u32[]{:S(2)}) collective-permute-start(s16[528,128]{1,0:T(8,128)(2,1)S(1)} %get-tuple-element.36), channel_id=1, source_target_pairs={{0,2},{2,0},{4,6},{6,4},{8,10},{10,8},{12,14},{14,12},{5,1},{15,3}... | collective-permute-start | bytes 405512 | tf_op jit(solution)/shard_map/ppermute | solution.py:571
  15.3 4.8 %collective-permute-start.5 = (s16[656,128]{1,0:T(8,128)(2,1)S(1)}, s16[656,128]{1,0:T(8,128)(2,1)S(1)}, u32[]{:S(2)}, u32[]{:S(2)}) collective-permute-start(s16[656,128]{1,0:T(8,128)(2,1)S(1)} %relay.4), channel_id=1, source_target_pairs={{0,4},{2,14},{4,8},{6,2},{8,12},{10,6},{12,0},{14,10},{1,3},{3,1},... | collective-permute-start | bytes 503816 | tf_op jit(solution)/shard_map/ppermute | solution.py:584
  17.5 5.0 %collective-permute-start.7 = (s16[528,128]{1,0:T(8,128)(2,1)S(1)}, s16[528,128]{1,0:T(8,128)(2,1)S(1)}, u32[]{:S(2)}, u32[]{:S(2)}) collective-permute-start(s16[528,128]{1,0:T(8,128)(2,1)S(1)} %relay.5), channel_id=1, source_target_pairs={{0,4},{2,14},{4,8},{6,2},{8,12},{10,6},{12,0},{14,10},{1,3},{3,1},... | collective-permute-start | bytes 405512 | tf_op jit(solution)/shard_map/ppermute | solution.py:584
  18.8 5.2 %collective-permute-start.2 = (s16[528,128]{1,0:T(8,128)(2,1)S(1)}, s16[528,128]{1,0:T(8,128)(2,1)S(1)}, u32[]{:S(2)}, u32[]{:S(2)}) collective-permute-start(s16[528,128]{1,0:T(8,128)(2,1)S(1)} %relay.3), channel_id=1, source_target_pairs={{0,4},{2,14},{4,8},{6,2},{8,12},{10,6},{12,0},{14,10},{1,3},{3,1},... | collective-permute-start | bytes 405512 | tf_op jit(solution)/shard_map/ppermute | solution.py:584
  20.2 5.3 %collective-permute-start.8 = (s16[656,128]{1,0:T(8,128)(2,1)S(1)}, s16[656,128]{1,0:T(8,128)(2,1)S(1)}, u32[]{:S(2)}, u32[]{:S(2)}) collective-permute-start(s16[656,128]{1,0:T(8,128)(2,1)S(1)} %settle.4.rest_0_), channel_id=1, source_target_pairs={{0,1},{1,0},{2,3},{3,2},{4,5},{5,4},{6,7},{7,6},{8,9},{9,8},{10,11... | collective-permute-start | bytes 503816 | tf_op jit(solution)/shard_map/ppermute | solution.py:602
  22.6 3.0 %collective-permute-start.9 = (s16[528,128]{1,0:T(8,128)(2,1)S(1)}, s16[528,128]{1,0:T(8,128)(2,1)S(1)}, u32[]{:S(2)}, u32[]{:S(2)}) collective-permute-start(s16[528,128]{1,0:T(8,128)(2,1)S(1)} %settle.5.rest_1_), channel_id=1, source_target_pairs={{0,1},{1,0},{2,3},{3,2},{4,5},{5,4},{6,7},{7,6},{8,9},{9,8},{10,11... | collective-permute-start | bytes 405512 | tf_op jit(solution)/shard_map/ppermute | solution.py:602
  24.1 2.9 %collective-permute-start.3 = (s16[528,128]{1,0:T(8,128)(2,1)S(1)}, s16[528,128]{1,0:T(8,128)(2,1)S(1)}, u32[]{:S(2)}, u32[]{:S(2)}) collective-permute-start(s16[528,128]{1,0:T(8,128)(2,1)S(1)} %settle.3.rest_2_), channel_id=1, source_target_pairs={{0,1},{1,0},{2,3},{3,2},{4,5},{5,4},{6,7},{7,6},{8,9},{9,8},{10,11... | collective-permute-start | bytes 405512 | tf_op jit(solution)/shard_map/ppermute | solution.py:602
